TPU v7x, 32 devices: a whole 2x2x4 slice. The times are simulated.
32 devices in a mesh: slide: 2 (over x), col: 16 (over z, y, core).
Axes of the slice: x: 2, y: 2, z: 4, core: 2. Of those that a mesh axis runs over, the one named last changes fastest.
Arguments:
- patches: bfloat16 [256, 128, 512], P(('slide', 'col')), parts along dimension 0, may hold values from -6 to 6
- tissue: int32 [256, 128], P(('slide', 'col')), parts along dimension 0, may hold values from 0 to 1, as said below
- w_query: bfloat16 [512, 512], replicated, may hold values from -0.25 to 0.25
- w_key: bfloat16 [512, 512], replicated, may hold values from -0.25 to 0.25
- w_value: bfloat16 [512, 512], replicated, may hold values from -0.25 to 0.25
- w_out: bfloat16 [512, 512], replicated, may hold values from -0.25 to 0.25
- agent_tokens: bfloat16 [256, 512], replicated, may hold values from -100 to 100
- kernel_seven: float32 [7, 7, 512], replicated, may hold values from -0.875 to 0.875
- kernel_five: float32 [5, 5, 512], replicated, may hold values from -1.25 to 1.25
- kernel_three: float32 [3, 3, 512], replicated, may hold values from -2 to 2
Outputs:
- mixed: bfloat16 [256, 128, 512], P(('slide', 'col')), parts along dimension 0
There are 2 independent parts, one for each index of `slide`. A program takes and returns all parts, laid end to end along the dimension named above; an argument that names none is the same for every part. Nothing has to cross between parts.
Inputs may be any that keep to these rules, and one draw needn't show every extreme that they name: tissue holds 0 or 1; each slide has at least one tissue patch.
All inputs are finite; a program needn't handle non-finite values.
Results may differ from a plain program's by a relative error of at most 0.007.
The roundings to bfloat16 on the way count: a program that leaves them out, or rounds other values in their place, can miss the bound.
Values may be sent and summed in bfloat16 or wider, within the bound.
No kernel may reach another device: no remote copies, remote signals or barrier semaphores. Data moves between devices by JAX's collectives and lax.ppermute only.
A program may use at most 128 MiB of HBM per device.

v0:
```python
import jax
import jax.numpy as jnp
from jax import lax
from jax.sharding import PartitionSpec as P

HEADS = 8


def with_halo(x, sides, width):
    for axis, dim in sides:
        peers, length = (lax.axis_size(axis), x.shape[dim])
        up = [(i, (i + 1) % peers) for i in range(peers - 1)]
        down = [(j, i) for i, j in up]
        last = lax.slice_in_dim(x, length - width, length, axis=dim)
        leading = lax.slice_in_dim(x, 0, width, axis=dim)
        before = lax.ppermute(last, axis, up)
        after = lax.ppermute(leading, axis, down)
        x = jnp.concatenate([before, x, after], axis=dim)
    return x


def joined_kernel(kernel_seven, kernel_five, kernel_three):
    merged = kernel_seven + jnp.pad(kernel_five, ((1, 1), (1, 1), (0, 0)))
    return merged + jnp.pad(kernel_three, ((2, 2), (2, 2), (0, 0)))


def depthwise(extended, kernel, out_rows, grid_width):
    padded = jnp.pad(extended.astype(jnp.float32), ((0, 0), (3, 3), (0, 0)))
    total = jnp.zeros((out_rows, grid_width, kernel.shape[2]), jnp.float32)
    for row_tap in range(7):
        for col_tap in range(7):
            total = (
                total
                + padded[row_tap : row_tap + out_rows, col_tap : col_tap + grid_width]
                * kernel[row_tap, col_tap]
            )
    return total


def rim_terms(rim, kernel, grid_width, lower_side):
    padded = jnp.pad(rim.astype(jnp.float32), ((0, 0), (3, 3), (0, 0)))
    out_list = []
    for out_row in range(3):
        total = jnp.zeros((grid_width, kernel.shape[2]), jnp.float32)
        for rim_row in range(3):
            row_tap = 6 + rim_row - out_row if lower_side else rim_row - out_row
            if 0 <= row_tap <= 6:
                for col_tap in range(7):
                    total = (
                        total
                        + padded[rim_row, col_tap : col_tap + grid_width] * kernel[row_tap, col_tap]
                    )
        out_list.append(total)
    return jnp.stack(out_list)


def on_device(
    patches,
    tissue,
    w_query,
    w_key,
    w_value,
    w_out,
    agent_tokens,
    kernel_seven,
    kernel_five,
    kernel_three,
):
    band_rows, grid_width, model_dim = patches.shape
    head_dim = model_dim // HEADS
    score_scale = head_dim ** (-0.5)
    flat_tokens = patches.reshape(band_rows * grid_width, model_dim)
    queries = jnp.dot(flat_tokens, w_query, preferred_element_type=jnp.float32).astype(jnp.bfloat16)
    keys_all = jnp.dot(flat_tokens, w_key, preferred_element_type=jnp.float32).astype(jnp.bfloat16)
    values_all = jnp.dot(flat_tokens, w_value, preferred_element_type=jnp.float32).astype(
        jnp.bfloat16
    )
    tissue_flat = tissue.reshape(-1) > 0
    kernel = joined_kernel(kernel_seven, kernel_five, kernel_three)
    peak_list = []
    total_list = []
    weighted_list = []
    for head_index in range(HEADS):
        lower = head_index * head_dim
        agent_head = agent_tokens[:, lower : lower + head_dim]
        scores = (
            lax.dot_general(
                agent_head,
                keys_all[:, lower : lower + head_dim],
                (((1,), (1,)), ((), ())),
                preferred_element_type=jnp.float32,
            )
            * score_scale
        )
        peak_head = jnp.max(jnp.where(tissue_flat[None, :], scores, -1e30), axis=1)
        expo = jnp.where(
            tissue_flat[None, :], jnp.exp(scores - peak_head[:, None]), jnp.float32(0.0)
        )
        total_list.append(jnp.sum(expo, axis=1))
        peak_list.append(peak_head)
        weighted_list.append(
            jnp.dot(
                expo.astype(jnp.bfloat16),
                values_all[:, lower : lower + head_dim],
                preferred_element_type=jnp.float32,
            )
        )
    band_peak = jnp.stack(peak_list)
    band_total = jnp.stack(total_list)
    band_weighted = jnp.stack(weighted_list)
    peak = lax.pmax(band_peak, "col")
    factor = jnp.exp(band_peak - peak)
    totals, weighted = lax.psum((band_total * factor, band_weighted * factor[..., None]), "col")
    agent_values = (weighted / totals[..., None]).astype(jnp.bfloat16)
    attended_list = []
    for head_index in range(HEADS):
        lower = head_index * head_dim
        agent_head = agent_tokens[:, lower : lower + head_dim]
        scores = (
            lax.dot_general(
                queries[:, lower : lower + head_dim],
                agent_head,
                (((1,), (1,)), ((), ())),
                preferred_element_type=jnp.float32,
            )
            * score_scale
        )
        top_score = jnp.max(scores, axis=1, keepdims=True)
        expo = jnp.exp(scores - top_score)
        token_weights = (expo / jnp.sum(expo, axis=1, keepdims=True)).astype(jnp.bfloat16)
        attended_list.append(
            jnp.dot(token_weights, agent_values[head_index], preferred_element_type=jnp.float32)
        )
    attended = jnp.concatenate(attended_list, axis=1).reshape(band_rows, grid_width, model_dim)
    value_grid = values_all.reshape(band_rows, grid_width, model_dim)
    blank_rows = jnp.zeros((3, grid_width, model_dim), jnp.bfloat16)
    local_ext = jnp.concatenate([blank_rows, value_grid, blank_rows], axis=0)
    position = depthwise(local_ext, kernel, band_rows, grid_width)
    extended = with_halo(value_grid, (("col", 0),), 3)
    upper_terms = rim_terms(extended[:3], kernel, grid_width, False)
    lower_terms = rim_terms(extended[-3:], kernel, grid_width, True)
    position = position.at[:3].add(upper_terms)
    position = position.at[band_rows - 3 :].add(lower_terms)
    blended = (attended + position).astype(jnp.bfloat16).reshape(band_rows * grid_width, model_dim)
    mixed = jnp.dot(blended, w_out, preferred_element_type=jnp.float32).astype(jnp.bfloat16)
    return mixed.reshape(band_rows, grid_width, model_dim)


def solution(mesh):
    return jax.shard_map(
        on_device,
        mesh=mesh,
        in_specs=(
            P(("slide", "col"), None, None),
            P(("slide", "col"), None),
            P(),
            P(),
            P(),
            P(),
            P(),
            P(),
            P(),
            P(),
        ),
        out_specs=P(("slide", "col"), None, None),
        check_vma=False,
    )
```

profile of v0, /device:TPU:0, one launch (start us, length us, event | category | flops | bytes accessed | tf_op | source)
XLA Modules:
  0.0 210.2 jit_solution(6135621556300776777)
XLA Ops:
  6.5 1.2 copy-done
  7.8 1.8 convolution_convert_fusion.2
  11.5 0.8 convolution_convert_fusion.1
  13.2 1.1 fusion.93
  16.2 1.5 fusion.91
  18.5 35.4 %pmax.7 = f32[8,256]{1,0:T(8,128)S(1)} all-reduce(f32[8,256]{1,0:T(8,128)S(1)} %stack.110), channel_id=1, replica_groups=mesh['slide'=2,'col'=16] {'col'}, use_global_device_ids=true, to_apply=%region_10.11 | all-reduce | flops 2048 | bytes 16384 | tf_op jit(solution)/shard_map/pmax | solution.py:111
  54.0 0.8 broadcast_multiply_fusion
  55.0 0.9 copy.28
  55.9 2.1 collective-permute-start
  58.2 1.3 collective-permute-start.1
  59.5 1.8 convolution_convert_fusion.3
  61.3 1.8 fusion.237
  63.1 1.9 fusion.238
  65.0 1.8 fusion.239
  66.9 2.0 fusion.240
  68.9 1.8 fusion.241
  70.7 0.9 fusion.242
  71.6 1.9 fusion.243
  73.6 1.9 fusion.244
  75.5 1.5 copy.40
  77.0 1.0 pad_add_fusion
  79.9 31.3 %psum.15 = f32[8,256]{1,0:T(8,128)S(1)} all-reduce(f32[8,256]{1,0:T(8,128)S(1)} %get-tuple-element.45), channel_id=1, replica_groups=mesh['slide'=2,'col'=16] {'col'}, use_global_device_ids=true, to_apply=%region_20.21 | all-reduce | flops 2048 | bytes 16384 | tf_op jit(solution)/shard_map/psum | solution.py:113
  111.3 2.1 %fusion.71 = f32[1024]{0:T(1024)} fusion(f32[1024,256]{0,1:T(8,128)} %get-tuple-element.103, f32[1024]{0:T(1024)} %get-tuple-element.102), kind=kLoop, calls=%fused_computation.163 | loop fusion | flops 523264 | bytes 1056768 | tf_op jit(solution)/shard_map/reduce_sum | solution.py:130
  113.5 2.0 fusion.72
  115.5 0.8 fusion.73
  116.2 0.8 fusion.74
  117.0 0.8 fusion.75
  117.7 0.8 fusion.76
  118.6 2.1 maximum_convert_fusion
  120.6 53.5 %fusion.3 = f32[8,128,512]{2,1,0:T(8,128)S(1)} fusion(f32[14,128,512]{2,1,0:T(8,128)} %maximum_convert_fusion, f32[512]{0:T(512)S(1)} %bitcast.145, f32[512]{0:T(512)S(1)} %bitcast.148, f32[512]{0:T(512)} %bitcast.151, f32[512]{0:T(512)} %bitcast.154, f32[512]{0:T(512)} %bitcast.157, f32[512]{0:T(512)} %bitcast.160, f32[512]{0:T(512)} %bitcast.163, ...), kind=kLoop, calls=%fused_computation.4 | loop fusion | flops 50855936 | bytes 20547584 | tf_op jit(solution)/shard_map/add | solution.py:33
  174.2 2.0 fusion.77
  176.2 2.0 fusion.78
  178.1 1.1 divide_convert_fusion.16
  179.3 2.4 %convolution_dynamic-update-slice_fusion.7 = f32[1024,512]{0,1:T(8,128)} fusion(f32[1024,256]{0,1:T(8,128)} %get-tuple-element.103, f32[1024]{0:T(1024)} %fusion.71, f32[1024]{0:T(1024)} %get-tuple-element.102, bf16[8,256,64]{1,2,0:T(8,128)(2,1)S(1)} %divide_convert_fusion.16), kind=kOutput, calls=%fused_computation.114 | convolution fusion | flops 34340864 | bytes 1351680 | tf_op jit(solution)/shard_map/dot_general | solution.py:132
  181.6 1.0 convolution_dynamic-update-slice_fusion.6
  182.9 1.0 convolution_dynamic-update-slice_fusion.5
  184.1 1.0 convolution_dynamic-update-slice_fusion.4
  185.3 1.0 convolution_dynamic-update-slice_fusion.3
  186.6 1.0 convolution_dynamic-update-slice_fusion.2
  187.8 1.0 convolution_dynamic-update-slice_fusion.1
  189.0 1.0 convolution_dynamic-update-slice_fusion
  190.0 2.9 %copy.39 = f32[1024,512]{1,0:T(8,128)} copy(f32[1024,512]{0,1:T(8,128)} %convolution_dynamic-update-slice_fusion) | data formatting | bytes 4194304 | tf_op jit(solution)/shard_map/reshape | solution.py:134
  193.1 1.1 convert_element_type.81
  194.4 1.4 fusion.165
  196.5 1.1 convert_element_type.82
  197.8 0.7 fusion.178
  199.5 1.1 copy-done.1
  201.7 1.7 convolution_convert_fusion
  (175 shorter events, 11.7 us)
Async XLA Ops:
  6.5 3.0 %copy-start.2 = (bf16[256,512]{1,0:T(8,128)(2,1)S(1)}, bf16[256,512]{1,0:T(8,128)(2,1)}, u32[]{:S(2)}) copy-start(bf16[256,512]{1,0:T(8,128)(2,1)} %param.20) | copy-start | bytes 786436
  6.5 171.6 %all-reduce.7.cloned.1.call-start = ((), (), s32[]{:S(2)}) async-start(), calls=%async_computation | async-start | bytes 1048576 | tf_op jit(solution)/shard_map/psum | solution.py:113
  12.3 42.6 %copy-start.14 = (bf16[1024,512]{0,1:T(8,128)(2,1)}, bf16[1024,512]{0,1:T(8,128)(2,1)S(1)}, u32[]{:S(2)}) copy-start(bf16[1024,512]{0,1:T(8,128)(2,1)S(1)} %convolution_convert_fusion.1) | copy-start | bytes 3145732
  55.9 137.2 %collective-permute-start = (bf16[3,128,512]{2,1,0:T(8,128)(2,1)}, bf16[3,128,512]{2,1,0:T(8,128)(2,1)}, u32[]{:S(2)}, u32[]{:S(2)}) collective-permute-start(bf16[3,128,512]{2,1,0:T(8,128)(2,1)} %bitcast.85), channel_id=1, source_target_pairs={{0,1},{1,2},{2,3},{3,4},{4,5},{5,6},{6,7},{7,8},{8,9},{9,10},{10,1... | collective-permute-start | bytes 1179656 | tf_op jit(solution)/shard_map/ppermute | solution.py:16
  58.2 138.3 %collective-permute-start.1 = (bf16[3,128,512]{2,1,0:T(8,128)(2,1)S(1)}, bf16[3,128,512]{2,1,0:T(8,128)(2,1)}, u32[]{:S(2)}, u32[]{:S(2)}) collective-permute-start(bf16[3,128,512]{2,1,0:T(8,128)(2,1)S(1)} %bitcast.144), channel_id=1, source_target_pairs={{1,0},{2,1},{3,2},{4,3},{5,4},{6,5},{7,6},{8,7},{9,8},{10,9},{11,1... | collective-permute-start | bytes 1179656 | tf_op jit(solution)/shard_map/ppermute | solution.py:17
  71.6 46.1 %copy-start.5 = (f32[1024,256]{0,1:T(8,128)}, f32[1024,256]{0,1:T(8,128)S(1)}, u32[]{:S(2)}) copy-start(f32[1024,256]{0,1:T(8,128)S(1)} %get-tuple-element.115) | copy-start | bytes 3145732
  111.3 4.2 %copy-start.11 = (f32[1024,256]{0,1:T(8,128)S(1)}, f32[1024,256]{0,1:T(8,128)}, u32[]{:S(2)}) copy-start(f32[1024,256]{0,1:T(8,128)} %get-tuple-element.109) | copy-start | bytes 3145732
  111.3 4.2 %copy-start.58 = (f32[1024]{0:T(1024)S(1)}, f32[1024]{0:T(1024)}, u32[]{:S(2)}) copy-start(f32[1024]{0:T(1024)} %get-tuple-element.108) | copy-start | bytes 12292
  111.3 4.9 %copy-start.9 = (f32[1024,256]{0,1:T(8,128)S(1)}, f32[1024,256]{0,1:T(8,128)}, u32[]{:S(2)}) copy-start(f32[1024,256]{0,1:T(8,128)} %get-tuple-element.111) | copy-start | bytes 3145732
  111.3 4.9 %copy-start.56 = (f32[1024]{0:T(1024)S(1)}, f32[1024]{0:T(1024)}, u32[]{:S(2)}) copy-start(f32[1024]{0:T(1024)} %get-tuple-element.110) | copy-start | bytes 12292
  111.3 5.7 %copy-start.7 = (f32[1024,256]{0,1:T(8,128)S(1)}, f32[1024,256]{0,1:T(8,128)}, u32[]{:S(2)}) copy-start(f32[1024,256]{0,1:T(8,128)} %get-tuple-element.113) | copy-start | bytes 3145732
  111.3 5.7 %copy-start.54 = (f32[1024]{0:T(1024)S(1)}, f32[1024]{0:T(1024)}, u32[]{:S(2)}) copy-start(f32[1024]{0:T(1024)} %get-tuple-element.112) | copy-start | bytes 12292
  113.5 4.3 %copy-start.52 = (f32[1024]{0:T(1024)S(1)}, f32[1024]{0:T(1024)}, u32[]{:S(2)}) copy-start(f32[1024]{0:T(1024)} %get-tuple-element.114) | copy-start | bytes 12292
  179.2 2.4 %copy-start.13 = (f32[1024,256]{0,1:T(8,128)S(1)}, f32[1024,256]{0,1:T(8,128)}, u32[]{:S(2)}) copy-start(f32[1024,256]{0,1:T(8,128)} %get-tuple-element.107) | copy-start | bytes 3145732
  179.2 2.4 %copy-start.60 = (f32[1024]{0:T(1024)S(1)}, f32[1024]{0:T(1024)}, u32[]{:S(2)}) copy-start(f32[1024]{0:T(1024)} %get-tuple-element.106) | copy-start | bytes 12292
  193.0 2.8 %copy-start.29 = (f32[1,1,512]{2,1,0:T(1,128)S(1)}, f32[1,1,512]{2,1,0:T(1,128)}, u32[]{:S(2)}) copy-start(f32[1,1,512]{2,1,0:T(1,128)} %get-tuple-element.53) | copy-start | bytes 6148
  193.0 2.9 %copy-start.30 = (f32[1,1,512]{2,1,0:T(1,128)S(1)}, f32[1,1,512]{2,1,0:T(1,128)}, u32[]{:S(2)}) copy-start(f32[1,1,512]{2,1,0:T(1,128)} %get-tuple-element.72) | copy-start | bytes 6148
  193.0 2.9 %copy-start.31 = (f32[1,1,512]{2,1,0:T(1,128)S(1)}, f32[1,1,512]{2,1,0:T(1,128)}, u32[]{:S(2)}) copy-start(f32[1,1,512]{2,1,0:T(1,128)} %get-tuple-element.90) | copy-start | bytes 6148
  193.0 2.9 %copy-start.32 = (f32[1,1,512]{2,1,0:T(1,128)S(1)}, f32[1,1,512]{2,1,0:T(1,128)}, u32[]{:S(2)}) copy-start(f32[1,1,512]{2,1,0:T(1,128)} %get-tuple-element.91) | copy-start | bytes 6148
  193.0 2.9 %copy-start.33 = (f32[1,1,512]{2,1,0:T(1,128)S(1)}, f32[1,1,512]{2,1,0:T(1,128)}, u32[]{:S(2)}) copy-start(f32[1,1,512]{2,1,0:T(1,128)} %get-tuple-element.92) | copy-start | bytes 6148
  193.0 2.9 %copy-start.34 = (f32[1,1,512]{2,1,0:T(1,128)S(1)}, f32[1,1,512]{2,1,0:T(1,128)}, u32[]{:S(2)}) copy-start(f32[1,1,512]{2,1,0:T(1,128)} %get-tuple-element.93) | copy-start | bytes 6148
  193.0 2.9 %copy-start.35 = (f32[1,1,512]{2,1,0:T(1,128)S(1)}, f32[1,1,512]{2,1,0:T(1,128)}, u32[]{:S(2)}) copy-start(f32[1,1,512]{2,1,0:T(1,128)} %get-tuple-element.94) | copy-start | bytes 6148
  193.0 2.9 %copy-start.36 = (f32[1,1,512]{2,1,0:T(1,128)S(1)}, f32[1,1,512]{2,1,0:T(1,128)}, u32[]{:S(2)}) copy-start(f32[1,1,512]{2,1,0:T(1,128)} %get-tuple-element.95) | copy-start | bytes 6148
  193.0 2.9 %copy-start.37 = (f32[1,1,512]{2,1,0:T(1,128)S(1)}, f32[1,1,512]{2,1,0:T(1,128)}, u32[]{:S(2)}) copy-start(f32[1,1,512]{2,1,0:T(1,128)} %get-tuple-element.96) | copy-start | bytes 6148
  193.0 2.9 %copy-start.38 = (f32[1,1,512]{2,1,0:T(1,128)S(1)}, f32[1,1,512]{2,1,0:T(1,128)}, u32[]{:S(2)}) copy-start(f32[1,1,512]{2,1,0:T(1,128)} %get-tuple-element.97) | copy-start | bytes 6148
  193.1 2.9 %copy-start.39 = (f32[1,1,512]{2,1,0:T(1,128)S(1)}, f32[1,1,512]{2,1,0:T(1,128)}, u32[]{:S(2)}) copy-start(f32[1,1,512]{2,1,0:T(1,128)} %get-tuple-element.98) | copy-start | bytes 6148
  193.1 2.9 %copy-start.40 = (f32[1,1,512]{2,1,0:T(1,128)S(1)}, f32[1,1,512]{2,1,0:T(1,128)}, u32[]{:S(2)}) copy-start(f32[1,1,512]{2,1,0:T(1,128)} %get-tuple-element.99) | copy-start | bytes 6148
  193.1 2.9 %copy-start.41 = (f32[1,1,512]{2,1,0:T(1,128)S(1)}, f32[1,1,512]{2,1,0:T(1,128)}, u32[]{:S(2)}) copy-start(f32[1,1,512]{2,1,0:T(1,128)} %get-tuple-element.100) | copy-start | bytes 6148
  193.1 2.9 %copy-start.42 = (f32[1,1,512]{2,1,0:T(1,128)S(1)}, f32[1,1,512]{2,1,0:T(1,128)}, u32[]{:S(2)}) copy-start(f32[1,1,512]{2,1,0:T(1,128)} %get-tuple-element.101) | copy-start | bytes 6148
  194.2 3.4 %copy-start.17 = (f32[1,1,512]{2,1,0:T(1,128)S(1)}, f32[1,1,512]{2,1,0:T(1,128)}, u32[]{:S(2)}) copy-start(f32[1,1,512]{2,1,0:T(1,128)} %get-tuple-element.56) | copy-start | bytes 6148
  194.2 3.4 %copy-start.18 = (f32[1,1,512]{2,1,0:T(1,128)S(1)}, f32[1,1,512]{2,1,0:T(1,128)}, u32[]{:S(2)}) copy-start(f32[1,1,512]{2,1,0:T(1,128)} %get-tuple-element.57) | copy-start | bytes 6148
  194.2 3.4 %copy-start.19 = (f32[1,1,512]{2,1,0:T(1,128)S(1)}, f32[1,1,512]{2,1,0:T(1,128)}, u32[]{:S(2)}) copy-start(f32[1,1,512]{2,1,0:T(1,128)} %get-tuple-element.58) | copy-start | bytes 6148
  194.2 3.4 %copy-start.20 = (f32[1,1,512]{2,1,0:T(1,128)S(1)}, f32[1,1,512]{2,1,0:T(1,128)}, u32[]{:S(2)}) copy-start(f32[1,1,512]{2,1,0:T(1,128)} %get-tuple-element.59) | copy-start | bytes 6148
  194.2 3.4 %copy-start.21 = (f32[1,1,512]{2,1,0:T(1,128)S(1)}, f32[1,1,512]{2,1,0:T(1,128)}, u32[]{:S(2)}) copy-start(f32[1,1,512]{2,1,0:T(1,128)} %get-tuple-element.60) | copy-start | bytes 6148
  194.2 3.4 %copy-start.22 = (f32[1,1,512]{2,1,0:T(1,128)S(1)}, f32[1,1,512]{2,1,0:T(1,128)}, u32[]{:S(2)}) copy-start(f32[1,1,512]{2,1,0:T(1,128)} %get-tuple-element.61) | copy-start | bytes 6148
  194.2 3.4 %copy-start.23 = (f32[1,1,512]{2,1,0:T(1,128)S(1)}, f32[1,1,512]{2,1,0:T(1,128)}, u32[]{:S(2)}) copy-start(f32[1,1,512]{2,1,0:T(1,128)} %get-tuple-element.62) | copy-start | bytes 6148
  194.3 3.4 %copy-start.24 = (f32[1,1,512]{2,1,0:T(1,128)S(1)}, f32[1,1,512]{2,1,0:T(1,128)}, u32[]{:S(2)}) copy-start(f32[1,1,512]{2,1,0:T(1,128)} %get-tuple-element.63) | copy-start | bytes 6148
  194.3 3.4 %copy-start.25 = (f32[1,1,512]{2,1,0:T(1,128)S(1)}, f32[1,1,512]{2,1,0:T(1,128)}, u32[]{:S(2)}) copy-start(f32[1,1,512]{2,1,0:T(1,128)} %get-tuple-element.64) | copy-start | bytes 6148
  194.3 3.4 %copy-start.26 = (f32[1,1,512]{2,1,0:T(1,128)S(1)}, f32[1,1,512]{2,1,0:T(1,128)}, u32[]{:S(2)}) copy-start(f32[1,1,512]{2,1,0:T(1,128)} %get-tuple-element.65) | copy-start | bytes 6148
  194.3 3.4 %copy-start.27 = (f32[1,1,512]{2,1,0:T(1,128)S(1)}, f32[1,1,512]{2,1,0:T(1,128)}, u32[]{:S(2)}) copy-start(f32[1,1,512]{2,1,0:T(1,128)} %get-tuple-element.66) | copy-start | bytes 6148
  194.3 3.4 %copy-start.28 = (f32[1,1,512]{2,1,0:T(1,128)S(1)}, f32[1,1,512]{2,1,0:T(1,128)}, u32[]{:S(2)}) copy-start(f32[1,1,512]{2,1,0:T(1,128)} %get-tuple-element.67) | copy-start | bytes 6148
  194.3 3.4 %copy-start.43 = (f32[1,1,512]{2,1,0:T(1,128)S(1)}, f32[1,1,512]{2,1,0:T(1,128)}, u32[]{:S(2)}) copy-start(f32[1,1,512]{2,1,0:T(1,128)} %get-tuple-element.68) | copy-start | bytes 6148
  194.3 3.4 %copy-start.44 = (f32[1,1,512]{2,1,0:T(1,128)S(1)}, f32[1,1,512]{2,1,0:T(1,128)}, u32[]{:S(2)}) copy-start(f32[1,1,512]{2,1,0:T(1,128)} %get-tuple-element.69) | copy-start | bytes 6148
  194.3 3.4 %copy-start.45 = (f32[1,1,512]{2,1,0:T(1,128)S(1)}, f32[1,1,512]{2,1,0:T(1,128)}, u32[]{:S(2)}) copy-start(f32[1,1,512]{2,1,0:T(1,128)} %get-tuple-element.70) | copy-start | bytes 6148
  194.3 3.4 %copy-start.46 = (f32[1,1,512]{2,1,0:T(1,128)S(1)}, f32[1,1,512]{2,1,0:T(1,128)}, u32[]{:S(2)}) copy-start(f32[1,1,512]{2,1,0:T(1,128)} %get-tuple-element.71) | copy-start | bytes 6148
  194.3 3.4 %copy-start.47 = (f32[1,1,512]{2,1,0:T(1,128)S(1)}, f32[1,1,512]{2,1,0:T(1,128)}, u32[]{:S(2)}) copy-start(f32[1,1,512]{2,1,0:T(1,128)} %get-tuple-element.73) | copy-start | bytes 6148
  194.4 3.4 %copy-start.48 = (f32[1,1,512]{2,1,0:T(1,128)S(1)}, f32[1,1,512]{2,1,0:T(1,128)}, u32[]{:S(2)}) copy-start(f32[1,1,512]{2,1,0:T(1,128)} %get-tuple-element.74) | copy-start | bytes 6148
  194.4 3.4 %copy-start.49 = (f32[1,1,512]{2,1,0:T(1,128)S(1)}, f32[1,1,512]{2,1,0:T(1,128)}, u32[]{:S(2)}) copy-start(f32[1,1,512]{2,1,0:T(1,128)} %get-tuple-element.75) | copy-start | bytes 6148
  (26 other events, 34.4 us)
Sparse Core Ops, SparseCore 0:
  55.0 87.2 all-reduce.6
where the time goes:
time: 211 us; the launch traced here: 210 us
  other arithmetic  77.5 us (37%)
  blocking collectives  66.8 us (32%)
  matrix products  36.2 us (17%)
  between operations  14.4 us (7%)
  local copies, waits for them, and re-layouts  12 us (6%)
  starting transfers between devices  3.36 us (2%)
    add x1, other arithmetic, depthwise(): total + padded[row_tap:row_tap + out_rows, col_tap:col_tap + grid_width]...  53.5 us
    pmax x1, blocking collectives, on_device(): peak = lax.pmax(band_peak, 'col')  35.4 us
    psum x1, blocking collectives, on_device(): lax.psum((band_total * factor, band_weighted * factor[..., None]), 'col')  31.3 us
    dot_general x8, matrix products, on_device(): lax.dot_general(queries[:, lower:lower + head_dim], agent_head, (((1,), (...  14.2 us
    reduce_sum x8, other arithmetic, on_device(): jnp.sum(expo, axis=1, keepdims=True)  11.1 us
    dot_general x8, matrix products, on_device(): jnp.dot(token_weights, agent_values[head_index], preferred_element_type=j...  9.51 us
    unnamed x142, local copies, waits for them, and re-layouts  4.33 us
  transfers between devices with their start and end apart: 3, of which 0 were waited for; matrix products, arithmetic and copies ran while one was open for 50% of the time, Pallas kernels for 0%

commit v1 on v0

v1 whole, which is shorter than its diff:
```python
import functools

import jax
import jax.numpy as jnp
from jax import lax
from jax.experimental import pallas as pl
from jax.experimental.pallas import tpu as pltpu
from jax.sharding import PartitionSpec as P

HEADS = 8
NO_SCORE = -1e30
F32 = jnp.float32
BF16 = jnp.bfloat16
VMEM = pltpu.VMEM


def dot_nt(a, b):
    return lax.dot_general(a, b, (((1,), (1,)), ((), ())), preferred_element_type=F32)


def dot_nn(a, b):
    return lax.dot_general(a, b, (((1,), (0,)), ((), ())), preferred_element_type=F32)


def head_tokens(pair, half, scale):
    lane = lax.broadcasted_iota(jnp.int32, pair.shape, 1)
    mine = (lane >= 64) if half else (lane < 64)
    return jnp.where(mine, pair.astype(F32) * scale, 0.0).astype(BF16)


def chunk_of_device():
    place = lax.axis_index("col")
    return (place & 1) * 2 + ((place >> 1) & 1)


def band_kernel(scale, own_ref, patches, tissue, w_key, w_value, agents, values, keep, send, keys, values_t, bias):
    tokens = patches.shape[0]
    grid_rows, grid_width = tissue.shape
    block = 256
    for at in range(0, tokens, block):
        rows = pl.ds(at, block)
        part = patches[rows, :]
        keys[rows, :] = dot_nn(part, w_key[...]).astype(BF16)
        value = dot_nn(part, w_value[...]).astype(BF16)
        values[rows, :] = value
        values_t[:, rows] = value.T
    for row in range(grid_rows):
        line = jnp.where(tissue[row : row + 1, :] > 0, 0.0, NO_SCORE).astype(F32)
        bias[row * grid_width : (row + 1) * grid_width, :] = jnp.broadcast_to(line, (128, grid_width)).T
    own = own_ref[0]
    for index in range(4):
        chunk = index ^ own
        lanes = pl.ds(pl.multiple_of(chunk * 128, 128), 128)
        pair_keys = keys[:, lanes]
        pair_agents = agents[:, lanes]
        out = keep if index < 2 else send
        for half in range(2):
            scores = dot_nt(pair_keys, head_tokens(pair_agents, half, scale))
            column = bias[...]
            scores = scores + jnp.concatenate([column, column], axis=1)
            peak = jnp.max(scores, axis=0, keepdims=True)
            expo = jnp.exp(scores - peak)
            total = jnp.sum(expo, axis=0, keepdims=True)
            value_rows = pl.ds(pl.multiple_of(chunk * 128 + half * 64, 64), 64)
            weighted = dot_nn(values_t[value_rows, :], expo.astype(BF16))
            cols = slice(half * 256, half * 256 + 256)
            out[index % 2, 0:64, cols] = weighted
            row_id = lax.broadcasted_iota(jnp.int32, (8, 256), 0)
            stats = jnp.where(row_id == 0, peak, jnp.where(row_id == 1, total, 0.0))
            out[index % 2, 64:72, cols] = stats


def merge(first, second):
    peak_1, total_1, weighted_1 = first
    peak_2, total_2, weighted_2 = second
    peak = jnp.maximum(peak_1, peak_2)
    factor_1 = jnp.exp(peak_1 - peak)
    factor_2 = jnp.exp(peak_2 - peak)
    return peak, total_1 * factor_1 + total_2 * factor_2, weighted_1 * factor_1 + weighted_2 * factor_2


def wide(ref, index=None):
    array = ref[...] if index is None else ref[index]
    return array[64:65], array[65:66], array[0:64]


def thirds(value):
    high = value.astype(BF16).astype(F32)
    rest = value - high
    middle = rest.astype(BF16).astype(F32)
    return high, middle, rest - middle


def put_wide(ref, state):
    peak, total, weighted = state
    row_id = lax.broadcasted_iota(jnp.int32, (8, weighted.shape[1]), 0)
    ref[0:64] = weighted
    ref[64:72] = jnp.where(row_id == 0, peak, jnp.where(row_id == 1, total, 0.0))


def put_narrow(ref, state):
    peak, total, weighted = state
    row_id = lax.broadcasted_iota(jnp.int32, (16, weighted.shape[1]), 0)
    stats = jnp.zeros((16, weighted.shape[1]), F32)
    for at, part in enumerate(thirds(peak) + thirds(total)):
        stats = jnp.where(row_id == at, part, stats)
    ref[0:64] = weighted.astype(BF16)
    ref[64:80] = stats.astype(BF16)


def narrow(ref):
    stats = ref[64:80].astype(F32)
    peak = stats[0:1] + stats[1:2] + stats[2:3]
    total = stats[3:4] + stats[4:5] + stats[5:6]
    return peak, total, ref[0:64].astype(F32)


def first_merge_kernel(keep, got, own, payload):
    put_narrow(payload, merge(wide(keep, 1), wide(got, 1)))
    put_wide(own, merge(wide(keep, 0), wide(got, 0)))


def next_merge_kernel(held, got, own, payload):
    state = merge(wide(held), narrow(got))
    put_narrow(payload, state)
    put_wide(own, state)


def last_merge_kernel(held, got, agent_values):
    _, total, weighted = merge(wide(held), narrow(got))
    agent_values[...] = (weighted / total).astype(BF16)


def token_kernel(scale, patches, w_query, agents, weights):
    queries = dot_nn(patches[...], w_query[...]).astype(BF16)
    for head in range(HEADS):
        lanes = slice(head // 2 * 128, head // 2 * 128 + 128)
        scores = dot_nt(queries[:, lanes], head_tokens(agents[:, lanes], head % 2, scale))
        expo = jnp.exp(scores - jnp.max(scores, axis=1, keepdims=True))
        part = expo * (1.0 / jnp.sum(expo, axis=1, keepdims=True))
        weights[:, head * 256 : head * 256 + 256] = part.astype(BF16)


def conv_kernel(values, above, below, seven, five, three, position, padded, taps):
    out_rows, width = values.shape[0], values.shape[1]
    lanes = values.shape[2]
    merged = [[seven[p, q : q + 1, :] for q in range(7)] for p in range(7)]
    for p in range(5):
        for q in range(5):
            merged[p + 1][q + 1] = merged[p + 1][q + 1] + five[p, q : q + 1, :]
    for p in range(3):
        for q in range(3):
            merged[p + 2][q + 2] = merged[p + 2][q + 2] + three[p, q : q + 1, :]
    for p in range(7):
        for q in range(7):
            taps[p, q] = jnp.broadcast_to(merged[p][q], (8, lanes))
    edge = jnp.zeros((out_rows + 6, 8, lanes), F32)
    padded[:, 0:8, :] = edge
    padded[:, 8 + width : 16 + width, :] = edge
    padded[0:3, 8 : 8 + width, :] = above[...].astype(F32)
    padded[3 : 3 + out_rows, 8 : 8 + width, :] = values[...].astype(F32)
    padded[3 + out_rows : 6 + out_rows, 8 : 8 + width, :] = below[...].astype(F32)
    for at in range(0, width, 8):
        totals = [jnp.zeros((8, lanes), F32)] * out_rows
        for q in range(7):
            lines = [padded[row, at + 5 + q : at + 13 + q, :] for row in range(out_rows + 6)]
            for p in range(7):
                tap = taps[p, q]
                for row in range(out_rows):
                    totals[row] = totals[row] + lines[row + p] * tap
        for row in range(out_rows):
            position[row, at : at + 8, :] = totals[row]


def out_kernel(own_ref, weights, own, near, side, far, position, w_out, mixed, spread):
    @pl.when(pl.program_id(0) == 0)
    def _():
        spread[...] = jnp.zeros_like(spread)
        for index, part in enumerate((own, near, side, far)):
            chunk = index ^ own_ref[0]
            group, place = chunk // 2, chunk % 2
            for half in range(2):
                rows = pl.ds(pl.multiple_of(place * 128 + half * 64, 64), 64)
                cols = pl.ds(pl.multiple_of(place * 512 + half * 256, 256), 256)
                spread[group, rows, cols] = part[:, half * 256 : half * 256 + 256]

    blended = []
    for group in range(2):
        attended = dot_nt(weights[:, group * 1024 : group * 1024 + 1024], spread[group])
        blended.append((attended + position[:, group * 256 : group * 256 + 256]).astype(BF16))
    mixed[...] = dot_nn(jnp.concatenate(blended, axis=1), w_out[...]).astype(BF16)


def params(megabytes=48):
    return pltpu.CompilerParams(vmem_limit_bytes=megabytes << 20)


def cost(flops, moved, exps=0):
    return pl.CostEstimate(flops=int(flops), bytes_accessed=int(moved), transcendentals=int(exps))


def shape(dims, dtype):
    return jax.ShapeDtypeStruct(dims, dtype)


def exchange(x, bit):
    peers = lax.axis_size("col")
    return lax.ppermute(x, "col", [(i, i ^ bit) for i in range(peers)])


def halo_rows(values):
    peers, rows = lax.axis_size("col"), values.shape[0]
    odd = lax.axis_index("col") % 2 == 1
    first, last = values[:3], values[rows - 3 :]
    pair = [(i, i ^ 1) for i in range(peers)]
    rest = [(i, i + 1) for i in range(1, peers - 1, 2)]
    inner = lax.ppermute(jnp.where(odd, first, last), "col", pair)
    outer = lax.ppermute(jnp.where(odd, last, first), "col", rest + [(j, i) for i, j in rest])
    return jnp.where(odd, inner, outer), jnp.where(odd, outer, inner)


def on_device(patches, tissue, w_query, w_key, w_value, w_out, agent_tokens, seven, five, three):
    band_rows, width, dim = patches.shape
    tokens = band_rows * width
    agents = agent_tokens.shape[0]
    scale = (dim // HEADS) ** (-0.5)
    flat = patches.reshape(tokens, dim)
    own_chunk = jnp.reshape(chunk_of_device(), (1,)).astype(jnp.int32)
    smem = pl.BlockSpec(memory_space=pltpu.SMEM)
    vmem = pl.BlockSpec(memory_space=VMEM)

    values, keep, send = pl.pallas_call(
        functools.partial(band_kernel, scale),
        out_shape=(shape((tokens, dim), BF16), shape((2, 72, 512), F32), shape((2, 72, 512), F32)),
        in_specs=[smem] + [vmem] * 5,
        out_specs=[vmem] * 3,
        scratch_shapes=[
            VMEM((tokens, dim), BF16),
            VMEM((dim, tokens), BF16),
            VMEM((tokens, 128), F32),
        ],
        compiler_params=params(),
        cost_estimate=cost(1.6e9, 4e6, 2e6),
        name="band",
    )(own_chunk, flat, tissue, w_key, w_value, agent_tokens)

    small = dict(in_specs=[vmem] * 2, compiler_params=params(16))
    wide_shape, narrow_shape = shape((72, 512), F32), shape((80, 512), BF16)
    got = exchange(send, 1)
    held, payload = pl.pallas_call(
        first_merge_kernel, out_shape=(wide_shape, narrow_shape), out_specs=[vmem] * 2,
        cost_estimate=cost(1e6, 1e6), name="merge_first", **small,
    )(keep, got)
    peers = lax.axis_size("col")
    bit = 2
    while bit * 2 < peers:
        got = exchange(payload, bit)
        held, payload = pl.pallas_call(
            next_merge_kernel, out_shape=(wide_shape, narrow_shape), out_specs=[vmem] * 2,
            cost_estimate=cost(1e6, 1e6), name="merge_next", **small,
        )(held, got)
        bit *= 2
    got = exchange(payload, bit)
    own = pl.pallas_call(
        last_merge_kernel, out_shape=shape((64, 512), BF16), out_specs=vmem,
        cost_estimate=cost(1e6, 1e6), name="merge_last", **small,
    )(held, got)
    near = exchange(own, 2)
    side = exchange(own, 1)
    far = exchange(near, 1)

    block = 256
    weights = pl.pallas_call(
        functools.partial(token_kernel, scale),
        grid=(tokens // block,),
        out_shape=shape((tokens, HEADS * agents), BF16),
        in_specs=[pl.BlockSpec((block, dim), lambda i: (i, 0)), vmem, vmem],
        out_specs=pl.BlockSpec((block, HEADS * agents), lambda i: (i, 0)),
        compiler_params=params(),
        cost_estimate=cost(1.1e9, 6e6, 2e6),
        name="token",
    )(flat, w_query, agent_tokens)

    grid_values = values.reshape(band_rows, width, dim)
    above, below = halo_rows(grid_values)

    def lane_block(rows, cols):
        return pl.BlockSpec((rows, cols, 128), lambda i: (0, 0, i))

    position = pl.pallas_call(
        conv_kernel,
        grid=(dim // 128,),
        out_shape=shape((band_rows, width, dim), F32),
        in_specs=[
            lane_block(band_rows, width),
            lane_block(3, width),
            lane_block(3, width),
            lane_block(7, 7),
            lane_block(5, 5),
            lane_block(3, 3),
        ],
        out_specs=lane_block(band_rows, width),
        scratch_shapes=[VMEM((band_rows + 6, width + 16, 128), F32), VMEM((7, 7, 8, 128), F32)],
        compiler_params=params(),
        cost_estimate=cost(3e9, 4e6),
        name="conv",
    )(grid_values, above, below, seven, five, three).reshape(tokens, dim)

    mixed = pl.pallas_call(
        out_kernel,
        grid=(tokens // block,),
        out_shape=shape((tokens, dim), BF16),
        in_specs=[
            smem,
            pl.BlockSpec((block, HEADS * agents), lambda i: (i, 0)),
            vmem,
            vmem,
            vmem,
            vmem,
            pl.BlockSpec((block, dim), lambda i: (i, 0)),
            vmem,
        ],
        out_specs=pl.BlockSpec((block, dim), lambda i: (i, 0)),
        scratch_shapes=[VMEM((2, 256, 1024), BF16)],
        compiler_params=params(),
        cost_estimate=cost(1.1e9, 8e6),
        name="out",
    )(own_chunk, weights, own, near, side, far, position, w_out)
    return mixed.reshape(band_rows, width, dim)


def solution(mesh):
    return jax.shard_map(
        on_device,
        mesh=mesh,
        in_specs=(
            P(("slide", "col"), None, None),
            P(("slide", "col"), None),
            P(),
            P(),
            P(),
            P(),
            P(),
            P(),
            P(),
            P(),
        ),
        out_specs=P(("slide", "col"), None, None),
        check_vma=False,
    )
```

time: 211 us -> 61.2 us (0.29)
  other arithmetic: 77.5 us -> 0.11 us
  blocking collectives: 66.8 us -> 0 us
  matrix products: 36.2 us -> 0 us
  Pallas kernels: 0 us -> 25 us
  waiting for transfers between devices: 0.02 us -> 14.4 us
  between operations: 14.4 us -> 0.17 us
  starting transfers between devices: 3.36 us -> 14.2 us
  local copies, waits for them, and re-layouts: 12 us -> 6.92 us
    add x6 -> x0, other arithmetic: 57.7 us -> none  [the longest x1 53.5 us: depthwise(): total + padded[row_tap:row_tap + out_rows, col_tap:col_tap + grid_width]...]
    dot_general x36 -> x0, matrix products: 36.2 us -> none  [the longest x8 14.2 us: on_device(): lax.dot_general(queries[:, lower:lower + head_dim], agent_head, (((1,), (...]
    pmax x1 -> x0, blocking collectives: 35.4 us -> none  [on_device(): peak = lax.pmax(band_peak, 'col')]
    psum x1 -> x0, blocking collectives: 31.3 us -> none  [on_device(): lax.psum((band_total * factor, band_weighted * factor[..., None]), 'col')]
    pallas_call x0 -> x8, Pallas kernels: none -> 25 us  [the longest x1 7.57 us: on_device(): pl.pallas_call(conv_kernel, grid=(dim // 128,), out_shape=shape((band_row...]
    ppermute x2 -> x9, waiting for transfers between devices: 0.01 us -> 14.4 us  [the longest x7 14.4 us: exchange(): return lax.ppermute(x, 'col', [(i, i ^ bit) for i in range(peers)])]
    reduce_sum x9 -> x0, other arithmetic: 12.6 us -> none  [the longest x8 11.1 us: on_device(): jnp.sum(expo, axis=1, keepdims=True)]
    ppermute x2 -> x9, starting transfers between devices: 3.36 us -> 14.2 us  [the longest x7 13.4 us: exchange(): return lax.ppermute(x, 'col', [(i, i ^ bit) for i in range(peers)])]
  transfers between devices with their start and end apart: 3 -> 9, of which waited for: 0 -> 4; matrix products, arithmetic and copies ran while one was open for 50% -> 0% of each run, Pallas kernels for 0% -> 20%
where the time goes in v1:
time: 61.2 us; the launch traced here: 60.7 us
  Pallas kernels  25 us (41%)
  waiting for transfers between devices  14.4 us (24%)
  starting transfers between devices  14.2 us (23%)
  local copies, waits for them, and re-layouts  6.92 us (11%)
    ppermute x7, waiting for transfers between devices, exchange(): return lax.ppermute(x, 'col', [(i, i ^ bit) for i in range(peers)])  14.4 us
    ppermute x7, starting transfers between devices, exchange(): return lax.ppermute(x, 'col', [(i, i ^ bit) for i in range(peers)])  13.4 us
    pallas_call x1, Pallas kernels, on_device(): pl.pallas_call(conv_kernel, grid=(dim // 128,), out_shape=shape((band_row...  7.57 us
    pallas_call x1, Pallas kernels, on_device(): pl.pallas_call(functools.partial(band_kernel, scale), out_shape=(shape((t...  7.44 us
    unnamed x26, local copies, waits for them, and re-layouts  6.92 us
    pallas_call x1, Pallas kernels, on_device(): pl.pallas_call(out_kernel, grid=(tokens // block,), out_shape=shape((toke...  5.54 us
    pallas_call x1, Pallas kernels, on_device(): pl.pallas_call(functools.partial(token_kernel, scale), grid=(tokens // bl...  4.2 us
  transfers between devices with their start and end apart: 9, of which 4 were waited for; matrix products, arithmetic and copies ran while one was open for 0% of the time, Pallas kernels for 20%

profile of v1, /device:TPU:0, one launch (start us, length us, event | category | flops | bytes accessed | tf_op | source)
XLA Modules:
  0.0 60.7 jit_solution(5360802700145268727)
XLA Ops:
  0.0 0.0 copy-start.1
  0.0 1.2 %copy-done.1 = bf16[8,128,512]{2,1,0:T(8,128)(2,1)S(1)} copy-done((bf16[8,128,512]{2,1,0:T(8,128)(2,1)S(1)}, bf16[8,128,512]{2,1,0:T(8,128)(2,1)}, u32[]{:S(2)}) %copy-start.1) | copy-done | bytes 1048600
  1.2 0.0 copy-start.5
  1.2 0.9 %copy-done.5 = bf16[256,512]{1,0:T(8,128)(2,1)S(1)} copy-done((bf16[256,512]{1,0:T(8,128)(2,1)S(1)}, bf16[256,512]{1,0:T(8,128)(2,1)}, u32[]{:S(2)}) %copy-start.5) | copy-done | bytes 262168
  2.2 0.0 copy-start.7
  2.2 1.0 %copy-done.7 = bf16[512,512]{1,0:T(8,128)(2,1)S(1)} copy-done((bf16[512,512]{1,0:T(8,128)(2,1)S(1)}, bf16[512,512]{1,0:T(8,128)(2,1)}, u32[]{:S(2)}) %copy-start.7) | copy-done | bytes 524312
  3.2 1.0 %copy-done.8 = bf16[512,512]{1,0:T(8,128)(2,1)S(1)} copy-done((bf16[512,512]{1,0:T(8,128)(2,1)S(1)}, bf16[512,512]{1,0:T(8,128)(2,1)}, u32[]{:S(2)}) %copy-start.8) | copy-done | bytes 524312
  4.3 0.7 %copy-done.12 = s32[8,128]{1,0:T(8,128)S(1)} copy-done((s32[8,128]{1,0:T(8,128)S(1)}, s32[8,128]{1,0:T(8,128)}, u32[]{:S(2)}) %copy-start.12) | copy-done | bytes 4120
  5.0 7.4 %band.1 = (bf16[1024,512]{1,0:T(8,128)(2,1)S(1)}, f32[2,72,512]{2,1,0:T(8,128)S(1)}, f32[2,72,512]{2,1,0:T(8,128)}) custom-call(s32[1]{0:T(128)} %bitcast.own_ref, bf16[1024,512]{1,0:T(8,128)(2,1)S(1)} %bitcast.8, s32[8,128]{1,0:T(8,128)S(1)} %copy-done.12, bf16[512,512]{1,0:T(8,128)(2,1)S(1)} %copy-done.7, bf16[512,512]{1,0:T(8,128)(2,1)S(1)} %copy-done.8, ...), custom_call_target="tpu_custom_call" | custom-call | flops 1600000000 | bytes 4000000 | tf_op jit(solution)/shard_map/band/pallas_call | solution.py:232
  12.4 0.5 collective-permute-start
  12.8 0.1 broadcast_select_fusion
  12.9 0.1 collective-permute-start.7
  13.0 0.7 %collective-permute-start.8 = (bf16[3,128,512]{2,1,0:T(8,128)(2,1)S(1)}, bf16[3,128,512]{2,1,0:T(8,128)(2,1)S(1)}, u32[]{:S(2)}, u32[]{:S(2)}) collective-permute-start(bf16[3,128,512]{2,1,0:T(8,128)(2,1)S(1)} %bitcast.11), channel_id=1, source_target_pairs={{1,2},{3,4},{5,6},{7,8},{9,10},{11,12},{13,14},{2,1},{4,3},{6,5},{... | collective-permute-start | bytes 1179656 | tf_op jit(solution)/shard_map/ppermute | solution.py:218
  13.7 0.6 collective-permute-done.got
  14.3 0.1 merge_first.1
  14.3 0.0 copy-start.9
  14.4 0.0 copy-start.10
  14.4 0.0 copy-start.11
  14.4 3.7 %collective-permute-start.1 = (bf16[80,512]{1,0:T(8,128)(2,1)S(1)}, bf16[80,512]{1,0:T(8,128)(2,1)S(1)}, u32[]{:S(2)}, u32[]{:S(2)}) collective-permute-start(bf16[80,512]{1,0:T(8,128)(2,1)S(1)} %get-tuple-element.17), channel_id=1, source_target_pairs={{0,2},{1,3},{2,0},{3,1},{4,6},{5,7},{6,4},{7,5},{8,10},{9,11},{10,... | collective-permute-start | bytes 245768 | tf_op jit(solution)/shard_map/ppermute | solution.py:208
  18.1 7.3 %collective-permute-done.1.got = bf16[80,512]{1,0:T(8,128)(2,1)S(1)} collective-permute-done((bf16[80,512]{1,0:T(8,128)(2,1)S(1)}, bf16[80,512]{1,0:T(8,128)(2,1)S(1)}, u32[]{:S(2)}, u32[]{:S(2)}) %collective-permute-start.1) | collective-permute-done | bytes 81952 | tf_op jit(solution)/shard_map/ppermute | solution.py:208
  25.4 0.1 merge_next.2
  25.5 6.0 %collective-permute-start.2 = (bf16[80,512]{1,0:T(8,128)(2,1)S(1)}, bf16[80,512]{1,0:T(8,128)(2,1)S(1)}, u32[]{:S(2)}, u32[]{:S(2)}) collective-permute-start(bf16[80,512]{1,0:T(8,128)(2,1)S(1)} %get-tuple-element.19), channel_id=1, source_target_pairs={{0,4},{1,5},{2,6},{3,7},{4,0},{5,1},{6,2},{7,3},{8,12},{9,13},{10,... | collective-permute-start | bytes 245768 | tf_op jit(solution)/shard_map/ppermute | solution.py:208
  31.4 2.4 %collective-permute-done.2.got = bf16[80,512]{1,0:T(8,128)(2,1)S(1)} collective-permute-done((bf16[80,512]{1,0:T(8,128)(2,1)S(1)}, bf16[80,512]{1,0:T(8,128)(2,1)S(1)}, u32[]{:S(2)}, u32[]{:S(2)}) %collective-permute-start.2) | collective-permute-done | bytes 81952 | tf_op jit(solution)/shard_map/ppermute | solution.py:208
  33.9 0.1 merge_next.3
  33.9 3.1 %collective-permute-start.3 = (bf16[80,512]{1,0:T(8,128)(2,1)S(1)}, bf16[80,512]{1,0:T(8,128)(2,1)S(1)}, u32[]{:S(2)}, u32[]{:S(2)}) collective-permute-start(bf16[80,512]{1,0:T(8,128)(2,1)S(1)} %get-tuple-element.21), channel_id=1, source_target_pairs={{0,8},{1,9},{2,10},{3,11},{4,12},{5,13},{6,14},{7,15},{8,0},{9,1},... | collective-permute-start | bytes 245768 | tf_op jit(solution)/shard_map/ppermute | solution.py:208
  37.0 0.0 copy-done.2
  37.0 0.0 copy-done.3
  37.0 0.0 copy-done.6
  37.0 4.2 %token_.1.weights = bf16[1024,2048]{1,0:T(8,128)(2,1)S(1)} custom-call(bf16[1024,512]{1,0:T(8,128)(2,1)S(1)} %bitcast.9, bf16[512,512]{1,0:T(8,128)(2,1)S(1)} %copy-done.3, bf16[256,512]{1,0:T(8,128)(2,1)S(1)} %copy-done.6), custom_call_target="tpu_custom_call" | custom-call | flops 1100000000 | bytes 6000000 | tf_op jit(solution)/shard_map/token/pallas_call | solution.py:273
  41.2 0.0 copy-start
  41.2 1.9 %copy-done = bf16[1024,2048]{1,0:T(8,128)(2,1)} copy-done((bf16[1024,2048]{1,0:T(8,128)(2,1)}, bf16[1024,2048]{1,0:T(8,128)(2,1)S(1)}, u32[]{:S(2)}) %copy-start) | copy-done | bytes 4194328
  43.2 0.0 collective-permute-done.3.got
  43.2 0.1 collective-permute-start.4
  43.3 0.0 collective-permute-done.7
  43.3 0.0 collective-permute-done.8
  43.3 0.1 broadcast_select_fusion.2
  43.4 0.1 collective-permute-start.5
  43.5 4.1 %collective-permute-done.4.near = bf16[64,512]{1,0:T(8,128)(2,1)S(1)} collective-permute-done((bf16[64,512]{1,0:T(8,128)(2,1)S(1)}, bf16[64,512]{1,0:T(8,128)(2,1)S(1)}, u32[]{:S(2)}, u32[]{:S(2)}) %collective-permute-start.4) | collective-permute-done | bytes 65568 | tf_op jit(solution)/shard_map/ppermute | solution.py:208
  47.6 0.0 collective-permute-start.6
  47.6 0.0 copy-done.9
  47.6 0.0 copy-done.10
  47.6 0.0 copy-done.11
  47.6 0.0 copy-start.4
  47.6 7.6 %conv.1 = f32[8,128,512]{2,1,0:T(8,128)S(1)} custom-call(bf16[8,128,512]{2,1,0:T(8,128)(2,1)S(1)} %bitcast.10, bf16[3,128,512]{2,1,0:T(8,128)(2,1)S(1)} %get-tuple-element.26.above, bf16[3,128,512]{2,1,0:T(8,128)(2,1)S(1)} %get-tuple-element.25.below, f32[7,7,512]{2,1,0:T(8,128)S(1)} %copy-done.9, f32[5,5,512]{2,1,0:T(8,128)S(1)} %copy-done.10, ...), custom_call_target="tpu_custom_call" | custom-call | flops 3000000000 | bytes 4000000 | tf_op jit(solution)/shard_map/conv/pallas_call | solution.py:290
  55.2 0.0 collective-permute-done.5.side
  55.2 0.0 collective-permute-done.6.far
  55.2 0.0 copy-done.4
  55.2 5.5 %out.1 = bf16[1024,512]{1,0:T(8,128)(2,1)} custom-call(s32[1]{0:T(128)} %bitcast.own_ref, bf16[1024,2048]{1,0:T(8,128)(2,1)} %copy-done, bf16[64,512]{1,0:T(8,128)(2,1)S(1)} %merge_last.1.own, bf16[64,512]{1,0:T(8,128)(2,1)S(1)} %collective-permute-done.4.near, bf16[64,512]{1,0:T(8,128)(2,1)S(1)} %collective-permute-done.5.side, ...), custom_call_target="tpu_custom_call" | custom-call | flops 1100000000 | bytes 8000000 | tf_op jit(solution)/shard_map/out/pallas_call | solution.py:309
  (6 shorter events, 0.1 us)
Async XLA Ops:
  0.0 1.2 %copy-start.1 = (bf16[8,128,512]{2,1,0:T(8,128)(2,1)S(1)}, bf16[8,128,512]{2,1,0:T(8,128)(2,1)}, u32[]{:S(2)}) copy-start(bf16[8,128,512]{2,1,0:T(8,128)(2,1)} %param.10) | copy-start | bytes 3145732
  1.2 0.9 %copy-start.5 = (bf16[256,512]{1,0:T(8,128)(2,1)S(1)}, bf16[256,512]{1,0:T(8,128)(2,1)}, u32[]{:S(2)}) copy-start(bf16[256,512]{1,0:T(8,128)(2,1)} %agents.3) | copy-start | bytes 786436
  2.2 1.0 %copy-start.7 = (bf16[512,512]{1,0:T(8,128)(2,1)S(1)}, bf16[512,512]{1,0:T(8,128)(2,1)}, u32[]{:S(2)}) copy-start(bf16[512,512]{1,0:T(8,128)(2,1)} %w_key.1) | copy-start | bytes 1572868
  3.2 1.0 %copy-start.8 = (bf16[512,512]{1,0:T(8,128)(2,1)S(1)}, bf16[512,512]{1,0:T(8,128)(2,1)}, u32[]{:S(2)}) copy-start(bf16[512,512]{1,0:T(8,128)(2,1)} %w_value.1) | copy-start | bytes 1572868
  4.3 0.7 %copy-start.12 = (s32[8,128]{1,0:T(8,128)S(1)}, s32[8,128]{1,0:T(8,128)}, u32[]{:S(2)}) copy-start(s32[8,128]{1,0:T(8,128)} %tissue.1) | copy-start | bytes 12292
  4.9 32.1 %copy-start.2 = (bf16[8,128,512]{2,1,0:T(8,128)(2,1)S(1)}, bf16[8,128,512]{2,1,0:T(8,128)(2,1)}, u32[]{:S(2)}) copy-start(bf16[8,128,512]{2,1,0:T(8,128)(2,1)} %param.10) | copy-start | bytes 3145732
  5.0 32.1 %copy-start.3 = (bf16[512,512]{1,0:T(8,128)(2,1)S(1)}, bf16[512,512]{1,0:T(8,128)(2,1)}, u32[]{:S(2)}) copy-start(bf16[512,512]{1,0:T(8,128)(2,1)} %w_query.1) | copy-start | bytes 1572868
  5.0 32.1 %copy-start.6 = (bf16[256,512]{1,0:T(8,128)(2,1)S(1)}, bf16[256,512]{1,0:T(8,128)(2,1)}, u32[]{:S(2)}) copy-start(bf16[256,512]{1,0:T(8,128)(2,1)} %agents.3) | copy-start | bytes 786436
  12.4 1.9 %collective-permute-start = (f32[2,72,512]{2,1,0:T(8,128)}, f32[2,72,512]{2,1,0:T(8,128)S(1)}, u32[]{:S(2)}, u32[]{:S(2)}) collective-permute-start(f32[2,72,512]{2,1,0:T(8,128)} %get-tuple-element.15), channel_id=1, source_target_pairs={{0,1},{1,0},{2,3},{3,2},{4,5},{5,4},{6,7},{7,6},{8,9},{9,8},{10,11... | collective-permute-start | bytes 884744 | tf_op jit(solution)/shard_map/ppermute | solution.py:208
  12.9 30.4 %collective-permute-start.7 = (bf16[3,128,512]{2,1,0:T(8,128)(2,1)S(1)}, bf16[3,128,512]{2,1,0:T(8,128)(2,1)S(1)}, u32[]{:S(2)}, u32[]{:S(2)}) collective-permute-start(bf16[3,128,512]{2,1,0:T(8,128)(2,1)S(1)} %bitcast.12), channel_id=1, source_target_pairs={{0,1},{1,0},{2,3},{3,2},{4,5},{5,4},{6,7},{7,6},{8,9},{9,8},{10,11... | collective-permute-start | bytes 1179656 | tf_op jit(solution)/shard_map/ppermute | solution.py:217
  13.0 30.3 %collective-permute-start.8 = (bf16[3,128,512]{2,1,0:T(8,128)(2,1)S(1)}, bf16[3,128,512]{2,1,0:T(8,128)(2,1)S(1)}, u32[]{:S(2)}, u32[]{:S(2)}) collective-permute-start(bf16[3,128,512]{2,1,0:T(8,128)(2,1)S(1)} %bitcast.11), channel_id=1, source_target_pairs={{1,2},{3,4},{5,6},{7,8},{9,10},{11,12},{13,14},{2,1},{4,3},{6,5},{... | collective-permute-start | bytes 1179656 | tf_op jit(solution)/shard_map/ppermute | solution.py:218
  14.3 33.2 %copy-start.9 = (f32[7,7,512]{2,1,0:T(8,128)S(1)}, f32[7,7,512]{2,1,0:T(8,128)}, u32[]{:S(2)}) copy-start(f32[7,7,512]{2,1,0:T(8,128)} %seven.1) | copy-start | bytes 301060
  14.4 33.2 %copy-start.10 = (f32[5,5,512]{2,1,0:T(8,128)S(1)}, f32[5,5,512]{2,1,0:T(8,128)}, u32[]{:S(2)}) copy-start(f32[5,5,512]{2,1,0:T(8,128)} %five.1) | copy-start | bytes 153604
  14.4 33.2 %copy-start.11 = (f32[3,3,512]{2,1,0:T(4,128)S(1)}, f32[3,3,512]{2,1,0:T(4,128)}, u32[]{:S(2)}) copy-start(f32[3,3,512]{2,1,0:T(4,128)} %three.1) | copy-start | bytes 55300
  14.4 11.0 %collective-permute-start.1 = (bf16[80,512]{1,0:T(8,128)(2,1)S(1)}, bf16[80,512]{1,0:T(8,128)(2,1)S(1)}, u32[]{:S(2)}, u32[]{:S(2)}) collective-permute-start(bf16[80,512]{1,0:T(8,128)(2,1)S(1)} %get-tuple-element.17), channel_id=1, source_target_pairs={{0,2},{1,3},{2,0},{3,1},{4,6},{5,7},{6,4},{7,5},{8,10},{9,11},{10,... | collective-permute-start | bytes 245768 | tf_op jit(solution)/shard_map/ppermute | solution.py:208
  25.5 8.4 %collective-permute-start.2 = (bf16[80,512]{1,0:T(8,128)(2,1)S(1)}, bf16[80,512]{1,0:T(8,128)(2,1)S(1)}, u32[]{:S(2)}, u32[]{:S(2)}) collective-permute-start(bf16[80,512]{1,0:T(8,128)(2,1)S(1)} %get-tuple-element.19), channel_id=1, source_target_pairs={{0,4},{1,5},{2,6},{3,7},{4,0},{5,1},{6,2},{7,3},{8,12},{9,13},{10,... | collective-permute-start | bytes 245768 | tf_op jit(solution)/shard_map/ppermute | solution.py:208
  33.9 9.3 %collective-permute-start.3 = (bf16[80,512]{1,0:T(8,128)(2,1)S(1)}, bf16[80,512]{1,0:T(8,128)(2,1)S(1)}, u32[]{:S(2)}, u32[]{:S(2)}) collective-permute-start(bf16[80,512]{1,0:T(8,128)(2,1)S(1)} %get-tuple-element.21), channel_id=1, source_target_pairs={{0,8},{1,9},{2,10},{3,11},{4,12},{5,13},{6,14},{7,15},{8,0},{9,1},... | collective-permute-start | bytes 245768 | tf_op jit(solution)/shard_map/ppermute | solution.py:208
  41.2 2.0 %copy-start = (bf16[1024,2048]{1,0:T(8,128)(2,1)}, bf16[1024,2048]{1,0:T(8,128)(2,1)S(1)}, u32[]{:S(2)}) copy-start(bf16[1024,2048]{1,0:T(8,128)(2,1)S(1)} %token_.1.weights) | copy-start | bytes 12582916
  43.2 4.3 %collective-permute-start.4 = (bf16[64,512]{1,0:T(8,128)(2,1)S(1)}, bf16[64,512]{1,0:T(8,128)(2,1)S(1)}, u32[]{:S(2)}, u32[]{:S(2)}) collective-permute-start(bf16[64,512]{1,0:T(8,128)(2,1)S(1)} %merge_last.1.own), channel_id=1, source_target_pairs={{0,2},{1,3},{2,0},{3,1},{4,6},{5,7},{6,4},{7,5},{8,10},{9,11},{10,... | collective-permute-start | bytes 196616 | tf_op jit(solution)/shard_map/ppermute | solution.py:208
  43.4 11.8 %collective-permute-start.5 = (bf16[64,512]{1,0:T(8,128)(2,1)S(1)}, bf16[64,512]{1,0:T(8,128)(2,1)S(1)}, u32[]{:S(2)}, u32[]{:S(2)}) collective-permute-start(bf16[64,512]{1,0:T(8,128)(2,1)S(1)} %merge_last.1.own), channel_id=1, source_target_pairs={{0,1},{1,0},{2,3},{3,2},{4,5},{5,4},{6,7},{7,6},{8,9},{9,8},{10,11... | collective-permute-start | bytes 196616 | tf_op jit(solution)/shard_map/ppermute | solution.py:208
  47.6 7.6 %collective-permute-start.6 = (bf16[64,512]{1,0:T(8,128)(2,1)S(1)}, bf16[64,512]{1,0:T(8,128)(2,1)S(1)}, u32[]{:S(2)}, u32[]{:S(2)}) collective-permute-start(bf16[64,512]{1,0:T(8,128)(2,1)S(1)} %collective-permute-done.4.near), channel_id=1, source_target_pairs={{0,1},{1,0},{2,3},{3,2},{4,5},{5,4},{6,7},{7,6},{8,9},{9,8},{10,11... | collective-permute-start | bytes 196616 | tf_op jit(solution)/shard_map/ppermute | solution.py:208
  47.6 7.6 %copy-start.4 = (bf16[512,512]{1,0:T(8,128)(2,1)S(1)}, bf16[512,512]{1,0:T(8,128)(2,1)}, u32[]{:S(2)}) copy-start(bf16[512,512]{1,0:T(8,128)(2,1)} %w_out.1) | copy-start | bytes 1572868

commit v2 on v1

v2 whole, which is shorter than its diff:
```python
import functools

import jax
import jax.numpy as jnp
from jax import lax
from jax.experimental import pallas as pl
from jax.experimental.pallas import tpu as pltpu
from jax.sharding import PartitionSpec as P

HEADS = 8
NO_SCORE = -1e30
F32 = jnp.float32
BF16 = jnp.bfloat16
VMEM = pltpu.VMEM


def dot_nt(a, b):
    return lax.dot_general(a, b, (((1,), (1,)), ((), ())), preferred_element_type=F32)


def dot_nn(a, b):
    return lax.dot_general(a, b, (((1,), (0,)), ((), ())), preferred_element_type=F32)


def head_tokens(pair, half, scale):
    lane = lax.broadcasted_iota(jnp.int32, pair.shape, 1)
    mine = (lane >= 64) if half else (lane < 64)
    return jnp.where(mine, pair.astype(F32) * scale, 0.0).astype(BF16)


def chunk_of_device():
    place = lax.axis_index("col")
    return (place & 1) * 2 + ((place >> 1) & 1)


def band_kernel(
    scale, own_ref, mine, other, tissue, other_tissue, w_key, w_value, agents, values, keep, payload, keys, vals
):
    tokens = mine.shape[0]
    block = 256
    own = own_ref[0]
    half_lanes = pl.ds(pl.multiple_of((own // 2) * 256, 256), 256)
    key_half = w_key[:, half_lanes]
    value_half = w_value[:, half_lanes]
    for at in range(0, tokens, block):
        rows = pl.ds(at, block)
        part = mine[rows, :]
        keys[rows, :] = dot_nn(part, key_half).astype(BF16)
        values[rows, :] = dot_nn(part, w_value[...]).astype(BF16)
        vals[rows, :] = values[rows, half_lanes]
    for at in range(0, tokens, block):
        rows = pl.ds(tokens + at, block)
        part = other[pl.ds(at, block), :]
        keys[rows, :] = dot_nn(part, key_half).astype(BF16)
        vals[rows, :] = dot_nn(part, value_half).astype(BF16)
    lines = []
    for grid in (tissue, other_tissue):
        bias = jnp.where(grid[...] > 0, 0.0, NO_SCORE).astype(F32)
        lines += [bias[row : row + 1] for row in range(bias.shape[0])]
    bias_line = jnp.concatenate(lines, axis=1)

    def lanes_of(index):
        return pl.ds(pl.multiple_of(((own % 2) ^ index) * 128, 128), 128)

    def scores_of(index, half):
        chunk_lanes = pl.ds(pl.multiple_of((own ^ index) * 128, 128), 128)
        tokens_of = head_tokens(agents[:, chunk_lanes], half, scale)
        return dot_nt(tokens_of, keys[:, lanes_of(index)]) + bias_line

    order = [(1, 0), (1, 1), (0, 0), (0, 1)]
    ahead = scores_of(*order[0])
    done = []
    for step, (index, half) in enumerate(order):
        scores = ahead
        if step + 1 < len(order):
            ahead = scores_of(*order[step + 1])
        peak = jnp.max(scores, axis=1, keepdims=True)
        expo = jnp.exp(scores - peak)
        total = jnp.sum(expo, axis=1, keepdims=True)
        done.append((peak, total, dot_nn(expo.astype(BF16), vals[:, lanes_of(index)])))
        if half == 1:
            lane = lax.broadcasted_iota(jnp.int32, (256, 128), 1)
            weighted = jnp.where(lane < 64, done[0][2], done[1][2]).T
            stats = jnp.zeros((256, 128), F32)
            for at, value in enumerate(done[0][:2] + done[1][:2]):
                stats = jnp.where(lane == at, value, stats)
            stats = stats.T
            sides = []
            for at in range(2):
                sides.append((stats[2 * at : 2 * at + 1], stats[2 * at + 1 : 2 * at + 2], weighted[64 * at : 64 * at + 64]))
            state = tuple(jnp.concatenate(pair, axis=1) for pair in zip(*sides))
            if index == 1:
                put_narrow(payload, state)
            else:
                put_wide(keep, state)
            done = []


def merge(first, second):
    peak_1, total_1, weighted_1 = first
    peak_2, total_2, weighted_2 = second
    peak = jnp.maximum(peak_1, peak_2)
    factor_1 = jnp.exp(peak_1 - peak)
    factor_2 = jnp.exp(peak_2 - peak)
    return peak, total_1 * factor_1 + total_2 * factor_2, weighted_1 * factor_1 + weighted_2 * factor_2


def wide(ref, index=None):
    array = ref[...] if index is None else ref[index]
    return array[64:65], array[65:66], array[0:64]


def thirds(value):
    high = value.astype(BF16).astype(F32)
    rest = value - high
    middle = rest.astype(BF16).astype(F32)
    return high, middle, rest - middle


def put_wide(ref, state):
    peak, total, weighted = state
    row_id = lax.broadcasted_iota(jnp.int32, (8, weighted.shape[1]), 0)
    ref[0:64] = weighted
    ref[64:72] = jnp.where(row_id == 0, peak, jnp.where(row_id == 1, total, 0.0))


def put_narrow(ref, state):
    peak, total, weighted = state
    row_id = lax.broadcasted_iota(jnp.int32, (16, weighted.shape[1]), 0)
    stats = jnp.zeros((16, weighted.shape[1]), F32)
    for at, part in enumerate(thirds(peak) + thirds(total)):
        stats = jnp.where(row_id == at, part, stats)
    ref[0:64] = weighted.astype(BF16)
    ref[64:80] = stats.astype(BF16)


def narrow(ref):
    stats = ref[64:80].astype(F32)
    peak = stats[0:1] + stats[1:2] + stats[2:3]
    total = stats[3:4] + stats[4:5] + stats[5:6]
    return peak, total, ref[0:64].astype(F32)


def next_merge_kernel(held, got, before, own, payload):
    state = merge(wide(held), narrow(got))
    put_narrow(payload, state)
    put_wide(own, state)


def last_merge_kernel(held, got, before, agent_values):
    _, total, weighted = merge(wide(held), narrow(got))
    agent_values[...] = (weighted / total).astype(BF16)


def token_kernel(scale, patches, w_query, agents, after, weights, queries):
    heads = weights.shape[1] // agents.shape[0]
    queries[...] = dot_nn(patches[...], w_query[...]).astype(BF16)

    def scores_of(head):
        lanes = slice(head // 2 * 128, head // 2 * 128 + 128)
        return dot_nt(queries[:, lanes], head_tokens(agents[:, lanes], head % 2, scale))

    ahead = scores_of(0)
    for head in range(heads):
        scores = ahead
        if head + 1 < heads:
            ahead = scores_of(head + 1)
        expo = jnp.exp(scores - jnp.max(scores, axis=1, keepdims=True))
        part = expo * (1.0 / jnp.sum(expo, axis=1, keepdims=True))
        weights[:, head * 256 : head * 256 + 256] = part.astype(BF16)


def halo_kernel(odd_ref, other, outer, w_value, above, below):
    rows = 3 * 128
    odd = odd_ref[0] == 1
    inner_part = other[pl.ds(pl.multiple_of(odd_ref[0] * (other.shape[0] - rows), 128), rows), :]
    inner = dot_nn(inner_part, w_value[...]).astype(BF16)
    outside = dot_nn(outer[...], w_value[...]).astype(BF16)
    above[...] = jnp.where(odd, inner, outside)
    below[...] = jnp.where(odd, outside, inner)


def border_kernel(odd_ref, flat, border, sem):
    rows = border.shape[0]
    start = pl.multiple_of(odd_ref[0] * (flat.shape[0] - rows), 128)
    copy = pltpu.make_async_copy(flat.at[pl.ds(start, rows), :], border, sem)
    copy.start()
    copy.wait()


def conv_kernel(first_lane, values, above, below, seven, five, three, after, position, padded, taps):
    out_rows, width = position.shape[0], position.shape[1]
    lanes = 128
    span = 3 * width
    edge = jnp.zeros((out_rows + 6, 8, lanes), F32)
    padded[:, 0:8, :] = edge
    padded[:, 8 + width : 16 + width, :] = edge
    for group in range(position.shape[2] // lanes):
        here = slice(first_lane + group * lanes, first_lane + (group + 1) * lanes)
        merged = [[seven[p, q : q + 1, here] for q in range(7)] for p in range(7)]
        for p in range(5):
            for q in range(5):
                merged[p + 1][q + 1] = merged[p + 1][q + 1] + five[p, q : q + 1, here]
        for p in range(3):
            for q in range(3):
                merged[p + 2][q + 2] = merged[p + 2][q + 2] + three[p, q : q + 1, here]
        for p in range(7):
            for q in range(7):
                taps[p, q] = jnp.broadcast_to(merged[p][q], (8, lanes))
        inside = slice(8, 8 + width)
        padded[0:3, inside, :] = above[0:span, here].astype(F32).reshape(3, width, lanes)
        padded[3 : 3 + out_rows, inside, :] = values[:, here].astype(F32).reshape(out_rows, width, lanes)
        padded[3 + out_rows : 6 + out_rows, inside, :] = below[0:span, here].astype(F32).reshape(3, width, lanes)
        for at in range(0, width, 8):
            totals = [jnp.zeros((8, lanes), F32)] * out_rows
            for q in range(7):
                lines = [padded[row, at + 5 + q : at + 13 + q, :] for row in range(out_rows + 6)]
                for p in range(7):
                    tap = taps[p, q]
                    for row in range(out_rows):
                        totals[row] = totals[row] + lines[row + p] * tap
            for row in range(out_rows):
                position[row, at : at + 8, group * lanes : (group + 1) * lanes] = totals[row]


def out_kernel(own_ref, weights_low, weights_high, own, near, side, far, position_low, position_high, w_out, mixed, spread):
    @pl.when(pl.program_id(0) == 0)
    def _():
        spread[...] = jnp.zeros_like(spread)
        for index, part in enumerate((own, near, side, far)):
            chunk = index ^ own_ref[0]
            group, place = chunk // 2, chunk % 2
            for half in range(2):
                rows = pl.ds(pl.multiple_of(place * 128 + half * 64, 64), 64)
                cols = pl.ds(pl.multiple_of(place * 512 + half * 256, 256), 256)
                spread[group, rows, cols] = part[:, half * 256 : half * 256 + 256]

    block = mixed.shape[0]
    here = pl.ds(pl.multiple_of(pl.program_id(0) * block, block), block)
    blended = []
    for group, (weights, position) in enumerate(((weights_low, position_low), (weights_high, position_high))):
        attended = dot_nt(weights[here, :], spread[group])
        blended.append((attended + position[here, :]).astype(BF16))
    mixed[...] = dot_nn(jnp.concatenate(blended, axis=1), w_out[...]).astype(BF16)


def params(megabytes=48):
    return pltpu.CompilerParams(vmem_limit_bytes=megabytes << 20)


def cost(flops, moved, exps=0):
    return pl.CostEstimate(flops=int(flops), bytes_accessed=int(moved), transcendentals=int(exps))


def shape(dims, dtype):
    return jax.ShapeDtypeStruct(dims, dtype)


def exchange(x, bit):
    peers = lax.axis_size("col")
    return lax.ppermute(x, "col", [(i, i ^ bit) for i in range(peers)])


def on_device(patches, tissue, w_query, w_key, w_value, w_out, agent_tokens, seven, five, three):
    band_rows, width, dim = patches.shape
    tokens = band_rows * width
    agents = agent_tokens.shape[0]
    half_dim = dim // 2
    scale = (dim // HEADS) ** (-0.5)
    flat = patches.reshape(tokens, dim)
    peers = lax.axis_size("col")
    place = lax.axis_index("col")
    odd = place % 2
    odd_word = jnp.reshape(odd, (1,)).astype(jnp.int32)
    own_chunk = jnp.reshape(chunk_of_device(), (1,)).astype(jnp.int32)
    smem = pl.BlockSpec(memory_space=pltpu.SMEM)
    vmem = pl.BlockSpec(memory_space=VMEM)
    anywhere = pl.BlockSpec(memory_space=pl.ANY)

    other = exchange(flat, 1)
    other_tissue = exchange(tissue, 1)
    rest = [(i, i + 1) for i in range(1, peers - 1, 2)]
    border = pl.pallas_call(
        border_kernel,
        out_shape=shape((3 * width, dim), BF16),
        in_specs=[smem, pl.BlockSpec(memory_space=pltpu.HBM)],
        out_specs=vmem,
        scratch_shapes=[pltpu.SemaphoreType.DMA],
        compiler_params=params(60),
        cost_estimate=cost(1e10, 1e6),
        name="border",
    )(odd_word, flat)
    outer = lax.ppermute(border, "col", rest + [(j, i) for i, j in rest])

    wide_shape, narrow_shape = shape((72, 512), F32), shape((80, 512), BF16)
    values, held, payload = pl.pallas_call(
        functools.partial(band_kernel, scale),
        out_shape=(shape((tokens, dim), BF16), wide_shape, narrow_shape),
        in_specs=[smem] + [vmem] * 7,
        out_specs=[vmem] * 3,
        scratch_shapes=[VMEM((2 * tokens, half_dim), BF16), VMEM((2 * tokens, half_dim), BF16)],
        compiler_params=params(24),
        cost_estimate=cost(1.8e9, 4e6, 2e6),
        name="band",
    )(own_chunk, flat, other, tissue, other_tissue, w_key, w_value, agent_tokens)

    def token(at, after):
        lanes = slice(at * half_dim, (at + 1) * half_dim)
        return pl.pallas_call(
            functools.partial(token_kernel, scale),
            out_shape=shape((tokens, HEADS // 2 * agents), BF16),
            grid=(1,),
            in_specs=[
                vmem,
                pl.BlockSpec((dim, half_dim), lambda i: (0, at)),
                pl.BlockSpec((agents, half_dim), lambda i: (0, at)),
                anywhere,
            ],
            out_specs=vmem,
            scratch_shapes=[VMEM((tokens, half_dim), BF16)],
            compiler_params=params(20),
            cost_estimate=cost(1.1e9, 6e6, 1e6),
            name="token",
        )(flat, w_query, agent_tokens, after)

    def conv(at, after):
        return pl.pallas_call(
            functools.partial(conv_kernel, at * half_dim),
            out_shape=shape((band_rows, width, half_dim), F32),
            in_specs=[vmem] * 6 + [anywhere],
            out_specs=vmem,
            scratch_shapes=[VMEM((band_rows + 6, width + 16, 128), F32), VMEM((7, 7, 8, 128), F32)],
            compiler_params=params(20),
            cost_estimate=cost(3e9, 4e6),
            name="conv",
        )(values, above, below, seven, five, three, after).reshape(tokens, half_dim)

    hop = dict(in_specs=[vmem, vmem, anywhere], compiler_params=params(16), cost_estimate=cost(1e6, 1e6))

    def next_merge(held, got, before):
        return pl.pallas_call(
            next_merge_kernel, out_shape=(wide_shape, narrow_shape), out_specs=[vmem] * 2, name="merge_next", **hop
        )(held, got, before)

    got = exchange(payload, 2)
    weights_low = token(0, payload)
    above, below = pl.pallas_call(
        halo_kernel,
        out_shape=(shape((3 * width, dim), BF16), shape((3 * width, dim), BF16)),
        in_specs=[smem] + [vmem] * 3,
        out_specs=[vmem] * 2,
        compiler_params=params(16),
        cost_estimate=cost(4e8, 2e6),
        name="halo",
    )(odd_word, other, outer, w_value)
    held, payload = next_merge(held, got, weights_low)
    bit = 4
    filler = weights_high = None
    while bit * 2 < peers:
        got = exchange(payload, bit)
        if weights_high is None:
            weights_high = filler = token(1, payload)
        held, payload = next_merge(held, got, filler)
        bit *= 2
    got = exchange(payload, bit)
    position_low = conv(0, payload)
    own = pl.pallas_call(
        last_merge_kernel, out_shape=shape((64, 512), BF16), out_specs=vmem, name="merge_last", **hop
    )(held, got, position_low)
    near = exchange(own, 2)
    side = exchange(own, 1)
    position_high = conv(1, own)
    far = exchange(near, 1)

    block = 256
    mixed = pl.pallas_call(
        out_kernel,
        grid=(tokens // block,),
        out_shape=shape((tokens, dim), BF16),
        in_specs=[smem] + [vmem] * 9,
        out_specs=pl.BlockSpec((block, dim), lambda i: (i, 0)),
        scratch_shapes=[VMEM((2, 256, 1024), BF16)],
        compiler_params=params(20),
        cost_estimate=cost(1.1e9, 8e6),
        name="out",
    )(own_chunk, weights_low, weights_high, own, near, side, far, position_low, position_high, w_out)
    return mixed.reshape(band_rows, width, dim)


def solution(mesh):
    return jax.shard_map(
        on_device,
        mesh=mesh,
        in_specs=(
            P(("slide", "col"), None, None),
            P(("slide", "col"), None),
            P(),
            P(),
            P(),
            P(),
            P(),
            P(),
            P(),
            P(),
        ),
        out_specs=P(("slide", "col"), None, None),
        check_vma=False,
    )
```

time: 61.2 us -> 43.4 us (0.71)
  waiting for transfers between devices: 14.4 us -> 7.03 us
  local copies, waits for them, and re-layouts: 6.92 us -> 0.99 us
  Pallas kernels: 25 us -> 21.9 us
  starting transfers between devices: 14.2 us -> 13.1 us
    ppermute x7 -> x8, waiting for transfers between devices: 14.4 us -> 7.03 us  [exchange(): return lax.ppermute(x, 'col', [(i, i ^ bit) for i in range(peers)])]
    unnamed x26 -> x22, local copies, waits for them, and re-layouts: 6.92 us -> 0.99 us
    pallas_call x1, Pallas kernels: 7.44 us -> 4.68 us  [on_device(): pl.pallas_call(functools.partial(band_kernel, scale), out_shape=(shape((t...]
    pallas_call x1, Pallas kernels: 5.54 us -> 3.64 us  [on_device(): pl.pallas_call(out_kernel, grid=(tokens // block,), out_shape=shape((toke...]
    pallas_call x5 -> x8, Pallas kernels: 11.9 us -> 13.5 us  [the longest x2 7.03 us: conv(): pl.pallas_call(functools.partial(conv_kernel, at * half_dim), out_shape=s...]
    ppermute x7 -> x8, starting transfers between devices: 13.4 us -> 12.4 us  [exchange(): return lax.ppermute(x, 'col', [(i, i ^ bit) for i in range(peers)])]
  transfers between devices with their start and end apart: 9 -> 9, of which waited for: 4 -> 5; matrix products, arithmetic and copies ran while one was open for 0% -> 0% of each run, Pallas kernels for 20% -> 42%
where the time goes in v2:
time: 43.4 us; the launch traced here: 43.2 us
  Pallas kernels  21.9 us (50%)
  starting transfers between devices  13.1 us (30%)
  waiting for transfers between devices  7.03 us (16%)
  local copies, waits for them, and re-layouts  0.99 us (2%)
    ppermute x8, starting transfers between devices, exchange(): return lax.ppermute(x, 'col', [(i, i ^ bit) for i in range(peers)])  12.4 us
    ppermute x8, waiting for transfers between devices, exchange(): return lax.ppermute(x, 'col', [(i, i ^ bit) for i in range(peers)])  7.03 us
    pallas_call x2, Pallas kernels, conv(): pl.pallas_call(functools.partial(conv_kernel, at * half_dim), out_shape=s...  7.03 us
    pallas_call x1, Pallas kernels, on_device(): pl.pallas_call(functools.partial(band_kernel, scale), out_shape=(shape((t...  4.68 us
    pallas_call x2, Pallas kernels, token(): pl.pallas_call(functools.partial(token_kernel, scale), out_shape=shape((t...  3.9 us
    pallas_call x1, Pallas kernels, on_device(): pl.pallas_call(out_kernel, grid=(tokens // block,), out_shape=shape((toke...  3.64 us
    pallas_call x1, Pallas kernels, on_device(): pl.pallas_call(border_kernel, out_shape=shape((3 * width, dim), BF16), in...  1.9 us
    unnamed x22, local copies, waits for them, and re-layouts  0.99 us
  transfers between devices with their start and end apart: 9, of which 5 were waited for; matrix products, arithmetic and copies ran while one was open for 0% of the time, Pallas kernels for 42%

profile of v2, /device:TPU:0, one launch (start us, length us, event | category | flops | bytes accessed | tf_op | source)
XLA Modules:
  0.0 43.2 jit_solution(442511565154889222)
XLA Ops:
  0.0 0.5 %collective-permute-start = (bf16[1024,512]{1,0:T(8,128)(2,1)}, bf16[1024,512]{1,0:T(8,128)(2,1)S(1)}, u32[]{:S(2)}, u32[]{:S(2)}) collective-permute-start(bf16[1024,512]{1,0:T(8,128)(2,1)} %bitcast.9), channel_id=1, source_target_pairs={{0,1},{1,0},{2,3},{3,2},{4,5},{5,4},{6,7},{7,6},{8,9},{9,8},{10,11... | collective-permute-start | bytes 3145736 | tf_op jit(solution)/shard_map/ppermute | solution.py:261
  0.5 0.0 copy-start.10
  0.5 0.0 copy-start
  0.5 0.0 copy-start.2
  0.5 0.0 copy-start.3
  0.5 1.9 %border.1 = bf16[384,512]{1,0:T(8,128)(2,1)} custom-call(s32[1]{0:T(128)} %bitcast.2.odd_ref, bf16[1024,512]{1,0:T(8,128)(2,1)} %bitcast.10), custom_call_target="tpu_custom_call" | custom-call | flops 10000000000 | bytes 1000000 | tf_op jit(solution)/shard_map/border/pallas_call | solution.py:283
  2.4 0.7 %collective-permute-start.5 = (bf16[384,512]{1,0:T(8,128)(2,1)}, bf16[384,512]{1,0:T(8,128)(2,1)S(1)}, u32[]{:S(2)}, u32[]{:S(2)}) collective-permute-start(bf16[384,512]{1,0:T(8,128)(2,1)} %border.1), channel_id=1, source_target_pairs={{1,2},{3,4},{5,6},{7,8},{9,10},{11,12},{13,14},{2,1},{4,3},{6,5},{... | collective-permute-start | bytes 1179656 | tf_op jit(solution)/shard_map/ppermute | solution.py:293
  3.1 0.0 copy-done.10
  3.1 3.9 %collective-permute-start.1 = (s32[8,128]{1,0:T(8,128)S(1)}, s32[8,128]{1,0:T(8,128)S(1)}, u32[]{:S(2)}, u32[]{:S(2)}) collective-permute-start(s32[8,128]{1,0:T(8,128)S(1)} %copy-done.10), channel_id=1, source_target_pairs={{0,1},{1,0},{2,3},{3,2},{4,5},{5,4},{6,7},{7,6},{8,9},{9,8},{10,11... | collective-permute-start | bytes 12296 | tf_op jit(solution)/shard_map/ppermute | solution.py:261
  7.0 0.8 %collective-permute-done.1.other_tissue = s32[8,128]{1,0:T(8,128)S(1)} collective-permute-done((s32[8,128]{1,0:T(8,128)S(1)}, s32[8,128]{1,0:T(8,128)S(1)}, u32[]{:S(2)}, u32[]{:S(2)}) %collective-permute-start.1) | collective-permute-done | bytes 4128 | tf_op jit(solution)/shard_map/ppermute | solution.py:261
  7.8 0.0 collective-permute-done.other
  7.8 0.0 copy-done
  7.8 0.0 copy-done.2
  7.8 0.0 copy-done.3
  7.9 0.0 copy-start.5
  7.9 0.9 %copy-done.5 = bf16[256,512]{1,0:T(8,128)(2,1)S(1)} copy-done((bf16[256,512]{1,0:T(8,128)(2,1)S(1)}, bf16[256,512]{1,0:T(8,128)(2,1)}, u32[]{:S(2)}) %copy-start.5) | copy-done | bytes 262168
  8.8 4.7 %band.1 = (bf16[1024,512]{1,0:T(8,128)(2,1)S(1)}, f32[72,512]{1,0:T(8,128)S(1)}, bf16[80,512]{1,0:T(8,128)(2,1)S(1)}) custom-call(s32[1]{0:T(128)} %bitcast.own_ref, bf16[1024,512]{1,0:T(8,128)(2,1)S(1)} %bitcast.11, bf16[1024,512]{1,0:T(8,128)(2,1)S(1)} %collective-permute-done.other, s32[8,128]{1,0:T(8,128)S(1)} %copy-done.10, ...), custom_call_target="tpu_custom_call" | custom-call | flops 1800000000 | bytes 4000000 | tf_op jit(solution)/shard_map/band/pallas_call | solution.py:296
  13.5 1.6 %collective-permute-start.2 = (bf16[80,512]{1,0:T(8,128)(2,1)S(1)}, bf16[80,512]{1,0:T(8,128)(2,1)S(1)}, u32[]{:S(2)}, u32[]{:S(2)}) collective-permute-start(bf16[80,512]{1,0:T(8,128)(2,1)S(1)} %get-tuple-element.14.after), channel_id=1, source_target_pairs={{0,2},{1,3},{2,0},{3,1},{4,6},{5,7},{6,4},{7,5},{8,10},{9,11},{10,... | collective-permute-start | bytes 245768 | tf_op jit(solution)/shard_map/ppermute | solution.py:261
  15.1 0.0 collective-permute-done.5.outer
  15.1 0.6 %halo.1 = (bf16[384,512]{1,0:T(8,128)(2,1)S(1)}, bf16[384,512]{1,0:T(8,128)(2,1)S(1)}) custom-call(s32[1]{0:T(128)} %bitcast.2.odd_ref, bf16[1024,512]{1,0:T(8,128)(2,1)S(1)} %collective-permute-done.other, bf16[384,512]{1,0:T(8,128)(2,1)S(1)} %collective-permute-done.5.outer, bf16[512,512]{1,0:T(8,128)(2,1)S(1)} %copy-done), custom_call_target="tpu_custom_call" | custom-call | flops 400000000 | bytes 2000000 | tf_op jit(solution)/shard_map/halo/pallas_call | solution.py:347
  15.7 0.0 copy-done.4
  15.7 0.0 copy-done.6
  15.7 2.0 %token_.2.before.weights_low = bf16[1024,1024]{1,0:T(8,128)(2,1)S(1)} custom-call(bf16[1024,512]{1,0:T(8,128)(2,1)S(1)} %bitcast.12, bf16[512,512]{1,0:T(8,128)(2,1)S(1)} %copy-done.4, bf16[256,512]{1,0:T(8,128)(2,1)S(1)} %copy-done.6, bf16[80,512]{1,0:T(8,128)(2,1)S(1)} %get-tuple-element.14.after), custom_call_target="tpu_custom_call" | custom-call | flops 1100000000 | bytes 6000000 | tf_op jit(solution)/shard_map/token/pallas_call | solution.py:309
  17.7 0.6 %collective-permute-done.2.got = bf16[80,512]{1,0:T(8,128)(2,1)S(1)} collective-permute-done((bf16[80,512]{1,0:T(8,128)(2,1)S(1)}, bf16[80,512]{1,0:T(8,128)(2,1)S(1)}, u32[]{:S(2)}, u32[]{:S(2)}) %collective-permute-start.2) | collective-permute-done | bytes 81952 | tf_op jit(solution)/shard_map/ppermute | solution.py:261
  18.3 0.1 merge_next.2
  18.3 2.7 %collective-permute-start.3 = (bf16[80,512]{1,0:T(8,128)(2,1)S(1)}, bf16[80,512]{1,0:T(8,128)(2,1)S(1)}, u32[]{:S(2)}, u32[]{:S(2)}) collective-permute-start(bf16[80,512]{1,0:T(8,128)(2,1)S(1)} %get-tuple-element.16.after), channel_id=1, source_target_pairs={{0,4},{1,5},{2,6},{3,7},{4,0},{5,1},{6,2},{7,3},{8,12},{9,13},{10,... | collective-permute-start | bytes 245768 | tf_op jit(solution)/shard_map/ppermute | solution.py:261
  21.0 1.9 %token_.3.before.weights_high = bf16[1024,1024]{1,0:T(8,128)(2,1)S(1)} custom-call(bf16[1024,512]{1,0:T(8,128)(2,1)S(1)} %bitcast.13, bf16[512,512]{1,0:T(8,128)(2,1)S(1)} %copy-done.4, bf16[256,512]{1,0:T(8,128)(2,1)S(1)} %copy-done.6, bf16[80,512]{1,0:T(8,128)(2,1)S(1)} %get-tuple-element.16.after), custom_call_target="tpu_custom_call" | custom-call | flops 1100000000 | bytes 6000000 | tf_op jit(solution)/shard_map/token/pallas_call | solution.py:309
  23.0 0.0 copy-start.7
  23.0 0.0 copy-start.8
  23.0 0.0 copy-start.9
  23.0 0.5 %collective-permute-done.3.got = bf16[80,512]{1,0:T(8,128)(2,1)S(1)} collective-permute-done((bf16[80,512]{1,0:T(8,128)(2,1)S(1)}, bf16[80,512]{1,0:T(8,128)(2,1)S(1)}, u32[]{:S(2)}, u32[]{:S(2)}) %collective-permute-start.3) | collective-permute-done | bytes 81952 | tf_op jit(solution)/shard_map/ppermute | solution.py:261
  23.5 0.1 merge_next.3
  23.6 3.4 %collective-permute-start.4 = (bf16[80,512]{1,0:T(8,128)(2,1)S(1)}, bf16[80,512]{1,0:T(8,128)(2,1)S(1)}, u32[]{:S(2)}, u32[]{:S(2)}) collective-permute-start(bf16[80,512]{1,0:T(8,128)(2,1)S(1)} %get-tuple-element.19.after), channel_id=1, source_target_pairs={{0,8},{1,9},{2,10},{3,11},{4,12},{5,13},{6,14},{7,15},{8,0},{9,1},... | collective-permute-start | bytes 245768 | tf_op jit(solution)/shard_map/ppermute | solution.py:261
  27.0 0.0 copy-done.7
  27.0 0.0 copy-done.8
  27.0 0.0 copy-done.9
  27.0 3.6 %conv.2 = f32[8,128,256]{2,1,0:T(8,128)S(1)} custom-call(bf16[1024,512]{1,0:T(8,128)(2,1)S(1)} %get-tuple-element.20.values, bf16[384,512]{1,0:T(8,128)(2,1)S(1)} %get-tuple-element.21.above, bf16[384,512]{1,0:T(8,128)(2,1)S(1)} %get-tuple-element.22.below, f32[7,7,512]{2,1,0:T(8,128)S(1)} %copy-done.7, f32[5,5,512]{2,1,0:T(8,128)S(1)} %copy-done.8, ...), custom_call_target="tpu_custom_call" | custom-call | flops 3000000000 | bytes 4000000 | tf_op jit(solution)/shard_map/conv/pallas_call | solution.py:327
  30.6 1.0 %collective-permute-done.4.got = bf16[80,512]{1,0:T(8,128)(2,1)S(1)} collective-permute-done((bf16[80,512]{1,0:T(8,128)(2,1)S(1)}, bf16[80,512]{1,0:T(8,128)(2,1)S(1)}, u32[]{:S(2)}, u32[]{:S(2)}) %collective-permute-start.4) | collective-permute-done | bytes 81952 | tf_op jit(solution)/shard_map/ppermute | solution.py:261
  31.7 0.0 copy-start.1
  31.7 0.3 collective-permute-start.6
  32.0 0.0 collective-permute-start.7
  32.0 4.0 %collective-permute-done.6.near = bf16[64,512]{1,0:T(8,128)(2,1)S(1)} collective-permute-done((bf16[64,512]{1,0:T(8,128)(2,1)S(1)}, bf16[64,512]{1,0:T(8,128)(2,1)S(1)}, u32[]{:S(2)}, u32[]{:S(2)}) %collective-permute-start.6) | collective-permute-done | bytes 65568 | tf_op jit(solution)/shard_map/ppermute | solution.py:261
  36.1 0.0 collective-permute-start.8
  36.1 3.4 %conv.3 = f32[8,128,256]{2,1,0:T(8,128)S(1)} custom-call(bf16[1024,512]{1,0:T(8,128)(2,1)S(1)} %get-tuple-element.20.values, bf16[384,512]{1,0:T(8,128)(2,1)S(1)} %get-tuple-element.21.above, bf16[384,512]{1,0:T(8,128)(2,1)S(1)} %get-tuple-element.22.below, f32[7,7,512]{2,1,0:T(8,128)S(1)} %copy-done.7, f32[5,5,512]{2,1,0:T(8,128)S(1)} %copy-done.8, ...), custom_call_target="tpu_custom_call" | custom-call | flops 3000000000 | bytes 4000000 | tf_op jit(solution)/shard_map/conv/pallas_call | solution.py:327
  39.5 0.0 collective-permute-done.7.side
  39.5 0.0 collective-permute-done.8.far
  39.5 0.0 copy-done.1
  39.5 3.6 %out.1 = bf16[1024,512]{1,0:T(8,128)(2,1)} custom-call(s32[1]{0:T(128)} %bitcast.own_ref, bf16[1024,1024]{1,0:T(8,128)(2,1)S(1)} %token_.2.before.weights_low, bf16[1024,1024]{1,0:T(8,128)(2,1)S(1)} %token_.3.before.weights_high, bf16[64,512]{1,0:T(8,128)(2,1)S(1)} %merge_last.1.after.own, bf16[64,512]{1,0:T(8,128)(2,1)S(1)} %collective-permute-done.6.near, ...), custom_call_target="tpu_custom_call" | custom-call | flops 1100000000 | bytes 8000000 | tf_op jit(solution)/shard_map/out/pallas_call | solution.py:376
  (3 shorter events, 0.0 us)
Async XLA Ops:
  0.0 7.8 %collective-permute-start = (bf16[1024,512]{1,0:T(8,128)(2,1)}, bf16[1024,512]{1,0:T(8,128)(2,1)S(1)}, u32[]{:S(2)}, u32[]{:S(2)}) collective-permute-start(bf16[1024,512]{1,0:T(8,128)(2,1)} %bitcast.9), channel_id=1, source_target_pairs={{0,1},{1,0},{2,3},{3,2},{4,5},{5,4},{6,7},{7,6},{8,9},{9,8},{10,11... | collective-permute-start | bytes 3145736 | tf_op jit(solution)/shard_map/ppermute | solution.py:261
  0.5 2.6 %copy-start.10 = (s32[8,128]{1,0:T(8,128)S(1)}, s32[8,128]{1,0:T(8,128)}, u32[]{:S(2)}) copy-start(s32[8,128]{1,0:T(8,128)} %tissue.1) | copy-start | bytes 12292
  0.5 7.4 %copy-start = (bf16[512,512]{1,0:T(8,128)(2,1)S(1)}, bf16[512,512]{1,0:T(8,128)(2,1)}, u32[]{:S(2)}) copy-start(bf16[512,512]{1,0:T(8,128)(2,1)} %w_value.3) | copy-start | bytes 1572868
  0.5 7.4 %copy-start.2 = (bf16[8,128,512]{2,1,0:T(8,128)(2,1)S(1)}, bf16[8,128,512]{2,1,0:T(8,128)(2,1)}, u32[]{:S(2)}) copy-start(bf16[8,128,512]{2,1,0:T(8,128)(2,1)} %param.10) | copy-start | bytes 3145732
  0.5 7.4 %copy-start.3 = (bf16[512,512]{1,0:T(8,128)(2,1)S(1)}, bf16[512,512]{1,0:T(8,128)(2,1)}, u32[]{:S(2)}) copy-start(bf16[512,512]{1,0:T(8,128)(2,1)} %w_key.1) | copy-start | bytes 1572868
  2.4 12.7 %collective-permute-start.5 = (bf16[384,512]{1,0:T(8,128)(2,1)}, bf16[384,512]{1,0:T(8,128)(2,1)S(1)}, u32[]{:S(2)}, u32[]{:S(2)}) collective-permute-start(bf16[384,512]{1,0:T(8,128)(2,1)} %border.1), channel_id=1, source_target_pairs={{1,2},{3,4},{5,6},{7,8},{9,10},{11,12},{13,14},{2,1},{4,3},{6,5},{... | collective-permute-start | bytes 1179656 | tf_op jit(solution)/shard_map/ppermute | solution.py:293
  3.1 4.8 %collective-permute-start.1 = (s32[8,128]{1,0:T(8,128)S(1)}, s32[8,128]{1,0:T(8,128)S(1)}, u32[]{:S(2)}, u32[]{:S(2)}) collective-permute-start(s32[8,128]{1,0:T(8,128)S(1)} %copy-done.10), channel_id=1, source_target_pairs={{0,1},{1,0},{2,3},{3,2},{4,5},{5,4},{6,7},{7,6},{8,9},{9,8},{10,11... | collective-permute-start | bytes 12296 | tf_op jit(solution)/shard_map/ppermute | solution.py:261
  7.9 1.0 %copy-start.5 = (bf16[256,512]{1,0:T(8,128)(2,1)S(1)}, bf16[256,512]{1,0:T(8,128)(2,1)}, u32[]{:S(2)}) copy-start(bf16[256,512]{1,0:T(8,128)(2,1)} %agents.5) | copy-start | bytes 786436
  8.8 6.9 %copy-start.4 = (bf16[512,512]{1,0:T(8,128)(2,1)S(1)}, bf16[512,512]{1,0:T(8,128)(2,1)}, u32[]{:S(2)}) copy-start(bf16[512,512]{1,0:T(8,128)(2,1)} %w_query.3) | copy-start | bytes 1572868
  8.8 6.9 %copy-start.6 = (bf16[256,512]{1,0:T(8,128)(2,1)S(1)}, bf16[256,512]{1,0:T(8,128)(2,1)}, u32[]{:S(2)}) copy-start(bf16[256,512]{1,0:T(8,128)(2,1)} %agents.5) | copy-start | bytes 786436
  13.5 4.8 %collective-permute-start.2 = (bf16[80,512]{1,0:T(8,128)(2,1)S(1)}, bf16[80,512]{1,0:T(8,128)(2,1)S(1)}, u32[]{:S(2)}, u32[]{:S(2)}) collective-permute-start(bf16[80,512]{1,0:T(8,128)(2,1)S(1)} %get-tuple-element.14.after), channel_id=1, source_target_pairs={{0,2},{1,3},{2,0},{3,1},{4,6},{5,7},{6,4},{7,5},{8,10},{9,11},{10,... | collective-permute-start | bytes 245768 | tf_op jit(solution)/shard_map/ppermute | solution.py:261
  18.3 5.2 %collective-permute-start.3 = (bf16[80,512]{1,0:T(8,128)(2,1)S(1)}, bf16[80,512]{1,0:T(8,128)(2,1)S(1)}, u32[]{:S(2)}, u32[]{:S(2)}) collective-permute-start(bf16[80,512]{1,0:T(8,128)(2,1)S(1)} %get-tuple-element.16.after), channel_id=1, source_target_pairs={{0,4},{1,5},{2,6},{3,7},{4,0},{5,1},{6,2},{7,3},{8,12},{9,13},{10,... | collective-permute-start | bytes 245768 | tf_op jit(solution)/shard_map/ppermute | solution.py:261
  23.0 4.0 %copy-start.7 = (f32[7,7,512]{2,1,0:T(8,128)S(1)}, f32[7,7,512]{2,1,0:T(8,128)}, u32[]{:S(2)}) copy-start(f32[7,7,512]{2,1,0:T(8,128)} %seven.3) | copy-start | bytes 301060
  23.0 4.0 %copy-start.8 = (f32[5,5,512]{2,1,0:T(8,128)S(1)}, f32[5,5,512]{2,1,0:T(8,128)}, u32[]{:S(2)}) copy-start(f32[5,5,512]{2,1,0:T(8,128)} %five.3) | copy-start | bytes 153604
  23.0 4.0 %copy-start.9 = (f32[3,3,512]{2,1,0:T(4,128)S(1)}, f32[3,3,512]{2,1,0:T(4,128)}, u32[]{:S(2)}) copy-start(f32[3,3,512]{2,1,0:T(4,128)} %three.3) | copy-start | bytes 55300
  23.6 8.1 %collective-permute-start.4 = (bf16[80,512]{1,0:T(8,128)(2,1)S(1)}, bf16[80,512]{1,0:T(8,128)(2,1)S(1)}, u32[]{:S(2)}, u32[]{:S(2)}) collective-permute-start(bf16[80,512]{1,0:T(8,128)(2,1)S(1)} %get-tuple-element.19.after), channel_id=1, source_target_pairs={{0,8},{1,9},{2,10},{3,11},{4,12},{5,13},{6,14},{7,15},{8,0},{9,1},... | collective-permute-start | bytes 245768 | tf_op jit(solution)/shard_map/ppermute | solution.py:261
  31.7 7.8 %copy-start.1 = (bf16[512,512]{1,0:T(8,128)(2,1)S(1)}, bf16[512,512]{1,0:T(8,128)(2,1)}, u32[]{:S(2)}) copy-start(bf16[512,512]{1,0:T(8,128)(2,1)} %w_out.1) | copy-start | bytes 1572868
  31.7 4.3 %collective-permute-start.6 = (bf16[64,512]{1,0:T(8,128)(2,1)S(1)}, bf16[64,512]{1,0:T(8,128)(2,1)S(1)}, u32[]{:S(2)}, u32[]{:S(2)}) collective-permute-start(bf16[64,512]{1,0:T(8,128)(2,1)S(1)} %merge_last.1.after.own), channel_id=1, source_target_pairs={{0,2},{1,3},{2,0},{3,1},{4,6},{5,7},{6,4},{7,5},{8,10},{9,11},{10,... | collective-permute-start | bytes 196616 | tf_op jit(solution)/shard_map/ppermute | solution.py:261
  32.0 7.5 %collective-permute-start.7 = (bf16[64,512]{1,0:T(8,128)(2,1)S(1)}, bf16[64,512]{1,0:T(8,128)(2,1)S(1)}, u32[]{:S(2)}, u32[]{:S(2)}) collective-permute-start(bf16[64,512]{1,0:T(8,128)(2,1)S(1)} %merge_last.1.after.own), channel_id=1, source_target_pairs={{0,1},{1,0},{2,3},{3,2},{4,5},{5,4},{6,7},{7,6},{8,9},{9,8},{10,11... | collective-permute-start | bytes 196616 | tf_op jit(solution)/shard_map/ppermute | solution.py:261
  36.1 3.4 %collective-permute-start.8 = (bf16[64,512]{1,0:T(8,128)(2,1)S(1)}, bf16[64,512]{1,0:T(8,128)(2,1)S(1)}, u32[]{:S(2)}, u32[]{:S(2)}) collective-permute-start(bf16[64,512]{1,0:T(8,128)(2,1)S(1)} %collective-permute-done.6.near), channel_id=1, source_target_pairs={{0,1},{1,0},{2,3},{3,2},{4,5},{5,4},{6,7},{7,6},{8,9},{9,8},{10,11... | collective-permute-start | bytes 196616 | tf_op jit(solution)/shard_map/ppermute | solution.py:261

commit v3 on v2

v3 whole, which is shorter than its diff:
```python
import functools

import jax
import jax.numpy as jnp
from jax import lax
from jax.experimental import pallas as pl
from jax.experimental.pallas import tpu as pltpu
from jax.sharding import PartitionSpec as P

HEADS = 8
NO_SCORE = -1e30
F32 = jnp.float32
BF16 = jnp.bfloat16
VMEM = pltpu.VMEM


def dot_nt(a, b):
    return lax.dot_general(a, b, (((1,), (1,)), ((), ())), preferred_element_type=F32)


def dot_nn(a, b):
    return lax.dot_general(a, b, (((1,), (0,)), ((), ())), preferred_element_type=F32)


def head_tokens(pair, half, scale):
    lane = lax.broadcasted_iota(jnp.int32, pair.shape, 1)
    mine = (lane >= 64) if half else (lane < 64)
    return jnp.where(mine, pair.astype(F32) * scale, 0.0).astype(BF16)


def chunk_of_device():
    place = lax.axis_index("col")
    return (place & 1) * 2 + ((place >> 1) & 1)


def chunk_state(index, own, scale, keys, vals, tissue, other_tissue, agents):
    lines = []
    for grid in (tissue, other_tissue):
        bias = jnp.where(grid[...] > 0, 0.0, NO_SCORE).astype(F32)
        lines += [bias[row : row + 1] for row in range(bias.shape[0])]
    bias_line = jnp.concatenate(lines, axis=1)
    lanes = pl.ds(pl.multiple_of(((own % 2) ^ index) * 128, 128), 128)
    pair_agents = agents[:, pl.ds(pl.multiple_of((own ^ index) * 128, 128), 128)]
    both = [dot_nt(head_tokens(pair_agents, half, scale), keys[:, lanes]) + bias_line for half in range(2)]
    done = []
    for scores in both:
        peak = jnp.max(scores, axis=1, keepdims=True)
        expo = jnp.exp(scores - peak)
        total = jnp.sum(expo, axis=1, keepdims=True)
        done.append((peak, total, dot_nn(expo.astype(BF16), vals[:, lanes])))
    lane = lax.broadcasted_iota(jnp.int32, done[0][2].shape, 1)
    weighted = jnp.where(lane < 64, done[0][2], done[1][2]).T
    stats = jnp.zeros(weighted.T.shape, F32)
    for at, value in enumerate(done[0][:2] + done[1][:2]):
        stats = jnp.where(lane == at, value, stats)
    stats = stats.T
    sides = []
    for at in range(2):
        sides.append((stats[2 * at : 2 * at + 1], stats[2 * at + 1 : 2 * at + 2], weighted[64 * at : 64 * at + 64]))
    return tuple(jnp.concatenate(pair, axis=1) for pair in zip(*sides))


def band_kernel(
    scale, own_ref, mine, other, tissue, other_tissue, w_key, w_value, agents, after, values, keys, vals, payload
):
    tokens = mine.shape[0]
    block = 256
    own = own_ref[0]
    half_lanes = pl.ds(pl.multiple_of((own // 2) * 256, 256), 256)
    key_half = w_key[:, half_lanes]
    value_half = w_value[:, half_lanes]
    for at in range(0, tokens, block):
        rows = pl.ds(at, block)
        part = mine[rows, :]
        keys[rows, :] = dot_nn(part, key_half).astype(BF16)
        values[rows, :] = dot_nn(part, w_value[...]).astype(BF16)
        vals[rows, :] = values[rows, half_lanes]
    for at in range(0, tokens, block):
        rows = pl.ds(tokens + at, block)
        part = other[pl.ds(at, block), :]
        keys[rows, :] = dot_nn(part, key_half).astype(BF16)
        vals[rows, :] = dot_nn(part, value_half).astype(BF16)
    put_narrow(payload, chunk_state(1, own, scale, keys, vals, tissue, other_tissue, agents))


def second_band_kernel(scale, own_ref, keys, vals, tissue, other_tissue, agents, keep):
    put_wide(keep, chunk_state(0, own_ref[0], scale, keys, vals, tissue, other_tissue, agents))


def merge(first, second):
    peak_1, total_1, weighted_1 = first
    peak_2, total_2, weighted_2 = second
    peak = jnp.maximum(peak_1, peak_2)
    factor_1 = jnp.exp(peak_1 - peak)
    factor_2 = jnp.exp(peak_2 - peak)
    return peak, total_1 * factor_1 + total_2 * factor_2, weighted_1 * factor_1 + weighted_2 * factor_2


def wide(ref, index=None):
    array = ref[...] if index is None else ref[index]
    return array[64:65], array[65:66], array[0:64]


def thirds(value):
    high = value.astype(BF16).astype(F32)
    rest = value - high
    middle = rest.astype(BF16).astype(F32)
    return high, middle, rest - middle


def put_wide(ref, state):
    peak, total, weighted = state
    row_id = lax.broadcasted_iota(jnp.int32, (8, weighted.shape[1]), 0)
    ref[0:64] = weighted
    ref[64:72] = jnp.where(row_id == 0, peak, jnp.where(row_id == 1, total, 0.0))


def put_narrow(ref, state):
    peak, total, weighted = state
    row_id = lax.broadcasted_iota(jnp.int32, (16, weighted.shape[1]), 0)
    stats = jnp.zeros((16, weighted.shape[1]), F32)
    for at, part in enumerate(thirds(peak) + thirds(total)):
        stats = jnp.where(row_id == at, part, stats)
    ref[0:64] = weighted.astype(BF16)
    ref[64:80] = stats.astype(BF16)


def narrow(ref):
    stats = ref[64:80].astype(F32)
    peak = stats[0:1] + stats[1:2] + stats[2:3]
    total = stats[3:4] + stats[4:5] + stats[5:6]
    return peak, total, ref[0:64].astype(F32)


def next_merge_kernel(held, got, before, own, payload):
    state = merge(wide(held), narrow(got))
    put_narrow(payload, state)
    put_wide(own, state)


def last_merge_kernel(held, got, before, agent_values):
    _, total, weighted = merge(wide(held), narrow(got))
    agent_values[...] = (weighted / total).astype(BF16)


def token_kernel(scale, patches, w_query, agents, after, weights, queries):
    heads = weights.shape[1] // agents.shape[0]
    queries[...] = dot_nn(patches[...], w_query[...]).astype(BF16)

    def scores_of(head):
        lanes = slice(head // 2 * 128, head // 2 * 128 + 128)
        return dot_nt(queries[:, lanes], head_tokens(agents[:, lanes], head % 2, scale))

    ahead = scores_of(0)
    for head in range(heads):
        scores = ahead
        if head + 1 < heads:
            ahead = scores_of(head + 1)
        expo = jnp.exp(scores - jnp.max(scores, axis=1, keepdims=True))
        part = expo * (1.0 / jnp.sum(expo, axis=1, keepdims=True))
        weights[:, head * 256 : head * 256 + 256] = part.astype(BF16)


def border_kernel(odd_ref, values, after, border):
    rows = border.shape[0]
    border[...] = values[pl.ds(pl.multiple_of(odd_ref[0] * (values.shape[0] - rows), 128), rows), :]


def halo_kernel(odd_ref, other, outer, w_value, above, below):
    rows = outer.shape[0]
    odd = odd_ref[0] == 1
    inner_part = other[pl.ds(pl.multiple_of(odd_ref[0] * (other.shape[0] - rows), 128), rows), :]
    inner = dot_nn(inner_part, w_value[...]).astype(BF16)
    above[...] = jnp.where(odd, inner, outer[...])
    below[...] = jnp.where(odd, outer[...], inner)


TAP_COUNTS = (2, 2, 2, 2, 2, 2, 2, 2, 1)


def split_rows(rows):
    return [
        [rows[at] - rows[at + 1] for at in range(0, len(rows) - 1, 2)],
        [rows[at + 1] for at in range(0, len(rows) - 1, 2)],
        [rows[at + 2] - rows[at + 1] for at in range(0, len(rows) - 2, 2)],
    ]


def split_taps(taps):
    even, odd = taps[0::2], taps[1::2]
    both = [even[at] + odd[at] if at < len(odd) else even[at] for at in range(len(even))]
    return [even, both, odd]


def joined_rows(first, second, third):
    return [row for a, b, c in zip(first, second, third) for row in (a + b, b + c)]


def taps_kernel(seven, five, three, taps, mark):
    mark[...] = jnp.zeros_like(mark)
    for q in range(7):
        column = [seven[p, q : q + 1, :] for p in range(7)]
        if 1 <= q <= 5:
            column[1:6] = [tap + five[p, q - 1 : q, :] for p, tap in enumerate(column[1:6])]
        if 2 <= q <= 4:
            column[2:5] = [tap + three[p, q - 2 : q - 1, :] for p, tap in enumerate(column[2:5])]
        parts = [tap for part in split_taps(column) for piece in split_taps(part) for tap in piece]
        parts += [jnp.zeros_like(parts[0])] * (taps.shape[1] - len(parts))
        taps[q] = jnp.concatenate(parts, axis=0)


def conv_kernel(first_lane, values, above, below, all_taps, after, position, points, taps):
    width = position.shape[1]
    lanes, step = 128, 16
    tap_count = sum(TAP_COUNTS)
    zero = jnp.zeros((8, lanes), F32)
    for group in range(position.shape[2] // lanes):
        here = slice(first_lane + group * lanes, first_lane + (group + 1) * lanes)
        there = slice(group * lanes, (group + 1) * lanes)
        for q in range(7):
            for at in range(tap_count):
                taps[q, at] = jnp.broadcast_to(all_taps[q, at : at + 1, here], (8, lanes))
        for at in range(points.shape[0]):
            points[at, 0:8, :] = zero
            points[at, 8 + width : 16 + width, :] = zero
        for at in range(0, width, step):
            rows = []
            for ref in (above, values, below):
                for row in range(0, ref.shape[0], width):
                    rows.append(ref[row + at : row + at + step, here].astype(F32))
            even, odd = rows[0::2], rows[1::2]
            streams = (
                [a - b for a, b in zip(even, odd)],
                odd,
                [a - b for a, b in zip(even[1:], odd)],
            )
            parts = [plane for stream in streams for piece in split_rows(stream) for plane in piece]
            for index, plane in enumerate(parts):
                points[index, 8 + at : 8 + at + step, :] = plane
        for at in range(0, width, step):
            columns = (at, at + 8)
            sums = [[[zero, zero] for _ in TAP_COUNTS] for _ in columns]
            for q in range(7):
                first_point = first_tap = 0
                for piece, count in enumerate(TAP_COUNTS):
                    tap = [taps[q, first_tap + k] for k in range(count)]
                    for total, column in zip(sums, columns):
                        start = column + 5 + q
                        point = [points[first_point + k, start : start + 8, :] for k in range(count + 1)]
                        for out in range(2):
                            for k in range(count):
                                total[piece][out] = total[piece][out] + point[out + k] * tap[k]
                    first_point += count + 1
                    first_tap += count
            for total, column in zip(sums, columns):
                thirds_of = [joined_rows(*total[3 * part : 3 * part + 3]) for part in range(3)]
                for row, plane in enumerate(joined_rows(*thirds_of)):
                    position[row, column : column + 8, there] = plane


def out_kernel(
    own_ref, weights_low, weights_high, own, near, side, far, position_low, position_high, w_out, mixed, spread, buffer, sems
):
    spread[...] = jnp.zeros_like(spread)
    for index, part in enumerate((own, near, side, far)):
        chunk = index ^ own_ref[0]
        group, place = chunk // 2, chunk % 2
        for half in range(2):
            rows = pl.ds(pl.multiple_of(place * 128 + half * 64, 64), 64)
            cols = pl.ds(pl.multiple_of(place * 512 + half * 256, 256), 256)
            spread[group, rows, cols] = part[:, half * 256 : half * 256 + 256]
    tokens = mixed.shape[0]
    block = tokens // 2
    copies = []
    for index in range(2):
        here = slice(index * block, index * block + block)
        blended = []
        for group, (weights, position) in enumerate(((weights_low, position_low), (weights_high, position_high))):
            attended = dot_nt(weights[here, :], spread[group])
            blended.append((attended + position[here, :]).astype(BF16))
        buffer[here, :] = dot_nn(jnp.concatenate(blended, axis=1), w_out[...]).astype(BF16)
        copies.append(pltpu.make_async_copy(buffer.at[here, :], mixed.at[here, :], sems.at[index]))
        copies[-1].start()
    for copy in copies:
        copy.wait()


def params(megabytes=48):
    return pltpu.CompilerParams(vmem_limit_bytes=megabytes << 20)


def cost(flops, moved, exps=0):
    return pl.CostEstimate(flops=int(flops), bytes_accessed=int(moved), transcendentals=int(exps))


def shape(dims, dtype):
    return jax.ShapeDtypeStruct(dims, dtype)


def exchange(x, bit):
    peers = lax.axis_size("col")
    return lax.ppermute(x, "col", [(i, i ^ bit) for i in range(peers)])


def on_device(patches, tissue, w_query, w_key, w_value, w_out, agent_tokens, seven, five, three):
    band_rows, width, dim = patches.shape
    tokens = band_rows * width
    agents = agent_tokens.shape[0]
    half_dim = dim // 2
    scale = (dim // HEADS) ** (-0.5)
    flat = patches.reshape(tokens, dim)
    peers = lax.axis_size("col")
    place = lax.axis_index("col")
    odd = place % 2
    odd_word = jnp.reshape(odd, (1,)).astype(jnp.int32)
    own_chunk = jnp.reshape(chunk_of_device(), (1,)).astype(jnp.int32)
    smem = pl.BlockSpec(memory_space=pltpu.SMEM)
    vmem = pl.BlockSpec(memory_space=VMEM)
    anywhere = pl.BlockSpec(memory_space=pl.ANY)

    other = exchange(flat, 1)
    other_tissue = exchange(tissue, 1)

    taps, mark = pl.pallas_call(
        taps_kernel,
        out_shape=(shape((7, 24, dim), F32), shape((8, 128), F32)),
        in_specs=[vmem] * 3,
        out_specs=[vmem] * 2,
        compiler_params=params(60),
        cost_estimate=cost(1e10, 1e6),
        name="taps",
    )(seven, five, three)

    wide_shape, narrow_shape = shape((72, 512), F32), shape((80, 512), BF16)
    both_bands = shape((2 * tokens, half_dim), BF16)
    values, keys, vals, payload = pl.pallas_call(
        functools.partial(band_kernel, scale),
        out_shape=(shape((tokens, dim), BF16), both_bands, both_bands, narrow_shape),
        in_specs=[smem] + [vmem] * 7 + [anywhere],
        out_specs=[vmem] * 4,
        compiler_params=params(20),
        cost_estimate=cost(1.8e9, 4e6, 1e6),
        name="band",
    )(own_chunk, flat, other, tissue, other_tissue, w_key, w_value, agent_tokens, mark)

    def token(at, after):
        lanes = slice(at * half_dim, (at + 1) * half_dim)
        return pl.pallas_call(
            functools.partial(token_kernel, scale),
            out_shape=shape((tokens, HEADS // 2 * agents), BF16),
            grid=(1,),
            in_specs=[
                vmem,
                pl.BlockSpec((dim, half_dim), lambda i: (0, at)),
                pl.BlockSpec((agents, half_dim), lambda i: (0, at)),
                anywhere,
            ],
            out_specs=vmem,
            scratch_shapes=[VMEM((tokens, half_dim), BF16)],
            compiler_params=params(20),
            cost_estimate=cost((1 + 4 * at) * 2e9, 6e6, 1e6),
            name="token",
        )(flat, w_query, agent_tokens, after)

    def conv(at, after):
        return pl.pallas_call(
            functools.partial(conv_kernel, at * half_dim),
            out_shape=shape((band_rows, width, half_dim), F32),
            in_specs=[vmem] * 4 + [anywhere],
            out_specs=vmem,
            scratch_shapes=[
                VMEM((sum(TAP_COUNTS) + len(TAP_COUNTS), width + 16, 128), F32),
                VMEM((7, sum(TAP_COUNTS), 8, 128), F32),
            ],
            compiler_params=params(20),
            cost_estimate=cost(3e9, 4e6),
            name="conv",
        )(values, above, below, taps, after).reshape(tokens, half_dim)

    hop = dict(in_specs=[vmem, vmem, anywhere], compiler_params=params(16), cost_estimate=cost(1e6, 1e6))

    def next_merge(held, got, before):
        return pl.pallas_call(
            next_merge_kernel, out_shape=(wide_shape, narrow_shape), out_specs=[vmem] * 2, name="merge_next", **hop
        )(held, got, before)

    got = exchange(payload, 2)
    held = pl.pallas_call(
        functools.partial(second_band_kernel, scale),
        out_shape=wide_shape,
        in_specs=[smem] + [vmem] * 5,
        out_specs=vmem,
        compiler_params=params(20),
        cost_estimate=cost(6e8, 4e6, 1e6),
        name="band_second",
    )(own_chunk, keys, vals, tissue, other_tissue, agent_tokens)
    weights_low = token(0, payload)
    held, payload = next_merge(held, got, weights_low)
    border = pl.pallas_call(
        border_kernel,
        out_shape=shape((3 * width, dim), BF16),
        in_specs=[smem, vmem, anywhere],
        out_specs=vmem,
        compiler_params=params(16),
        cost_estimate=cost(3e9, 1e6),
        name="border",
    )(odd_word, values, payload)
    rest = [(i, i + 1) for i in range(1, peers - 1, 2)]
    outer = lax.ppermute(border, "col", rest + [(j, i) for i, j in rest])
    bit = 4
    while bit * 2 < peers:
        got = exchange(payload, bit)
        held, payload = next_merge(held, got, border)
        bit *= 2
    got = exchange(payload, bit)
    weights_high = token(1, payload)
    above, below = pl.pallas_call(
        halo_kernel,
        out_shape=(shape((3 * width, dim), BF16), shape((3 * width, dim), BF16)),
        in_specs=[smem] + [vmem] * 3,
        out_specs=[vmem] * 2,
        compiler_params=params(16),
        cost_estimate=cost(4e8, 2e6),
        name="halo",
    )(odd_word, other, outer, w_value)
    position_low = conv(0, weights_high)
    own = pl.pallas_call(
        last_merge_kernel, out_shape=shape((64, 512), BF16), out_specs=vmem, name="merge_last", **hop
    )(held, got, position_low)
    near = exchange(own, 2)
    far = exchange(own, 3)
    side = exchange(own, 1)
    position_high = conv(1, own)

    mixed = pl.pallas_call(
        out_kernel,
        out_shape=shape((tokens, dim), BF16),
        in_specs=[smem] + [vmem] * 9,
        out_specs=anywhere,
        scratch_shapes=[
            VMEM((2, 256, 1024), BF16),
            VMEM((tokens, dim), BF16),
            pltpu.SemaphoreType.DMA((2,)),
        ],
        compiler_params=params(20),
        cost_estimate=cost(1.1e9, 8e6),
        name="out",
    )(own_chunk, weights_low, weights_high, own, near, side, far, position_low, position_high, w_out)
    return mixed.reshape(band_rows, width, dim)


def solution(mesh):
    return jax.shard_map(
        on_device,
        mesh=mesh,
        in_specs=(
            P(("slide", "col"), None, None),
            P(("slide", "col"), None),
            P(),
            P(),
            P(),
            P(),
            P(),
            P(),
            P(),
            P(),
        ),
        out_specs=P(("slide", "col"), None, None),
        check_vma=False,
    )
```

time: 43.4 us -> 40 us (0.922)
  Pallas kernels: 21.9 us -> 19 us
  starting transfers between devices: 13.1 us -> 11.9 us
  waiting for transfers between devices: 7.03 us -> 7.92 us
    pallas_call x1 -> x3, Pallas kernels: 3.64 us -> 6.52 us  [the longest x1 2.77 us: on_device(): pl.pallas_call(out_kernel, out_shape=shape((tokens, dim), BF16), in_specs...]
    pallas_call x2, Pallas kernels: 7.03 us -> 4.61 us  [conv(): pl.pallas_call(functools.partial(conv_kernel, at * half_dim), out_shape=s...]
    pallas_call x1, Pallas kernels: 1.9 us -> 0.03 us  [on_device(): pl.pallas_call(border_kernel, out_shape=shape((3 * width, dim), BF16), in...]
    ppermute x8, starting transfers between devices: 12.4 us -> 11 us  [exchange(): return lax.ppermute(x, 'col', [(i, i ^ bit) for i in range(peers)])]
    pallas_call x1, Pallas kernels: 4.68 us -> 3.39 us  [on_device(): pl.pallas_call(functools.partial(band_kernel, scale), out_shape=(shape((t...]
    ppermute x8, waiting for transfers between devices: 7.03 us -> 7.91 us  [exchange(): return lax.ppermute(x, 'col', [(i, i ^ bit) for i in range(peers)])]
    unnamed x22 -> x18, local copies, waits for them, and re-layouts: 0.99 us -> 0.71 us
  transfers between devices with their start and end apart: 9 -> 9, of which waited for: 5 -> 4; matrix products, arithmetic and copies ran while one was open for 0% -> 0% of each run, Pallas kernels for 42% -> 32%
where the time goes in v3:
time: 40 us; the launch traced here: 39.8 us
  Pallas kernels  19 us (48%)
  starting transfers between devices  11.9 us (30%)
  waiting for transfers between devices  7.92 us (20%)
  local copies, waits for them, and re-layouts  0.71 us (2%)
    ppermute x8, starting transfers between devices, exchange(): return lax.ppermute(x, 'col', [(i, i ^ bit) for i in range(peers)])  11 us
    ppermute x8, waiting for transfers between devices, exchange(): return lax.ppermute(x, 'col', [(i, i ^ bit) for i in range(peers)])  7.91 us
    pallas_call x2, Pallas kernels, conv(): pl.pallas_call(functools.partial(conv_kernel, at * half_dim), out_shape=s...  4.61 us
    pallas_call x2, Pallas kernels, token(): pl.pallas_call(functools.partial(token_kernel, scale), out_shape=shape((t...  3.9 us
    pallas_call x1, Pallas kernels, on_device(): pl.pallas_call(functools.partial(band_kernel, scale), out_shape=(shape((t...  3.39 us
    pallas_call x1, Pallas kernels, on_device(): pl.pallas_call(out_kernel, out_shape=shape((tokens, dim), BF16), in_specs...  2.77 us
    pallas_call x1, Pallas kernels, on_device(): pl.pallas_call(taps_kernel, out_shape=(shape((7, 24, dim), F32), shape((8...  1.91 us
    pallas_call x1, Pallas kernels, on_device(): pl.pallas_call(functools.partial(second_band_kernel, scale), out_shape=wi...  1.85 us
  transfers between devices with their start and end apart: 9, of which 4 were waited for; matrix products, arithmetic and copies ran while one was open for 0% of the time, Pallas kernels for 32%

profile of v3, /device:TPU:0, one launch (start us, length us, event | category | flops | bytes accessed | tf_op | source)
XLA Modules:
  0.0 39.8 jit_solution(1127568198424650226)
XLA Ops:
  0.0 0.0 copy-start
  0.0 0.0 copy-start.2
  0.0 0.0 copy-start.3
  0.0 0.0 copy-start.4
  0.0 0.0 copy-start.5
  0.0 0.5 %collective-permute-start = (bf16[1024,512]{1,0:T(8,128)(2,1)}, bf16[1024,512]{1,0:T(8,128)(2,1)S(1)}, u32[]{:S(2)}, u32[]{:S(2)}) collective-permute-start(bf16[1024,512]{1,0:T(8,128)(2,1)} %bitcast.9), channel_id=1, source_target_pairs={{0,1},{1,0},{2,3},{3,2},{4,5},{5,4},{6,7},{7,6},{8,9},{9,8},{10,11... | collective-permute-start | bytes 3145736 | tf_op jit(solution)/shard_map/ppermute | solution.py:302
  0.5 0.1 collective-permute-start.1
  0.6 1.9 %taps.1 = (f32[7,24,512]{2,1,0:T(8,128)}, f32[8,128]{1,0:T(8,128)}) custom-call(f32[7,7,512]{2,1,0:T(8,128)} %seven.1, f32[5,5,512]{2,1,0:T(8,128)} %five.1, f32[3,3,512]{2,1,0:T(4,128)} %three.1), custom_call_target="tpu_custom_call" | custom-call | flops 10000000000 | bytes 1000000 | tf_op jit(solution)/shard_map/taps/pallas_call | solution.py:324
  2.5 0.5 %collective-permute-done.1.other_tissue = s32[8,128]{1,0:T(8,128)S(1)} collective-permute-done((s32[8,128]{1,0:T(8,128)}, s32[8,128]{1,0:T(8,128)S(1)}, u32[]{:S(2)}, u32[]{:S(2)}) %collective-permute-start.1) | collective-permute-done | bytes 4128 | tf_op jit(solution)/shard_map/ppermute | solution.py:302
  3.1 0.0 collective-permute-done.other
  3.1 0.0 copy-done
  3.1 0.0 copy-done.2
  3.1 0.0 copy-done.3
  3.1 0.0 copy-done.4
  3.1 0.0 copy-done.5
  3.1 0.0 copy-start.8
  3.1 0.7 %copy-done.8 = f32[8,128]{1,0:T(8,128)S(1)} copy-done((f32[8,128]{1,0:T(8,128)S(1)}, f32[8,128]{1,0:T(8,128)}, u32[]{:S(2)}) %copy-start.8) | copy-done | bytes 4120
  3.8 0.0 copy-start.6
  3.8 3.4 %band.1 = (bf16[1024,512]{1,0:T(8,128)(2,1)S(1)}, bf16[2048,256]{1,0:T(8,128)(2,1)S(1)}, bf16[2048,256]{1,0:T(8,128)(2,1)S(1)}, bf16[80,512]{1,0:T(8,128)(2,1)S(1)}) custom-call(s32[1]{0:T(128)} %bitcast.own_ref, bf16[1024,512]{1,0:T(8,128)(2,1)S(1)} %bitcast.10, bf16[1024,512]{1,0:T(8,128)(2,1)S(1)} %collective-permute-done.other, s32[8,128]{1,0:T(8,128)S(1)} %copy-done.3, ...), custom_call_target="tpu_custom_call" | custom-call | flops 1800000000 | bytes 4000000 | tf_op jit(solution)/shard_map/band/pallas_call | solution.py:336
  7.2 3.0 %collective-permute-start.2 = (bf16[80,512]{1,0:T(8,128)(2,1)S(1)}, bf16[80,512]{1,0:T(8,128)(2,1)S(1)}, u32[]{:S(2)}, u32[]{:S(2)}) collective-permute-start(bf16[80,512]{1,0:T(8,128)(2,1)S(1)} %get-tuple-element.18.after), channel_id=1, source_target_pairs={{0,2},{1,3},{2,0},{3,1},{4,6},{5,7},{6,4},{7,5},{8,10},{9,11},{10,... | collective-permute-start | bytes 245768 | tf_op jit(solution)/shard_map/ppermute | solution.py:302
  10.1 0.0 copy-done.6
  10.1 2.0 %token_.2.before.weights_low = bf16[1024,1024]{1,0:T(8,128)(2,1)S(1)} custom-call(bf16[1024,512]{1,0:T(8,128)(2,1)S(1)} %bitcast.11, bf16[512,512]{1,0:T(8,128)(2,1)S(1)} %copy-done.6, bf16[256,512]{1,0:T(8,128)(2,1)S(1)} %copy-done.2, bf16[80,512]{1,0:T(8,128)(2,1)S(1)} %get-tuple-element.18.after), custom_call_target="tpu_custom_call" | custom-call | flops 2000000000 | bytes 6000000 | tf_op jit(solution)/shard_map/token/pallas_call | solution.py:348
  12.1 1.8 %band_second.1.held = f32[72,512]{1,0:T(8,128)S(1)} custom-call(s32[1]{0:T(128)} %bitcast.own_ref, bf16[2048,256]{1,0:T(8,128)(2,1)S(1)} %get-tuple-element.19.keys, bf16[2048,256]{1,0:T(8,128)(2,1)S(1)} %get-tuple-element.20.vals, s32[8,128]{1,0:T(8,128)S(1)} %copy-done.3, s32[8,128]{1,0:T(8,128)S(1)} %collective-permute-done.1.other_tissue, ...), custom_call_target="tpu_custom_call" | custom-call | flops 600000000 | bytes 4000000 | tf_op jit(solution)/shard_map/band_second/pallas_call | solution.py:388
  13.9 0.0 collective-permute-done.2.got
  13.9 0.1 merge_next.2
  14.0 1.6 %collective-permute-start.3 = (bf16[80,512]{1,0:T(8,128)(2,1)S(1)}, bf16[80,512]{1,0:T(8,128)(2,1)S(1)}, u32[]{:S(2)}, u32[]{:S(2)}) collective-permute-start(bf16[80,512]{1,0:T(8,128)(2,1)S(1)} %get-tuple-element.22.after), channel_id=1, source_target_pairs={{0,4},{1,5},{2,6},{3,7},{4,0},{5,1},{6,2},{7,3},{8,12},{9,13},{10,... | collective-permute-start | bytes 245768 | tf_op jit(solution)/shard_map/ppermute | solution.py:302
  15.7 0.9 %collective-permute-start.5 = (bf16[384,512]{1,0:T(8,128)(2,1)S(1)}, bf16[384,512]{1,0:T(8,128)(2,1)S(1)}, u32[]{:S(2)}, u32[]{:S(2)}) collective-permute-start(bf16[384,512]{1,0:T(8,128)(2,1)S(1)} %border.1.before), channel_id=1, source_target_pairs={{1,2},{3,4},{5,6},{7,8},{9,10},{11,12},{13,14},{2,1},{4,3},{6,5},{... | collective-permute-start | bytes 1179656 | tf_op jit(solution)/shard_map/ppermute | solution.py:409
  16.6 2.0 %collective-permute-done.3.got = bf16[80,512]{1,0:T(8,128)(2,1)S(1)} collective-permute-done((bf16[80,512]{1,0:T(8,128)(2,1)S(1)}, bf16[80,512]{1,0:T(8,128)(2,1)S(1)}, u32[]{:S(2)}, u32[]{:S(2)}) %collective-permute-start.3) | collective-permute-done | bytes 81952 | tf_op jit(solution)/shard_map/ppermute | solution.py:302
  18.5 0.1 merge_next.3
  18.6 0.0 copy-start.7
  18.6 2.7 %collective-permute-start.4 = (bf16[80,512]{1,0:T(8,128)(2,1)S(1)}, bf16[80,512]{1,0:T(8,128)(2,1)S(1)}, u32[]{:S(2)}, u32[]{:S(2)}) collective-permute-start(bf16[80,512]{1,0:T(8,128)(2,1)S(1)} %get-tuple-element.24.after), channel_id=1, source_target_pairs={{0,8},{1,9},{2,10},{3,11},{4,12},{5,13},{6,14},{7,15},{8,0},{9,1},... | collective-permute-start | bytes 245768 | tf_op jit(solution)/shard_map/ppermute | solution.py:302
  21.2 1.9 %token_.3.after.weights_high = bf16[1024,1024]{1,0:T(8,128)(2,1)S(1)} custom-call(bf16[1024,512]{1,0:T(8,128)(2,1)S(1)} %bitcast.12, bf16[512,512]{1,0:T(8,128)(2,1)S(1)} %copy-done.6, bf16[256,512]{1,0:T(8,128)(2,1)S(1)} %copy-done.2, bf16[80,512]{1,0:T(8,128)(2,1)S(1)} %get-tuple-element.24.after), custom_call_target="tpu_custom_call" | custom-call | flops 10000000000 | bytes 6000000 | tf_op jit(solution)/shard_map/token/pallas_call | solution.py:348
  23.2 0.0 collective-permute-done.5.outer
  23.2 0.4 halo.1
  23.6 0.0 copy-done.7
  23.6 2.3 %conv.2 = f32[8,128,256]{2,1,0:T(8,128)S(1)} custom-call(bf16[1024,512]{1,0:T(8,128)(2,1)S(1)} %get-tuple-element.23.values, bf16[384,512]{1,0:T(8,128)(2,1)S(1)} %get-tuple-element.26.above, bf16[384,512]{1,0:T(8,128)(2,1)S(1)} %get-tuple-element.27.below, f32[7,24,512]{2,1,0:T(8,128)S(1)} %copy-done.7, bf16[1024,1024]{1,0:T(8,128)(2,1)S(1)} %token_.3.after.weights_high), custom_call_target="tpu_custom_call" | custom-call | flops 3000000000 | bytes 4000000 | tf_op jit(solution)/shard_map/conv/pallas_call | solution.py:366
  25.9 3.5 %collective-permute-done.4.got = bf16[80,512]{1,0:T(8,128)(2,1)S(1)} collective-permute-done((bf16[80,512]{1,0:T(8,128)(2,1)S(1)}, bf16[80,512]{1,0:T(8,128)(2,1)S(1)}, u32[]{:S(2)}, u32[]{:S(2)}) %collective-permute-start.4) | collective-permute-done | bytes 81952 | tf_op jit(solution)/shard_map/ppermute | solution.py:302
  29.5 0.0 copy-start.1
  29.5 0.1 collective-permute-start.8
  29.6 3.0 %collective-permute-start.7 = (bf16[64,512]{1,0:T(8,128)(2,1)S(1)}, bf16[64,512]{1,0:T(8,128)(2,1)S(1)}, u32[]{:S(2)}, u32[]{:S(2)}) collective-permute-start(bf16[64,512]{1,0:T(8,128)(2,1)S(1)} %merge_last.1.after.own), channel_id=1, source_target_pairs={{0,1},{1,0},{2,3},{3,2},{4,5},{5,4},{6,7},{7,6},{8,9},{9,8},{10,11... | collective-permute-start | bytes 196616 | tf_op jit(solution)/shard_map/ppermute | solution.py:302
  32.6 0.0 collective-permute-start.6
  32.7 2.3 %conv.3 = f32[8,128,256]{2,1,0:T(8,128)S(1)} custom-call(bf16[1024,512]{1,0:T(8,128)(2,1)S(1)} %get-tuple-element.23.values, bf16[384,512]{1,0:T(8,128)(2,1)S(1)} %get-tuple-element.26.above, bf16[384,512]{1,0:T(8,128)(2,1)S(1)} %get-tuple-element.27.below, f32[7,24,512]{2,1,0:T(8,128)S(1)} %copy-done.7, bf16[64,512]{1,0:T(8,128)(2,1)S(1)} %merge_last.1.after.own), custom_call_target="tpu_custom_call" | custom-call | flops 3000000000 | bytes 4000000 | tf_op jit(solution)/shard_map/conv/pallas_call | solution.py:366
  35.0 0.0 collective-permute-done.8.far
  35.0 0.0 collective-permute-done.7.side
  35.0 1.9 %collective-permute-done.6.near = bf16[64,512]{1,0:T(8,128)(2,1)S(1)} collective-permute-done((bf16[64,512]{1,0:T(8,128)(2,1)S(1)}, bf16[64,512]{1,0:T(8,128)(2,1)S(1)}, u32[]{:S(2)}, u32[]{:S(2)}) %collective-permute-start.6) | collective-permute-done | bytes 65568 | tf_op jit(solution)/shard_map/ppermute | solution.py:302
  36.9 0.0 copy-done.1
  36.9 2.8 %out.1 = bf16[1024,512]{1,0:T(8,128)(2,1)} custom-call(s32[1]{0:T(128)} %bitcast.own_ref, bf16[1024,1024]{1,0:T(8,128)(2,1)S(1)} %token_.2.before.weights_low, bf16[1024,1024]{1,0:T(8,128)(2,1)S(1)} %token_.3.after.weights_high, bf16[64,512]{1,0:T(8,128)(2,1)S(1)} %merge_last.1.after.own, bf16[64,512]{1,0:T(8,128)(2,1)S(1)} %collective-permute-done.6.near, ...), custom_call_target="tpu_custom_call" | custom-call | flops 1100000000 | bytes 8000000 | tf_op jit(solution)/shard_map/out/pallas_call | solution.py:435
  (2 shorter events, 0.1 us)
Async XLA Ops:
  0.0 3.1 %copy-start = (bf16[512,512]{1,0:T(8,128)(2,1)S(1)}, bf16[512,512]{1,0:T(8,128)(2,1)}, u32[]{:S(2)}) copy-start(bf16[512,512]{1,0:T(8,128)(2,1)} %w_value.3) | copy-start | bytes 1572868
  0.0 3.1 %copy-start.2 = (bf16[256,512]{1,0:T(8,128)(2,1)S(1)}, bf16[256,512]{1,0:T(8,128)(2,1)}, u32[]{:S(2)}) copy-start(bf16[256,512]{1,0:T(8,128)(2,1)} %agents.7) | copy-start | bytes 786436
  0.0 3.1 %copy-start.3 = (s32[8,128]{1,0:T(8,128)S(1)}, s32[8,128]{1,0:T(8,128)}, u32[]{:S(2)}) copy-start(s32[8,128]{1,0:T(8,128)} %tissue.3) | copy-start | bytes 12292
  0.0 3.1 %copy-start.4 = (bf16[8,128,512]{2,1,0:T(8,128)(2,1)S(1)}, bf16[8,128,512]{2,1,0:T(8,128)(2,1)}, u32[]{:S(2)}) copy-start(bf16[8,128,512]{2,1,0:T(8,128)(2,1)} %param.10) | copy-start | bytes 3145732
  0.0 3.1 %copy-start.5 = (bf16[512,512]{1,0:T(8,128)(2,1)S(1)}, bf16[512,512]{1,0:T(8,128)(2,1)}, u32[]{:S(2)}) copy-start(bf16[512,512]{1,0:T(8,128)(2,1)} %w_key.1) | copy-start | bytes 1572868
  0.0 3.0 %collective-permute-start = (bf16[1024,512]{1,0:T(8,128)(2,1)}, bf16[1024,512]{1,0:T(8,128)(2,1)S(1)}, u32[]{:S(2)}, u32[]{:S(2)}) collective-permute-start(bf16[1024,512]{1,0:T(8,128)(2,1)} %bitcast.9), channel_id=1, source_target_pairs={{0,1},{1,0},{2,3},{3,2},{4,5},{5,4},{6,7},{7,6},{8,9},{9,8},{10,11... | collective-permute-start | bytes 3145736 | tf_op jit(solution)/shard_map/ppermute | solution.py:302
  0.5 2.5 %collective-permute-start.1 = (s32[8,128]{1,0:T(8,128)}, s32[8,128]{1,0:T(8,128)S(1)}, u32[]{:S(2)}, u32[]{:S(2)}) collective-permute-start(s32[8,128]{1,0:T(8,128)} %tissue.3), channel_id=1, source_target_pairs={{0,1},{1,0},{2,3},{3,2},{4,5},{5,4},{6,7},{7,6},{8,9},{9,8},{10,11... | collective-permute-start | bytes 12296 | tf_op jit(solution)/shard_map/ppermute | solution.py:302
  3.1 0.7 %copy-start.8 = (f32[8,128]{1,0:T(8,128)S(1)}, f32[8,128]{1,0:T(8,128)}, u32[]{:S(2)}) copy-start(f32[8,128]{1,0:T(8,128)} %get-tuple-element.17.after) | copy-start | bytes 12292
  3.8 6.4 %copy-start.6 = (bf16[512,512]{1,0:T(8,128)(2,1)S(1)}, bf16[512,512]{1,0:T(8,128)(2,1)}, u32[]{:S(2)}) copy-start(bf16[512,512]{1,0:T(8,128)(2,1)} %w_query.3) | copy-start | bytes 1572868
  7.2 6.8 %collective-permute-start.2 = (bf16[80,512]{1,0:T(8,128)(2,1)S(1)}, bf16[80,512]{1,0:T(8,128)(2,1)S(1)}, u32[]{:S(2)}, u32[]{:S(2)}) collective-permute-start(bf16[80,512]{1,0:T(8,128)(2,1)S(1)} %get-tuple-element.18.after), channel_id=1, source_target_pairs={{0,2},{1,3},{2,0},{3,1},{4,6},{5,7},{6,4},{7,5},{8,10},{9,11},{10,... | collective-permute-start | bytes 245768 | tf_op jit(solution)/shard_map/ppermute | solution.py:302
  14.0 4.5 %collective-permute-start.3 = (bf16[80,512]{1,0:T(8,128)(2,1)S(1)}, bf16[80,512]{1,0:T(8,128)(2,1)S(1)}, u32[]{:S(2)}, u32[]{:S(2)}) collective-permute-start(bf16[80,512]{1,0:T(8,128)(2,1)S(1)} %get-tuple-element.22.after), channel_id=1, source_target_pairs={{0,4},{1,5},{2,6},{3,7},{4,0},{5,1},{6,2},{7,3},{8,12},{9,13},{10,... | collective-permute-start | bytes 245768 | tf_op jit(solution)/shard_map/ppermute | solution.py:302
  15.7 7.5 %collective-permute-start.5 = (bf16[384,512]{1,0:T(8,128)(2,1)S(1)}, bf16[384,512]{1,0:T(8,128)(2,1)S(1)}, u32[]{:S(2)}, u32[]{:S(2)}) collective-permute-start(bf16[384,512]{1,0:T(8,128)(2,1)S(1)} %border.1.before), channel_id=1, source_target_pairs={{1,2},{3,4},{5,6},{7,8},{9,10},{11,12},{13,14},{2,1},{4,3},{6,5},{... | collective-permute-start | bytes 1179656 | tf_op jit(solution)/shard_map/ppermute | solution.py:409
  18.6 5.0 %copy-start.7 = (f32[7,24,512]{2,1,0:T(8,128)S(1)}, f32[7,24,512]{2,1,0:T(8,128)}, u32[]{:S(2)}) copy-start(f32[7,24,512]{2,1,0:T(8,128)} %get-tuple-element.28.all_taps) | copy-start | bytes 1032196
  18.6 10.9 %collective-permute-start.4 = (bf16[80,512]{1,0:T(8,128)(2,1)S(1)}, bf16[80,512]{1,0:T(8,128)(2,1)S(1)}, u32[]{:S(2)}, u32[]{:S(2)}) collective-permute-start(bf16[80,512]{1,0:T(8,128)(2,1)S(1)} %get-tuple-element.24.after), channel_id=1, source_target_pairs={{0,8},{1,9},{2,10},{3,11},{4,12},{5,13},{6,14},{7,15},{8,0},{9,1},... | collective-permute-start | bytes 245768 | tf_op jit(solution)/shard_map/ppermute | solution.py:302
  29.5 7.4 %copy-start.1 = (bf16[512,512]{1,0:T(8,128)(2,1)S(1)}, bf16[512,512]{1,0:T(8,128)(2,1)}, u32[]{:S(2)}) copy-start(bf16[512,512]{1,0:T(8,128)(2,1)} %w_out.1) | copy-start | bytes 1572868
  29.5 5.5 %collective-permute-start.8 = (bf16[64,512]{1,0:T(8,128)(2,1)S(1)}, bf16[64,512]{1,0:T(8,128)(2,1)S(1)}, u32[]{:S(2)}, u32[]{:S(2)}) collective-permute-start(bf16[64,512]{1,0:T(8,128)(2,1)S(1)} %merge_last.1.after.own), channel_id=1, source_target_pairs={{0,3},{1,2},{2,1},{3,0},{4,7},{5,6},{6,5},{7,4},{8,11},{9,10},{10,... | collective-permute-start | bytes 196616 | tf_op jit(solution)/shard_map/ppermute | solution.py:302
  29.6 5.4 %collective-permute-start.7 = (bf16[64,512]{1,0:T(8,128)(2,1)S(1)}, bf16[64,512]{1,0:T(8,128)(2,1)S(1)}, u32[]{:S(2)}, u32[]{:S(2)}) collective-permute-start(bf16[64,512]{1,0:T(8,128)(2,1)S(1)} %merge_last.1.after.own), channel_id=1, source_target_pairs={{0,1},{1,0},{2,3},{3,2},{4,5},{5,4},{6,7},{7,6},{8,9},{9,8},{10,11... | collective-permute-start | bytes 196616 | tf_op jit(solution)/shard_map/ppermute | solution.py:302
  32.6 4.3 %collective-permute-start.6 = (bf16[64,512]{1,0:T(8,128)(2,1)S(1)}, bf16[64,512]{1,0:T(8,128)(2,1)S(1)}, u32[]{:S(2)}, u32[]{:S(2)}) collective-permute-start(bf16[64,512]{1,0:T(8,128)(2,1)S(1)} %merge_last.1.after.own), channel_id=1, source_target_pairs={{0,2},{1,3},{2,0},{3,1},{4,6},{5,7},{6,4},{7,5},{8,10},{9,11},{10,... | collective-permute-start | bytes 196616 | tf_op jit(solution)/shard_map/ppermute | solution.py:302

commit v4 on v3

--- a/solution.py
+++ b/solution.py
@@ -60,13 +60,10 @@
     return tuple(jnp.concatenate(pair, axis=1) for pair in zip(*sides))
 
 
-def band_kernel(
-    scale, own_ref, mine, other, tissue, other_tissue, w_key, w_value, agents, after, values, keys, vals, payload
-):
+def project_kernel(own_ref, mine, other, w_key, w_value, values, keys, vals):
     tokens = mine.shape[0]
     block = 256
-    own = own_ref[0]
-    half_lanes = pl.ds(pl.multiple_of((own // 2) * 256, 256), 256)
+    half_lanes = pl.ds(pl.multiple_of((own_ref[0] // 2) * 256, 256), 256)
     key_half = w_key[:, half_lanes]
     value_half = w_value[:, half_lanes]
     for at in range(0, tokens, block):
@@ -80,7 +77,10 @@
         part = other[pl.ds(at, block), :]
         keys[rows, :] = dot_nn(part, key_half).astype(BF16)
         vals[rows, :] = dot_nn(part, value_half).astype(BF16)
-    put_narrow(payload, chunk_state(1, own, scale, keys, vals, tissue, other_tissue, agents))
+
+
+def first_band_kernel(scale, own_ref, keys, vals, tissue, other_tissue, agents, payload):
+    put_narrow(payload, chunk_state(1, own_ref[0], scale, keys, vals, tissue, other_tissue, agents))
 
 
 def second_band_kernel(scale, own_ref, keys, vals, tissue, other_tissue, agents, keep):
@@ -161,18 +161,26 @@
         weights[:, head * 256 : head * 256 + 256] = part.astype(BF16)
 
 
-def border_kernel(odd_ref, values, after, border):
+def border_kernel(odd_ref, flat, border, sem):
     rows = border.shape[0]
-    border[...] = values[pl.ds(pl.multiple_of(odd_ref[0] * (values.shape[0] - rows), 128), rows), :]
-
-
-def halo_kernel(odd_ref, other, outer, w_value, above, below):
+    start = pl.multiple_of(odd_ref[0] * (flat.shape[0] - rows), 128)
+    copy = pltpu.make_async_copy(flat.at[pl.ds(start, rows), :], border, sem)
+    copy.start()
+    copy.wait()
+
+
+def halo_kernel(odd_ref, other, outer, w_value, after, above, below):
     rows = outer.shape[0]
     odd = odd_ref[0] == 1
     inner_part = other[pl.ds(pl.multiple_of(odd_ref[0] * (other.shape[0] - rows), 128), rows), :]
     inner = dot_nn(inner_part, w_value[...]).astype(BF16)
-    above[...] = jnp.where(odd, inner, outer[...])
-    below[...] = jnp.where(odd, outer[...], inner)
+    outside = dot_nn(outer[...], w_value[...]).astype(BF16)
+    above[...] = jnp.where(odd, inner, outside)
+    below[...] = jnp.where(odd, outside, inner)
+
+
+def relay_kernel(near, after, again):
+    again[...] = near[...]
 
 
 TAP_COUNTS = (2, 2, 2, 2, 2, 2, 2, 2, 1)
@@ -196,8 +204,7 @@
     return [row for a, b, c in zip(first, second, third) for row in (a + b, b + c)]
 
 
-def taps_kernel(seven, five, three, taps, mark):
-    mark[...] = jnp.zeros_like(mark)
+def taps_kernel(seven, five, three, after, taps):
     for q in range(7):
         column = [seven[p, q : q + 1, :] for p in range(7)]
         if 1 <= q <= 5:
@@ -321,27 +328,43 @@
     other = exchange(flat, 1)
     other_tissue = exchange(tissue, 1)
 
-    taps, mark = pl.pallas_call(
-        taps_kernel,
-        out_shape=(shape((7, 24, dim), F32), shape((8, 128), F32)),
-        in_specs=[vmem] * 3,
-        out_specs=[vmem] * 2,
+    border = pl.pallas_call(
+        border_kernel,
+        out_shape=shape((3 * width, dim), BF16),
+        in_specs=[smem, anywhere],
+        out_specs=anywhere,
+        scratch_shapes=[pltpu.SemaphoreType.DMA],
         compiler_params=params(60),
         cost_estimate=cost(1e10, 1e6),
-        name="taps",
-    )(seven, five, three)
+        name="border",
+    )(odd_word, flat)
+    rest = [(i, i + 1) for i in range(1, peers - 1, 2)]
+    outer = lax.ppermute(border, "col", rest + [(j, i) for i, j in rest])
 
     wide_shape, narrow_shape = shape((72, 512), F32), shape((80, 512), BF16)
     both_bands = shape((2 * tokens, half_dim), BF16)
-    values, keys, vals, payload = pl.pallas_call(
-        functools.partial(band_kernel, scale),
-        out_shape=(shape((tokens, dim), BF16), both_bands, both_bands, narrow_shape),
-        in_specs=[smem] + [vmem] * 7 + [anywhere],
-        out_specs=[vmem] * 4,
+    values, keys, vals = pl.pallas_call(
+        project_kernel,
+        out_shape=(shape((tokens, dim), BF16), both_bands, both_bands),
+        in_specs=[smem] + [vmem] * 4,
+        out_specs=[vmem] * 3,
         compiler_params=params(20),
-        cost_estimate=cost(1.8e9, 4e6, 1e6),
-        name="band",
-    )(own_chunk, flat, other, tissue, other_tissue, w_key, w_value, agent_tokens, mark)
+        cost_estimate=cost(1.3e9, 4e6),
+        name="project",
+    )(own_chunk, flat, other, w_key, w_value)
+
+    def band(kernel, out_shape):
+        return pl.pallas_call(
+            functools.partial(kernel, scale),
+            out_shape=out_shape,
+            in_specs=[smem] + [vmem] * 5,
+            out_specs=vmem,
+            compiler_params=params(20),
+            cost_estimate=cost(6e8, 4e6, 1e6),
+            name="band",
+        )(own_chunk, keys, vals, tissue, other_tissue, agent_tokens)
+
+    payload = band(first_band_kernel, narrow_shape)
 
     def token(at, after):
         lanes = slice(at * half_dim, (at + 1) * half_dim)
@@ -358,7 +381,7 @@
             out_specs=vmem,
             scratch_shapes=[VMEM((tokens, half_dim), BF16)],
             compiler_params=params(20),
-            cost_estimate=cost((1 + 4 * at) * 2e9, 6e6, 1e6),
+            cost_estimate=cost(2e9, 6e6, 1e6),
             name="token",
         )(flat, w_query, agent_tokens, after)
 
@@ -385,52 +408,53 @@
         )(held, got, before)
 
     got = exchange(payload, 2)
-    held = pl.pallas_call(
-        functools.partial(second_band_kernel, scale),
-        out_shape=wide_shape,
-        in_specs=[smem] + [vmem] * 5,
-        out_specs=vmem,
-        compiler_params=params(20),
-        cost_estimate=cost(6e8, 4e6, 1e6),
-        name="band_second",
-    )(own_chunk, keys, vals, tissue, other_tissue, agent_tokens)
-    weights_low = token(0, payload)
-    held, payload = next_merge(held, got, weights_low)
-    border = pl.pallas_call(
-        border_kernel,
-        out_shape=shape((3 * width, dim), BF16),
-        in_specs=[smem, vmem, anywhere],
+    held = band(second_band_kernel, wide_shape)
+    taps = pl.pallas_call(
+        taps_kernel,
+        out_shape=shape((7, 24, dim), F32),
+        in_specs=[vmem] * 3 + [anywhere],
         out_specs=vmem,
         compiler_params=params(16),
-        cost_estimate=cost(3e9, 1e6),
-        name="border",
-    )(odd_word, values, payload)
-    rest = [(i, i + 1) for i in range(1, peers - 1, 2)]
-    outer = lax.ppermute(border, "col", rest + [(j, i) for i, j in rest])
+        cost_estimate=cost(5e8, 1e6),
+        name="taps",
+    )(seven, five, three, payload)
+    held, payload = next_merge(held, got, taps)
     bit = 4
+    weights_low = None
     while bit * 2 < peers:
         got = exchange(payload, bit)
-        held, payload = next_merge(held, got, border)
+        if weights_low is None:
+            weights_low = token(0, payload)
+            above, below = pl.pallas_call(
+                halo_kernel,
+                out_shape=(shape((3 * width, dim), BF16), shape((3 * width, dim), BF16)),
+                in_specs=[smem] + [vmem] * 3 + [anywhere],
+                out_specs=[vmem] * 2,
+                compiler_params=params(16),
+                cost_estimate=cost(4e8, 2e6),
+                name="halo",
+            )(odd_word, other, outer, w_value, weights_low)
+        held, payload = next_merge(held, got, weights_low)
         bit *= 2
     got = exchange(payload, bit)
     weights_high = token(1, payload)
-    above, below = pl.pallas_call(
-        halo_kernel,
-        out_shape=(shape((3 * width, dim), BF16), shape((3 * width, dim), BF16)),
-        in_specs=[smem] + [vmem] * 3,
-        out_specs=[vmem] * 2,
-        compiler_params=params(16),
-        cost_estimate=cost(4e8, 2e6),
-        name="halo",
-    )(odd_word, other, outer, w_value)
     position_low = conv(0, weights_high)
     own = pl.pallas_call(
         last_merge_kernel, out_shape=shape((64, 512), BF16), out_specs=vmem, name="merge_last", **hop
     )(held, got, position_low)
     near = exchange(own, 2)
-    far = exchange(own, 3)
     side = exchange(own, 1)
     position_high = conv(1, own)
+    again = pl.pallas_call(
+        relay_kernel,
+        out_shape=shape((64, 512), BF16),
+        in_specs=[vmem, anywhere],
+        out_specs=vmem,
+        compiler_params=params(16),
+        cost_estimate=cost(1e6, 1e6),
+        name="relay",
+    )(near, position_high)
+    far = exchange(again, 1)
 
     mixed = pl.pallas_call(
         out_kernel,

time: 40 us -> 50.7 us (1.27)
  Pallas kernels: 19 us -> 30.6 us
  waiting for transfers between devices: 7.92 us -> 4.73 us
  starting transfers between devices: 11.9 us -> 14.8 us
  local copies, waits for them, and re-layouts: 0.71 us -> 0.06 us
    pallas_call x1, Pallas kernels: 0.03 us -> 13 us  [on_device(): pl.pallas_call(border_kernel, out_shape=shape((3 * width, dim), BF16), in...]
    ppermute x8, waiting for transfers between devices: 7.91 us -> 4.72 us  [exchange(): return lax.ppermute(x, 'col', [(i, i ^ bit) for i in range(peers)])]
    ppermute x8, starting transfers between devices: 11 us -> 14.1 us  [exchange(): return lax.ppermute(x, 'col', [(i, i ^ bit) for i in range(peers)])]
    pallas_call x3 -> x5, Pallas kernels: 7.15 us -> 5.4 us  [the longest x2 3.7 us: band(): pl.pallas_call(functools.partial(kernel, scale), out_shape=out_shape, in_...]
    unnamed x18 -> x20, local copies, waits for them, and re-layouts: 0.71 us -> 0.06 us
  transfers between devices with their start and end apart: 9 -> 9, of which waited for: 4 -> 3; matrix products, arithmetic and copies ran while one was open for 0% -> 0% of each run, Pallas kernels for 32% -> 55%
where the time goes in v4:
time: 50.7 us; the launch traced here: 50.6 us
  Pallas kernels  30.6 us (60%)
  starting transfers between devices  14.8 us (29%)
  waiting for transfers between devices  4.73 us (9%)
    ppermute x8, starting transfers between devices, exchange(): return lax.ppermute(x, 'col', [(i, i ^ bit) for i in range(peers)])  14.1 us
    pallas_call x1, Pallas kernels, on_device(): pl.pallas_call(border_kernel, out_shape=shape((3 * width, dim), BF16), in...  13 us
    pallas_call x2, Pallas kernels, conv(): pl.pallas_call(functools.partial(conv_kernel, at * half_dim), out_shape=s...  4.78 us
    ppermute x8, waiting for transfers between devices, exchange(): return lax.ppermute(x, 'col', [(i, i ^ bit) for i in range(peers)])  4.72 us
    pallas_call x2, Pallas kernels, token(): pl.pallas_call(functools.partial(token_kernel, scale), out_shape=shape((t...  3.91 us
    pallas_call x2, Pallas kernels, band(): pl.pallas_call(functools.partial(kernel, scale), out_shape=out_shape, in_...  3.7 us
    pallas_call x1, Pallas kernels, on_device(): pl.pallas_call(out_kernel, out_shape=shape((tokens, dim), BF16), in_specs...  2.73 us
    pallas_call x1, Pallas kernels, on_device(): pl.pallas_call(project_kernel, out_shape=(shape((tokens, dim), BF16), bot...  1.54 us
  transfers between devices with their start and end apart: 9, of which 3 were waited for; matrix products, arithmetic and copies ran while one was open for 0% of the time, Pallas kernels for 55%

profile of v4, /device:TPU:0, one launch (start us, length us, event | category | flops | bytes accessed | tf_op | source)
XLA Modules:
  0.0 50.6 jit_solution(13129737267226628995)
XLA Ops:
  0.0 0.5 collective-permute-start
  0.5 0.1 collective-permute-start.1
  0.5 13.0 %border.1 = bf16[384,512]{1,0:T(8,128)(2,1)} custom-call(s32[1]{0:T(128)} %bitcast.2.odd_ref, bf16[1024,512]{1,0:T(8,128)(2,1)} %bitcast.11), custom_call_target="tpu_custom_call" | custom-call | flops 10000000000 | bytes 1000000 | tf_op jit(solution)/shard_map/border/pallas_call | solution.py:331
  13.5 0.7 %collective-permute-start.5 = (bf16[384,512]{1,0:T(8,128)(2,1)}, bf16[384,512]{1,0:T(8,128)(2,1)S(1)}, u32[]{:S(2)}, u32[]{:S(2)}) collective-permute-start(bf16[384,512]{1,0:T(8,128)(2,1)} %border.1), channel_id=1, source_target_pairs={{1,2},{3,4},{5,6},{7,8},{9,10},{11,12},{13,14},{2,1},{4,3},{6,5},{... | collective-permute-start | bytes 1179656 | tf_op jit(solution)/shard_map/ppermute | solution.py:342
  14.2 0.0 collective-permute-done.other
  14.3 0.0 copy-done.1
  14.3 0.0 copy-done.4
  14.3 0.0 copy-done.5
  14.3 0.0 copy-start
  14.3 0.0 copy-start.3
  14.3 1.5 %project.1 = (bf16[1024,512]{1,0:T(8,128)(2,1)S(1)}, bf16[2048,256]{1,0:T(8,128)(2,1)S(1)}, bf16[2048,256]{1,0:T(8,128)(2,1)S(1)}) custom-call(s32[1]{0:T(128)} %bitcast.own_ref, bf16[1024,512]{1,0:T(8,128)(2,1)S(1)} %bitcast.12, bf16[1024,512]{1,0:T(8,128)(2,1)S(1)} %collective-permute-done.other, bf16[512,512]{1,0:T(8,128)(2,1)S(1)} %copy-done.5, ...), custom_call_target="tpu_custom_call" | custom-call | flops 1300000000 | bytes 4000000 | tf_op jit(solution)/shard_map/project/pallas_call | solution.py:346
  15.9 0.0 copy-start.7
  15.9 0.0 copy-start.8
  15.9 0.0 copy-start.9
  15.9 0.0 collective-permute-done.1.other_tissue
  15.9 0.0 copy-done
  15.9 0.0 copy-done.3
  15.9 1.9 %band.3.after = bf16[80,512]{1,0:T(8,128)(2,1)S(1)} custom-call(s32[1]{0:T(128)} %bitcast.own_ref, bf16[2048,256]{1,0:T(8,128)(2,1)S(1)} %get-tuple-element.14.keys, bf16[2048,256]{1,0:T(8,128)(2,1)S(1)} %get-tuple-element.15.vals, s32[8,128]{1,0:T(8,128)S(1)} %copy-done.3, s32[8,128]{1,0:T(8,128)S(1)} %collective-permute-done.1.other_tissue, ...), custom_call_target="tpu_custom_call" | custom-call | flops 600000000 | bytes 4000000 | tf_op jit(solution)/shard_map/band/pallas_call | solution.py:357
  17.8 0.0 copy-start.6
  17.8 4.3 %collective-permute-start.2 = (bf16[80,512]{1,0:T(8,128)(2,1)S(1)}, bf16[80,512]{1,0:T(8,128)(2,1)S(1)}, u32[]{:S(2)}, u32[]{:S(2)}) collective-permute-start(bf16[80,512]{1,0:T(8,128)(2,1)S(1)} %band.3.after), channel_id=1, source_target_pairs={{0,2},{1,3},{2,0},{3,1},{4,6},{5,7},{6,4},{7,5},{8,10},{9,11},{10,... | collective-permute-start | bytes 245768 | tf_op jit(solution)/shard_map/ppermute | solution.py:309
  22.1 0.0 copy-done.7
  22.1 0.0 copy-done.8
  22.1 0.0 copy-done.9
  22.1 0.1 taps.1.before.all_taps
  22.2 1.8 %band.2.held = f32[72,512]{1,0:T(8,128)S(1)} custom-call(s32[1]{0:T(128)} %bitcast.own_ref, bf16[2048,256]{1,0:T(8,128)(2,1)S(1)} %get-tuple-element.14.keys, bf16[2048,256]{1,0:T(8,128)(2,1)S(1)} %get-tuple-element.15.vals, s32[8,128]{1,0:T(8,128)S(1)} %copy-done.3, s32[8,128]{1,0:T(8,128)S(1)} %collective-permute-done.1.other_tissue, ...), custom_call_target="tpu_custom_call" | custom-call | flops 600000000 | bytes 4000000 | tf_op jit(solution)/shard_map/band/pallas_call | solution.py:357
  24.1 2.3 %collective-permute-done.2.got = bf16[80,512]{1,0:T(8,128)(2,1)S(1)} collective-permute-done((bf16[80,512]{1,0:T(8,128)(2,1)S(1)}, bf16[80,512]{1,0:T(8,128)(2,1)S(1)}, u32[]{:S(2)}, u32[]{:S(2)}) %collective-permute-start.2) | collective-permute-done | bytes 81952 | tf_op jit(solution)/shard_map/ppermute | solution.py:309
  26.3 0.1 merge_next.2
  26.4 5.8 %collective-permute-start.3 = (bf16[80,512]{1,0:T(8,128)(2,1)S(1)}, bf16[80,512]{1,0:T(8,128)(2,1)S(1)}, u32[]{:S(2)}, u32[]{:S(2)}) collective-permute-start(bf16[80,512]{1,0:T(8,128)(2,1)S(1)} %get-tuple-element.16.after), channel_id=1, source_target_pairs={{0,4},{1,5},{2,6},{3,7},{4,0},{5,1},{6,2},{7,3},{8,12},{9,13},{10,... | collective-permute-start | bytes 245768 | tf_op jit(solution)/shard_map/ppermute | solution.py:309
  32.2 0.0 copy-done.6
  32.2 2.0 %token_.2.before.after.weights_low = bf16[1024,1024]{1,0:T(8,128)(2,1)S(1)} custom-call(bf16[1024,512]{1,0:T(8,128)(2,1)S(1)} %bitcast.13, bf16[512,512]{1,0:T(8,128)(2,1)S(1)} %copy-done.6, bf16[256,512]{1,0:T(8,128)(2,1)S(1)} %copy-done, bf16[80,512]{1,0:T(8,128)(2,1)S(1)} %get-tuple-element.16.after), custom_call_target="tpu_custom_call" | custom-call | flops 2000000000 | bytes 6000000 | tf_op jit(solution)/shard_map/token/pallas_call | solution.py:371
  34.1 0.0 collective-permute-done.5.outer
  34.1 0.6 %halo.1 = (bf16[384,512]{1,0:T(8,128)(2,1)S(1)}, bf16[384,512]{1,0:T(8,128)(2,1)S(1)}) custom-call(s32[1]{0:T(128)} %bitcast.2.odd_ref, bf16[1024,512]{1,0:T(8,128)(2,1)S(1)} %collective-permute-done.other, bf16[384,512]{1,0:T(8,128)(2,1)S(1)} %collective-permute-done.5.outer, bf16[512,512]{1,0:T(8,128)(2,1)S(1)} %copy-done.1, ...), custom_call_target="tpu_custom_call" | custom-call | flops 400000000 | bytes 2000000 | tf_op jit(solution)/shard_map/halo/pallas_call | solution.py:428
  34.7 0.0 collective-permute-done.3.got
  34.7 0.1 merge_next.3
  34.8 2.9 %collective-permute-start.4 = (bf16[80,512]{1,0:T(8,128)(2,1)S(1)}, bf16[80,512]{1,0:T(8,128)(2,1)S(1)}, u32[]{:S(2)}, u32[]{:S(2)}) collective-permute-start(bf16[80,512]{1,0:T(8,128)(2,1)S(1)} %get-tuple-element.18.after), channel_id=1, source_target_pairs={{0,8},{1,9},{2,10},{3,11},{4,12},{5,13},{6,14},{7,15},{8,0},{9,1},... | collective-permute-start | bytes 245768 | tf_op jit(solution)/shard_map/ppermute | solution.py:309
  37.7 2.0 %token_.3.after.weights_high = bf16[1024,1024]{1,0:T(8,128)(2,1)S(1)} custom-call(bf16[1024,512]{1,0:T(8,128)(2,1)S(1)} %bitcast.14, bf16[512,512]{1,0:T(8,128)(2,1)S(1)} %copy-done.6, bf16[256,512]{1,0:T(8,128)(2,1)S(1)} %copy-done, bf16[80,512]{1,0:T(8,128)(2,1)S(1)} %get-tuple-element.18.after), custom_call_target="tpu_custom_call" | custom-call | flops 2000000000 | bytes 6000000 | tf_op jit(solution)/shard_map/token/pallas_call | solution.py:371
  39.7 2.3 %conv.2 = f32[8,128,256]{2,1,0:T(8,128)S(1)} custom-call(bf16[1024,512]{1,0:T(8,128)(2,1)S(1)} %get-tuple-element.20.values, bf16[384,512]{1,0:T(8,128)(2,1)S(1)} %get-tuple-element.21.above, bf16[384,512]{1,0:T(8,128)(2,1)S(1)} %get-tuple-element.22.below, f32[7,24,512]{2,1,0:T(8,128)S(1)} %taps.1.before.all_taps, ...), custom_call_target="tpu_custom_call" | custom-call | flops 3000000000 | bytes 4000000 | tf_op jit(solution)/shard_map/conv/pallas_call | solution.py:389
  42.0 0.0 collective-permute-done.4.got
  42.1 0.0 copy-start.2
  42.1 0.6 %collective-permute-start.6 = (bf16[64,512]{1,0:T(8,128)(2,1)S(1)}, bf16[64,512]{1,0:T(8,128)(2,1)S(1)}, u32[]{:S(2)}, u32[]{:S(2)}) collective-permute-start(bf16[64,512]{1,0:T(8,128)(2,1)S(1)} %merge_last.1.after.own), channel_id=1, source_target_pairs={{0,2},{1,3},{2,0},{3,1},{4,6},{5,7},{6,4},{7,5},{8,10},{9,11},{10,... | collective-permute-start | bytes 196616 | tf_op jit(solution)/shard_map/ppermute | solution.py:309
  42.7 2.5 %conv.3 = f32[8,128,256]{2,1,0:T(8,128)S(1)} custom-call(bf16[1024,512]{1,0:T(8,128)(2,1)S(1)} %get-tuple-element.20.values, bf16[384,512]{1,0:T(8,128)(2,1)S(1)} %get-tuple-element.21.above, bf16[384,512]{1,0:T(8,128)(2,1)S(1)} %get-tuple-element.22.below, f32[7,24,512]{2,1,0:T(8,128)S(1)} %taps.1.before.all_taps, bf16[64,512]{1,0:T(8,128)(2,1)S(1)} %merge_last.1.after.own), custom_call_target="tpu_custom_call" | custom-call | flops 3000000000 | bytes 4000000 | tf_op jit(solution)/shard_map/conv/pallas_call | solution.py:389
  45.1 0.1 collective-permute-start.7
  45.2 1.2 %collective-permute-done.6.near = bf16[64,512]{1,0:T(8,128)(2,1)S(1)} collective-permute-done((bf16[64,512]{1,0:T(8,128)(2,1)S(1)}, bf16[64,512]{1,0:T(8,128)(2,1)S(1)}, u32[]{:S(2)}, u32[]{:S(2)}) %collective-permute-start.6) | collective-permute-done | bytes 65568 | tf_op jit(solution)/shard_map/ppermute | solution.py:309
  46.4 0.0 collective-permute-start.8
  46.4 0.0 collective-permute-done.7.side
  46.5 1.2 %collective-permute-done.8.far = bf16[64,512]{1,0:T(8,128)(2,1)S(1)} collective-permute-done((bf16[64,512]{1,0:T(8,128)(2,1)S(1)}, bf16[64,512]{1,0:T(8,128)(2,1)S(1)}, u32[]{:S(2)}, u32[]{:S(2)}) %collective-permute-start.8) | collective-permute-done | bytes 65568 | tf_op jit(solution)/shard_map/ppermute | solution.py:309
  47.7 0.0 copy-done.2
  47.7 2.7 %out.1 = bf16[1024,512]{1,0:T(8,128)(2,1)} custom-call(s32[1]{0:T(128)} %bitcast.own_ref, bf16[1024,1024]{1,0:T(8,128)(2,1)S(1)} %token_.2.before.after.weights_low, bf16[1024,1024]{1,0:T(8,128)(2,1)S(1)} %token_.3.after.weights_high, bf16[64,512]{1,0:T(8,128)(2,1)S(1)} %merge_last.1.after.own, bf16[64,512]{1,0:T(8,128)(2,1)S(1)} %collective-permute-done.6.near, ...), custom_call_target="tpu_custom_call" | custom-call | flops 1100000000 | bytes 8000000 | tf_op jit(solution)/shard_map/out/pallas_call | solution.py:459
  (5 shorter events, 0.1 us)
Async XLA Ops:
  0.0 14.2 %collective-permute-start = (bf16[1024,512]{1,0:T(8,128)(2,1)}, bf16[1024,512]{1,0:T(8,128)(2,1)S(1)}, u32[]{:S(2)}, u32[]{:S(2)}) collective-permute-start(bf16[1024,512]{1,0:T(8,128)(2,1)} %bitcast.10), channel_id=1, source_target_pairs={{0,1},{1,0},{2,3},{3,2},{4,5},{5,4},{6,7},{7,6},{8,9},{9,8},{10,11... | collective-permute-start | bytes 3145736 | tf_op jit(solution)/shard_map/ppermute | solution.py:309
  0.5 15.4 %collective-permute-start.1 = (s32[8,128]{1,0:T(8,128)}, s32[8,128]{1,0:T(8,128)S(1)}, u32[]{:S(2)}, u32[]{:S(2)}) collective-permute-start(s32[8,128]{1,0:T(8,128)} %tissue.3), channel_id=1, source_target_pairs={{0,1},{1,0},{2,3},{3,2},{4,5},{5,4},{6,7},{7,6},{8,9},{9,8},{10,11... | collective-permute-start | bytes 12296 | tf_op jit(solution)/shard_map/ppermute | solution.py:309
  0.5 13.7 %copy-start.1 = (bf16[512,512]{1,0:T(8,128)(2,1)S(1)}, bf16[512,512]{1,0:T(8,128)(2,1)}, u32[]{:S(2)}) copy-start(bf16[512,512]{1,0:T(8,128)(2,1)} %w_value.3) | copy-start | bytes 1572868
  0.5 13.8 %copy-start.4 = (bf16[8,128,512]{2,1,0:T(8,128)(2,1)S(1)}, bf16[8,128,512]{2,1,0:T(8,128)(2,1)}, u32[]{:S(2)}) copy-start(bf16[8,128,512]{2,1,0:T(8,128)(2,1)} %param.10) | copy-start | bytes 3145732
  0.5 13.8 %copy-start.5 = (bf16[512,512]{1,0:T(8,128)(2,1)S(1)}, bf16[512,512]{1,0:T(8,128)(2,1)}, u32[]{:S(2)}) copy-start(bf16[512,512]{1,0:T(8,128)(2,1)} %w_key.1) | copy-start | bytes 1572868
  13.5 20.6 %collective-permute-start.5 = (bf16[384,512]{1,0:T(8,128)(2,1)}, bf16[384,512]{1,0:T(8,128)(2,1)S(1)}, u32[]{:S(2)}, u32[]{:S(2)}) collective-permute-start(bf16[384,512]{1,0:T(8,128)(2,1)} %border.1), channel_id=1, source_target_pairs={{1,2},{3,4},{5,6},{7,8},{9,10},{11,12},{13,14},{2,1},{4,3},{6,5},{... | collective-permute-start | bytes 1179656 | tf_op jit(solution)/shard_map/ppermute | solution.py:342
  14.3 1.6 %copy-start = (bf16[256,512]{1,0:T(8,128)(2,1)S(1)}, bf16[256,512]{1,0:T(8,128)(2,1)}, u32[]{:S(2)}) copy-start(bf16[256,512]{1,0:T(8,128)(2,1)} %agents.7) | copy-start | bytes 786436
  14.3 1.6 %copy-start.3 = (s32[8,128]{1,0:T(8,128)S(1)}, s32[8,128]{1,0:T(8,128)}, u32[]{:S(2)}) copy-start(s32[8,128]{1,0:T(8,128)} %tissue.3) | copy-start | bytes 12292
  15.9 6.2 %copy-start.7 = (f32[7,7,512]{2,1,0:T(8,128)S(1)}, f32[7,7,512]{2,1,0:T(8,128)}, u32[]{:S(2)}) copy-start(f32[7,7,512]{2,1,0:T(8,128)} %seven.1) | copy-start | bytes 301060
  15.9 6.2 %copy-start.8 = (f32[5,5,512]{2,1,0:T(8,128)S(1)}, f32[5,5,512]{2,1,0:T(8,128)}, u32[]{:S(2)}) copy-start(f32[5,5,512]{2,1,0:T(8,128)} %five.1) | copy-start | bytes 153604
  15.9 6.2 %copy-start.9 = (f32[3,3,512]{2,1,0:T(4,128)S(1)}, f32[3,3,512]{2,1,0:T(4,128)}, u32[]{:S(2)}) copy-start(f32[3,3,512]{2,1,0:T(4,128)} %three.1) | copy-start | bytes 55300
  17.8 14.4 %copy-start.6 = (bf16[512,512]{1,0:T(8,128)(2,1)S(1)}, bf16[512,512]{1,0:T(8,128)(2,1)}, u32[]{:S(2)}) copy-start(bf16[512,512]{1,0:T(8,128)(2,1)} %w_query.3) | copy-start | bytes 1572868
  17.8 8.5 %collective-permute-start.2 = (bf16[80,512]{1,0:T(8,128)(2,1)S(1)}, bf16[80,512]{1,0:T(8,128)(2,1)S(1)}, u32[]{:S(2)}, u32[]{:S(2)}) collective-permute-start(bf16[80,512]{1,0:T(8,128)(2,1)S(1)} %band.3.after), channel_id=1, source_target_pairs={{0,2},{1,3},{2,0},{3,1},{4,6},{5,7},{6,4},{7,5},{8,10},{9,11},{10,... | collective-permute-start | bytes 245768 | tf_op jit(solution)/shard_map/ppermute | solution.py:309
  26.4 8.3 %collective-permute-start.3 = (bf16[80,512]{1,0:T(8,128)(2,1)S(1)}, bf16[80,512]{1,0:T(8,128)(2,1)S(1)}, u32[]{:S(2)}, u32[]{:S(2)}) collective-permute-start(bf16[80,512]{1,0:T(8,128)(2,1)S(1)} %get-tuple-element.16.after), channel_id=1, source_target_pairs={{0,4},{1,5},{2,6},{3,7},{4,0},{5,1},{6,2},{7,3},{8,12},{9,13},{10,... | collective-permute-start | bytes 245768 | tf_op jit(solution)/shard_map/ppermute | solution.py:309
  34.8 7.2 %collective-permute-start.4 = (bf16[80,512]{1,0:T(8,128)(2,1)S(1)}, bf16[80,512]{1,0:T(8,128)(2,1)S(1)}, u32[]{:S(2)}, u32[]{:S(2)}) collective-permute-start(bf16[80,512]{1,0:T(8,128)(2,1)S(1)} %get-tuple-element.18.after), channel_id=1, source_target_pairs={{0,8},{1,9},{2,10},{3,11},{4,12},{5,13},{6,14},{7,15},{8,0},{9,1},... | collective-permute-start | bytes 245768 | tf_op jit(solution)/shard_map/ppermute | solution.py:309
  42.1 5.6 %copy-start.2 = (bf16[512,512]{1,0:T(8,128)(2,1)S(1)}, bf16[512,512]{1,0:T(8,128)(2,1)}, u32[]{:S(2)}) copy-start(bf16[512,512]{1,0:T(8,128)(2,1)} %w_out.1) | copy-start | bytes 1572868
  42.1 4.3 %collective-permute-start.6 = (bf16[64,512]{1,0:T(8,128)(2,1)S(1)}, bf16[64,512]{1,0:T(8,128)(2,1)S(1)}, u32[]{:S(2)}, u32[]{:S(2)}) collective-permute-start(bf16[64,512]{1,0:T(8,128)(2,1)S(1)} %merge_last.1.after.own), channel_id=1, source_target_pairs={{0,2},{1,3},{2,0},{3,1},{4,6},{5,7},{6,4},{7,5},{8,10},{9,11},{10,... | collective-permute-start | bytes 196616 | tf_op jit(solution)/shard_map/ppermute | solution.py:309
  45.1 1.3 %collective-permute-start.7 = (bf16[64,512]{1,0:T(8,128)(2,1)S(1)}, bf16[64,512]{1,0:T(8,128)(2,1)S(1)}, u32[]{:S(2)}, u32[]{:S(2)}) collective-permute-start(bf16[64,512]{1,0:T(8,128)(2,1)S(1)} %merge_last.1.after.own), channel_id=1, source_target_pairs={{0,1},{1,0},{2,3},{3,2},{4,5},{5,4},{6,7},{7,6},{8,9},{9,8},{10,11... | collective-permute-start | bytes 196616 | tf_op jit(solution)/shard_map/ppermute | solution.py:309
  46.4 1.3 %collective-permute-start.8 = (bf16[64,512]{1,0:T(8,128)(2,1)S(1)}, bf16[64,512]{1,0:T(8,128)(2,1)S(1)}, u32[]{:S(2)}, u32[]{:S(2)}) collective-permute-start(bf16[64,512]{1,0:T(8,128)(2,1)S(1)} %relay.1), channel_id=1, source_target_pairs={{0,1},{1,0},{2,3},{3,2},{4,5},{5,4},{6,7},{7,6},{8,9},{9,8},{10,11... | collective-permute-start | bytes 196616 | tf_op jit(solution)/shard_map/ppermute | solution.py:309

commit v5 on v4

--- a/solution.py
+++ b/solution.py
@@ -161,12 +161,9 @@
         weights[:, head * 256 : head * 256 + 256] = part.astype(BF16)
 
 
-def border_kernel(odd_ref, flat, border, sem):
+def border_kernel(odd_ref, flat, border):
     rows = border.shape[0]
-    start = pl.multiple_of(odd_ref[0] * (flat.shape[0] - rows), 128)
-    copy = pltpu.make_async_copy(flat.at[pl.ds(start, rows), :], border, sem)
-    copy.start()
-    copy.wait()
+    border[...] = flat[pl.ds(pl.multiple_of(odd_ref[0] * (flat.shape[0] - rows), 128), rows), :]
 
 
 def halo_kernel(odd_ref, other, outer, w_value, after, above, below):
@@ -331,10 +328,9 @@
     border = pl.pallas_call(
         border_kernel,
         out_shape=shape((3 * width, dim), BF16),
-        in_specs=[smem, anywhere],
-        out_specs=anywhere,
-        scratch_shapes=[pltpu.SemaphoreType.DMA],
-        compiler_params=params(60),
+        in_specs=[smem, vmem],
+        out_specs=vmem,
+        compiler_params=params(16),
         cost_estimate=cost(1e10, 1e6),
         name="border",
     )(odd_word, flat)

time: 50.7 us -> 40 us (0.79)
  Pallas kernels: 30.6 us -> 19 us
  local copies, waits for them, and re-layouts: 0.06 us -> 1.44 us
    pallas_call x1, Pallas kernels: 13 us -> 0.77 us  [on_device(): pl.pallas_call(border_kernel, out_shape=shape((3 * width, dim), BF16), in...]
    unnamed x20 -> x22, local copies, waits for them, and re-layouts: 0.06 us -> 1.44 us
    pallas_call x2, Pallas kernels: 4.78 us -> 5.35 us  [conv(): pl.pallas_call(functools.partial(conv_kernel, at * half_dim), out_shape=s...]
  transfers between devices with their start and end apart: 9 -> 9, of which waited for: 3 -> 3; matrix products, arithmetic and copies ran while one was open for 0% -> 0% of each run, Pallas kernels for 55% -> 41%
where the time goes in v5:
time: 40 us; the launch traced here: 39.8 us
  Pallas kernels  19 us (48%)
  starting transfers between devices  14.4 us (36%)
  waiting for transfers between devices  4.62 us (12%)
  local copies, waits for them, and re-layouts  1.44 us (4%)
    ppermute x8, starting transfers between devices, exchange(): return lax.ppermute(x, 'col', [(i, i ^ bit) for i in range(peers)])  13.7 us
    pallas_call x2, Pallas kernels, conv(): pl.pallas_call(functools.partial(conv_kernel, at * half_dim), out_shape=s...  5.35 us
    ppermute x8, waiting for transfers between devices, exchange(): return lax.ppermute(x, 'col', [(i, i ^ bit) for i in range(peers)])  4.62 us
    pallas_call x2, Pallas kernels, token(): pl.pallas_call(functools.partial(token_kernel, scale), out_shape=shape((t...  3.9 us
    pallas_call x2, Pallas kernels, band(): pl.pallas_call(functools.partial(kernel, scale), out_shape=out_shape, in_...  3.78 us
    pallas_call x1, Pallas kernels, on_device(): pl.pallas_call(out_kernel, out_shape=shape((tokens, dim), BF16), in_specs...  2.76 us
    pallas_call x1, Pallas kernels, on_device(): pl.pallas_call(project_kernel, out_shape=(shape((tokens, dim), BF16), bot...  1.56 us
    unnamed x22, local copies, waits for them, and re-layouts  1.44 us
  transfers between devices with their start and end apart: 9, of which 3 were waited for; matrix products, arithmetic and copies ran while one was open for 0% of the time, Pallas kernels for 41%

profile of v5, /device:TPU:0, one launch (start us, length us, event | category | flops | bytes accessed | tf_op | source)
XLA Modules:
  0.0 39.8 jit_solution(12254030917257586862)
XLA Ops:
  0.0 0.5 %collective-permute-start = (bf16[1024,512]{1,0:T(8,128)(2,1)}, bf16[1024,512]{1,0:T(8,128)(2,1)S(1)}, u32[]{:S(2)}, u32[]{:S(2)}) collective-permute-start(bf16[1024,512]{1,0:T(8,128)(2,1)} %bitcast.10), channel_id=1, source_target_pairs={{0,1},{1,0},{2,3},{3,2},{4,5},{5,4},{6,7},{7,6},{8,9},{9,8},{10,11... | collective-permute-start | bytes 3145736 | tf_op jit(solution)/shard_map/ppermute | solution.py:306
  0.5 0.1 collective-permute-start.1
  0.5 0.0 copy-start.4
  0.5 1.2 %copy-done.4 = bf16[8,128,512]{2,1,0:T(8,128)(2,1)S(1)} copy-done((bf16[8,128,512]{2,1,0:T(8,128)(2,1)S(1)}, bf16[8,128,512]{2,1,0:T(8,128)(2,1)}, u32[]{:S(2)}) %copy-start.4) | copy-done | bytes 1048600
  1.7 0.8 %border.1 = bf16[384,512]{1,0:T(8,128)(2,1)} custom-call(s32[1]{0:T(128)} %bitcast.2.odd_ref, bf16[1024,512]{1,0:T(8,128)(2,1)S(1)} %bitcast.11), custom_call_target="tpu_custom_call" | custom-call | flops 10000000000 | bytes 1000000 | tf_op jit(solution)/shard_map/border/pallas_call | solution.py:328
  2.5 0.7 %collective-permute-start.5 = (bf16[384,512]{1,0:T(8,128)(2,1)}, bf16[384,512]{1,0:T(8,128)(2,1)S(1)}, u32[]{:S(2)}, u32[]{:S(2)}) collective-permute-start(bf16[384,512]{1,0:T(8,128)(2,1)} %border.1), channel_id=1, source_target_pairs={{1,2},{3,4},{5,6},{7,8},{9,10},{11,12},{13,14},{2,1},{4,3},{6,5},{... | collective-permute-start | bytes 1179656 | tf_op jit(solution)/shard_map/ppermute | solution.py:338
  3.2 0.0 collective-permute-done.other
  3.2 0.0 copy-done.1
  3.2 0.0 copy-done.5
  3.3 0.1 copy-done.6
  3.4 1.6 %project.1 = (bf16[1024,512]{1,0:T(8,128)(2,1)S(1)}, bf16[2048,256]{1,0:T(8,128)(2,1)S(1)}, bf16[2048,256]{1,0:T(8,128)(2,1)S(1)}) custom-call(s32[1]{0:T(128)} %bitcast.own_ref, bf16[1024,512]{1,0:T(8,128)(2,1)S(1)} %bitcast.12, bf16[1024,512]{1,0:T(8,128)(2,1)S(1)} %collective-permute-done.other, bf16[512,512]{1,0:T(8,128)(2,1)S(1)} %copy-done.6, ...), custom_call_target="tpu_custom_call" | custom-call | flops 1300000000 | bytes 4000000 | tf_op jit(solution)/shard_map/project/pallas_call | solution.py:342
  5.0 0.0 copy-start.8
  5.0 0.0 copy-start.9
  5.0 0.0 copy-start.10
  5.0 0.0 collective-permute-done.1.other_tissue
  5.0 0.0 copy-done
  5.0 0.0 copy-done.3
  5.0 1.9 %band.3.after = bf16[80,512]{1,0:T(8,128)(2,1)S(1)} custom-call(s32[1]{0:T(128)} %bitcast.own_ref, bf16[2048,256]{1,0:T(8,128)(2,1)S(1)} %get-tuple-element.14.keys, bf16[2048,256]{1,0:T(8,128)(2,1)S(1)} %get-tuple-element.15.vals, s32[8,128]{1,0:T(8,128)S(1)} %copy-done.3, s32[8,128]{1,0:T(8,128)S(1)} %collective-permute-done.1.other_tissue, ...), custom_call_target="tpu_custom_call" | custom-call | flops 600000000 | bytes 4000000 | tf_op jit(solution)/shard_map/band/pallas_call | solution.py:353
  6.9 0.0 copy-start.7
  7.0 4.1 %collective-permute-start.2 = (bf16[80,512]{1,0:T(8,128)(2,1)S(1)}, bf16[80,512]{1,0:T(8,128)(2,1)S(1)}, u32[]{:S(2)}, u32[]{:S(2)}) collective-permute-start(bf16[80,512]{1,0:T(8,128)(2,1)S(1)} %band.3.after), channel_id=1, source_target_pairs={{0,2},{1,3},{2,0},{3,1},{4,6},{5,7},{6,4},{7,5},{8,10},{9,11},{10,... | collective-permute-start | bytes 245768 | tf_op jit(solution)/shard_map/ppermute | solution.py:306
  11.1 0.0 copy-done.8
  11.1 0.0 copy-done.9
  11.1 0.0 copy-done.10
  11.1 0.1 taps.1.before.all_taps
  11.3 1.9 %band.2.held = f32[72,512]{1,0:T(8,128)S(1)} custom-call(s32[1]{0:T(128)} %bitcast.own_ref, bf16[2048,256]{1,0:T(8,128)(2,1)S(1)} %get-tuple-element.14.keys, bf16[2048,256]{1,0:T(8,128)(2,1)S(1)} %get-tuple-element.15.vals, s32[8,128]{1,0:T(8,128)S(1)} %copy-done.3, s32[8,128]{1,0:T(8,128)S(1)} %collective-permute-done.1.other_tissue, ...), custom_call_target="tpu_custom_call" | custom-call | flops 600000000 | bytes 4000000 | tf_op jit(solution)/shard_map/band/pallas_call | solution.py:353
  13.1 2.2 %collective-permute-done.2.got = bf16[80,512]{1,0:T(8,128)(2,1)S(1)} collective-permute-done((bf16[80,512]{1,0:T(8,128)(2,1)S(1)}, bf16[80,512]{1,0:T(8,128)(2,1)S(1)}, u32[]{:S(2)}, u32[]{:S(2)}) %collective-permute-start.2) | collective-permute-done | bytes 81952 | tf_op jit(solution)/shard_map/ppermute | solution.py:306
  15.3 0.1 merge_next.2
  15.4 5.8 %collective-permute-start.3 = (bf16[80,512]{1,0:T(8,128)(2,1)S(1)}, bf16[80,512]{1,0:T(8,128)(2,1)S(1)}, u32[]{:S(2)}, u32[]{:S(2)}) collective-permute-start(bf16[80,512]{1,0:T(8,128)(2,1)S(1)} %get-tuple-element.16.after), channel_id=1, source_target_pairs={{0,4},{1,5},{2,6},{3,7},{4,0},{5,1},{6,2},{7,3},{8,12},{9,13},{10,... | collective-permute-start | bytes 245768 | tf_op jit(solution)/shard_map/ppermute | solution.py:306
  21.1 0.0 copy-done.7
  21.1 2.0 %token_.2.before.after.weights_low = bf16[1024,1024]{1,0:T(8,128)(2,1)S(1)} custom-call(bf16[1024,512]{1,0:T(8,128)(2,1)S(1)} %bitcast.13, bf16[512,512]{1,0:T(8,128)(2,1)S(1)} %copy-done.7, bf16[256,512]{1,0:T(8,128)(2,1)S(1)} %copy-done, bf16[80,512]{1,0:T(8,128)(2,1)S(1)} %get-tuple-element.16.after), custom_call_target="tpu_custom_call" | custom-call | flops 2000000000 | bytes 6000000 | tf_op jit(solution)/shard_map/token/pallas_call | solution.py:367
  23.1 0.0 collective-permute-done.5.outer
  23.1 0.6 %halo.1 = (bf16[384,512]{1,0:T(8,128)(2,1)S(1)}, bf16[384,512]{1,0:T(8,128)(2,1)S(1)}) custom-call(s32[1]{0:T(128)} %bitcast.2.odd_ref, bf16[1024,512]{1,0:T(8,128)(2,1)S(1)} %collective-permute-done.other, bf16[384,512]{1,0:T(8,128)(2,1)S(1)} %collective-permute-done.5.outer, bf16[512,512]{1,0:T(8,128)(2,1)S(1)} %copy-done.1, ...), custom_call_target="tpu_custom_call" | custom-call | flops 400000000 | bytes 2000000 | tf_op jit(solution)/shard_map/halo/pallas_call | solution.py:424
  23.7 0.0 collective-permute-done.3.got
  23.7 0.1 merge_next.3
  23.7 2.9 %collective-permute-start.4 = (bf16[80,512]{1,0:T(8,128)(2,1)S(1)}, bf16[80,512]{1,0:T(8,128)(2,1)S(1)}, u32[]{:S(2)}, u32[]{:S(2)}) collective-permute-start(bf16[80,512]{1,0:T(8,128)(2,1)S(1)} %get-tuple-element.18.after), channel_id=1, source_target_pairs={{0,8},{1,9},{2,10},{3,11},{4,12},{5,13},{6,14},{7,15},{8,0},{9,1},... | collective-permute-start | bytes 245768 | tf_op jit(solution)/shard_map/ppermute | solution.py:306
  26.7 2.0 %token_.3.after.weights_high = bf16[1024,1024]{1,0:T(8,128)(2,1)S(1)} custom-call(bf16[1024,512]{1,0:T(8,128)(2,1)S(1)} %bitcast.14, bf16[512,512]{1,0:T(8,128)(2,1)S(1)} %copy-done.7, bf16[256,512]{1,0:T(8,128)(2,1)S(1)} %copy-done, bf16[80,512]{1,0:T(8,128)(2,1)S(1)} %get-tuple-element.18.after), custom_call_target="tpu_custom_call" | custom-call | flops 2000000000 | bytes 6000000 | tf_op jit(solution)/shard_map/token/pallas_call | solution.py:367
  28.6 2.6 %conv.2 = f32[8,128,256]{2,1,0:T(8,128)S(1)} custom-call(bf16[1024,512]{1,0:T(8,128)(2,1)S(1)} %get-tuple-element.20.values, bf16[384,512]{1,0:T(8,128)(2,1)S(1)} %get-tuple-element.21.above, bf16[384,512]{1,0:T(8,128)(2,1)S(1)} %get-tuple-element.22.below, f32[7,24,512]{2,1,0:T(8,128)S(1)} %taps.1.before.all_taps, ...), custom_call_target="tpu_custom_call" | custom-call | flops 3000000000 | bytes 4000000 | tf_op jit(solution)/shard_map/conv/pallas_call | solution.py:385
  31.2 0.0 collective-permute-done.4.got
  31.3 0.0 copy-start.2
  31.3 0.3 collective-permute-start.6
  31.6 2.8 %conv.3 = f32[8,128,256]{2,1,0:T(8,128)S(1)} custom-call(bf16[1024,512]{1,0:T(8,128)(2,1)S(1)} %get-tuple-element.20.values, bf16[384,512]{1,0:T(8,128)(2,1)S(1)} %get-tuple-element.21.above, bf16[384,512]{1,0:T(8,128)(2,1)S(1)} %get-tuple-element.22.below, f32[7,24,512]{2,1,0:T(8,128)S(1)} %taps.1.before.all_taps, bf16[64,512]{1,0:T(8,128)(2,1)S(1)} %merge_last.1.after.own), custom_call_target="tpu_custom_call" | custom-call | flops 3000000000 | bytes 4000000 | tf_op jit(solution)/shard_map/conv/pallas_call | solution.py:385
  34.3 0.1 collective-permute-start.7
  34.4 1.2 %collective-permute-done.6.near = bf16[64,512]{1,0:T(8,128)(2,1)S(1)} collective-permute-done((bf16[64,512]{1,0:T(8,128)(2,1)S(1)}, bf16[64,512]{1,0:T(8,128)(2,1)S(1)}, u32[]{:S(2)}, u32[]{:S(2)}) %collective-permute-start.6) | collective-permute-done | bytes 65568 | tf_op jit(solution)/shard_map/ppermute | solution.py:306
  35.6 0.0 collective-permute-start.8
  35.6 0.0 collective-permute-done.7.side
  35.7 1.2 %collective-permute-done.8.far = bf16[64,512]{1,0:T(8,128)(2,1)S(1)} collective-permute-done((bf16[64,512]{1,0:T(8,128)(2,1)S(1)}, bf16[64,512]{1,0:T(8,128)(2,1)S(1)}, u32[]{:S(2)}, u32[]{:S(2)}) %collective-permute-start.8) | collective-permute-done | bytes 65568 | tf_op jit(solution)/shard_map/ppermute | solution.py:306
  36.9 0.0 copy-done.2
  36.9 2.8 %out.1 = bf16[1024,512]{1,0:T(8,128)(2,1)} custom-call(s32[1]{0:T(128)} %bitcast.own_ref, bf16[1024,1024]{1,0:T(8,128)(2,1)S(1)} %token_.2.before.after.weights_low, bf16[1024,1024]{1,0:T(8,128)(2,1)S(1)} %token_.3.after.weights_high, bf16[64,512]{1,0:T(8,128)(2,1)S(1)} %merge_last.1.after.own, bf16[64,512]{1,0:T(8,128)(2,1)S(1)} %collective-permute-done.6.near, ...), custom_call_target="tpu_custom_call" | custom-call | flops 1100000000 | bytes 8000000 | tf_op jit(solution)/shard_map/out/pallas_call | solution.py:455
  (7 shorter events, 0.1 us)
Async XLA Ops:
  0.0 3.2 %collective-permute-start = (bf16[1024,512]{1,0:T(8,128)(2,1)}, bf16[1024,512]{1,0:T(8,128)(2,1)S(1)}, u32[]{:S(2)}, u32[]{:S(2)}) collective-permute-start(bf16[1024,512]{1,0:T(8,128)(2,1)} %bitcast.10), channel_id=1, source_target_pairs={{0,1},{1,0},{2,3},{3,2},{4,5},{5,4},{6,7},{7,6},{8,9},{9,8},{10,11... | collective-permute-start | bytes 3145736 | tf_op jit(solution)/shard_map/ppermute | solution.py:306
  0.5 4.6 %collective-permute-start.1 = (s32[8,128]{1,0:T(8,128)}, s32[8,128]{1,0:T(8,128)S(1)}, u32[]{:S(2)}, u32[]{:S(2)}) collective-permute-start(s32[8,128]{1,0:T(8,128)} %tissue.3), channel_id=1, source_target_pairs={{0,1},{1,0},{2,3},{3,2},{4,5},{5,4},{6,7},{7,6},{8,9},{9,8},{10,11... | collective-permute-start | bytes 12296 | tf_op jit(solution)/shard_map/ppermute | solution.py:306
  0.5 1.2 %copy-start.4 = (bf16[8,128,512]{2,1,0:T(8,128)(2,1)S(1)}, bf16[8,128,512]{2,1,0:T(8,128)(2,1)}, u32[]{:S(2)}) copy-start(bf16[8,128,512]{2,1,0:T(8,128)(2,1)} %param.10) | copy-start | bytes 3145732
  1.7 1.5 %copy-start.1 = (bf16[512,512]{1,0:T(8,128)(2,1)S(1)}, bf16[512,512]{1,0:T(8,128)(2,1)}, u32[]{:S(2)}) copy-start(bf16[512,512]{1,0:T(8,128)(2,1)} %w_value.3) | copy-start | bytes 1572868
  1.7 1.5 %copy-start.5 = (bf16[8,128,512]{2,1,0:T(8,128)(2,1)S(1)}, bf16[8,128,512]{2,1,0:T(8,128)(2,1)}, u32[]{:S(2)}) copy-start(bf16[8,128,512]{2,1,0:T(8,128)(2,1)} %param.10) | copy-start | bytes 3145732
  1.7 1.7 %copy-start.6 = (bf16[512,512]{1,0:T(8,128)(2,1)S(1)}, bf16[512,512]{1,0:T(8,128)(2,1)}, u32[]{:S(2)}) copy-start(bf16[512,512]{1,0:T(8,128)(2,1)} %w_key.1) | copy-start | bytes 1572868
  2.5 20.6 %collective-permute-start.5 = (bf16[384,512]{1,0:T(8,128)(2,1)}, bf16[384,512]{1,0:T(8,128)(2,1)S(1)}, u32[]{:S(2)}, u32[]{:S(2)}) collective-permute-start(bf16[384,512]{1,0:T(8,128)(2,1)} %border.1), channel_id=1, source_target_pairs={{1,2},{3,4},{5,6},{7,8},{9,10},{11,12},{13,14},{2,1},{4,3},{6,5},{... | collective-permute-start | bytes 1179656 | tf_op jit(solution)/shard_map/ppermute | solution.py:338
  3.4 1.6 %copy-start = (bf16[256,512]{1,0:T(8,128)(2,1)S(1)}, bf16[256,512]{1,0:T(8,128)(2,1)}, u32[]{:S(2)}) copy-start(bf16[256,512]{1,0:T(8,128)(2,1)} %agents.7) | copy-start | bytes 786436
  3.4 1.6 %copy-start.3 = (s32[8,128]{1,0:T(8,128)S(1)}, s32[8,128]{1,0:T(8,128)}, u32[]{:S(2)}) copy-start(s32[8,128]{1,0:T(8,128)} %tissue.3) | copy-start | bytes 12292
  5.0 6.1 %copy-start.8 = (f32[7,7,512]{2,1,0:T(8,128)S(1)}, f32[7,7,512]{2,1,0:T(8,128)}, u32[]{:S(2)}) copy-start(f32[7,7,512]{2,1,0:T(8,128)} %seven.1) | copy-start | bytes 301060
  5.0 6.1 %copy-start.9 = (f32[5,5,512]{2,1,0:T(8,128)S(1)}, f32[5,5,512]{2,1,0:T(8,128)}, u32[]{:S(2)}) copy-start(f32[5,5,512]{2,1,0:T(8,128)} %five.1) | copy-start | bytes 153604
  5.0 6.1 %copy-start.10 = (f32[3,3,512]{2,1,0:T(4,128)S(1)}, f32[3,3,512]{2,1,0:T(4,128)}, u32[]{:S(2)}) copy-start(f32[3,3,512]{2,1,0:T(4,128)} %three.1) | copy-start | bytes 55300
  6.9 14.2 %copy-start.7 = (bf16[512,512]{1,0:T(8,128)(2,1)S(1)}, bf16[512,512]{1,0:T(8,128)(2,1)}, u32[]{:S(2)}) copy-start(bf16[512,512]{1,0:T(8,128)(2,1)} %w_query.3) | copy-start | bytes 1572868
  7.0 8.3 %collective-permute-start.2 = (bf16[80,512]{1,0:T(8,128)(2,1)S(1)}, bf16[80,512]{1,0:T(8,128)(2,1)S(1)}, u32[]{:S(2)}, u32[]{:S(2)}) collective-permute-start(bf16[80,512]{1,0:T(8,128)(2,1)S(1)} %band.3.after), channel_id=1, source_target_pairs={{0,2},{1,3},{2,0},{3,1},{4,6},{5,7},{6,4},{7,5},{8,10},{9,11},{10,... | collective-permute-start | bytes 245768 | tf_op jit(solution)/shard_map/ppermute | solution.py:306
  15.4 8.3 %collective-permute-start.3 = (bf16[80,512]{1,0:T(8,128)(2,1)S(1)}, bf16[80,512]{1,0:T(8,128)(2,1)S(1)}, u32[]{:S(2)}, u32[]{:S(2)}) collective-permute-start(bf16[80,512]{1,0:T(8,128)(2,1)S(1)} %get-tuple-element.16.after), channel_id=1, source_target_pairs={{0,4},{1,5},{2,6},{3,7},{4,0},{5,1},{6,2},{7,3},{8,12},{9,13},{10,... | collective-permute-start | bytes 245768 | tf_op jit(solution)/shard_map/ppermute | solution.py:306
  23.7 7.5 %collective-permute-start.4 = (bf16[80,512]{1,0:T(8,128)(2,1)S(1)}, bf16[80,512]{1,0:T(8,128)(2,1)S(1)}, u32[]{:S(2)}, u32[]{:S(2)}) collective-permute-start(bf16[80,512]{1,0:T(8,128)(2,1)S(1)} %get-tuple-element.18.after), channel_id=1, source_target_pairs={{0,8},{1,9},{2,10},{3,11},{4,12},{5,13},{6,14},{7,15},{8,0},{9,1},... | collective-permute-start | bytes 245768 | tf_op jit(solution)/shard_map/ppermute | solution.py:306
  31.3 5.6 %copy-start.2 = (bf16[512,512]{1,0:T(8,128)(2,1)S(1)}, bf16[512,512]{1,0:T(8,128)(2,1)}, u32[]{:S(2)}) copy-start(bf16[512,512]{1,0:T(8,128)(2,1)} %w_out.1) | copy-start | bytes 1572868
  31.3 4.3 %collective-permute-start.6 = (bf16[64,512]{1,0:T(8,128)(2,1)S(1)}, bf16[64,512]{1,0:T(8,128)(2,1)S(1)}, u32[]{:S(2)}, u32[]{:S(2)}) collective-permute-start(bf16[64,512]{1,0:T(8,128)(2,1)S(1)} %merge_last.1.after.own), channel_id=1, source_target_pairs={{0,2},{1,3},{2,0},{3,1},{4,6},{5,7},{6,4},{7,5},{8,10},{9,11},{10,... | collective-permute-start | bytes 196616 | tf_op jit(solution)/shard_map/ppermute | solution.py:306
  34.3 1.3 %collective-permute-start.7 = (bf16[64,512]{1,0:T(8,128)(2,1)S(1)}, bf16[64,512]{1,0:T(8,128)(2,1)S(1)}, u32[]{:S(2)}, u32[]{:S(2)}) collective-permute-start(bf16[64,512]{1,0:T(8,128)(2,1)S(1)} %merge_last.1.after.own), channel_id=1, source_target_pairs={{0,1},{1,0},{2,3},{3,2},{4,5},{5,4},{6,7},{7,6},{8,9},{9,8},{10,11... | collective-permute-start | bytes 196616 | tf_op jit(solution)/shard_map/ppermute | solution.py:306
  35.6 1.3 %collective-permute-start.8 = (bf16[64,512]{1,0:T(8,128)(2,1)S(1)}, bf16[64,512]{1,0:T(8,128)(2,1)S(1)}, u32[]{:S(2)}, u32[]{:S(2)}) collective-permute-start(bf16[64,512]{1,0:T(8,128)(2,1)S(1)} %relay.1), channel_id=1, source_target_pairs={{0,1},{1,0},{2,3},{3,2},{4,5},{5,4},{6,7},{7,6},{8,9},{9,8},{10,11... | collective-permute-start | bytes 196616 | tf_op jit(solution)/shard_map/ppermute | solution.py:306

commit v6 on v5

--- a/solution.py
+++ b/solution.py
@@ -30,7 +30,7 @@
 
 def chunk_of_device():
     place = lax.axis_index("col")
-    return (place & 1) * 2 + ((place >> 1) & 1)
+    return (place & 1) * 2 + ((place >> 2) & 1)
 
 
 def chunk_state(index, own, scale, keys, vals, tissue, other_tissue, agents):
@@ -161,9 +161,8 @@
         weights[:, head * 256 : head * 256 + 256] = part.astype(BF16)
 
 
-def border_kernel(odd_ref, flat, border):
-    rows = border.shape[0]
-    border[...] = flat[pl.ds(pl.multiple_of(odd_ref[0] * (flat.shape[0] - rows), 128), rows), :]
+def border_kernel(odd_ref, first, last, border):
+    border[...] = jnp.where(odd_ref[0] == 1, last[...], first[...])
 
 
 def halo_kernel(odd_ref, other, outer, w_value, after, above, below):
@@ -328,12 +327,12 @@
     border = pl.pallas_call(
         border_kernel,
         out_shape=shape((3 * width, dim), BF16),
-        in_specs=[smem, vmem],
+        in_specs=[smem, vmem, vmem],
         out_specs=vmem,
         compiler_params=params(16),
         cost_estimate=cost(1e10, 1e6),
         name="border",
-    )(odd_word, flat)
+    )(odd_word, flat[: 3 * width], flat[tokens - 3 * width :])
     rest = [(i, i + 1) for i in range(1, peers - 1, 2)]
     outer = lax.ppermute(border, "col", rest + [(j, i) for i, j in rest])
 
@@ -403,7 +402,7 @@
             next_merge_kernel, out_shape=(wide_shape, narrow_shape), out_specs=[vmem] * 2, name="merge_next", **hop
         )(held, got, before)
 
-    got = exchange(payload, 2)
+    got = exchange(payload, 4)
     held = band(second_band_kernel, wide_shape)
     taps = pl.pallas_call(
         taps_kernel,
@@ -415,9 +414,9 @@
         name="taps",
     )(seven, five, three, payload)
     held, payload = next_merge(held, got, taps)
-    bit = 4
+    bit = 8
     weights_low = None
-    while bit * 2 < peers:
+    while bit < peers:
         got = exchange(payload, bit)
         if weights_low is None:
             weights_low = token(0, payload)
@@ -430,15 +429,15 @@
                 cost_estimate=cost(4e8, 2e6),
                 name="halo",
             )(odd_word, other, outer, w_value, weights_low)
-        held, payload = next_merge(held, got, weights_low)
+            weights_high = token(1, above)
+        held, payload = next_merge(held, got, weights_high)
         bit *= 2
-    got = exchange(payload, bit)
-    weights_high = token(1, payload)
-    position_low = conv(0, weights_high)
+    got = exchange(payload, 2)
+    position_low = conv(0, payload)
     own = pl.pallas_call(
         last_merge_kernel, out_shape=shape((64, 512), BF16), out_specs=vmem, name="merge_last", **hop
     )(held, got, position_low)
-    near = exchange(own, 2)
+    near = exchange(own, 4)
     side = exchange(own, 1)
     position_high = conv(1, own)
     again = pl.pallas_call(

time: 40 us -> 37.2 us (0.930)
  starting transfers between devices: 14.4 us -> 12.4 us
  waiting for transfers between devices: 4.62 us -> 3.55 us
  local copies, waits for them, and re-layouts: 1.44 us -> 2.26 us
  Pallas kernels: 19 us -> 18.5 us
    ppermute x8, starting transfers between devices: 13.7 us -> 11.7 us  [exchange(): return lax.ppermute(x, 'col', [(i, i ^ bit) for i in range(peers)])]
    slice x0 -> x1, local copies, waits for them, and re-layouts: none -> 1.17 us  [on_device(): flat[tokens - 3 * width:]]
    ppermute x8, waiting for transfers between devices: 4.62 us -> 3.55 us  [exchange(): return lax.ppermute(x, 'col', [(i, i ^ bit) for i in range(peers)])]
    pallas_call x2, Pallas kernels: 5.35 us -> 4.79 us  [conv(): pl.pallas_call(functools.partial(conv_kernel, at * half_dim), out_shape=s...]
    unnamed x22 -> x20, local copies, waits for them, and re-layouts: 1.44 us -> 1.09 us
  transfers between devices with their start and end apart: 9 -> 9, of which waited for: 3 -> 6; matrix products, arithmetic and copies ran while one was open for 0% -> 3% of each run, Pallas kernels for 41% -> 42%
where the time goes in v6:
time: 37.2 us; the launch traced here: 37 us
  Pallas kernels  18.5 us (50%)
  starting transfers between devices  12.4 us (33%)
  waiting for transfers between devices  3.55 us (10%)
  local copies, waits for them, and re-layouts  2.26 us (6%)
    ppermute x8, starting transfers between devices, exchange(): return lax.ppermute(x, 'col', [(i, i ^ bit) for i in range(peers)])  11.7 us
    pallas_call x2, Pallas kernels, conv(): pl.pallas_call(functools.partial(conv_kernel, at * half_dim), out_shape=s...  4.79 us
    pallas_call x2, Pallas kernels, token(): pl.pallas_call(functools.partial(token_kernel, scale), out_shape=shape((t...  3.92 us
    pallas_call x2, Pallas kernels, band(): pl.pallas_call(functools.partial(kernel, scale), out_shape=out_shape, in_...  3.78 us
    ppermute x8, waiting for transfers between devices, exchange(): return lax.ppermute(x, 'col', [(i, i ^ bit) for i in range(peers)])  3.55 us
    pallas_call x1, Pallas kernels, on_device(): pl.pallas_call(out_kernel, out_shape=shape((tokens, dim), BF16), in_specs...  2.8 us
    pallas_call x1, Pallas kernels, on_device(): pl.pallas_call(project_kernel, out_shape=(shape((tokens, dim), BF16), bot...  1.54 us
    slice x1, local copies, waits for them, and re-layouts, on_device(): flat[tokens - 3 * width:]  1.17 us
  transfers between devices with their start and end apart: 9, of which 6 were waited for; matrix products, arithmetic and copies ran while one was open for 3% of the time, Pallas kernels for 42%

profile of v6, /device:TPU:0, one launch (start us, length us, event | category | flops | bytes accessed | tf_op | source)
XLA Modules:
  0.0 37.0 jit_solution(8163838730952499395)
XLA Ops:
  0.0 0.5 %collective-permute-start.1 = (s32[8,128]{1,0:T(8,128)}, s32[8,128]{1,0:T(8,128)S(1)}, u32[]{:S(2)}, u32[]{:S(2)}) collective-permute-start(s32[8,128]{1,0:T(8,128)} %tissue.3), channel_id=1, source_target_pairs={{0,1},{1,0},{2,3},{3,2},{4,5},{5,4},{6,7},{7,6},{8,9},{9,8},{10,11... | collective-permute-start | bytes 12296 | tf_op jit(solution)/shard_map/ppermute | solution.py:305
  0.5 0.1 collective-permute-start
  0.5 1.2 %fusion = (bf16[3,128,512]{2,1,0:T(8,128)(2,1)S(1)}, bf16[3,128,512]{2,1,0:T(8,128)(2,1)S(1)}) fusion(bf16[8,128,512]{2,1,0:T(8,128)(2,1)} %param.10), kind=kLoop, calls=%fused_computation | loop fusion | bytes 1572864 | tf_op jit(solution)/shard_map/slice | solution.py:335
  1.7 0.0 copy-start.1
  1.7 0.0 copy-start.2
  1.7 0.8 %border.1 = bf16[384,512]{1,0:T(8,128)(2,1)} custom-call(s32[1]{0:T(128)} %bitcast.2.odd_ref, bf16[384,512]{1,0:T(8,128)(2,1)S(1)} %bitcast.17, bf16[384,512]{1,0:T(8,128)(2,1)S(1)} %bitcast.16), custom_call_target="tpu_custom_call" | custom-call | flops 10000000000 | bytes 1000000 | tf_op jit(solution)/shard_map/border/pallas_call | solution.py:327
  2.5 0.7 %collective-permute-start.3 = (bf16[384,512]{1,0:T(8,128)(2,1)}, bf16[384,512]{1,0:T(8,128)(2,1)S(1)}, u32[]{:S(2)}, u32[]{:S(2)}) collective-permute-start(bf16[384,512]{1,0:T(8,128)(2,1)} %border.1), channel_id=1, source_target_pairs={{1,2},{3,4},{5,6},{7,8},{9,10},{11,12},{13,14},{2,1},{4,3},{6,5},{... | collective-permute-start | bytes 1179656 | tf_op jit(solution)/shard_map/ppermute | solution.py:337
  3.2 0.1 collective-permute-done.other
  3.3 0.0 copy-done.1
  3.3 0.0 copy-done.2
  3.3 1.0 %copy-done.5 = bf16[512,512]{1,0:T(8,128)(2,1)S(1)} copy-done((bf16[512,512]{1,0:T(8,128)(2,1)S(1)}, bf16[512,512]{1,0:T(8,128)(2,1)}, u32[]{:S(2)}) %copy-start.5) | copy-done | bytes 524312
  4.4 1.5 %project.1 = (bf16[1024,512]{1,0:T(8,128)(2,1)S(1)}, bf16[2048,256]{1,0:T(8,128)(2,1)S(1)}, bf16[2048,256]{1,0:T(8,128)(2,1)S(1)}) custom-call(s32[1]{0:T(128)} %bitcast.own_ref, bf16[1024,512]{1,0:T(8,128)(2,1)S(1)} %bitcast.13, bf16[1024,512]{1,0:T(8,128)(2,1)S(1)} %collective-permute-done.other, bf16[512,512]{1,0:T(8,128)(2,1)S(1)} %copy-done.5, ...), custom_call_target="tpu_custom_call" | custom-call | flops 1300000000 | bytes 4000000 | tf_op jit(solution)/shard_map/project/pallas_call | solution.py:341
  5.9 0.0 copy-start.7
  5.9 0.0 copy-start.8
  6.0 0.0 copy-start.9
  6.0 0.0 collective-permute-done.1.other_tissue
  6.0 0.0 copy-done
  6.0 0.0 copy-done.4
  6.0 1.9 %band.3.after = bf16[80,512]{1,0:T(8,128)(2,1)S(1)} custom-call(s32[1]{0:T(128)} %bitcast.own_ref, bf16[2048,256]{1,0:T(8,128)(2,1)S(1)} %get-tuple-element.14.keys, bf16[2048,256]{1,0:T(8,128)(2,1)S(1)} %get-tuple-element.15.vals, s32[8,128]{1,0:T(8,128)S(1)} %copy-done.4, s32[8,128]{1,0:T(8,128)S(1)} %collective-permute-done.1.other_tissue, ...), custom_call_target="tpu_custom_call" | custom-call | flops 600000000 | bytes 4000000 | tf_op jit(solution)/shard_map/band/pallas_call | solution.py:352
  7.9 0.0 copy-start.6
  7.9 5.2 %collective-permute-start.2 = (bf16[80,512]{1,0:T(8,128)(2,1)S(1)}, bf16[80,512]{1,0:T(8,128)(2,1)S(1)}, u32[]{:S(2)}, u32[]{:S(2)}) collective-permute-start(bf16[80,512]{1,0:T(8,128)(2,1)S(1)} %band.3.after), channel_id=1, source_target_pairs={{0,4},{1,5},{2,6},{3,7},{4,0},{5,1},{6,2},{7,3},{8,12},{9,13},{10,... | collective-permute-start | bytes 245768 | tf_op jit(solution)/shard_map/ppermute | solution.py:305
  13.1 0.0 copy-done.7
  13.1 0.0 copy-done.8
  13.1 0.0 copy-done.9
  13.1 0.1 taps.1.before.all_taps
  13.3 1.9 %band.2.held = f32[72,512]{1,0:T(8,128)S(1)} custom-call(s32[1]{0:T(128)} %bitcast.own_ref, bf16[2048,256]{1,0:T(8,128)(2,1)S(1)} %get-tuple-element.14.keys, bf16[2048,256]{1,0:T(8,128)(2,1)S(1)} %get-tuple-element.15.vals, s32[8,128]{1,0:T(8,128)S(1)} %copy-done.4, s32[8,128]{1,0:T(8,128)S(1)} %collective-permute-done.1.other_tissue, ...), custom_call_target="tpu_custom_call" | custom-call | flops 600000000 | bytes 4000000 | tf_op jit(solution)/shard_map/band/pallas_call | solution.py:352
  15.2 1.2 %collective-permute-done.2.got = bf16[80,512]{1,0:T(8,128)(2,1)S(1)} collective-permute-done((bf16[80,512]{1,0:T(8,128)(2,1)S(1)}, bf16[80,512]{1,0:T(8,128)(2,1)S(1)}, u32[]{:S(2)}, u32[]{:S(2)}) %collective-permute-start.2) | collective-permute-done | bytes 81952 | tf_op jit(solution)/shard_map/ppermute | solution.py:305
  16.3 0.1 merge_next.2
  16.4 2.8 %collective-permute-start.4 = (bf16[80,512]{1,0:T(8,128)(2,1)S(1)}, bf16[80,512]{1,0:T(8,128)(2,1)S(1)}, u32[]{:S(2)}, u32[]{:S(2)}) collective-permute-start(bf16[80,512]{1,0:T(8,128)(2,1)S(1)} %get-tuple-element.16.after), channel_id=1, source_target_pairs={{0,8},{1,9},{2,10},{3,11},{4,12},{5,13},{6,14},{7,15},{8,0},{9,1},... | collective-permute-start | bytes 245768 | tf_op jit(solution)/shard_map/ppermute | solution.py:305
  19.2 2.0 %token_.2.after.weights_low = bf16[1024,1024]{1,0:T(8,128)(2,1)S(1)} custom-call(bf16[1024,512]{1,0:T(8,128)(2,1)S(1)} %bitcast.14, bf16[512,512]{1,0:T(8,128)(2,1)S(1)} %copy-done.6, bf16[256,512]{1,0:T(8,128)(2,1)S(1)} %copy-done, bf16[80,512]{1,0:T(8,128)(2,1)S(1)} %get-tuple-element.16.after), custom_call_target="tpu_custom_call" | custom-call | flops 2000000000 | bytes 6000000 | tf_op jit(solution)/shard_map/token/pallas_call | solution.py:366
  21.2 0.0 collective-permute-done.3.outer
  21.2 0.6 %halo.1 = (bf16[384,512]{1,0:T(8,128)(2,1)S(1)}, bf16[384,512]{1,0:T(8,128)(2,1)S(1)}) custom-call(s32[1]{0:T(128)} %bitcast.2.odd_ref, bf16[1024,512]{1,0:T(8,128)(2,1)S(1)} %collective-permute-done.other, bf16[384,512]{1,0:T(8,128)(2,1)S(1)} %collective-permute-done.3.outer, bf16[512,512]{1,0:T(8,128)(2,1)S(1)} %copy-done.2, ...), custom_call_target="tpu_custom_call" | custom-call | flops 400000000 | bytes 2000000 | tf_op jit(solution)/shard_map/halo/pallas_call | solution.py:423
  21.8 2.0 %token_.3.before.weights_high = bf16[1024,1024]{1,0:T(8,128)(2,1)S(1)} custom-call(bf16[1024,512]{1,0:T(8,128)(2,1)S(1)} %bitcast.15, bf16[512,512]{1,0:T(8,128)(2,1)S(1)} %copy-done.6, bf16[256,512]{1,0:T(8,128)(2,1)S(1)} %copy-done, bf16[384,512]{1,0:T(8,128)(2,1)S(1)} %get-tuple-element.17.after.above), custom_call_target="tpu_custom_call" | custom-call | flops 2000000000 | bytes 6000000 | tf_op jit(solution)/shard_map/token/pallas_call | solution.py:366
  23.8 0.0 collective-permute-done.4.got
  23.8 0.1 merge_next.3
  23.8 1.0 %collective-permute-start.5 = (bf16[80,512]{1,0:T(8,128)(2,1)S(1)}, bf16[80,512]{1,0:T(8,128)(2,1)S(1)}, u32[]{:S(2)}, u32[]{:S(2)}) collective-permute-start(bf16[80,512]{1,0:T(8,128)(2,1)S(1)} %get-tuple-element.20.after), channel_id=1, source_target_pairs={{0,2},{1,3},{2,0},{3,1},{4,6},{5,7},{6,4},{7,5},{8,10},{9,11},{10,... | collective-permute-start | bytes 245768 | tf_op jit(solution)/shard_map/ppermute | solution.py:305
  24.8 2.3 %conv.2 = f32[8,128,256]{2,1,0:T(8,128)S(1)} custom-call(bf16[1024,512]{1,0:T(8,128)(2,1)S(1)} %get-tuple-element.21.values, bf16[384,512]{1,0:T(8,128)(2,1)S(1)} %get-tuple-element.17.after.above, bf16[384,512]{1,0:T(8,128)(2,1)S(1)} %get-tuple-element.22.below, f32[7,24,512]{2,1,0:T(8,128)S(1)} %taps.1.before.all_taps, ...), custom_call_target="tpu_custom_call" | custom-call | flops 3000000000 | bytes 4000000 | tf_op jit(solution)/shard_map/conv/pallas_call | solution.py:384
  27.1 1.2 %collective-permute-done.5.got = bf16[80,512]{1,0:T(8,128)(2,1)S(1)} collective-permute-done((bf16[80,512]{1,0:T(8,128)(2,1)S(1)}, bf16[80,512]{1,0:T(8,128)(2,1)S(1)}, u32[]{:S(2)}, u32[]{:S(2)}) %collective-permute-start.5) | collective-permute-done | bytes 81952 | tf_op jit(solution)/shard_map/ppermute | solution.py:305
  28.4 0.0 copy-start.3
  28.4 1.6 %collective-permute-start.6 = (bf16[64,512]{1,0:T(8,128)(2,1)S(1)}, bf16[64,512]{1,0:T(8,128)(2,1)S(1)}, u32[]{:S(2)}, u32[]{:S(2)}) collective-permute-start(bf16[64,512]{1,0:T(8,128)(2,1)S(1)} %merge_last.1.after.own), channel_id=1, source_target_pairs={{0,4},{1,5},{2,6},{3,7},{4,0},{5,1},{6,2},{7,3},{8,12},{9,13},{10,... | collective-permute-start | bytes 196616 | tf_op jit(solution)/shard_map/ppermute | solution.py:305
  30.0 2.5 %conv.3 = f32[8,128,256]{2,1,0:T(8,128)S(1)} custom-call(bf16[1024,512]{1,0:T(8,128)(2,1)S(1)} %get-tuple-element.21.values, bf16[384,512]{1,0:T(8,128)(2,1)S(1)} %get-tuple-element.17.after.above, bf16[384,512]{1,0:T(8,128)(2,1)S(1)} %get-tuple-element.22.below, f32[7,24,512]{2,1,0:T(8,128)S(1)} %taps.1.before.all_taps, bf16[64,512]{1,0:T(8,128)(2,1)S(1)} %merge_last.1.after.own), custom_call_target="tpu_custom_call" | custom-call | flops 3000000000 | bytes 4000000 | tf_op jit(solution)/shard_map/conv/pallas_call | solution.py:384
  32.5 0.1 collective-permute-start.7
  32.6 0.1 collective-permute-done.6.near
  32.7 0.4 %collective-permute-start.8 = (bf16[64,512]{1,0:T(8,128)(2,1)S(1)}, bf16[64,512]{1,0:T(8,128)(2,1)S(1)}, u32[]{:S(2)}, u32[]{:S(2)}) collective-permute-start(bf16[64,512]{1,0:T(8,128)(2,1)S(1)} %relay.1), channel_id=1, source_target_pairs={{0,1},{1,0},{2,3},{3,2},{4,5},{5,4},{6,7},{7,6},{8,9},{9,8},{10,11... | collective-permute-start | bytes 196616 | tf_op jit(solution)/shard_map/ppermute | solution.py:305
  33.2 0.7 %collective-permute-done.7.side = bf16[64,512]{1,0:T(8,128)(2,1)S(1)} collective-permute-done((bf16[64,512]{1,0:T(8,128)(2,1)S(1)}, bf16[64,512]{1,0:T(8,128)(2,1)S(1)}, u32[]{:S(2)}, u32[]{:S(2)}) %collective-permute-start.7) | collective-permute-done | bytes 65568 | tf_op jit(solution)/shard_map/ppermute | solution.py:305
  33.8 0.2 collective-permute-done.8.far
  34.1 0.0 copy-done.3
  34.1 2.8 %out.1 = bf16[1024,512]{1,0:T(8,128)(2,1)} custom-call(s32[1]{0:T(128)} %bitcast.own_ref, bf16[1024,1024]{1,0:T(8,128)(2,1)S(1)} %token_.2.after.weights_low, bf16[1024,1024]{1,0:T(8,128)(2,1)S(1)} %token_.3.before.weights_high, bf16[64,512]{1,0:T(8,128)(2,1)S(1)} %merge_last.1.after.own, bf16[64,512]{1,0:T(8,128)(2,1)S(1)} %collective-permute-done.6.near, ...), custom_call_target="tpu_custom_call" | custom-call | flops 1100000000 | bytes 8000000 | tf_op jit(solution)/shard_map/out/pallas_call | solution.py:454
  (6 shorter events, 0.1 us)
Async XLA Ops:
  0.0 6.0 %collective-permute-start.1 = (s32[8,128]{1,0:T(8,128)}, s32[8,128]{1,0:T(8,128)S(1)}, u32[]{:S(2)}, u32[]{:S(2)}) collective-permute-start(s32[8,128]{1,0:T(8,128)} %tissue.3), channel_id=1, source_target_pairs={{0,1},{1,0},{2,3},{3,2},{4,5},{5,4},{6,7},{7,6},{8,9},{9,8},{10,11... | collective-permute-start | bytes 12296 | tf_op jit(solution)/shard_map/ppermute | solution.py:305
  0.5 2.9 %collective-permute-start = (bf16[1024,512]{1,0:T(8,128)(2,1)}, bf16[1024,512]{1,0:T(8,128)(2,1)S(1)}, u32[]{:S(2)}, u32[]{:S(2)}) collective-permute-start(bf16[1024,512]{1,0:T(8,128)(2,1)} %bitcast.12), channel_id=1, source_target_pairs={{0,1},{1,0},{2,3},{3,2},{4,5},{5,4},{6,7},{7,6},{8,9},{9,8},{10,11... | collective-permute-start | bytes 3145736 | tf_op jit(solution)/shard_map/ppermute | solution.py:305
  1.7 1.6 %copy-start.1 = (bf16[8,128,512]{2,1,0:T(8,128)(2,1)S(1)}, bf16[8,128,512]{2,1,0:T(8,128)(2,1)}, u32[]{:S(2)}) copy-start(bf16[8,128,512]{2,1,0:T(8,128)(2,1)} %param.10) | copy-start | bytes 3145732
  1.7 1.6 %copy-start.2 = (bf16[512,512]{1,0:T(8,128)(2,1)S(1)}, bf16[512,512]{1,0:T(8,128)(2,1)}, u32[]{:S(2)}) copy-start(bf16[512,512]{1,0:T(8,128)(2,1)} %w_value.3) | copy-start | bytes 1572868
  2.5 18.7 %collective-permute-start.3 = (bf16[384,512]{1,0:T(8,128)(2,1)}, bf16[384,512]{1,0:T(8,128)(2,1)S(1)}, u32[]{:S(2)}, u32[]{:S(2)}) collective-permute-start(bf16[384,512]{1,0:T(8,128)(2,1)} %border.1), channel_id=1, source_target_pairs={{1,2},{3,4},{5,6},{7,8},{9,10},{11,12},{13,14},{2,1},{4,3},{6,5},{... | collective-permute-start | bytes 1179656 | tf_op jit(solution)/shard_map/ppermute | solution.py:337
  3.3 1.0 %copy-start.5 = (bf16[512,512]{1,0:T(8,128)(2,1)S(1)}, bf16[512,512]{1,0:T(8,128)(2,1)}, u32[]{:S(2)}) copy-start(bf16[512,512]{1,0:T(8,128)(2,1)} %w_key.1) | copy-start | bytes 1572868
  4.4 1.6 %copy-start = (bf16[256,512]{1,0:T(8,128)(2,1)S(1)}, bf16[256,512]{1,0:T(8,128)(2,1)}, u32[]{:S(2)}) copy-start(bf16[256,512]{1,0:T(8,128)(2,1)} %agents.7) | copy-start | bytes 786436
  4.4 1.6 %copy-start.4 = (s32[8,128]{1,0:T(8,128)S(1)}, s32[8,128]{1,0:T(8,128)}, u32[]{:S(2)}) copy-start(s32[8,128]{1,0:T(8,128)} %tissue.3) | copy-start | bytes 12292
  5.9 7.2 %copy-start.7 = (f32[7,7,512]{2,1,0:T(8,128)S(1)}, f32[7,7,512]{2,1,0:T(8,128)}, u32[]{:S(2)}) copy-start(f32[7,7,512]{2,1,0:T(8,128)} %seven.1) | copy-start | bytes 301060
  5.9 7.2 %copy-start.8 = (f32[5,5,512]{2,1,0:T(8,128)S(1)}, f32[5,5,512]{2,1,0:T(8,128)}, u32[]{:S(2)}) copy-start(f32[5,5,512]{2,1,0:T(8,128)} %five.1) | copy-start | bytes 153604
  6.0 7.2 %copy-start.9 = (f32[3,3,512]{2,1,0:T(4,128)S(1)}, f32[3,3,512]{2,1,0:T(4,128)}, u32[]{:S(2)}) copy-start(f32[3,3,512]{2,1,0:T(4,128)} %three.1) | copy-start | bytes 55300
  7.9 11.3 %copy-start.6 = (bf16[512,512]{1,0:T(8,128)(2,1)S(1)}, bf16[512,512]{1,0:T(8,128)(2,1)}, u32[]{:S(2)}) copy-start(bf16[512,512]{1,0:T(8,128)(2,1)} %w_query.3) | copy-start | bytes 1572868
  7.9 8.4 %collective-permute-start.2 = (bf16[80,512]{1,0:T(8,128)(2,1)S(1)}, bf16[80,512]{1,0:T(8,128)(2,1)S(1)}, u32[]{:S(2)}, u32[]{:S(2)}) collective-permute-start(bf16[80,512]{1,0:T(8,128)(2,1)S(1)} %band.3.after), channel_id=1, source_target_pairs={{0,4},{1,5},{2,6},{3,7},{4,0},{5,1},{6,2},{7,3},{8,12},{9,13},{10,... | collective-permute-start | bytes 245768 | tf_op jit(solution)/shard_map/ppermute | solution.py:305
  16.4 7.4 %collective-permute-start.4 = (bf16[80,512]{1,0:T(8,128)(2,1)S(1)}, bf16[80,512]{1,0:T(8,128)(2,1)S(1)}, u32[]{:S(2)}, u32[]{:S(2)}) collective-permute-start(bf16[80,512]{1,0:T(8,128)(2,1)S(1)} %get-tuple-element.16.after), channel_id=1, source_target_pairs={{0,8},{1,9},{2,10},{3,11},{4,12},{5,13},{6,14},{7,15},{8,0},{9,1},... | collective-permute-start | bytes 245768 | tf_op jit(solution)/shard_map/ppermute | solution.py:305
  23.8 4.5 %collective-permute-start.5 = (bf16[80,512]{1,0:T(8,128)(2,1)S(1)}, bf16[80,512]{1,0:T(8,128)(2,1)S(1)}, u32[]{:S(2)}, u32[]{:S(2)}) collective-permute-start(bf16[80,512]{1,0:T(8,128)(2,1)S(1)} %get-tuple-element.20.after), channel_id=1, source_target_pairs={{0,2},{1,3},{2,0},{3,1},{4,6},{5,7},{6,4},{7,5},{8,10},{9,11},{10,... | collective-permute-start | bytes 245768 | tf_op jit(solution)/shard_map/ppermute | solution.py:305
  28.4 5.7 %copy-start.3 = (bf16[512,512]{1,0:T(8,128)(2,1)S(1)}, bf16[512,512]{1,0:T(8,128)(2,1)}, u32[]{:S(2)}) copy-start(bf16[512,512]{1,0:T(8,128)(2,1)} %w_out.1) | copy-start | bytes 1572868
  28.4 4.3 %collective-permute-start.6 = (bf16[64,512]{1,0:T(8,128)(2,1)S(1)}, bf16[64,512]{1,0:T(8,128)(2,1)S(1)}, u32[]{:S(2)}, u32[]{:S(2)}) collective-permute-start(bf16[64,512]{1,0:T(8,128)(2,1)S(1)} %merge_last.1.after.own), channel_id=1, source_target_pairs={{0,4},{1,5},{2,6},{3,7},{4,0},{5,1},{6,2},{7,3},{8,12},{9,13},{10,... | collective-permute-start | bytes 196616 | tf_op jit(solution)/shard_map/ppermute | solution.py:305
  32.5 1.3 %collective-permute-start.7 = (bf16[64,512]{1,0:T(8,128)(2,1)S(1)}, bf16[64,512]{1,0:T(8,128)(2,1)S(1)}, u32[]{:S(2)}, u32[]{:S(2)}) collective-permute-start(bf16[64,512]{1,0:T(8,128)(2,1)S(1)} %merge_last.1.after.own), channel_id=1, source_target_pairs={{0,1},{1,0},{2,3},{3,2},{4,5},{5,4},{6,7},{7,6},{8,9},{9,8},{10,11... | collective-permute-start | bytes 196616 | tf_op jit(solution)/shard_map/ppermute | solution.py:305
  32.7 1.3 %collective-permute-start.8 = (bf16[64,512]{1,0:T(8,128)(2,1)S(1)}, bf16[64,512]{1,0:T(8,128)(2,1)S(1)}, u32[]{:S(2)}, u32[]{:S(2)}) collective-permute-start(bf16[64,512]{1,0:T(8,128)(2,1)S(1)} %relay.1), channel_id=1, source_target_pairs={{0,1},{1,0},{2,3},{3,2},{4,5},{5,4},{6,7},{7,6},{8,9},{9,8},{10,11... | collective-permute-start | bytes 196616 | tf_op jit(solution)/shard_map/ppermute | solution.py:305

commit v7 on v6

--- a/solution.py
+++ b/solution.py
@@ -161,8 +161,8 @@
         weights[:, head * 256 : head * 256 + 256] = part.astype(BF16)
 
 
-def border_kernel(odd_ref, first, last, border):
-    border[...] = jnp.where(odd_ref[0] == 1, last[...], first[...])
+def pass_kernel(border, same):
+    del border, same
 
 
 def halo_kernel(odd_ref, other, outer, w_value, after, above, below):
@@ -175,8 +175,9 @@
     below[...] = jnp.where(odd, outside, inner)
 
 
-def relay_kernel(near, after, again):
-    again[...] = near[...]
+def relay_kernel(own, near, after, both):
+    both[0:64] = own[...]
+    both[64:128] = near[...]
 
 
 TAP_COUNTS = (2, 2, 2, 2, 2, 2, 2, 2, 1)
@@ -261,27 +262,50 @@
                     position[row, column : column + 8, there] = plane
 
 
-def out_kernel(
-    own_ref, weights_low, weights_high, own, near, side, far, position_low, position_high, w_out, mixed, spread, buffer, sems
-):
+def blend_block(here, weights, position, spread, w_out, rows):
+    blended = (dot_nt(weights[here, :], spread[...]) + position[here, :]).astype(BF16)
+    return dot_nn(blended, w_out[rows, :])
+
+
+def fill_spread(own_ref, pair, spread):
     spread[...] = jnp.zeros_like(spread)
-    for index, part in enumerate((own, near, side, far)):
-        chunk = index ^ own_ref[0]
-        group, place = chunk // 2, chunk % 2
+    for index in range(2):
+        place = (own_ref[0] % 2) ^ index
         for half in range(2):
             rows = pl.ds(pl.multiple_of(place * 128 + half * 64, 64), 64)
             cols = pl.ds(pl.multiple_of(place * 512 + half * 256, 256), 256)
-            spread[group, rows, cols] = part[:, half * 256 : half * 256 + 256]
-    tokens = mixed.shape[0]
-    block = tokens // 2
+            spread[rows, cols] = pair[index * 64 : index * 64 + 64, half * 256 : half * 256 + 256]
+
+
+def own_out_kernel(own_ref, weights_low, weights_high, pair, position_low, position_high, w_out, partial, spread):
+    fill_spread(own_ref, pair, spread)
+    block = partial.shape[0] // 2
+    for group, (weights, position) in enumerate(((weights_low, position_low), (weights_high, position_high))):
+
+        @pl.when(own_ref[0] // 2 == group)
+        def _(group=group, weights=weights, position=position):
+            rows = slice(group * 256, group * 256 + 256)
+            for index in range(2):
+                here = slice(index * block, index * block + block)
+                partial[here, :] = blend_block(here, weights, position, spread, w_out, rows)
+
+
+def out_kernel(
+    own_ref, weights_low, weights_high, pair, position_low, position_high, w_out, partial, mixed, spread, buffer, sems
+):
+    fill_spread(own_ref, pair, spread)
+    block = partial.shape[0] // 2
     copies = []
     for index in range(2):
         here = slice(index * block, index * block + block)
-        blended = []
         for group, (weights, position) in enumerate(((weights_low, position_low), (weights_high, position_high))):
-            attended = dot_nt(weights[here, :], spread[group])
-            blended.append((attended + position[here, :]).astype(BF16))
-        buffer[here, :] = dot_nn(jnp.concatenate(blended, axis=1), w_out[...]).astype(BF16)
+
+            @pl.when(own_ref[0] // 2 != group)
+            def _(group=group, weights=weights, position=position, here=here):
+                rows = slice(group * 256, group * 256 + 256)
+                total = partial[here, :] + blend_block(here, weights, position, spread, w_out, rows)
+                buffer[here, :] = total.astype(BF16)
+
         copies.append(pltpu.make_async_copy(buffer.at[here, :], mixed.at[here, :], sems.at[index]))
         copies[-1].start()
     for copy in copies:
@@ -324,15 +348,17 @@
     other = exchange(flat, 1)
     other_tissue = exchange(tissue, 1)
 
+    border = lax.dynamic_slice_in_dim(flat, odd * (tokens - 3 * width), 3 * width, 0)
     border = pl.pallas_call(
-        border_kernel,
+        pass_kernel,
         out_shape=shape((3 * width, dim), BF16),
-        in_specs=[smem, vmem, vmem],
-        out_specs=vmem,
+        in_specs=[anywhere],
+        out_specs=anywhere,
+        input_output_aliases={0: 0},
         compiler_params=params(16),
-        cost_estimate=cost(1e10, 1e6),
-        name="border",
-    )(odd_word, flat[: 3 * width], flat[tokens - 3 * width :])
+        cost_estimate=cost(1e11, 1e6),
+        name="pass",
+    )(border)
     rest = [(i, i + 1) for i in range(1, peers - 1, 2)]
     outer = lax.ppermute(border, "col", rest + [(j, i) for i, j in rest])
 
@@ -438,33 +464,42 @@
         last_merge_kernel, out_shape=shape((64, 512), BF16), out_specs=vmem, name="merge_last", **hop
     )(held, got, position_low)
     near = exchange(own, 4)
-    side = exchange(own, 1)
     position_high = conv(1, own)
-    again = pl.pallas_call(
+    pair = pl.pallas_call(
         relay_kernel,
-        out_shape=shape((64, 512), BF16),
-        in_specs=[vmem, anywhere],
+        out_shape=shape((128, 512), BF16),
+        in_specs=[vmem, vmem, anywhere],
         out_specs=vmem,
         compiler_params=params(16),
         cost_estimate=cost(1e6, 1e6),
         name="relay",
-    )(near, position_high)
-    far = exchange(again, 1)
-
+    )(own, near, position_high)
+    other_pair = exchange(pair, 1)
+
+    partial = pl.pallas_call(
+        own_out_kernel,
+        out_shape=shape((tokens, dim), F32),
+        in_specs=[smem] + [vmem] * 6,
+        out_specs=vmem,
+        scratch_shapes=[VMEM((256, 1024), BF16)],
+        compiler_params=params(20),
+        cost_estimate=cost(1.1e9, 4e6),
+        name="own_out",
+    )(own_chunk, weights_low, weights_high, pair, position_low, position_high, w_out)
     mixed = pl.pallas_call(
         out_kernel,
         out_shape=shape((tokens, dim), BF16),
-        in_specs=[smem] + [vmem] * 9,
+        in_specs=[smem] + [vmem] * 7,
         out_specs=anywhere,
         scratch_shapes=[
-            VMEM((2, 256, 1024), BF16),
+            VMEM((256, 1024), BF16),
             VMEM((tokens, dim), BF16),
             pltpu.SemaphoreType.DMA((2,)),
         ],
         compiler_params=params(20),
         cost_estimate=cost(1.1e9, 8e6),
         name="out",
-    )(own_chunk, weights_low, weights_high, own, near, side, far, position_low, position_high, w_out)
+    )(own_chunk, weights_low, weights_high, other_pair, position_low, position_high, w_out, partial)
     return mixed.reshape(band_rows, width, dim)
 
 

time: 37.2 us -> 36.9 us (level)
  starting transfers between devices: 12.4 us -> 11.3 us
  Pallas kernels: 18.5 us -> 19.3 us
    ppermute x8 -> x7, starting transfers between devices: 11.7 us -> 10.5 us  [exchange(): return lax.ppermute(x, 'col', [(i, i ^ bit) for i in range(peers)])]
    slice x1 -> x0, local copies, waits for them, and re-layouts: 1.17 us -> none  [on_device(): flat[tokens - 3 * width:]]
    pallas_call x2 -> x3, Pallas kernels: 0.79 us -> 1.84 us  [the longest x1 1.83 us: on_device(): pl.pallas_call(own_out_kernel, out_shape=shape((tokens, dim), F32), in_sp...]
    dynamic_slice x0 -> x1, local copies, waits for them, and re-layouts: none -> 1.02 us  [on_device(): lax.dynamic_slice_in_dim(flat, odd * (tokens - 3 * width), 3 * width, 0)]
    ppermute x8 -> x7, waiting for transfers between devices: 3.55 us -> 3.51 us  [exchange(): return lax.ppermute(x, 'col', [(i, i ^ bit) for i in range(peers)])]
  transfers between devices with their start and end apart: 9 -> 8, of which waited for: 6 -> 4; matrix products, arithmetic and copies ran while one was open for 3% -> 3% of each run, Pallas kernels for 42% -> 45%
where the time goes in v7:
time: 36.9 us; the launch traced here: 36.6 us
  Pallas kernels  19.3 us (52%)
  starting transfers between devices  11.3 us (31%)
  waiting for transfers between devices  3.51 us (10%)
  local copies, waits for them, and re-layouts  2.12 us (6%)
  between operations  0.39 us (1%)
    ppermute x7, starting transfers between devices, exchange(): return lax.ppermute(x, 'col', [(i, i ^ bit) for i in range(peers)])  10.5 us
    pallas_call x2, Pallas kernels, conv(): pl.pallas_call(functools.partial(conv_kernel, at * half_dim), out_shape=s...  4.79 us
    pallas_call x2, Pallas kernels, token(): pl.pallas_call(functools.partial(token_kernel, scale), out_shape=shape((t...  3.9 us
    pallas_call x2, Pallas kernels, band(): pl.pallas_call(functools.partial(kernel, scale), out_shape=out_shape, in_...  3.78 us
    ppermute x7, waiting for transfers between devices, exchange(): return lax.ppermute(x, 'col', [(i, i ^ bit) for i in range(peers)])  3.51 us
    pallas_call x1, Pallas kernels, on_device(): pl.pallas_call(out_kernel, out_shape=shape((tokens, dim), BF16), in_specs...  2.6 us
    pallas_call x1, Pallas kernels, on_device(): pl.pallas_call(own_out_kernel, out_shape=shape((tokens, dim), F32), in_sp...  1.83 us
    pallas_call x1, Pallas kernels, on_device(): pl.pallas_call(project_kernel, out_shape=(shape((tokens, dim), BF16), bot...  1.54 us
  transfers between devices with their start and end apart: 8, of which 4 were waited for; matrix products, arithmetic and copies ran while one was open for 3% of the time, Pallas kernels for 45%

profile of v7, /device:TPU:0, one launch (start us, length us, event | category | flops | bytes accessed | tf_op | source)
XLA Modules:
  0.0 36.6 jit_solution(12183794330094408112)
XLA Ops:
  0.0 0.5 %collective-permute-start.1 = (s32[8,128]{1,0:T(8,128)}, s32[8,128]{1,0:T(8,128)S(1)}, u32[]{:S(2)}, u32[]{:S(2)}) collective-permute-start(s32[8,128]{1,0:T(8,128)} %tissue.3), channel_id=1, source_target_pairs={{0,1},{1,0},{2,3},{3,2},{4,5},{5,4},{6,7},{7,6},{8,9},{9,8},{10,11... | collective-permute-start | bytes 12296 | tf_op jit(solution)/shard_map/ppermute | solution.py:329
  0.5 0.1 collective-permute-start
  0.5 1.0 %constant_dynamic-slice_fusion.border = bf16[384,512]{1,0:T(8,128)(2,1)S(1)} fusion(bf16[1024,512]{1,0:T(8,128)(2,1)} %bitcast.13, s32[]{:T(128)S(6)} %select_n.11), kind=kLoop, calls=%fused_computation | loop fusion | bytes 786436 | tf_op jit(solution)/shard_map/dynamic_slice | solution.py:351
  1.5 0.0 copy-start.2
  1.5 0.0 copy-start.3
  1.6 0.8 %collective-permute-start.3 = (bf16[384,512]{1,0:T(8,128)(2,1)S(1)}, bf16[384,512]{1,0:T(8,128)(2,1)S(1)}, u32[]{:S(2)}, u32[]{:S(2)}) collective-permute-start(bf16[384,512]{1,0:T(8,128)(2,1)S(1)} %pass.1), channel_id=1, source_target_pairs={{1,2},{3,4},{5,6},{7,8},{9,10},{11,12},{13,14},{2,1},{4,3},{6,5},{... | collective-permute-start | bytes 1179656 | tf_op jit(solution)/shard_map/ppermute | solution.py:363
  2.4 0.9 %collective-permute-done.other = bf16[1024,512]{1,0:T(8,128)(2,1)S(1)} collective-permute-done((bf16[1024,512]{1,0:T(8,128)(2,1)}, bf16[1024,512]{1,0:T(8,128)(2,1)S(1)}, u32[]{:S(2)}, u32[]{:S(2)}) %collective-permute-start) | collective-permute-done | bytes 1048608 | tf_op jit(solution)/shard_map/ppermute | solution.py:329
  3.3 0.0 copy-done.2
  3.3 0.0 copy-done.3
  3.3 0.0 copy-start.5
  3.3 1.0 %copy-done.5 = bf16[512,512]{1,0:T(8,128)(2,1)S(1)} copy-done((bf16[512,512]{1,0:T(8,128)(2,1)S(1)}, bf16[512,512]{1,0:T(8,128)(2,1)}, u32[]{:S(2)}) %copy-start.5) | copy-done | bytes 524312
  4.4 1.5 %project.1 = (bf16[1024,512]{1,0:T(8,128)(2,1)S(1)}, bf16[2048,256]{1,0:T(8,128)(2,1)S(1)}, bf16[2048,256]{1,0:T(8,128)(2,1)S(1)}) custom-call(s32[1]{0:T(128)} %bitcast.own_ref, bf16[1024,512]{1,0:T(8,128)(2,1)S(1)} %bitcast.14, bf16[1024,512]{1,0:T(8,128)(2,1)S(1)} %collective-permute-done.other, bf16[512,512]{1,0:T(8,128)(2,1)S(1)} %copy-done.5, ...), custom_call_target="tpu_custom_call" | custom-call | flops 1300000000 | bytes 4000000 | tf_op jit(solution)/shard_map/project/pallas_call | solution.py:367
  5.9 0.0 copy-start.7
  5.9 0.0 copy-start.8
  6.0 0.0 copy-start.9
  6.0 0.0 collective-permute-done.1.other_tissue
  6.0 0.0 copy-done.1
  6.0 0.0 copy-done.4
  6.0 1.9 %band.3.after = bf16[80,512]{1,0:T(8,128)(2,1)S(1)} custom-call(s32[1]{0:T(128)} %bitcast.own_ref, bf16[2048,256]{1,0:T(8,128)(2,1)S(1)} %get-tuple-element.14.keys, bf16[2048,256]{1,0:T(8,128)(2,1)S(1)} %get-tuple-element.15.vals, s32[8,128]{1,0:T(8,128)S(1)} %copy-done.4, s32[8,128]{1,0:T(8,128)S(1)} %collective-permute-done.1.other_tissue, ...), custom_call_target="tpu_custom_call" | custom-call | flops 600000000 | bytes 4000000 | tf_op jit(solution)/shard_map/band/pallas_call | solution.py:378
  7.9 0.0 copy-start.6
  7.9 4.4 %collective-permute-start.2 = (bf16[80,512]{1,0:T(8,128)(2,1)S(1)}, bf16[80,512]{1,0:T(8,128)(2,1)S(1)}, u32[]{:S(2)}, u32[]{:S(2)}) collective-permute-start(bf16[80,512]{1,0:T(8,128)(2,1)S(1)} %band.3.after), channel_id=1, source_target_pairs={{0,4},{1,5},{2,6},{3,7},{4,0},{5,1},{6,2},{7,3},{8,12},{9,13},{10,... | collective-permute-start | bytes 245768 | tf_op jit(solution)/shard_map/ppermute | solution.py:329
  12.3 0.0 copy-done.7
  12.3 0.0 copy-done.8
  12.3 0.0 copy-done.9
  12.3 0.1 taps.1.before.all_taps
  12.5 1.9 %band.2.held = f32[72,512]{1,0:T(8,128)S(1)} custom-call(s32[1]{0:T(128)} %bitcast.own_ref, bf16[2048,256]{1,0:T(8,128)(2,1)S(1)} %get-tuple-element.14.keys, bf16[2048,256]{1,0:T(8,128)(2,1)S(1)} %get-tuple-element.15.vals, s32[8,128]{1,0:T(8,128)S(1)} %copy-done.4, s32[8,128]{1,0:T(8,128)S(1)} %collective-permute-done.1.other_tissue, ...), custom_call_target="tpu_custom_call" | custom-call | flops 600000000 | bytes 4000000 | tf_op jit(solution)/shard_map/band/pallas_call | solution.py:378
  14.4 1.2 %collective-permute-done.2.got = bf16[80,512]{1,0:T(8,128)(2,1)S(1)} collective-permute-done((bf16[80,512]{1,0:T(8,128)(2,1)S(1)}, bf16[80,512]{1,0:T(8,128)(2,1)S(1)}, u32[]{:S(2)}, u32[]{:S(2)}) %collective-permute-start.2) | collective-permute-done | bytes 81952 | tf_op jit(solution)/shard_map/ppermute | solution.py:329
  15.5 0.1 merge_next.2
  15.6 2.8 %collective-permute-start.4 = (bf16[80,512]{1,0:T(8,128)(2,1)S(1)}, bf16[80,512]{1,0:T(8,128)(2,1)S(1)}, u32[]{:S(2)}, u32[]{:S(2)}) collective-permute-start(bf16[80,512]{1,0:T(8,128)(2,1)S(1)} %get-tuple-element.16.after), channel_id=1, source_target_pairs={{0,8},{1,9},{2,10},{3,11},{4,12},{5,13},{6,14},{7,15},{8,0},{9,1},... | collective-permute-start | bytes 245768 | tf_op jit(solution)/shard_map/ppermute | solution.py:329
  18.4 0.0 copy-done.6
  18.5 2.0 %token_.2.after.weights_low = bf16[1024,1024]{1,0:T(8,128)(2,1)S(1)} custom-call(bf16[1024,512]{1,0:T(8,128)(2,1)S(1)} %bitcast.15, bf16[512,512]{1,0:T(8,128)(2,1)S(1)} %copy-done.6, bf16[256,512]{1,0:T(8,128)(2,1)S(1)} %copy-done.1, bf16[80,512]{1,0:T(8,128)(2,1)S(1)} %get-tuple-element.16.after), custom_call_target="tpu_custom_call" | custom-call | flops 2000000000 | bytes 6000000 | tf_op jit(solution)/shard_map/token/pallas_call | solution.py:392
  20.4 0.0 collective-permute-done.3.outer
  20.4 0.6 %halo.1 = (bf16[384,512]{1,0:T(8,128)(2,1)S(1)}, bf16[384,512]{1,0:T(8,128)(2,1)S(1)}) custom-call(s32[1]{0:T(128)} %bitcast.2.odd_ref, bf16[1024,512]{1,0:T(8,128)(2,1)S(1)} %collective-permute-done.other, bf16[384,512]{1,0:T(8,128)(2,1)S(1)} %collective-permute-done.3.outer, bf16[512,512]{1,0:T(8,128)(2,1)S(1)} %copy-done.2, ...), custom_call_target="tpu_custom_call" | custom-call | flops 400000000 | bytes 2000000 | tf_op jit(solution)/shard_map/halo/pallas_call | solution.py:449
  21.0 2.0 %token_.3.before.weights_high = bf16[1024,1024]{1,0:T(8,128)(2,1)S(1)} custom-call(bf16[1024,512]{1,0:T(8,128)(2,1)S(1)} %bitcast.16, bf16[512,512]{1,0:T(8,128)(2,1)S(1)} %copy-done.6, bf16[256,512]{1,0:T(8,128)(2,1)S(1)} %copy-done.1, bf16[384,512]{1,0:T(8,128)(2,1)S(1)} %get-tuple-element.17.after.above), custom_call_target="tpu_custom_call" | custom-call | flops 2000000000 | bytes 6000000 | tf_op jit(solution)/shard_map/token/pallas_call | solution.py:392
  23.0 0.0 collective-permute-done.4.got
  23.0 0.1 merge_next.3
  23.0 1.0 %collective-permute-start.5 = (bf16[80,512]{1,0:T(8,128)(2,1)S(1)}, bf16[80,512]{1,0:T(8,128)(2,1)S(1)}, u32[]{:S(2)}, u32[]{:S(2)}) collective-permute-start(bf16[80,512]{1,0:T(8,128)(2,1)S(1)} %get-tuple-element.20.after), channel_id=1, source_target_pairs={{0,2},{1,3},{2,0},{3,1},{4,6},{5,7},{6,4},{7,5},{8,10},{9,11},{10,... | collective-permute-start | bytes 245768 | tf_op jit(solution)/shard_map/ppermute | solution.py:329
  24.0 2.3 %conv.2 = f32[8,128,256]{2,1,0:T(8,128)S(1)} custom-call(bf16[1024,512]{1,0:T(8,128)(2,1)S(1)} %get-tuple-element.21.values, bf16[384,512]{1,0:T(8,128)(2,1)S(1)} %get-tuple-element.17.after.above, bf16[384,512]{1,0:T(8,128)(2,1)S(1)} %get-tuple-element.22.below, f32[7,24,512]{2,1,0:T(8,128)S(1)} %taps.1.before.all_taps, ...), custom_call_target="tpu_custom_call" | custom-call | flops 3000000000 | bytes 4000000 | tf_op jit(solution)/shard_map/conv/pallas_call | solution.py:410
  26.3 1.2 %collective-permute-done.5.got = bf16[80,512]{1,0:T(8,128)(2,1)S(1)} collective-permute-done((bf16[80,512]{1,0:T(8,128)(2,1)S(1)}, bf16[80,512]{1,0:T(8,128)(2,1)S(1)}, u32[]{:S(2)}, u32[]{:S(2)}) %collective-permute-start.5) | collective-permute-done | bytes 81952 | tf_op jit(solution)/shard_map/ppermute | solution.py:329
  27.6 0.0 copy-start
  27.6 1.6 %collective-permute-start.6 = (bf16[64,512]{1,0:T(8,128)(2,1)S(1)}, bf16[64,512]{1,0:T(8,128)(2,1)S(1)}, u32[]{:S(2)}, u32[]{:S(2)}) collective-permute-start(bf16[64,512]{1,0:T(8,128)(2,1)S(1)} %merge_last.1.after.own), channel_id=1, source_target_pairs={{0,4},{1,5},{2,6},{3,7},{4,0},{5,1},{6,2},{7,3},{8,12},{9,13},{10,... | collective-permute-start | bytes 196616 | tf_op jit(solution)/shard_map/ppermute | solution.py:329
  29.2 2.5 %conv.3 = f32[8,128,256]{2,1,0:T(8,128)S(1)} custom-call(bf16[1024,512]{1,0:T(8,128)(2,1)S(1)} %get-tuple-element.21.values, bf16[384,512]{1,0:T(8,128)(2,1)S(1)} %get-tuple-element.17.after.above, bf16[384,512]{1,0:T(8,128)(2,1)S(1)} %get-tuple-element.22.below, f32[7,24,512]{2,1,0:T(8,128)S(1)} %taps.1.before.all_taps, bf16[64,512]{1,0:T(8,128)(2,1)S(1)} %merge_last.1.after.own), custom_call_target="tpu_custom_call" | custom-call | flops 3000000000 | bytes 4000000 | tf_op jit(solution)/shard_map/conv/pallas_call | solution.py:410
  31.7 0.2 collective-permute-done.6.near
  31.9 0.1 collective-permute-start.7
  32.0 0.0 copy-done
  32.0 1.8 %own_out.1.partial = f32[1024,512]{1,0:T(8,128)S(1)} custom-call(s32[1]{0:T(128)} %bitcast.own_ref, bf16[1024,1024]{1,0:T(8,128)(2,1)S(1)} %token_.2.after.weights_low, bf16[1024,1024]{1,0:T(8,128)(2,1)S(1)} %token_.3.before.weights_high, bf16[128,512]{1,0:T(8,128)(2,1)S(1)} %relay.1.pair, f32[1024,256]{1,0:T(8,128)S(1)} %bitcast.10, ...), custom_call_target="tpu_custom_call" | custom-call | flops 1100000000 | bytes 4000000 | tf_op jit(solution)/shard_map/own_out/pallas_call | solution.py:479
  33.9 0.0 collective-permute-done.7.pair
  33.9 2.6 %out.1 = bf16[1024,512]{1,0:T(8,128)(2,1)} custom-call(s32[1]{0:T(128)} %bitcast.own_ref, bf16[1024,1024]{1,0:T(8,128)(2,1)S(1)} %token_.2.after.weights_low, bf16[1024,1024]{1,0:T(8,128)(2,1)S(1)} %token_.3.before.weights_high, bf16[128,512]{1,0:T(8,128)(2,1)S(1)} %collective-permute-done.7.pair, f32[1024,256]{1,0:T(8,128)S(1)} %bitcast.11, ...), custom_call_target="tpu_custom_call" | custom-call | flops 1100000000 | bytes 8000000 | tf_op jit(solution)/shard_map/out/pallas_call | solution.py:489
  (5 shorter events, 0.1 us)
Async XLA Ops:
  0.0 6.0 %collective-permute-start.1 = (s32[8,128]{1,0:T(8,128)}, s32[8,128]{1,0:T(8,128)S(1)}, u32[]{:S(2)}, u32[]{:S(2)}) collective-permute-start(s32[8,128]{1,0:T(8,128)} %tissue.3), channel_id=1, source_target_pairs={{0,1},{1,0},{2,3},{3,2},{4,5},{5,4},{6,7},{7,6},{8,9},{9,8},{10,11... | collective-permute-start | bytes 12296 | tf_op jit(solution)/shard_map/ppermute | solution.py:329
  0.5 2.9 %collective-permute-start = (bf16[1024,512]{1,0:T(8,128)(2,1)}, bf16[1024,512]{1,0:T(8,128)(2,1)S(1)}, u32[]{:S(2)}, u32[]{:S(2)}) collective-permute-start(bf16[1024,512]{1,0:T(8,128)(2,1)} %bitcast.12), channel_id=1, source_target_pairs={{0,1},{1,0},{2,3},{3,2},{4,5},{5,4},{6,7},{7,6},{8,9},{9,8},{10,11... | collective-permute-start | bytes 3145736 | tf_op jit(solution)/shard_map/ppermute | solution.py:329
  1.5 1.8 %copy-start.2 = (bf16[512,512]{1,0:T(8,128)(2,1)S(1)}, bf16[512,512]{1,0:T(8,128)(2,1)}, u32[]{:S(2)}) copy-start(bf16[512,512]{1,0:T(8,128)(2,1)} %w_value.3) | copy-start | bytes 1572868
  1.5 1.8 %copy-start.3 = (bf16[8,128,512]{2,1,0:T(8,128)(2,1)S(1)}, bf16[8,128,512]{2,1,0:T(8,128)(2,1)}, u32[]{:S(2)}) copy-start(bf16[8,128,512]{2,1,0:T(8,128)(2,1)} %param.10) | copy-start | bytes 3145732
  1.6 18.8 %collective-permute-start.3 = (bf16[384,512]{1,0:T(8,128)(2,1)S(1)}, bf16[384,512]{1,0:T(8,128)(2,1)S(1)}, u32[]{:S(2)}, u32[]{:S(2)}) collective-permute-start(bf16[384,512]{1,0:T(8,128)(2,1)S(1)} %pass.1), channel_id=1, source_target_pairs={{1,2},{3,4},{5,6},{7,8},{9,10},{11,12},{13,14},{2,1},{4,3},{6,5},{... | collective-permute-start | bytes 1179656 | tf_op jit(solution)/shard_map/ppermute | solution.py:363
  3.3 1.0 %copy-start.5 = (bf16[512,512]{1,0:T(8,128)(2,1)S(1)}, bf16[512,512]{1,0:T(8,128)(2,1)}, u32[]{:S(2)}) copy-start(bf16[512,512]{1,0:T(8,128)(2,1)} %w_key.1) | copy-start | bytes 1572868
  4.4 1.6 %copy-start.1 = (bf16[256,512]{1,0:T(8,128)(2,1)S(1)}, bf16[256,512]{1,0:T(8,128)(2,1)}, u32[]{:S(2)}) copy-start(bf16[256,512]{1,0:T(8,128)(2,1)} %agents.7) | copy-start | bytes 786436
  4.4 1.6 %copy-start.4 = (s32[8,128]{1,0:T(8,128)S(1)}, s32[8,128]{1,0:T(8,128)}, u32[]{:S(2)}) copy-start(s32[8,128]{1,0:T(8,128)} %tissue.3) | copy-start | bytes 12292
  5.9 6.4 %copy-start.7 = (f32[7,7,512]{2,1,0:T(8,128)S(1)}, f32[7,7,512]{2,1,0:T(8,128)}, u32[]{:S(2)}) copy-start(f32[7,7,512]{2,1,0:T(8,128)} %seven.1) | copy-start | bytes 301060
  5.9 6.4 %copy-start.8 = (f32[5,5,512]{2,1,0:T(8,128)S(1)}, f32[5,5,512]{2,1,0:T(8,128)}, u32[]{:S(2)}) copy-start(f32[5,5,512]{2,1,0:T(8,128)} %five.1) | copy-start | bytes 153604
  6.0 6.4 %copy-start.9 = (f32[3,3,512]{2,1,0:T(4,128)S(1)}, f32[3,3,512]{2,1,0:T(4,128)}, u32[]{:S(2)}) copy-start(f32[3,3,512]{2,1,0:T(4,128)} %three.1) | copy-start | bytes 55300
  7.9 10.6 %copy-start.6 = (bf16[512,512]{1,0:T(8,128)(2,1)S(1)}, bf16[512,512]{1,0:T(8,128)(2,1)}, u32[]{:S(2)}) copy-start(bf16[512,512]{1,0:T(8,128)(2,1)} %w_query.3) | copy-start | bytes 1572868
  7.9 7.6 %collective-permute-start.2 = (bf16[80,512]{1,0:T(8,128)(2,1)S(1)}, bf16[80,512]{1,0:T(8,128)(2,1)S(1)}, u32[]{:S(2)}, u32[]{:S(2)}) collective-permute-start(bf16[80,512]{1,0:T(8,128)(2,1)S(1)} %band.3.after), channel_id=1, source_target_pairs={{0,4},{1,5},{2,6},{3,7},{4,0},{5,1},{6,2},{7,3},{8,12},{9,13},{10,... | collective-permute-start | bytes 245768 | tf_op jit(solution)/shard_map/ppermute | solution.py:329
  15.6 7.4 %collective-permute-start.4 = (bf16[80,512]{1,0:T(8,128)(2,1)S(1)}, bf16[80,512]{1,0:T(8,128)(2,1)S(1)}, u32[]{:S(2)}, u32[]{:S(2)}) collective-permute-start(bf16[80,512]{1,0:T(8,128)(2,1)S(1)} %get-tuple-element.16.after), channel_id=1, source_target_pairs={{0,8},{1,9},{2,10},{3,11},{4,12},{5,13},{6,14},{7,15},{8,0},{9,1},... | collective-permute-start | bytes 245768 | tf_op jit(solution)/shard_map/ppermute | solution.py:329
  23.0 4.5 %collective-permute-start.5 = (bf16[80,512]{1,0:T(8,128)(2,1)S(1)}, bf16[80,512]{1,0:T(8,128)(2,1)S(1)}, u32[]{:S(2)}, u32[]{:S(2)}) collective-permute-start(bf16[80,512]{1,0:T(8,128)(2,1)S(1)} %get-tuple-element.20.after), channel_id=1, source_target_pairs={{0,2},{1,3},{2,0},{3,1},{4,6},{5,7},{6,4},{7,5},{8,10},{9,11},{10,... | collective-permute-start | bytes 245768 | tf_op jit(solution)/shard_map/ppermute | solution.py:329
  27.6 4.4 %copy-start = (bf16[512,512]{1,0:T(8,128)(2,1)S(1)}, bf16[512,512]{1,0:T(8,128)(2,1)}, u32[]{:S(2)}) copy-start(bf16[512,512]{1,0:T(8,128)(2,1)} %w_out.3) | copy-start | bytes 1572868
  27.6 4.3 %collective-permute-start.6 = (bf16[64,512]{1,0:T(8,128)(2,1)S(1)}, bf16[64,512]{1,0:T(8,128)(2,1)S(1)}, u32[]{:S(2)}, u32[]{:S(2)}) collective-permute-start(bf16[64,512]{1,0:T(8,128)(2,1)S(1)} %merge_last.1.after.own), channel_id=1, source_target_pairs={{0,4},{1,5},{2,6},{3,7},{4,0},{5,1},{6,2},{7,3},{8,12},{9,13},{10,... | collective-permute-start | bytes 196616 | tf_op jit(solution)/shard_map/ppermute | solution.py:329
  31.9 1.9 %collective-permute-start.7 = (bf16[128,512]{1,0:T(8,128)(2,1)S(1)}, bf16[128,512]{1,0:T(8,128)(2,1)S(1)}, u32[]{:S(2)}, u32[]{:S(2)}) collective-permute-start(bf16[128,512]{1,0:T(8,128)(2,1)S(1)} %relay.1.pair), channel_id=1, source_target_pairs={{0,1},{1,0},{2,3},{3,2},{4,5},{5,4},{6,7},{7,6},{8,9},{9,8},{10,11... | collective-permute-start | bytes 393224 | tf_op jit(solution)/shard_map/ppermute | solution.py:329

commit v8 on v7

--- a/solution.py
+++ b/solution.py
@@ -33,24 +33,24 @@
     return (place & 1) * 2 + ((place >> 2) & 1)
 
 
-def chunk_state(index, own, scale, keys, vals, tissue, other_tissue, agents):
+def chunk_state(index, scale, both, tissue, other_tissue, agents):
     lines = []
     for grid in (tissue, other_tissue):
         bias = jnp.where(grid[...] > 0, 0.0, NO_SCORE).astype(F32)
         lines += [bias[row : row + 1] for row in range(bias.shape[0])]
     bias_line = jnp.concatenate(lines, axis=1)
-    lanes = pl.ds(pl.multiple_of(((own % 2) ^ index) * 128, 128), 128)
-    pair_agents = agents[:, pl.ds(pl.multiple_of((own ^ index) * 128, 128), 128)]
-    both = [dot_nt(head_tokens(pair_agents, half, scale), keys[:, lanes]) + bias_line for half in range(2)]
+    pair_agents = agents[:, chunk_lanes(index)]
+    keys, vals = both[:, 0:128], both[:, 128:256]
+    all_scores = [dot_nt(head_tokens(pair_agents, half, scale), keys) + bias_line for half in range(2)]
     done = []
-    for scores in both:
+    for scores in all_scores:
         peak = jnp.max(scores, axis=1, keepdims=True)
         expo = jnp.exp(scores - peak)
         total = jnp.sum(expo, axis=1, keepdims=True)
-        done.append((peak, total, dot_nn(expo.astype(BF16), vals[:, lanes])))
+        done.append((peak, total, dot_nn(expo.astype(BF16), vals)))
     lane = lax.broadcasted_iota(jnp.int32, done[0][2].shape, 1)
     weighted = jnp.where(lane < 64, done[0][2], done[1][2]).T
-    stats = jnp.zeros(weighted.T.shape, F32)
+    stats = jnp.zeros(lane.shape, F32)
     for at, value in enumerate(done[0][:2] + done[1][:2]):
         stats = jnp.where(lane == at, value, stats)
     stats = stats.T
@@ -60,31 +60,41 @@
     return tuple(jnp.concatenate(pair, axis=1) for pair in zip(*sides))
 
 
-def project_kernel(own_ref, mine, other, w_key, w_value, values, keys, vals):
+def chunk_lanes(index):
+    return pl.ds(pl.multiple_of((chunk_of_device() ^ index) * 128, 128), 128)
+
+
+def project_chunk(index, mine, other, w_key, w_value, both):
+    lanes = chunk_lanes(index)
+    weights = jnp.concatenate([w_key[:, lanes], w_value[:, lanes]], axis=1)
     tokens = mine.shape[0]
-    block = 256
-    half_lanes = pl.ds(pl.multiple_of((own_ref[0] // 2) * 256, 256), 256)
-    key_half = w_key[:, half_lanes]
-    value_half = w_value[:, half_lanes]
-    for at in range(0, tokens, block):
-        rows = pl.ds(at, block)
-        part = mine[rows, :]
-        keys[rows, :] = dot_nn(part, key_half).astype(BF16)
-        values[rows, :] = dot_nn(part, w_value[...]).astype(BF16)
-        vals[rows, :] = values[rows, half_lanes]
-    for at in range(0, tokens, block):
-        rows = pl.ds(tokens + at, block)
-        part = other[pl.ds(at, block), :]
-        keys[rows, :] = dot_nn(part, key_half).astype(BF16)
-        vals[rows, :] = dot_nn(part, value_half).astype(BF16)
-
-
-def first_band_kernel(scale, own_ref, keys, vals, tissue, other_tissue, agents, payload):
-    put_narrow(payload, chunk_state(1, own_ref[0], scale, keys, vals, tissue, other_tissue, agents))
-
-
-def second_band_kernel(scale, own_ref, keys, vals, tissue, other_tissue, agents, keep):
-    put_wide(keep, chunk_state(0, own_ref[0], scale, keys, vals, tissue, other_tissue, agents))
+    block = 512
+    for source, start in ((mine, 0), (other, tokens)):
+        for at in range(0, tokens, block):
+            both[start + at : start + at + block, :] = dot_nn(source[at : at + block, :], weights).astype(BF16)
+
+
+def project_kernel(mine, other, w_key, w_value, both):
+    project_chunk(1, mine, other, w_key, w_value, both)
+
+
+def second_project_kernel(mine, other, w_key, w_value, first, after, both, values):
+    project_chunk(0, mine, other, w_key, w_value, both)
+    tokens = mine.shape[0]
+    values[:, chunk_lanes(0)] = both[0:tokens, 128:256]
+    values[:, chunk_lanes(1)] = first[0:tokens, 128:256]
+    lanes = pl.ds(pl.multiple_of((1 - chunk_of_device() // 2) * 256, 256), 256)
+    weights = w_value[:, lanes]
+    for at in range(0, tokens, 512):
+        values[at : at + 512, lanes] = dot_nn(mine[at : at + 512, :], weights).astype(BF16)
+
+
+def first_band_kernel(scale, both, tissue, other_tissue, agents, payload):
+    put_narrow(payload, chunk_state(1, scale, both, tissue, other_tissue, agents))
+
+
+def second_band_kernel(scale, both, tissue, other_tissue, agents, keep):
+    put_wide(keep, chunk_state(0, scale, both, tissue, other_tissue, agents))
 
 
 def merge(first, second):
@@ -165,10 +175,10 @@
     del border, same
 
 
-def halo_kernel(odd_ref, other, outer, w_value, after, above, below):
+def halo_kernel(other, outer, w_value, after, above, below):
     rows = outer.shape[0]
-    odd = odd_ref[0] == 1
-    inner_part = other[pl.ds(pl.multiple_of(odd_ref[0] * (other.shape[0] - rows), 128), rows), :]
+    odd = (lax.axis_index("col") % 2) == 1
+    inner_part = other[pl.ds(pl.multiple_of((lax.axis_index("col") % 2) * (other.shape[0] - rows), 128), rows), :]
     inner = dot_nn(inner_part, w_value[...]).astype(BF16)
     outside = dot_nn(outer[...], w_value[...]).astype(BF16)
     above[...] = jnp.where(odd, inner, outside)
@@ -263,26 +273,26 @@
 
 
 def blend_block(here, weights, position, spread, w_out, rows):
-    blended = (dot_nt(weights[here, :], spread[...]) + position[here, :]).astype(BF16)
+    parts = [dot_nt(weights[here, at * 512 : at * 512 + 512], spread[at]) for at in range(2)]
+    blended = (jnp.concatenate(parts, axis=1) + position[here, :]).astype(BF16)
     return dot_nn(blended, w_out[rows, :])
 
 
-def fill_spread(own_ref, pair, spread):
+def fill_spread(pair, spread):
     spread[...] = jnp.zeros_like(spread)
     for index in range(2):
-        place = (own_ref[0] % 2) ^ index
+        place = (chunk_of_device() % 2) ^ index
         for half in range(2):
-            rows = pl.ds(pl.multiple_of(place * 128 + half * 64, 64), 64)
-            cols = pl.ds(pl.multiple_of(place * 512 + half * 256, 256), 256)
-            spread[rows, cols] = pair[index * 64 : index * 64 + 64, half * 256 : half * 256 + 256]
-
-
-def own_out_kernel(own_ref, weights_low, weights_high, pair, position_low, position_high, w_out, partial, spread):
-    fill_spread(own_ref, pair, spread)
+            cols = slice(half * 256, half * 256 + 256)
+            spread[place, half * 64 : half * 64 + 64, cols] = pair[index * 64 : index * 64 + 64, cols]
+
+
+def own_out_kernel(weights_low, weights_high, pair, position_low, position_high, w_out, partial, spread):
+    fill_spread(pair, spread)
     block = partial.shape[0] // 2
     for group, (weights, position) in enumerate(((weights_low, position_low), (weights_high, position_high))):
 
-        @pl.when(own_ref[0] // 2 == group)
+        @pl.when(chunk_of_device() // 2 == group)
         def _(group=group, weights=weights, position=position):
             rows = slice(group * 256, group * 256 + 256)
             for index in range(2):
@@ -291,16 +301,16 @@
 
 
 def out_kernel(
-    own_ref, weights_low, weights_high, pair, position_low, position_high, w_out, partial, mixed, spread, buffer, sems
+    weights_low, weights_high, pair, position_low, position_high, w_out, partial, mixed, spread, buffer, sems
 ):
-    fill_spread(own_ref, pair, spread)
+    fill_spread(pair, spread)
     block = partial.shape[0] // 2
     copies = []
     for index in range(2):
         here = slice(index * block, index * block + block)
         for group, (weights, position) in enumerate(((weights_low, position_low), (weights_high, position_high))):
 
-            @pl.when(own_ref[0] // 2 != group)
+            @pl.when(chunk_of_device() // 2 != group)
             def _(group=group, weights=weights, position=position, here=here):
                 rows = slice(group * 256, group * 256 + 256)
                 total = partial[here, :] + blend_block(here, weights, position, spread, w_out, rows)
@@ -339,9 +349,6 @@
     peers = lax.axis_size("col")
     place = lax.axis_index("col")
     odd = place % 2
-    odd_word = jnp.reshape(odd, (1,)).astype(jnp.int32)
-    own_chunk = jnp.reshape(chunk_of_device(), (1,)).astype(jnp.int32)
-    smem = pl.BlockSpec(memory_space=pltpu.SMEM)
     vmem = pl.BlockSpec(memory_space=VMEM)
     anywhere = pl.BlockSpec(memory_space=pl.ANY)
 
@@ -364,28 +371,28 @@
 
     wide_shape, narrow_shape = shape((72, 512), F32), shape((80, 512), BF16)
     both_bands = shape((2 * tokens, half_dim), BF16)
-    values, keys, vals = pl.pallas_call(
+    first = pl.pallas_call(
         project_kernel,
-        out_shape=(shape((tokens, dim), BF16), both_bands, both_bands),
-        in_specs=[smem] + [vmem] * 4,
-        out_specs=[vmem] * 3,
+        out_shape=both_bands,
+        in_specs=[vmem] * 4,
+        out_specs=vmem,
         compiler_params=params(20),
-        cost_estimate=cost(1.3e9, 4e6),
+        cost_estimate=cost(6e8, 4e6),
         name="project",
-    )(own_chunk, flat, other, w_key, w_value)
-
-    def band(kernel, out_shape):
+    )(flat, other, w_key, w_value)
+
+    def band(kernel, out_shape, both):
         return pl.pallas_call(
             functools.partial(kernel, scale),
             out_shape=out_shape,
-            in_specs=[smem] + [vmem] * 5,
+            in_specs=[vmem] * 4,
             out_specs=vmem,
             compiler_params=params(20),
             cost_estimate=cost(6e8, 4e6, 1e6),
             name="band",
-        )(own_chunk, keys, vals, tissue, other_tissue, agent_tokens)
-
-    payload = band(first_band_kernel, narrow_shape)
+        )(both, tissue, other_tissue, agent_tokens)
+
+    payload = band(first_band_kernel, narrow_shape, first)
 
     def token(at, after):
         lanes = slice(at * half_dim, (at + 1) * half_dim)
@@ -429,7 +436,16 @@
         )(held, got, before)
 
     got = exchange(payload, 4)
-    held = band(second_band_kernel, wide_shape)
+    second, values = pl.pallas_call(
+        second_project_kernel,
+        out_shape=(both_bands, shape((tokens, dim), BF16)),
+        in_specs=[vmem] * 5 + [anywhere],
+        out_specs=[vmem] * 2,
+        compiler_params=params(20),
+        cost_estimate=cost(8e8, 4e6),
+        name="project_second",
+    )(flat, other, w_key, w_value, first, payload)
+    held = band(second_band_kernel, wide_shape, second)
     taps = pl.pallas_call(
         taps_kernel,
         out_shape=shape((7, 24, dim), F32),
@@ -449,12 +465,12 @@
             above, below = pl.pallas_call(
                 halo_kernel,
                 out_shape=(shape((3 * width, dim), BF16), shape((3 * width, dim), BF16)),
-                in_specs=[smem] + [vmem] * 3 + [anywhere],
+                in_specs=[vmem] * 3 + [anywhere],
                 out_specs=[vmem] * 2,
                 compiler_params=params(16),
                 cost_estimate=cost(4e8, 2e6),
                 name="halo",
-            )(odd_word, other, outer, w_value, weights_low)
+            )(other, outer, w_value, weights_low)
             weights_high = token(1, above)
         held, payload = next_merge(held, got, weights_high)
         bit *= 2
@@ -479,27 +495,27 @@
     partial = pl.pallas_call(
         own_out_kernel,
         out_shape=shape((tokens, dim), F32),
-        in_specs=[smem] + [vmem] * 6,
+        in_specs=[vmem] * 6,
         out_specs=vmem,
-        scratch_shapes=[VMEM((256, 1024), BF16)],
+        scratch_shapes=[VMEM((2, 128, 512), BF16)],
         compiler_params=params(20),
         cost_estimate=cost(1.1e9, 4e6),
         name="own_out",
-    )(own_chunk, weights_low, weights_high, pair, position_low, position_high, w_out)
+    )(weights_low, weights_high, pair, position_low, position_high, w_out)
     mixed = pl.pallas_call(
         out_kernel,
         out_shape=shape((tokens, dim), BF16),
-        in_specs=[smem] + [vmem] * 7,
+        in_specs=[vmem] * 7,
         out_specs=anywhere,
         scratch_shapes=[
-            VMEM((256, 1024), BF16),
+            VMEM((2, 128, 512), BF16),
             VMEM((tokens, dim), BF16),
             pltpu.SemaphoreType.DMA((2,)),
         ],
         compiler_params=params(20),
         cost_estimate=cost(1.1e9, 8e6),
         name="out",
-    )(own_chunk, weights_low, weights_high, other_pair, position_low, position_high, w_out, partial)
+    )(weights_low, weights_high, other_pair, position_low, position_high, w_out, partial)
     return mixed.reshape(band_rows, width, dim)
 
 

time: 36.9 us -> 35.1 us (0.951)
  waiting for transfers between devices: 3.51 us -> 6.49 us
  starting transfers between devices: 11.3 us -> 8.83 us
  Pallas kernels: 19.3 us -> 18.1 us
  local copies, waits for them, and re-layouts: 2.12 us -> 1.08 us
    ppermute x7, waiting for transfers between devices: 3.51 us -> 6.48 us  [exchange(): return lax.ppermute(x, 'col', [(i, i ^ bit) for i in range(peers)])]
    ppermute x7, starting transfers between devices: 10.5 us -> 8.01 us  [exchange(): return lax.ppermute(x, 'col', [(i, i ^ bit) for i in range(peers)])]
    unnamed x20, local copies, waits for them, and re-layouts: 1.09 us -> 0.06 us
    pallas_call x1, Pallas kernels: 1.83 us -> 1 us  [on_device(): pl.pallas_call(own_out_kernel, out_shape=shape((tokens, dim), F32), in_sp...]
    pallas_call x1, Pallas kernels: 2.6 us -> 1.98 us  [on_device(): pl.pallas_call(out_kernel, out_shape=shape((tokens, dim), BF16), in_specs...]
    pallas_call x1 -> x2, Pallas kernels: 1.54 us -> 1.83 us  [the longest x1 1.1 us: on_device(): pl.pallas_call(second_project_kernel, out_shape=(both_bands, shape((token...]
  transfers between devices with their start and end apart: 8 -> 8, of which waited for: 4 -> 5; matrix products, arithmetic and copies ran while one was open for 3% -> 3% of each run, Pallas kernels for 45% -> 46%
where the time goes in v8:
time: 35.1 us; the launch traced here: 35 us
  Pallas kernels  18.1 us (52%)
  starting transfers between devices  8.83 us (25%)
  waiting for transfers between devices  6.49 us (18%)
  local copies, waits for them, and re-layouts  1.08 us (3%)
  between operations  0.45 us (1%)
    ppermute x7, starting transfers between devices, exchange(): return lax.ppermute(x, 'col', [(i, i ^ bit) for i in range(peers)])  8.01 us
    ppermute x7, waiting for transfers between devices, exchange(): return lax.ppermute(x, 'col', [(i, i ^ bit) for i in range(peers)])  6.48 us
    pallas_call x2, Pallas kernels, conv(): pl.pallas_call(functools.partial(conv_kernel, at * half_dim), out_shape=s...  4.78 us
    pallas_call x2, Pallas kernels, token(): pl.pallas_call(functools.partial(token_kernel, scale), out_shape=shape((t...  3.9 us
    pallas_call x2, Pallas kernels, band(): pl.pallas_call(functools.partial(kernel, scale), out_shape=out_shape, in_...  3.76 us
    pallas_call x1, Pallas kernels, on_device(): pl.pallas_call(out_kernel, out_shape=shape((tokens, dim), BF16), in_specs...  1.98 us
    pallas_call x1, Pallas kernels, on_device(): pl.pallas_call(second_project_kernel, out_shape=(both_bands, shape((token...  1.1 us
    dynamic_slice x1, local copies, waits for them, and re-layouts, on_device(): lax.dynamic_slice_in_dim(flat, odd * (tokens - 3 * width), 3 * width, 0)  1.02 us
  transfers between devices with their start and end apart: 8, of which 5 were waited for; matrix products, arithmetic and copies ran while one was open for 3% of the time, Pallas kernels for 46%

profile of v8, /device:TPU:0, one launch (start us, length us, event | category | flops | bytes accessed | tf_op | source)
XLA Modules:
  0.0 35.0 jit_solution(15711829033271440421)
XLA Ops:
  0.0 0.5 %collective-permute-start.1 = (s32[8,128]{1,0:T(8,128)}, s32[8,128]{1,0:T(8,128)S(1)}, u32[]{:S(2)}, u32[]{:S(2)}) collective-permute-start(s32[8,128]{1,0:T(8,128)} %tissue.3), channel_id=1, source_target_pairs={{0,1},{1,0},{2,3},{3,2},{4,5},{5,4},{6,7},{7,6},{8,9},{9,8},{10,11... | collective-permute-start | bytes 12296 | tf_op jit(solution)/shard_map/ppermute | solution.py:339
  0.5 0.1 collective-permute-start
  0.5 1.0 %constant_dynamic-slice_fusion.border = bf16[384,512]{1,0:T(8,128)(2,1)S(1)} fusion(bf16[1024,512]{1,0:T(8,128)(2,1)} %bitcast.11, s32[]{:T(128)S(6)} %select_n.11), kind=kLoop, calls=%fused_computation | loop fusion | bytes 786436 | tf_op jit(solution)/shard_map/dynamic_slice | solution.py:358
  1.5 0.0 copy-start
  1.5 0.0 copy-start.1
  1.6 0.0 copy-start.3
  1.6 0.0 copy-start.5
  1.6 0.0 copy-start.9
  1.6 0.8 %collective-permute-start.3 = (bf16[384,512]{1,0:T(8,128)(2,1)S(1)}, bf16[384,512]{1,0:T(8,128)(2,1)S(1)}, u32[]{:S(2)}, u32[]{:S(2)}) collective-permute-start(bf16[384,512]{1,0:T(8,128)(2,1)S(1)} %pass.1), channel_id=1, source_target_pairs={{1,2},{3,4},{5,6},{7,8},{9,10},{11,12},{13,14},{2,1},{4,3},{6,5},{... | collective-permute-start | bytes 1179656 | tf_op jit(solution)/shard_map/ppermute | solution.py:370
  2.4 0.9 %collective-permute-done.other = bf16[1024,512]{1,0:T(8,128)(2,1)S(1)} collective-permute-done((bf16[1024,512]{1,0:T(8,128)(2,1)}, bf16[1024,512]{1,0:T(8,128)(2,1)S(1)}, u32[]{:S(2)}, u32[]{:S(2)}) %collective-permute-start) | collective-permute-done | bytes 1048608 | tf_op jit(solution)/shard_map/ppermute | solution.py:339
  3.3 0.0 copy-done
  3.3 0.0 copy-done.1
  3.3 0.0 copy-done.3
  3.3 0.7 %project.1.both.first = bf16[2048,256]{1,0:T(8,128)(2,1)S(1)} custom-call(bf16[1024,512]{1,0:T(8,128)(2,1)S(1)} %bitcast.12, bf16[1024,512]{1,0:T(8,128)(2,1)S(1)} %collective-permute-done.other, bf16[512,512]{1,0:T(8,128)(2,1)S(1)} %copy-done.3, bf16[512,512]{1,0:T(8,128)(2,1)S(1)} %copy-done.1), custom_call_target="tpu_custom_call" | custom-call | flops 600000000 | bytes 4000000 | tf_op jit(solution)/shard_map/project/pallas_call | solution.py:374
  4.1 0.0 collective-permute-done.1.other_tissue
  4.1 0.0 copy-done.5
  4.1 1.8 %band.2.after = bf16[80,512]{1,0:T(8,128)(2,1)S(1)} custom-call(bf16[2048,256]{1,0:T(8,128)(2,1)S(1)} %project.1.both.first, s32[8,128]{1,0:T(8,128)S(1)} %copy-done.9, s32[8,128]{1,0:T(8,128)S(1)} %collective-permute-done.1.other_tissue, bf16[256,512]{1,0:T(8,128)(2,1)S(1)} %copy-done.5), custom_call_target="tpu_custom_call" | custom-call | flops 600000000 | bytes 4000000 | tf_op jit(solution)/shard_map/band/pallas_call | solution.py:385
  6.0 0.0 copy-start.6
  6.0 0.0 copy-start.7
  6.0 0.0 copy-start.8
  6.0 4.5 %collective-permute-start.2 = (bf16[80,512]{1,0:T(8,128)(2,1)S(1)}, bf16[80,512]{1,0:T(8,128)(2,1)S(1)}, u32[]{:S(2)}, u32[]{:S(2)}) collective-permute-start(bf16[80,512]{1,0:T(8,128)(2,1)S(1)} %band.2.after), channel_id=1, source_target_pairs={{0,4},{1,5},{2,6},{3,7},{4,0},{5,1},{6,2},{7,3},{8,12},{9,13},{10,... | collective-permute-start | bytes 245768 | tf_op jit(solution)/shard_map/ppermute | solution.py:339
  10.4 1.1 %project_second.1 = (bf16[2048,256]{1,0:T(8,128)(2,1)S(1)}, bf16[1024,512]{1,0:T(8,128)(2,1)S(1)}) custom-call(bf16[1024,512]{1,0:T(8,128)(2,1)S(1)} %bitcast.13, bf16[1024,512]{1,0:T(8,128)(2,1)S(1)} %collective-permute-done.other, bf16[512,512]{1,0:T(8,128)(2,1)S(1)} %copy-done.3, bf16[512,512]{1,0:T(8,128)(2,1)S(1)} %copy-done.1, ...), custom_call_target="tpu_custom_call" | custom-call | flops 800000000 | bytes 4000000 | tf_op jit(solution)/shard_map/project_second/pallas_call | solution.py:439
  11.6 0.0 copy-done.6
  11.6 0.0 copy-done.7
  11.6 0.0 copy-done.8
  11.6 0.0 copy-start.4
  11.6 0.1 taps.1.before.all_taps
  11.7 1.9 %band.3.held = f32[72,512]{1,0:T(8,128)S(1)} custom-call(bf16[2048,256]{1,0:T(8,128)(2,1)S(1)} %get-tuple-element.13.both, s32[8,128]{1,0:T(8,128)S(1)} %copy-done.9, s32[8,128]{1,0:T(8,128)S(1)} %collective-permute-done.1.other_tissue, bf16[256,512]{1,0:T(8,128)(2,1)S(1)} %copy-done.5), custom_call_target="tpu_custom_call" | custom-call | flops 600000000 | bytes 4000000 | tf_op jit(solution)/shard_map/band/pallas_call | solution.py:385
  13.7 1.6 %collective-permute-done.2.got = bf16[80,512]{1,0:T(8,128)(2,1)S(1)} collective-permute-done((bf16[80,512]{1,0:T(8,128)(2,1)S(1)}, bf16[80,512]{1,0:T(8,128)(2,1)S(1)}, u32[]{:S(2)}, u32[]{:S(2)}) %collective-permute-start.2) | collective-permute-done | bytes 81952 | tf_op jit(solution)/shard_map/ppermute | solution.py:339
  15.2 0.1 merge_next.2
  15.3 2.7 %collective-permute-start.4 = (bf16[80,512]{1,0:T(8,128)(2,1)S(1)}, bf16[80,512]{1,0:T(8,128)(2,1)S(1)}, u32[]{:S(2)}, u32[]{:S(2)}) collective-permute-start(bf16[80,512]{1,0:T(8,128)(2,1)S(1)} %get-tuple-element.14.after), channel_id=1, source_target_pairs={{0,8},{1,9},{2,10},{3,11},{4,12},{5,13},{6,14},{7,15},{8,0},{9,1},... | collective-permute-start | bytes 245768 | tf_op jit(solution)/shard_map/ppermute | solution.py:339
  17.9 1.9 %token_.2.after.weights_low = bf16[1024,1024]{1,0:T(8,128)(2,1)S(1)} custom-call(bf16[1024,512]{1,0:T(8,128)(2,1)S(1)} %bitcast.14, bf16[512,512]{1,0:T(8,128)(2,1)S(1)} %copy-done.4, bf16[256,512]{1,0:T(8,128)(2,1)S(1)} %copy-done.5, bf16[80,512]{1,0:T(8,128)(2,1)S(1)} %get-tuple-element.14.after), custom_call_target="tpu_custom_call" | custom-call | flops 2000000000 | bytes 6000000 | tf_op jit(solution)/shard_map/token/pallas_call | solution.py:399
  19.9 0.0 collective-permute-done.3.outer
  19.9 0.6 %halo.1 = (bf16[384,512]{1,0:T(8,128)(2,1)S(1)}, bf16[384,512]{1,0:T(8,128)(2,1)S(1)}) custom-call(bf16[1024,512]{1,0:T(8,128)(2,1)S(1)} %collective-permute-done.other, bf16[384,512]{1,0:T(8,128)(2,1)S(1)} %collective-permute-done.3.outer, bf16[512,512]{1,0:T(8,128)(2,1)S(1)} %copy-done.1, bf16[1024,1024]{1,0:T(8,128)(2,1)S(1)} %token_.2.after.weights_low), custom_call_target="tpu_custom_call" | custom-call | flops 400000000 | bytes 2000000 | tf_op jit(solution)/shard_map/halo/pallas_call | solution.py:465
  20.5 2.0 %token_.3.before.weights_high = bf16[1024,1024]{1,0:T(8,128)(2,1)S(1)} custom-call(bf16[1024,512]{1,0:T(8,128)(2,1)S(1)} %bitcast.15, bf16[512,512]{1,0:T(8,128)(2,1)S(1)} %copy-done.4, bf16[256,512]{1,0:T(8,128)(2,1)S(1)} %copy-done.5, bf16[384,512]{1,0:T(8,128)(2,1)S(1)} %get-tuple-element.15.after.above), custom_call_target="tpu_custom_call" | custom-call | flops 2000000000 | bytes 6000000 | tf_op jit(solution)/shard_map/token/pallas_call | solution.py:399
  22.4 0.0 collective-permute-done.4.got
  22.5 0.1 merge_next.3
  22.5 0.1 collective-permute-start.5
  22.6 2.3 %conv.2 = f32[8,128,256]{2,1,0:T(8,128)S(1)} custom-call(bf16[1024,512]{1,0:T(8,128)(2,1)S(1)} %get-tuple-element.19.values, bf16[384,512]{1,0:T(8,128)(2,1)S(1)} %get-tuple-element.15.after.above, bf16[384,512]{1,0:T(8,128)(2,1)S(1)} %get-tuple-element.20.below, f32[7,24,512]{2,1,0:T(8,128)S(1)} %taps.1.before.all_taps, ...), custom_call_target="tpu_custom_call" | custom-call | flops 3000000000 | bytes 4000000 | tf_op jit(solution)/shard_map/conv/pallas_call | solution.py:417
  24.9 2.1 %collective-permute-done.5.got = bf16[80,512]{1,0:T(8,128)(2,1)S(1)} collective-permute-done((bf16[80,512]{1,0:T(8,128)(2,1)S(1)}, bf16[80,512]{1,0:T(8,128)(2,1)S(1)}, u32[]{:S(2)}, u32[]{:S(2)}) %collective-permute-start.5) | collective-permute-done | bytes 81952 | tf_op jit(solution)/shard_map/ppermute | solution.py:339
  27.1 0.0 copy-start.2
  27.1 0.3 collective-permute-start.6
  27.3 2.5 %conv.3 = f32[8,128,256]{2,1,0:T(8,128)S(1)} custom-call(bf16[1024,512]{1,0:T(8,128)(2,1)S(1)} %get-tuple-element.19.values, bf16[384,512]{1,0:T(8,128)(2,1)S(1)} %get-tuple-element.15.after.above, bf16[384,512]{1,0:T(8,128)(2,1)S(1)} %get-tuple-element.20.below, f32[7,24,512]{2,1,0:T(8,128)S(1)} %taps.1.before.all_taps, bf16[64,512]{1,0:T(8,128)(2,1)S(1)} %merge_last.1.after.own), custom_call_target="tpu_custom_call" | custom-call | flops 3000000000 | bytes 4000000 | tf_op jit(solution)/shard_map/conv/pallas_call | solution.py:417
  29.8 1.6 %collective-permute-done.6.near = bf16[64,512]{1,0:T(8,128)(2,1)S(1)} collective-permute-done((bf16[64,512]{1,0:T(8,128)(2,1)S(1)}, bf16[64,512]{1,0:T(8,128)(2,1)S(1)}, u32[]{:S(2)}, u32[]{:S(2)}) %collective-permute-start.6) | collective-permute-done | bytes 65568 | tf_op jit(solution)/shard_map/ppermute | solution.py:339
  31.4 0.1 collective-permute-start.7
  31.5 1.0 %own_out.1.partial = f32[1024,512]{1,0:T(8,128)S(1)} custom-call(bf16[1024,1024]{1,0:T(8,128)(2,1)S(1)} %token_.2.after.weights_low, bf16[1024,1024]{1,0:T(8,128)(2,1)S(1)} %token_.3.before.weights_high, bf16[128,512]{1,0:T(8,128)(2,1)S(1)} %relay.1.pair, f32[1024,256]{1,0:T(8,128)S(1)} %bitcast.8, f32[1024,256]{1,0:T(8,128)S(1)} %bitcast.5, ...), custom_call_target="tpu_custom_call" | custom-call | flops 1100000000 | bytes 4000000 | tf_op jit(solution)/shard_map/own_out/pallas_call | solution.py:495
  32.5 0.3 collective-permute-done.7.pair
  32.8 2.0 %out.1 = bf16[1024,512]{1,0:T(8,128)(2,1)} custom-call(bf16[1024,1024]{1,0:T(8,128)(2,1)S(1)} %token_.2.after.weights_low, bf16[1024,1024]{1,0:T(8,128)(2,1)S(1)} %token_.3.before.weights_high, bf16[128,512]{1,0:T(8,128)(2,1)S(1)} %collective-permute-done.7.pair, f32[1024,256]{1,0:T(8,128)S(1)} %bitcast.9, f32[1024,256]{1,0:T(8,128)S(1)} %bitcast.6, ...), custom_call_target="tpu_custom_call" | custom-call | flops 1100000000 | bytes 8000000 | tf_op jit(solution)/shard_map/out/pallas_call | solution.py:505
  (6 shorter events, 0.1 us)
Async XLA Ops:
  0.0 4.1 %collective-permute-start.1 = (s32[8,128]{1,0:T(8,128)}, s32[8,128]{1,0:T(8,128)S(1)}, u32[]{:S(2)}, u32[]{:S(2)}) collective-permute-start(s32[8,128]{1,0:T(8,128)} %tissue.3), channel_id=1, source_target_pairs={{0,1},{1,0},{2,3},{3,2},{4,5},{5,4},{6,7},{7,6},{8,9},{9,8},{10,11... | collective-permute-start | bytes 12296 | tf_op jit(solution)/shard_map/ppermute | solution.py:339
  0.5 2.9 %collective-permute-start = (bf16[1024,512]{1,0:T(8,128)(2,1)}, bf16[1024,512]{1,0:T(8,128)(2,1)S(1)}, u32[]{:S(2)}, u32[]{:S(2)}) collective-permute-start(bf16[1024,512]{1,0:T(8,128)(2,1)} %bitcast.10), channel_id=1, source_target_pairs={{0,1},{1,0},{2,3},{3,2},{4,5},{5,4},{6,7},{7,6},{8,9},{9,8},{10,11... | collective-permute-start | bytes 3145736 | tf_op jit(solution)/shard_map/ppermute | solution.py:339
  1.5 1.8 %copy-start = (bf16[8,128,512]{2,1,0:T(8,128)(2,1)S(1)}, bf16[8,128,512]{2,1,0:T(8,128)(2,1)}, u32[]{:S(2)}) copy-start(bf16[8,128,512]{2,1,0:T(8,128)(2,1)} %param.10) | copy-start | bytes 3145732
  1.5 1.8 %copy-start.1 = (bf16[512,512]{1,0:T(8,128)(2,1)S(1)}, bf16[512,512]{1,0:T(8,128)(2,1)}, u32[]{:S(2)}) copy-start(bf16[512,512]{1,0:T(8,128)(2,1)} %w_value.5) | copy-start | bytes 1572868
  1.6 1.8 %copy-start.3 = (bf16[512,512]{1,0:T(8,128)(2,1)S(1)}, bf16[512,512]{1,0:T(8,128)(2,1)}, u32[]{:S(2)}) copy-start(bf16[512,512]{1,0:T(8,128)(2,1)} %w_key.3) | copy-start | bytes 1572868
  1.6 2.5 %copy-start.5 = (bf16[256,512]{1,0:T(8,128)(2,1)S(1)}, bf16[256,512]{1,0:T(8,128)(2,1)}, u32[]{:S(2)}) copy-start(bf16[256,512]{1,0:T(8,128)(2,1)} %agents.7) | copy-start | bytes 786436
  1.6 2.5 %copy-start.9 = (s32[8,128]{1,0:T(8,128)S(1)}, s32[8,128]{1,0:T(8,128)}, u32[]{:S(2)}) copy-start(s32[8,128]{1,0:T(8,128)} %tissue.3) | copy-start | bytes 12292
  1.6 18.3 %collective-permute-start.3 = (bf16[384,512]{1,0:T(8,128)(2,1)S(1)}, bf16[384,512]{1,0:T(8,128)(2,1)S(1)}, u32[]{:S(2)}, u32[]{:S(2)}) collective-permute-start(bf16[384,512]{1,0:T(8,128)(2,1)S(1)} %pass.1), channel_id=1, source_target_pairs={{1,2},{3,4},{5,6},{7,8},{9,10},{11,12},{13,14},{2,1},{4,3},{6,5},{... | collective-permute-start | bytes 1179656 | tf_op jit(solution)/shard_map/ppermute | solution.py:370
  6.0 5.6 %copy-start.6 = (f32[7,7,512]{2,1,0:T(8,128)S(1)}, f32[7,7,512]{2,1,0:T(8,128)}, u32[]{:S(2)}) copy-start(f32[7,7,512]{2,1,0:T(8,128)} %seven.1) | copy-start | bytes 301060
  6.0 5.6 %copy-start.7 = (f32[5,5,512]{2,1,0:T(8,128)S(1)}, f32[5,5,512]{2,1,0:T(8,128)}, u32[]{:S(2)}) copy-start(f32[5,5,512]{2,1,0:T(8,128)} %five.1) | copy-start | bytes 153604
  6.0 5.6 %copy-start.8 = (f32[3,3,512]{2,1,0:T(4,128)S(1)}, f32[3,3,512]{2,1,0:T(4,128)}, u32[]{:S(2)}) copy-start(f32[3,3,512]{2,1,0:T(4,128)} %three.1) | copy-start | bytes 55300
  6.0 9.2 %collective-permute-start.2 = (bf16[80,512]{1,0:T(8,128)(2,1)S(1)}, bf16[80,512]{1,0:T(8,128)(2,1)S(1)}, u32[]{:S(2)}, u32[]{:S(2)}) collective-permute-start(bf16[80,512]{1,0:T(8,128)(2,1)S(1)} %band.2.after), channel_id=1, source_target_pairs={{0,4},{1,5},{2,6},{3,7},{4,0},{5,1},{6,2},{7,3},{8,12},{9,13},{10,... | collective-permute-start | bytes 245768 | tf_op jit(solution)/shard_map/ppermute | solution.py:339
  11.6 6.4 %copy-start.4 = (bf16[512,512]{1,0:T(8,128)(2,1)S(1)}, bf16[512,512]{1,0:T(8,128)(2,1)}, u32[]{:S(2)}) copy-start(bf16[512,512]{1,0:T(8,128)(2,1)} %w_query.3) | copy-start | bytes 1572868
  15.3 7.2 %collective-permute-start.4 = (bf16[80,512]{1,0:T(8,128)(2,1)S(1)}, bf16[80,512]{1,0:T(8,128)(2,1)S(1)}, u32[]{:S(2)}, u32[]{:S(2)}) collective-permute-start(bf16[80,512]{1,0:T(8,128)(2,1)S(1)} %get-tuple-element.14.after), channel_id=1, source_target_pairs={{0,8},{1,9},{2,10},{3,11},{4,12},{5,13},{6,14},{7,15},{8,0},{9,1},... | collective-permute-start | bytes 245768 | tf_op jit(solution)/shard_map/ppermute | solution.py:339
  22.5 4.5 %collective-permute-start.5 = (bf16[80,512]{1,0:T(8,128)(2,1)S(1)}, bf16[80,512]{1,0:T(8,128)(2,1)S(1)}, u32[]{:S(2)}, u32[]{:S(2)}) collective-permute-start(bf16[80,512]{1,0:T(8,128)(2,1)S(1)} %get-tuple-element.18.after), channel_id=1, source_target_pairs={{0,2},{1,3},{2,0},{3,1},{4,6},{5,7},{6,4},{7,5},{8,10},{9,11},{10,... | collective-permute-start | bytes 245768 | tf_op jit(solution)/shard_map/ppermute | solution.py:339
  27.1 4.4 %copy-start.2 = (bf16[512,512]{1,0:T(8,128)(2,1)S(1)}, bf16[512,512]{1,0:T(8,128)(2,1)}, u32[]{:S(2)}) copy-start(bf16[512,512]{1,0:T(8,128)(2,1)} %w_out.3) | copy-start | bytes 1572868
  27.1 4.3 %collective-permute-start.6 = (bf16[64,512]{1,0:T(8,128)(2,1)S(1)}, bf16[64,512]{1,0:T(8,128)(2,1)S(1)}, u32[]{:S(2)}, u32[]{:S(2)}) collective-permute-start(bf16[64,512]{1,0:T(8,128)(2,1)S(1)} %merge_last.1.after.own), channel_id=1, source_target_pairs={{0,4},{1,5},{2,6},{3,7},{4,0},{5,1},{6,2},{7,3},{8,12},{9,13},{10,... | collective-permute-start | bytes 196616 | tf_op jit(solution)/shard_map/ppermute | solution.py:339
  31.4 1.4 %collective-permute-start.7 = (bf16[128,512]{1,0:T(8,128)(2,1)S(1)}, bf16[128,512]{1,0:T(8,128)(2,1)S(1)}, u32[]{:S(2)}, u32[]{:S(2)}) collective-permute-start(bf16[128,512]{1,0:T(8,128)(2,1)S(1)} %relay.1.pair), channel_id=1, source_target_pairs={{0,1},{1,0},{2,3},{3,2},{4,5},{5,4},{6,7},{7,6},{8,9},{9,8},{10,11... | collective-permute-start | bytes 393224 | tf_op jit(solution)/shard_map/ppermute | solution.py:339

commit v9 on v8

--- a/solution.py
+++ b/solution.py
@@ -127,19 +127,18 @@
 
 def put_narrow(ref, state):
     peak, total, weighted = state
-    row_id = lax.broadcasted_iota(jnp.int32, (16, weighted.shape[1]), 0)
-    stats = jnp.zeros((16, weighted.shape[1]), F32)
+    row_id = lax.broadcasted_iota(jnp.int32, (8, weighted.shape[1]), 0)
+    stats = jnp.zeros((8, weighted.shape[1]), F32)
     for at, part in enumerate(thirds(peak) + thirds(total)):
         stats = jnp.where(row_id == at, part, stats)
-    ref[0:64] = weighted.astype(BF16)
-    ref[64:80] = stats.astype(BF16)
+    ref[...] = jnp.concatenate([weighted, stats], axis=0).astype(BF16)
 
 
 def narrow(ref):
-    stats = ref[64:80].astype(F32)
-    peak = stats[0:1] + stats[1:2] + stats[2:3]
-    total = stats[3:4] + stats[4:5] + stats[5:6]
-    return peak, total, ref[0:64].astype(F32)
+    rows = ref[...].astype(F32)
+    peak = rows[64:65] + rows[65:66] + rows[66:67]
+    total = rows[67:68] + rows[68:69] + rows[69:70]
+    return peak, total, rows[0:64]
 
 
 def next_merge_kernel(held, got, before, own, payload):
@@ -304,21 +303,22 @@
     weights_low, weights_high, pair, position_low, position_high, w_out, partial, mixed, spread, buffer, sems
 ):
     fill_spread(pair, spread)
-    block = partial.shape[0] // 2
+    block = partial.shape[0] // sems.shape[0]
     copies = []
-    for index in range(2):
+    for index in range(sems.shape[0]):
         here = slice(index * block, index * block + block)
-        for group, (weights, position) in enumerate(((weights_low, position_low), (weights_high, position_high))):
-
-            @pl.when(chunk_of_device() // 2 != group)
-            def _(group=group, weights=weights, position=position, here=here):
-                rows = slice(group * 256, group * 256 + 256)
+        copies.append((here, pltpu.make_async_copy(buffer.at[here, :], mixed.at[here, :], sems.at[index])))
+    for group, (weights, position) in enumerate(((weights_low, position_low), (weights_high, position_high))):
+
+        @pl.when(chunk_of_device() // 2 != group)
+        def _(group=group, weights=weights, position=position):
+            rows = slice(group * 256, group * 256 + 256)
+            for here, copy in copies:
                 total = partial[here, :] + blend_block(here, weights, position, spread, w_out, rows)
                 buffer[here, :] = total.astype(BF16)
-
-        copies.append(pltpu.make_async_copy(buffer.at[here, :], mixed.at[here, :], sems.at[index]))
-        copies[-1].start()
-    for copy in copies:
+                copy.start()
+
+    for _, copy in copies:
         copy.wait()
 
 
@@ -369,7 +369,7 @@
     rest = [(i, i + 1) for i in range(1, peers - 1, 2)]
     outer = lax.ppermute(border, "col", rest + [(j, i) for i, j in rest])
 
-    wide_shape, narrow_shape = shape((72, 512), F32), shape((80, 512), BF16)
+    wide_shape, narrow_shape = shape((72, 512), F32), shape((72, 512), BF16)
     both_bands = shape((2 * tokens, half_dim), BF16)
     first = pl.pallas_call(
         project_kernel,

time: 35.1 us -> 34.7 us (0.989)
  no operation moved by 1% of the time
where the time goes in v9:
time: 34.7 us; the launch traced here: 34.6 us
  Pallas kernels  18 us (52%)
  starting transfers between devices  8.83 us (25%)
  waiting for transfers between devices  6.22 us (18%)
  local copies, waits for them, and re-layouts  1.08 us (3%)
  between operations  0.45 us (1%)
    ppermute x7, starting transfers between devices, exchange(): return lax.ppermute(x, 'col', [(i, i ^ bit) for i in range(peers)])  8.01 us
    ppermute x7, waiting for transfers between devices, exchange(): return lax.ppermute(x, 'col', [(i, i ^ bit) for i in range(peers)])  6.22 us
    pallas_call x2, Pallas kernels, conv(): pl.pallas_call(functools.partial(conv_kernel, at * half_dim), out_shape=s...  4.78 us
    pallas_call x2, Pallas kernels, token(): pl.pallas_call(functools.partial(token_kernel, scale), out_shape=shape((t...  3.9 us
    pallas_call x2, Pallas kernels, band(): pl.pallas_call(functools.partial(kernel, scale), out_shape=out_shape, in_...  3.76 us
    pallas_call x1, Pallas kernels, on_device(): pl.pallas_call(out_kernel, out_shape=shape((tokens, dim), BF16), in_specs...  1.82 us
    pallas_call x1, Pallas kernels, on_device(): pl.pallas_call(second_project_kernel, out_shape=(both_bands, shape((token...  1.1 us
    dynamic_slice x1, local copies, waits for them, and re-layouts, on_device(): lax.dynamic_slice_in_dim(flat, odd * (tokens - 3 * width), 3 * width, 0)  1.02 us
  transfers between devices with their start and end apart: 8, of which 5 were waited for; matrix products, arithmetic and copies ran while one was open for 3% of the time, Pallas kernels for 46%

profile of v9, /device:TPU:0, one launch (start us, length us, event | category | flops | bytes accessed | tf_op | source)
XLA Modules:
  0.0 34.6 jit_solution(16088099216401667943)
XLA Ops:
  0.0 0.5 %collective-permute-start.1 = (s32[8,128]{1,0:T(8,128)}, s32[8,128]{1,0:T(8,128)S(1)}, u32[]{:S(2)}, u32[]{:S(2)}) collective-permute-start(s32[8,128]{1,0:T(8,128)} %tissue.3), channel_id=1, source_target_pairs={{0,1},{1,0},{2,3},{3,2},{4,5},{5,4},{6,7},{7,6},{8,9},{9,8},{10,11... | collective-permute-start | bytes 12296 | tf_op jit(solution)/shard_map/ppermute | solution.py:339
  0.5 0.1 collective-permute-start
  0.5 1.0 %constant_dynamic-slice_fusion.border = bf16[384,512]{1,0:T(8,128)(2,1)S(1)} fusion(bf16[1024,512]{1,0:T(8,128)(2,1)} %bitcast.11, s32[]{:T(128)S(6)} %select_n.11), kind=kLoop, calls=%fused_computation | loop fusion | bytes 786436 | tf_op jit(solution)/shard_map/dynamic_slice | solution.py:358
  1.5 0.0 copy-start
  1.5 0.0 copy-start.1
  1.6 0.0 copy-start.3
  1.6 0.0 copy-start.5
  1.6 0.0 copy-start.9
  1.6 0.8 %collective-permute-start.3 = (bf16[384,512]{1,0:T(8,128)(2,1)S(1)}, bf16[384,512]{1,0:T(8,128)(2,1)S(1)}, u32[]{:S(2)}, u32[]{:S(2)}) collective-permute-start(bf16[384,512]{1,0:T(8,128)(2,1)S(1)} %pass.1), channel_id=1, source_target_pairs={{1,2},{3,4},{5,6},{7,8},{9,10},{11,12},{13,14},{2,1},{4,3},{6,5},{... | collective-permute-start | bytes 1179656 | tf_op jit(solution)/shard_map/ppermute | solution.py:370
  2.4 0.9 %collective-permute-done.other = bf16[1024,512]{1,0:T(8,128)(2,1)S(1)} collective-permute-done((bf16[1024,512]{1,0:T(8,128)(2,1)}, bf16[1024,512]{1,0:T(8,128)(2,1)S(1)}, u32[]{:S(2)}, u32[]{:S(2)}) %collective-permute-start) | collective-permute-done | bytes 1048608 | tf_op jit(solution)/shard_map/ppermute | solution.py:339
  3.3 0.0 copy-done
  3.3 0.0 copy-done.1
  3.3 0.0 copy-done.3
  3.3 0.7 %project.1.both.first = bf16[2048,256]{1,0:T(8,128)(2,1)S(1)} custom-call(bf16[1024,512]{1,0:T(8,128)(2,1)S(1)} %bitcast.12, bf16[1024,512]{1,0:T(8,128)(2,1)S(1)} %collective-permute-done.other, bf16[512,512]{1,0:T(8,128)(2,1)S(1)} %copy-done.3, bf16[512,512]{1,0:T(8,128)(2,1)S(1)} %copy-done.1), custom_call_target="tpu_custom_call" | custom-call | flops 600000000 | bytes 4000000 | tf_op jit(solution)/shard_map/project/pallas_call | solution.py:374
  4.1 0.0 collective-permute-done.1.other_tissue
  4.1 0.0 copy-done.5
  4.1 0.0 copy-done.9
  4.1 1.8 %band.2.after = bf16[72,512]{1,0:T(8,128)(2,1)S(1)} custom-call(bf16[2048,256]{1,0:T(8,128)(2,1)S(1)} %project.1.both.first, s32[8,128]{1,0:T(8,128)S(1)} %copy-done.9, s32[8,128]{1,0:T(8,128)S(1)} %collective-permute-done.1.other_tissue, bf16[256,512]{1,0:T(8,128)(2,1)S(1)} %copy-done.5), custom_call_target="tpu_custom_call" | custom-call | flops 600000000 | bytes 4000000 | tf_op jit(solution)/shard_map/band/pallas_call | solution.py:385
  6.0 0.0 copy-start.6
  6.0 0.0 copy-start.7
  6.0 0.0 copy-start.8
  6.0 4.5 %collective-permute-start.2 = (bf16[72,512]{1,0:T(8,128)(2,1)S(1)}, bf16[72,512]{1,0:T(8,128)(2,1)S(1)}, u32[]{:S(2)}, u32[]{:S(2)}) collective-permute-start(bf16[72,512]{1,0:T(8,128)(2,1)S(1)} %band.2.after), channel_id=1, source_target_pairs={{0,4},{1,5},{2,6},{3,7},{4,0},{5,1},{6,2},{7,3},{8,12},{9,13},{10,... | collective-permute-start | bytes 221192 | tf_op jit(solution)/shard_map/ppermute | solution.py:339
  10.4 1.1 %project_second.1 = (bf16[2048,256]{1,0:T(8,128)(2,1)S(1)}, bf16[1024,512]{1,0:T(8,128)(2,1)S(1)}) custom-call(bf16[1024,512]{1,0:T(8,128)(2,1)S(1)} %bitcast.13, bf16[1024,512]{1,0:T(8,128)(2,1)S(1)} %collective-permute-done.other, bf16[512,512]{1,0:T(8,128)(2,1)S(1)} %copy-done.3, bf16[512,512]{1,0:T(8,128)(2,1)S(1)} %copy-done.1, ...), custom_call_target="tpu_custom_call" | custom-call | flops 800000000 | bytes 4000000 | tf_op jit(solution)/shard_map/project_second/pallas_call | solution.py:439
  11.6 0.0 copy-done.6
  11.6 0.0 copy-done.7
  11.6 0.0 copy-start.4
  11.6 0.1 taps.1.before.all_taps
  11.7 1.9 %band.3.held = f32[72,512]{1,0:T(8,128)S(1)} custom-call(bf16[2048,256]{1,0:T(8,128)(2,1)S(1)} %get-tuple-element.13.both, s32[8,128]{1,0:T(8,128)S(1)} %copy-done.9, s32[8,128]{1,0:T(8,128)S(1)} %collective-permute-done.1.other_tissue, bf16[256,512]{1,0:T(8,128)(2,1)S(1)} %copy-done.5), custom_call_target="tpu_custom_call" | custom-call | flops 600000000 | bytes 4000000 | tf_op jit(solution)/shard_map/band/pallas_call | solution.py:385
  13.7 1.4 %collective-permute-done.2.got = bf16[72,512]{1,0:T(8,128)(2,1)S(1)} collective-permute-done((bf16[72,512]{1,0:T(8,128)(2,1)S(1)}, bf16[72,512]{1,0:T(8,128)(2,1)S(1)}, u32[]{:S(2)}, u32[]{:S(2)}) %collective-permute-start.2) | collective-permute-done | bytes 73760 | tf_op jit(solution)/shard_map/ppermute | solution.py:339
  15.0 0.1 merge_next.2
  15.1 2.7 %collective-permute-start.4 = (bf16[72,512]{1,0:T(8,128)(2,1)S(1)}, bf16[72,512]{1,0:T(8,128)(2,1)S(1)}, u32[]{:S(2)}, u32[]{:S(2)}) collective-permute-start(bf16[72,512]{1,0:T(8,128)(2,1)S(1)} %get-tuple-element.14.after), channel_id=1, source_target_pairs={{0,8},{1,9},{2,10},{3,11},{4,12},{5,13},{6,14},{7,15},{8,0},{9,1},... | collective-permute-start | bytes 221192 | tf_op jit(solution)/shard_map/ppermute | solution.py:339
  17.8 1.9 %token_.2.after.weights_low = bf16[1024,1024]{1,0:T(8,128)(2,1)S(1)} custom-call(bf16[1024,512]{1,0:T(8,128)(2,1)S(1)} %bitcast.14, bf16[512,512]{1,0:T(8,128)(2,1)S(1)} %copy-done.4, bf16[256,512]{1,0:T(8,128)(2,1)S(1)} %copy-done.5, bf16[72,512]{1,0:T(8,128)(2,1)S(1)} %get-tuple-element.14.after), custom_call_target="tpu_custom_call" | custom-call | flops 2000000000 | bytes 6000000 | tf_op jit(solution)/shard_map/token/pallas_call | solution.py:399
  19.7 0.0 collective-permute-done.3.outer
  19.7 0.6 %halo.1 = (bf16[384,512]{1,0:T(8,128)(2,1)S(1)}, bf16[384,512]{1,0:T(8,128)(2,1)S(1)}) custom-call(bf16[1024,512]{1,0:T(8,128)(2,1)S(1)} %collective-permute-done.other, bf16[384,512]{1,0:T(8,128)(2,1)S(1)} %collective-permute-done.3.outer, bf16[512,512]{1,0:T(8,128)(2,1)S(1)} %copy-done.1, bf16[1024,1024]{1,0:T(8,128)(2,1)S(1)} %token_.2.after.weights_low), custom_call_target="tpu_custom_call" | custom-call | flops 400000000 | bytes 2000000 | tf_op jit(solution)/shard_map/halo/pallas_call | solution.py:465
  20.3 2.0 %token_.3.before.weights_high = bf16[1024,1024]{1,0:T(8,128)(2,1)S(1)} custom-call(bf16[1024,512]{1,0:T(8,128)(2,1)S(1)} %bitcast.15, bf16[512,512]{1,0:T(8,128)(2,1)S(1)} %copy-done.4, bf16[256,512]{1,0:T(8,128)(2,1)S(1)} %copy-done.5, bf16[384,512]{1,0:T(8,128)(2,1)S(1)} %get-tuple-element.15.after.above), custom_call_target="tpu_custom_call" | custom-call | flops 2000000000 | bytes 6000000 | tf_op jit(solution)/shard_map/token/pallas_call | solution.py:399
  22.3 0.0 collective-permute-done.4.got
  22.3 0.1 merge_next.3
  22.3 0.1 collective-permute-start.5
  22.4 2.3 %conv.2 = f32[8,128,256]{2,1,0:T(8,128)S(1)} custom-call(bf16[1024,512]{1,0:T(8,128)(2,1)S(1)} %get-tuple-element.19.values, bf16[384,512]{1,0:T(8,128)(2,1)S(1)} %get-tuple-element.15.after.above, bf16[384,512]{1,0:T(8,128)(2,1)S(1)} %get-tuple-element.20.below, f32[7,24,512]{2,1,0:T(8,128)S(1)} %taps.1.before.all_taps, ...), custom_call_target="tpu_custom_call" | custom-call | flops 3000000000 | bytes 4000000 | tf_op jit(solution)/shard_map/conv/pallas_call | solution.py:417
  24.7 2.0 %collective-permute-done.5.got = bf16[72,512]{1,0:T(8,128)(2,1)S(1)} collective-permute-done((bf16[72,512]{1,0:T(8,128)(2,1)S(1)}, bf16[72,512]{1,0:T(8,128)(2,1)S(1)}, u32[]{:S(2)}, u32[]{:S(2)}) %collective-permute-start.5) | collective-permute-done | bytes 73760 | tf_op jit(solution)/shard_map/ppermute | solution.py:339
  26.8 0.0 copy-start.2
  26.8 0.3 collective-permute-start.6
  27.1 2.5 %conv.3 = f32[8,128,256]{2,1,0:T(8,128)S(1)} custom-call(bf16[1024,512]{1,0:T(8,128)(2,1)S(1)} %get-tuple-element.19.values, bf16[384,512]{1,0:T(8,128)(2,1)S(1)} %get-tuple-element.15.after.above, bf16[384,512]{1,0:T(8,128)(2,1)S(1)} %get-tuple-element.20.below, f32[7,24,512]{2,1,0:T(8,128)S(1)} %taps.1.before.all_taps, bf16[64,512]{1,0:T(8,128)(2,1)S(1)} %merge_last.1.after.own), custom_call_target="tpu_custom_call" | custom-call | flops 3000000000 | bytes 4000000 | tf_op jit(solution)/shard_map/conv/pallas_call | solution.py:417
  29.6 1.6 %collective-permute-done.6.near = bf16[64,512]{1,0:T(8,128)(2,1)S(1)} collective-permute-done((bf16[64,512]{1,0:T(8,128)(2,1)S(1)}, bf16[64,512]{1,0:T(8,128)(2,1)S(1)}, u32[]{:S(2)}, u32[]{:S(2)}) %collective-permute-start.6) | collective-permute-done | bytes 65568 | tf_op jit(solution)/shard_map/ppermute | solution.py:339
  31.2 0.1 collective-permute-start.7
  31.3 1.0 %own_out.1.partial = f32[1024,512]{1,0:T(8,128)S(1)} custom-call(bf16[1024,1024]{1,0:T(8,128)(2,1)S(1)} %token_.2.after.weights_low, bf16[1024,1024]{1,0:T(8,128)(2,1)S(1)} %token_.3.before.weights_high, bf16[128,512]{1,0:T(8,128)(2,1)S(1)} %relay.1.pair, f32[1024,256]{1,0:T(8,128)S(1)} %bitcast.8, f32[1024,256]{1,0:T(8,128)S(1)} %bitcast.5, ...), custom_call_target="tpu_custom_call" | custom-call | flops 1100000000 | bytes 4000000 | tf_op jit(solution)/shard_map/own_out/pallas_call | solution.py:495
  32.3 0.3 collective-permute-done.7.pair
  32.6 1.8 %out.1 = bf16[1024,512]{1,0:T(8,128)(2,1)} custom-call(bf16[1024,1024]{1,0:T(8,128)(2,1)S(1)} %token_.2.after.weights_low, bf16[1024,1024]{1,0:T(8,128)(2,1)S(1)} %token_.3.before.weights_high, bf16[128,512]{1,0:T(8,128)(2,1)S(1)} %collective-permute-done.7.pair, f32[1024,256]{1,0:T(8,128)S(1)} %bitcast.9, f32[1024,256]{1,0:T(8,128)S(1)} %bitcast.6, ...), custom_call_target="tpu_custom_call" | custom-call | flops 1100000000 | bytes 8000000 | tf_op jit(solution)/shard_map/out/pallas_call | solution.py:505
  (6 shorter events, 0.1 us)
Async XLA Ops:
  0.0 4.1 %collective-permute-start.1 = (s32[8,128]{1,0:T(8,128)}, s32[8,128]{1,0:T(8,128)S(1)}, u32[]{:S(2)}, u32[]{:S(2)}) collective-permute-start(s32[8,128]{1,0:T(8,128)} %tissue.3), channel_id=1, source_target_pairs={{0,1},{1,0},{2,3},{3,2},{4,5},{5,4},{6,7},{7,6},{8,9},{9,8},{10,11... | collective-permute-start | bytes 12296 | tf_op jit(solution)/shard_map/ppermute | solution.py:339
  0.5 2.9 %collective-permute-start = (bf16[1024,512]{1,0:T(8,128)(2,1)}, bf16[1024,512]{1,0:T(8,128)(2,1)S(1)}, u32[]{:S(2)}, u32[]{:S(2)}) collective-permute-start(bf16[1024,512]{1,0:T(8,128)(2,1)} %bitcast.10), channel_id=1, source_target_pairs={{0,1},{1,0},{2,3},{3,2},{4,5},{5,4},{6,7},{7,6},{8,9},{9,8},{10,11... | collective-permute-start | bytes 3145736 | tf_op jit(solution)/shard_map/ppermute | solution.py:339
  1.5 1.8 %copy-start = (bf16[8,128,512]{2,1,0:T(8,128)(2,1)S(1)}, bf16[8,128,512]{2,1,0:T(8,128)(2,1)}, u32[]{:S(2)}) copy-start(bf16[8,128,512]{2,1,0:T(8,128)(2,1)} %param.10) | copy-start | bytes 3145732
  1.5 1.8 %copy-start.1 = (bf16[512,512]{1,0:T(8,128)(2,1)S(1)}, bf16[512,512]{1,0:T(8,128)(2,1)}, u32[]{:S(2)}) copy-start(bf16[512,512]{1,0:T(8,128)(2,1)} %w_value.5) | copy-start | bytes 1572868
  1.6 1.8 %copy-start.3 = (bf16[512,512]{1,0:T(8,128)(2,1)S(1)}, bf16[512,512]{1,0:T(8,128)(2,1)}, u32[]{:S(2)}) copy-start(bf16[512,512]{1,0:T(8,128)(2,1)} %w_key.3) | copy-start | bytes 1572868
  1.6 2.5 %copy-start.5 = (bf16[256,512]{1,0:T(8,128)(2,1)S(1)}, bf16[256,512]{1,0:T(8,128)(2,1)}, u32[]{:S(2)}) copy-start(bf16[256,512]{1,0:T(8,128)(2,1)} %agents.7) | copy-start | bytes 786436
  1.6 2.5 %copy-start.9 = (s32[8,128]{1,0:T(8,128)S(1)}, s32[8,128]{1,0:T(8,128)}, u32[]{:S(2)}) copy-start(s32[8,128]{1,0:T(8,128)} %tissue.3) | copy-start | bytes 12292
  1.6 18.1 %collective-permute-start.3 = (bf16[384,512]{1,0:T(8,128)(2,1)S(1)}, bf16[384,512]{1,0:T(8,128)(2,1)S(1)}, u32[]{:S(2)}, u32[]{:S(2)}) collective-permute-start(bf16[384,512]{1,0:T(8,128)(2,1)S(1)} %pass.1), channel_id=1, source_target_pairs={{1,2},{3,4},{5,6},{7,8},{9,10},{11,12},{13,14},{2,1},{4,3},{6,5},{... | collective-permute-start | bytes 1179656 | tf_op jit(solution)/shard_map/ppermute | solution.py:370
  6.0 5.6 %copy-start.6 = (f32[7,7,512]{2,1,0:T(8,128)S(1)}, f32[7,7,512]{2,1,0:T(8,128)}, u32[]{:S(2)}) copy-start(f32[7,7,512]{2,1,0:T(8,128)} %seven.1) | copy-start | bytes 301060
  6.0 5.6 %copy-start.7 = (f32[5,5,512]{2,1,0:T(8,128)S(1)}, f32[5,5,512]{2,1,0:T(8,128)}, u32[]{:S(2)}) copy-start(f32[5,5,512]{2,1,0:T(8,128)} %five.1) | copy-start | bytes 153604
  6.0 5.6 %copy-start.8 = (f32[3,3,512]{2,1,0:T(4,128)S(1)}, f32[3,3,512]{2,1,0:T(4,128)}, u32[]{:S(2)}) copy-start(f32[3,3,512]{2,1,0:T(4,128)} %three.1) | copy-start | bytes 55300
  6.0 9.1 %collective-permute-start.2 = (bf16[72,512]{1,0:T(8,128)(2,1)S(1)}, bf16[72,512]{1,0:T(8,128)(2,1)S(1)}, u32[]{:S(2)}, u32[]{:S(2)}) collective-permute-start(bf16[72,512]{1,0:T(8,128)(2,1)S(1)} %band.2.after), channel_id=1, source_target_pairs={{0,4},{1,5},{2,6},{3,7},{4,0},{5,1},{6,2},{7,3},{8,12},{9,13},{10,... | collective-permute-start | bytes 221192 | tf_op jit(solution)/shard_map/ppermute | solution.py:339
  11.6 6.2 %copy-start.4 = (bf16[512,512]{1,0:T(8,128)(2,1)S(1)}, bf16[512,512]{1,0:T(8,128)(2,1)}, u32[]{:S(2)}) copy-start(bf16[512,512]{1,0:T(8,128)(2,1)} %w_query.3) | copy-start | bytes 1572868
  15.1 7.2 %collective-permute-start.4 = (bf16[72,512]{1,0:T(8,128)(2,1)S(1)}, bf16[72,512]{1,0:T(8,128)(2,1)S(1)}, u32[]{:S(2)}, u32[]{:S(2)}) collective-permute-start(bf16[72,512]{1,0:T(8,128)(2,1)S(1)} %get-tuple-element.14.after), channel_id=1, source_target_pairs={{0,8},{1,9},{2,10},{3,11},{4,12},{5,13},{6,14},{7,15},{8,0},{9,1},... | collective-permute-start | bytes 221192 | tf_op jit(solution)/shard_map/ppermute | solution.py:339
  22.3 4.4 %collective-permute-start.5 = (bf16[72,512]{1,0:T(8,128)(2,1)S(1)}, bf16[72,512]{1,0:T(8,128)(2,1)S(1)}, u32[]{:S(2)}, u32[]{:S(2)}) collective-permute-start(bf16[72,512]{1,0:T(8,128)(2,1)S(1)} %get-tuple-element.18.after), channel_id=1, source_target_pairs={{0,2},{1,3},{2,0},{3,1},{4,6},{5,7},{6,4},{7,5},{8,10},{9,11},{10,... | collective-permute-start | bytes 221192 | tf_op jit(solution)/shard_map/ppermute | solution.py:339
  26.8 4.4 %copy-start.2 = (bf16[512,512]{1,0:T(8,128)(2,1)S(1)}, bf16[512,512]{1,0:T(8,128)(2,1)}, u32[]{:S(2)}) copy-start(bf16[512,512]{1,0:T(8,128)(2,1)} %w_out.3) | copy-start | bytes 1572868
  26.8 4.3 %collective-permute-start.6 = (bf16[64,512]{1,0:T(8,128)(2,1)S(1)}, bf16[64,512]{1,0:T(8,128)(2,1)S(1)}, u32[]{:S(2)}, u32[]{:S(2)}) collective-permute-start(bf16[64,512]{1,0:T(8,128)(2,1)S(1)} %merge_last.1.after.own), channel_id=1, source_target_pairs={{0,4},{1,5},{2,6},{3,7},{4,0},{5,1},{6,2},{7,3},{8,12},{9,13},{10,... | collective-permute-start | bytes 196616 | tf_op jit(solution)/shard_map/ppermute | solution.py:339
  31.2 1.4 %collective-permute-start.7 = (bf16[128,512]{1,0:T(8,128)(2,1)S(1)}, bf16[128,512]{1,0:T(8,128)(2,1)S(1)}, u32[]{:S(2)}, u32[]{:S(2)}) collective-permute-start(bf16[128,512]{1,0:T(8,128)(2,1)S(1)} %relay.1.pair), channel_id=1, source_target_pairs={{0,1},{1,0},{2,3},{3,2},{4,5},{5,4},{6,7},{7,6},{8,9},{9,8},{10,11... | collective-permute-start | bytes 393224 | tf_op jit(solution)/shard_map/ppermute | solution.py:339

commit v10 on v9

--- a/solution.py
+++ b/solution.py
@@ -456,26 +456,26 @@
         name="taps",
     )(seven, five, three, payload)
     held, payload = next_merge(held, got, taps)
+    got = exchange(payload, 2)
+    weights_low = token(0, payload)
+    above, below = pl.pallas_call(
+        halo_kernel,
+        out_shape=(shape((3 * width, dim), BF16), shape((3 * width, dim), BF16)),
+        in_specs=[vmem] * 3 + [anywhere],
+        out_specs=[vmem] * 2,
+        compiler_params=params(16),
+        cost_estimate=cost(4e8, 2e6),
+        name="halo",
+    )(other, outer, w_value, weights_low)
+    held, payload = next_merge(held, got, above)
     bit = 8
-    weights_low = None
-    while bit < peers:
+    while bit * 2 < peers:
         got = exchange(payload, bit)
-        if weights_low is None:
-            weights_low = token(0, payload)
-            above, below = pl.pallas_call(
-                halo_kernel,
-                out_shape=(shape((3 * width, dim), BF16), shape((3 * width, dim), BF16)),
-                in_specs=[vmem] * 3 + [anywhere],
-                out_specs=[vmem] * 2,
-                compiler_params=params(16),
-                cost_estimate=cost(4e8, 2e6),
-                name="halo",
-            )(other, outer, w_value, weights_low)
-            weights_high = token(1, above)
-        held, payload = next_merge(held, got, weights_high)
+        held, payload = next_merge(held, got, payload)
         bit *= 2
-    got = exchange(payload, 2)
-    position_low = conv(0, payload)
+    got = exchange(payload, bit)
+    weights_high = token(1, payload)
+    position_low = conv(0, weights_high)
     own = pl.pallas_call(
         last_merge_kernel, out_shape=shape((64, 512), BF16), out_specs=vmem, name="merge_last", **hop
     )(held, got, position_low)

time: 34.7 us -> 34.5 us (level)
  transfers between devices with their start and end apart: 8 -> 8, of which waited for: 5 -> 5; matrix products, arithmetic and copies ran while one was open for 3% -> 3% of each run, Pallas kernels for 46% -> 47%
where the time goes in v10:
time: 34.5 us; the launch traced here: 34.3 us
  Pallas kernels  17.9 us (52%)
  starting transfers between devices  8.95 us (26%)
  waiting for transfers between devices  5.93 us (17%)
  local copies, waits for them, and re-layouts  1.08 us (3%)
  between operations  0.45 us (1%)
    ppermute x7, starting transfers between devices, exchange(): return lax.ppermute(x, 'col', [(i, i ^ bit) for i in range(peers)])  8.14 us
    ppermute x7, waiting for transfers between devices, exchange(): return lax.ppermute(x, 'col', [(i, i ^ bit) for i in range(peers)])  5.92 us
    pallas_call x2, Pallas kernels, conv(): pl.pallas_call(functools.partial(conv_kernel, at * half_dim), out_shape=s...  4.78 us
    pallas_call x2, Pallas kernels, token(): pl.pallas_call(functools.partial(token_kernel, scale), out_shape=shape((t...  3.9 us
    pallas_call x2, Pallas kernels, band(): pl.pallas_call(functools.partial(kernel, scale), out_shape=out_shape, in_...  3.68 us
    pallas_call x1, Pallas kernels, on_device(): pl.pallas_call(out_kernel, out_shape=shape((tokens, dim), BF16), in_specs...  1.82 us
    pallas_call x1, Pallas kernels, on_device(): pl.pallas_call(second_project_kernel, out_shape=(both_bands, shape((token...  1.1 us
    dynamic_slice x1, local copies, waits for them, and re-layouts, on_device(): lax.dynamic_slice_in_dim(flat, odd * (tokens - 3 * width), 3 * width, 0)  1.02 us
  transfers between devices with their start and end apart: 8, of which 5 were waited for; matrix products, arithmetic and copies ran while one was open for 3% of the time, Pallas kernels for 47%

profile of v10, /device:TPU:0, one launch (start us, length us, event | category | flops | bytes accessed | tf_op | source)
XLA Modules:
  0.0 34.3 jit_solution(11046347623861273918)
XLA Ops:
  0.0 0.5 %collective-permute-start.1 = (s32[8,128]{1,0:T(8,128)}, s32[8,128]{1,0:T(8,128)S(1)}, u32[]{:S(2)}, u32[]{:S(2)}) collective-permute-start(s32[8,128]{1,0:T(8,128)} %tissue.3), channel_id=1, source_target_pairs={{0,1},{1,0},{2,3},{3,2},{4,5},{5,4},{6,7},{7,6},{8,9},{9,8},{10,11... | collective-permute-start | bytes 12296 | tf_op jit(solution)/shard_map/ppermute | solution.py:339
  0.5 0.1 collective-permute-start
  0.5 1.0 %constant_dynamic-slice_fusion.border = bf16[384,512]{1,0:T(8,128)(2,1)S(1)} fusion(bf16[1024,512]{1,0:T(8,128)(2,1)} %bitcast.11, s32[]{:T(128)S(6)} %select_n.11), kind=kLoop, calls=%fused_computation | loop fusion | bytes 786436 | tf_op jit(solution)/shard_map/dynamic_slice | solution.py:358
  1.5 0.0 copy-start
  1.5 0.0 copy-start.1
  1.6 0.0 copy-start.3
  1.6 0.0 copy-start.5
  1.6 0.0 copy-start.9
  1.6 0.8 %collective-permute-start.4 = (bf16[384,512]{1,0:T(8,128)(2,1)S(1)}, bf16[384,512]{1,0:T(8,128)(2,1)S(1)}, u32[]{:S(2)}, u32[]{:S(2)}) collective-permute-start(bf16[384,512]{1,0:T(8,128)(2,1)S(1)} %pass.1), channel_id=1, source_target_pairs={{1,2},{3,4},{5,6},{7,8},{9,10},{11,12},{13,14},{2,1},{4,3},{6,5},{... | collective-permute-start | bytes 1179656 | tf_op jit(solution)/shard_map/ppermute | solution.py:370
  2.4 0.9 %collective-permute-done.other = bf16[1024,512]{1,0:T(8,128)(2,1)S(1)} collective-permute-done((bf16[1024,512]{1,0:T(8,128)(2,1)}, bf16[1024,512]{1,0:T(8,128)(2,1)S(1)}, u32[]{:S(2)}, u32[]{:S(2)}) %collective-permute-start) | collective-permute-done | bytes 1048608 | tf_op jit(solution)/shard_map/ppermute | solution.py:339
  3.3 0.0 copy-done
  3.3 0.0 copy-done.1
  3.3 0.0 copy-done.3
  3.3 0.7 %project.1.both.first = bf16[2048,256]{1,0:T(8,128)(2,1)S(1)} custom-call(bf16[1024,512]{1,0:T(8,128)(2,1)S(1)} %bitcast.12, bf16[1024,512]{1,0:T(8,128)(2,1)S(1)} %collective-permute-done.other, bf16[512,512]{1,0:T(8,128)(2,1)S(1)} %copy-done.3, bf16[512,512]{1,0:T(8,128)(2,1)S(1)} %copy-done.1), custom_call_target="tpu_custom_call" | custom-call | flops 600000000 | bytes 4000000 | tf_op jit(solution)/shard_map/project/pallas_call | solution.py:374
  4.1 0.0 collective-permute-done.1.other_tissue
  4.1 0.0 copy-done.5
  4.1 1.8 %band.2.after = bf16[72,512]{1,0:T(8,128)(2,1)S(1)} custom-call(bf16[2048,256]{1,0:T(8,128)(2,1)S(1)} %project.1.both.first, s32[8,128]{1,0:T(8,128)S(1)} %copy-done.9, s32[8,128]{1,0:T(8,128)S(1)} %collective-permute-done.1.other_tissue, bf16[256,512]{1,0:T(8,128)(2,1)S(1)} %copy-done.5), custom_call_target="tpu_custom_call" | custom-call | flops 600000000 | bytes 4000000 | tf_op jit(solution)/shard_map/band/pallas_call | solution.py:385
  6.0 0.0 copy-start.6
  6.0 0.0 copy-start.7
  6.0 0.0 copy-start.8
  6.0 4.5 %collective-permute-start.2 = (bf16[72,512]{1,0:T(8,128)(2,1)S(1)}, bf16[72,512]{1,0:T(8,128)(2,1)S(1)}, u32[]{:S(2)}, u32[]{:S(2)}) collective-permute-start(bf16[72,512]{1,0:T(8,128)(2,1)S(1)} %band.2.after), channel_id=1, source_target_pairs={{0,4},{1,5},{2,6},{3,7},{4,0},{5,1},{6,2},{7,3},{8,12},{9,13},{10,... | collective-permute-start | bytes 221192 | tf_op jit(solution)/shard_map/ppermute | solution.py:339
  10.4 1.1 %project_second.1 = (bf16[2048,256]{1,0:T(8,128)(2,1)S(1)}, bf16[1024,512]{1,0:T(8,128)(2,1)S(1)}) custom-call(bf16[1024,512]{1,0:T(8,128)(2,1)S(1)} %bitcast.13, bf16[1024,512]{1,0:T(8,128)(2,1)S(1)} %collective-permute-done.other, bf16[512,512]{1,0:T(8,128)(2,1)S(1)} %copy-done.3, bf16[512,512]{1,0:T(8,128)(2,1)S(1)} %copy-done.1, ...), custom_call_target="tpu_custom_call" | custom-call | flops 800000000 | bytes 4000000 | tf_op jit(solution)/shard_map/project_second/pallas_call | solution.py:439
  11.6 0.0 copy-done.6
  11.6 0.0 copy-done.7
  11.6 0.0 copy-done.8
  11.6 0.0 copy-start.4
  11.6 0.1 taps.1.before.all_taps
  11.7 1.8 %band.3.held = f32[72,512]{1,0:T(8,128)S(1)} custom-call(bf16[2048,256]{1,0:T(8,128)(2,1)S(1)} %get-tuple-element.13.both, s32[8,128]{1,0:T(8,128)S(1)} %copy-done.9, s32[8,128]{1,0:T(8,128)S(1)} %collective-permute-done.1.other_tissue, bf16[256,512]{1,0:T(8,128)(2,1)S(1)} %copy-done.5), custom_call_target="tpu_custom_call" | custom-call | flops 600000000 | bytes 4000000 | tf_op jit(solution)/shard_map/band/pallas_call | solution.py:385
  13.6 1.5 %collective-permute-done.2.got = bf16[72,512]{1,0:T(8,128)(2,1)S(1)} collective-permute-done((bf16[72,512]{1,0:T(8,128)(2,1)S(1)}, bf16[72,512]{1,0:T(8,128)(2,1)S(1)}, u32[]{:S(2)}, u32[]{:S(2)}) %collective-permute-start.2) | collective-permute-done | bytes 73760 | tf_op jit(solution)/shard_map/ppermute | solution.py:339
  15.0 0.1 merge_next.2
  15.1 0.1 collective-permute-start.3
  15.2 2.0 %token_.2.after.weights_low = bf16[1024,1024]{1,0:T(8,128)(2,1)S(1)} custom-call(bf16[1024,512]{1,0:T(8,128)(2,1)S(1)} %bitcast.14, bf16[512,512]{1,0:T(8,128)(2,1)S(1)} %copy-done.4, bf16[256,512]{1,0:T(8,128)(2,1)S(1)} %copy-done.5, bf16[72,512]{1,0:T(8,128)(2,1)S(1)} %get-tuple-element.14.after), custom_call_target="tpu_custom_call" | custom-call | flops 2000000000 | bytes 6000000 | tf_op jit(solution)/shard_map/token/pallas_call | solution.py:399
  17.2 0.0 collective-permute-done.4.outer
  17.2 0.6 %halo.1 = (bf16[384,512]{1,0:T(8,128)(2,1)S(1)}, bf16[384,512]{1,0:T(8,128)(2,1)S(1)}) custom-call(bf16[1024,512]{1,0:T(8,128)(2,1)S(1)} %collective-permute-done.other, bf16[384,512]{1,0:T(8,128)(2,1)S(1)} %collective-permute-done.4.outer, bf16[512,512]{1,0:T(8,128)(2,1)S(1)} %copy-done.1, bf16[1024,1024]{1,0:T(8,128)(2,1)S(1)} %token_.2.after.weights_low), custom_call_target="tpu_custom_call" | custom-call | flops 400000000 | bytes 2000000 | tf_op jit(solution)/shard_map/halo/pallas_call | solution.py:461
  17.7 1.8 %collective-permute-done.3.got = bf16[72,512]{1,0:T(8,128)(2,1)S(1)} collective-permute-done((bf16[72,512]{1,0:T(8,128)(2,1)S(1)}, bf16[72,512]{1,0:T(8,128)(2,1)S(1)}, u32[]{:S(2)}, u32[]{:S(2)}) %collective-permute-start.3) | collective-permute-done | bytes 73760 | tf_op jit(solution)/shard_map/ppermute | solution.py:339
  19.5 0.1 merge_next.3
  19.6 2.7 %collective-permute-start.5 = (bf16[72,512]{1,0:T(8,128)(2,1)S(1)}, bf16[72,512]{1,0:T(8,128)(2,1)S(1)}, u32[]{:S(2)}, u32[]{:S(2)}) collective-permute-start(bf16[72,512]{1,0:T(8,128)(2,1)S(1)} %get-tuple-element.17.after), channel_id=1, source_target_pairs={{0,8},{1,9},{2,10},{3,11},{4,12},{5,13},{6,14},{7,15},{8,0},{9,1},... | collective-permute-start | bytes 221192 | tf_op jit(solution)/shard_map/ppermute | solution.py:339
  22.2 1.9 %token_.3.after.weights_high = bf16[1024,1024]{1,0:T(8,128)(2,1)S(1)} custom-call(bf16[1024,512]{1,0:T(8,128)(2,1)S(1)} %bitcast.15, bf16[512,512]{1,0:T(8,128)(2,1)S(1)} %copy-done.4, bf16[256,512]{1,0:T(8,128)(2,1)S(1)} %copy-done.5, bf16[72,512]{1,0:T(8,128)(2,1)S(1)} %get-tuple-element.17.after), custom_call_target="tpu_custom_call" | custom-call | flops 2000000000 | bytes 6000000 | tf_op jit(solution)/shard_map/token/pallas_call | solution.py:399
  24.2 2.3 %conv.2 = f32[8,128,256]{2,1,0:T(8,128)S(1)} custom-call(bf16[1024,512]{1,0:T(8,128)(2,1)S(1)} %get-tuple-element.19.values, bf16[384,512]{1,0:T(8,128)(2,1)S(1)} %get-tuple-element.16.before.above, bf16[384,512]{1,0:T(8,128)(2,1)S(1)} %get-tuple-element.20.below, f32[7,24,512]{2,1,0:T(8,128)S(1)} %taps.1.before.all_taps, ...), custom_call_target="tpu_custom_call" | custom-call | flops 3000000000 | bytes 4000000 | tf_op jit(solution)/shard_map/conv/pallas_call | solution.py:417
  26.5 0.0 collective-permute-done.5.got
  26.6 0.0 copy-start.2
  26.6 0.4 %collective-permute-start.6 = (bf16[64,512]{1,0:T(8,128)(2,1)S(1)}, bf16[64,512]{1,0:T(8,128)(2,1)S(1)}, u32[]{:S(2)}, u32[]{:S(2)}) collective-permute-start(bf16[64,512]{1,0:T(8,128)(2,1)S(1)} %merge_last.1.after.own), channel_id=1, source_target_pairs={{0,4},{1,5},{2,6},{3,7},{4,0},{5,1},{6,2},{7,3},{8,12},{9,13},{10,... | collective-permute-start | bytes 196616 | tf_op jit(solution)/shard_map/ppermute | solution.py:339
  26.9 2.5 %conv.3 = f32[8,128,256]{2,1,0:T(8,128)S(1)} custom-call(bf16[1024,512]{1,0:T(8,128)(2,1)S(1)} %get-tuple-element.19.values, bf16[384,512]{1,0:T(8,128)(2,1)S(1)} %get-tuple-element.16.before.above, bf16[384,512]{1,0:T(8,128)(2,1)S(1)} %get-tuple-element.20.below, f32[7,24,512]{2,1,0:T(8,128)S(1)} %taps.1.before.all_taps, ...), custom_call_target="tpu_custom_call" | custom-call | flops 3000000000 | bytes 4000000 | tf_op jit(solution)/shard_map/conv/pallas_call | solution.py:417
  29.4 1.5 %collective-permute-done.6.near = bf16[64,512]{1,0:T(8,128)(2,1)S(1)} collective-permute-done((bf16[64,512]{1,0:T(8,128)(2,1)S(1)}, bf16[64,512]{1,0:T(8,128)(2,1)S(1)}, u32[]{:S(2)}, u32[]{:S(2)}) %collective-permute-start.6) | collective-permute-done | bytes 65568 | tf_op jit(solution)/shard_map/ppermute | solution.py:339
  30.9 0.1 collective-permute-start.7
  31.0 1.0 %own_out.1.partial = f32[1024,512]{1,0:T(8,128)S(1)} custom-call(bf16[1024,1024]{1,0:T(8,128)(2,1)S(1)} %token_.2.after.weights_low, bf16[1024,1024]{1,0:T(8,128)(2,1)S(1)} %token_.3.after.weights_high, bf16[128,512]{1,0:T(8,128)(2,1)S(1)} %relay.1.pair, f32[1024,256]{1,0:T(8,128)S(1)} %bitcast.8, f32[1024,256]{1,0:T(8,128)S(1)} %bitcast.5, ...), custom_call_target="tpu_custom_call" | custom-call | flops 1100000000 | bytes 4000000 | tf_op jit(solution)/shard_map/own_out/pallas_call | solution.py:495
  32.0 0.3 collective-permute-done.7.pair
  32.3 1.8 %out.1 = bf16[1024,512]{1,0:T(8,128)(2,1)} custom-call(bf16[1024,1024]{1,0:T(8,128)(2,1)S(1)} %token_.2.after.weights_low, bf16[1024,1024]{1,0:T(8,128)(2,1)S(1)} %token_.3.after.weights_high, bf16[128,512]{1,0:T(8,128)(2,1)S(1)} %collective-permute-done.7.pair, f32[1024,256]{1,0:T(8,128)S(1)} %bitcast.9, f32[1024,256]{1,0:T(8,128)S(1)} %bitcast.6, ...), custom_call_target="tpu_custom_call" | custom-call | flops 1100000000 | bytes 8000000 | tf_op jit(solution)/shard_map/out/pallas_call | solution.py:505
  (6 shorter events, 0.1 us)
Async XLA Ops:
  0.0 4.1 %collective-permute-start.1 = (s32[8,128]{1,0:T(8,128)}, s32[8,128]{1,0:T(8,128)S(1)}, u32[]{:S(2)}, u32[]{:S(2)}) collective-permute-start(s32[8,128]{1,0:T(8,128)} %tissue.3), channel_id=1, source_target_pairs={{0,1},{1,0},{2,3},{3,2},{4,5},{5,4},{6,7},{7,6},{8,9},{9,8},{10,11... | collective-permute-start | bytes 12296 | tf_op jit(solution)/shard_map/ppermute | solution.py:339
  0.5 2.9 %collective-permute-start = (bf16[1024,512]{1,0:T(8,128)(2,1)}, bf16[1024,512]{1,0:T(8,128)(2,1)S(1)}, u32[]{:S(2)}, u32[]{:S(2)}) collective-permute-start(bf16[1024,512]{1,0:T(8,128)(2,1)} %bitcast.10), channel_id=1, source_target_pairs={{0,1},{1,0},{2,3},{3,2},{4,5},{5,4},{6,7},{7,6},{8,9},{9,8},{10,11... | collective-permute-start | bytes 3145736 | tf_op jit(solution)/shard_map/ppermute | solution.py:339
  1.5 1.8 %copy-start = (bf16[8,128,512]{2,1,0:T(8,128)(2,1)S(1)}, bf16[8,128,512]{2,1,0:T(8,128)(2,1)}, u32[]{:S(2)}) copy-start(bf16[8,128,512]{2,1,0:T(8,128)(2,1)} %param.10) | copy-start | bytes 3145732
  1.5 1.8 %copy-start.1 = (bf16[512,512]{1,0:T(8,128)(2,1)S(1)}, bf16[512,512]{1,0:T(8,128)(2,1)}, u32[]{:S(2)}) copy-start(bf16[512,512]{1,0:T(8,128)(2,1)} %w_value.5) | copy-start | bytes 1572868
  1.6 1.8 %copy-start.3 = (bf16[512,512]{1,0:T(8,128)(2,1)S(1)}, bf16[512,512]{1,0:T(8,128)(2,1)}, u32[]{:S(2)}) copy-start(bf16[512,512]{1,0:T(8,128)(2,1)} %w_key.3) | copy-start | bytes 1572868
  1.6 2.5 %copy-start.5 = (bf16[256,512]{1,0:T(8,128)(2,1)S(1)}, bf16[256,512]{1,0:T(8,128)(2,1)}, u32[]{:S(2)}) copy-start(bf16[256,512]{1,0:T(8,128)(2,1)} %agents.7) | copy-start | bytes 786436
  1.6 2.5 %copy-start.9 = (s32[8,128]{1,0:T(8,128)S(1)}, s32[8,128]{1,0:T(8,128)}, u32[]{:S(2)}) copy-start(s32[8,128]{1,0:T(8,128)} %tissue.3) | copy-start | bytes 12292
  1.6 15.5 %collective-permute-start.4 = (bf16[384,512]{1,0:T(8,128)(2,1)S(1)}, bf16[384,512]{1,0:T(8,128)(2,1)S(1)}, u32[]{:S(2)}, u32[]{:S(2)}) collective-permute-start(bf16[384,512]{1,0:T(8,128)(2,1)S(1)} %pass.1), channel_id=1, source_target_pairs={{1,2},{3,4},{5,6},{7,8},{9,10},{11,12},{13,14},{2,1},{4,3},{6,5},{... | collective-permute-start | bytes 1179656 | tf_op jit(solution)/shard_map/ppermute | solution.py:370
  6.0 5.6 %copy-start.6 = (f32[7,7,512]{2,1,0:T(8,128)S(1)}, f32[7,7,512]{2,1,0:T(8,128)}, u32[]{:S(2)}) copy-start(f32[7,7,512]{2,1,0:T(8,128)} %seven.1) | copy-start | bytes 301060
  6.0 5.6 %copy-start.7 = (f32[5,5,512]{2,1,0:T(8,128)S(1)}, f32[5,5,512]{2,1,0:T(8,128)}, u32[]{:S(2)}) copy-start(f32[5,5,512]{2,1,0:T(8,128)} %five.1) | copy-start | bytes 153604
  6.0 5.6 %copy-start.8 = (f32[3,3,512]{2,1,0:T(4,128)S(1)}, f32[3,3,512]{2,1,0:T(4,128)}, u32[]{:S(2)}) copy-start(f32[3,3,512]{2,1,0:T(4,128)} %three.1) | copy-start | bytes 55300
  6.0 9.1 %collective-permute-start.2 = (bf16[72,512]{1,0:T(8,128)(2,1)S(1)}, bf16[72,512]{1,0:T(8,128)(2,1)S(1)}, u32[]{:S(2)}, u32[]{:S(2)}) collective-permute-start(bf16[72,512]{1,0:T(8,128)(2,1)S(1)} %band.2.after), channel_id=1, source_target_pairs={{0,4},{1,5},{2,6},{3,7},{4,0},{5,1},{6,2},{7,3},{8,12},{9,13},{10,... | collective-permute-start | bytes 221192 | tf_op jit(solution)/shard_map/ppermute | solution.py:339
  11.6 3.6 %copy-start.4 = (bf16[512,512]{1,0:T(8,128)(2,1)S(1)}, bf16[512,512]{1,0:T(8,128)(2,1)}, u32[]{:S(2)}) copy-start(bf16[512,512]{1,0:T(8,128)(2,1)} %w_query.3) | copy-start | bytes 1572868
  15.1 4.4 %collective-permute-start.3 = (bf16[72,512]{1,0:T(8,128)(2,1)S(1)}, bf16[72,512]{1,0:T(8,128)(2,1)S(1)}, u32[]{:S(2)}, u32[]{:S(2)}) collective-permute-start(bf16[72,512]{1,0:T(8,128)(2,1)S(1)} %get-tuple-element.14.after), channel_id=1, source_target_pairs={{0,2},{1,3},{2,0},{3,1},{4,6},{5,7},{6,4},{7,5},{8,10},{9,11},{10,... | collective-permute-start | bytes 221192 | tf_op jit(solution)/shard_map/ppermute | solution.py:339
  19.6 6.9 %collective-permute-start.5 = (bf16[72,512]{1,0:T(8,128)(2,1)S(1)}, bf16[72,512]{1,0:T(8,128)(2,1)S(1)}, u32[]{:S(2)}, u32[]{:S(2)}) collective-permute-start(bf16[72,512]{1,0:T(8,128)(2,1)S(1)} %get-tuple-element.17.after), channel_id=1, source_target_pairs={{0,8},{1,9},{2,10},{3,11},{4,12},{5,13},{6,14},{7,15},{8,0},{9,1},... | collective-permute-start | bytes 221192 | tf_op jit(solution)/shard_map/ppermute | solution.py:339
  26.6 4.4 %copy-start.2 = (bf16[512,512]{1,0:T(8,128)(2,1)S(1)}, bf16[512,512]{1,0:T(8,128)(2,1)}, u32[]{:S(2)}) copy-start(bf16[512,512]{1,0:T(8,128)(2,1)} %w_out.3) | copy-start | bytes 1572868
  26.6 4.3 %collective-permute-start.6 = (bf16[64,512]{1,0:T(8,128)(2,1)S(1)}, bf16[64,512]{1,0:T(8,128)(2,1)S(1)}, u32[]{:S(2)}, u32[]{:S(2)}) collective-permute-start(bf16[64,512]{1,0:T(8,128)(2,1)S(1)} %merge_last.1.after.own), channel_id=1, source_target_pairs={{0,4},{1,5},{2,6},{3,7},{4,0},{5,1},{6,2},{7,3},{8,12},{9,13},{10,... | collective-permute-start | bytes 196616 | tf_op jit(solution)/shard_map/ppermute | solution.py:339
  30.9 1.4 %collective-permute-start.7 = (bf16[128,512]{1,0:T(8,128)(2,1)S(1)}, bf16[128,512]{1,0:T(8,128)(2,1)S(1)}, u32[]{:S(2)}, u32[]{:S(2)}) collective-permute-start(bf16[128,512]{1,0:T(8,128)(2,1)S(1)} %relay.1.pair), channel_id=1, source_target_pairs={{0,1},{1,0},{2,3},{3,2},{4,5},{5,4},{6,7},{7,6},{8,9},{9,8},{10,11... | collective-permute-start | bytes 393224 | tf_op jit(solution)/shard_map/ppermute | solution.py:339

commit v11 on v10

--- a/solution.py
+++ b/solution.py
@@ -222,14 +222,14 @@
         taps[q] = jnp.concatenate(parts, axis=0)
 
 
-def conv_kernel(first_lane, values, above, below, all_taps, after, position, points, taps):
-    width = position.shape[1]
+def conv_kernel(first_lane, values, above, below, all_taps, after, *rest):
+    positions, points, taps = rest[:-2], rest[-2], rest[-1]
+    width = positions[0].shape[1]
     lanes, step = 128, 16
     tap_count = sum(TAP_COUNTS)
     zero = jnp.zeros((8, lanes), F32)
-    for group in range(position.shape[2] // lanes):
+    for group, position in enumerate(positions):
         here = slice(first_lane + group * lanes, first_lane + (group + 1) * lanes)
-        there = slice(group * lanes, (group + 1) * lanes)
         for q in range(7):
             for at in range(tap_count):
                 taps[q, at] = jnp.broadcast_to(all_taps[q, at : at + 1, here], (8, lanes))
@@ -268,13 +268,14 @@
             for total, column in zip(sums, columns):
                 thirds_of = [joined_rows(*total[3 * part : 3 * part + 3]) for part in range(3)]
                 for row, plane in enumerate(joined_rows(*thirds_of)):
-                    position[row, column : column + 8, there] = plane
-
-
-def blend_block(here, weights, position, spread, w_out, rows):
-    parts = [dot_nt(weights[here, at * 512 : at * 512 + 512], spread[at]) for at in range(2)]
-    blended = (jnp.concatenate(parts, axis=1) + position[here, :]).astype(BF16)
-    return dot_nn(blended, w_out[rows, :])
+                    position[row, column : column + 8, :] = plane
+
+
+def blend_block(here, weights, positions, spread, w_out, rows):
+    parts = [
+        dot_nt(weights[here, at * 512 : at * 512 + 512], spread[at]) + positions[at][here, :] for at in range(2)
+    ]
+    return dot_nn(jnp.concatenate(parts, axis=1).astype(BF16), w_out[rows, :])
 
 
 def fill_spread(pair, spread):
@@ -286,10 +287,10 @@
             spread[place, half * 64 : half * 64 + 64, cols] = pair[index * 64 : index * 64 + 64, cols]
 
 
-def own_out_kernel(weights_low, weights_high, pair, position_low, position_high, w_out, partial, spread):
+def own_out_kernel(weights_low, weights_high, pair, p_0, p_1, p_2, p_3, w_out, partial, spread):
     fill_spread(pair, spread)
     block = partial.shape[0] // 2
-    for group, (weights, position) in enumerate(((weights_low, position_low), (weights_high, position_high))):
+    for group, (weights, position) in enumerate(((weights_low, (p_0, p_1)), (weights_high, (p_2, p_3)))):
 
         @pl.when(chunk_of_device() // 2 == group)
         def _(group=group, weights=weights, position=position):
@@ -299,16 +300,14 @@
                 partial[here, :] = blend_block(here, weights, position, spread, w_out, rows)
 
 
-def out_kernel(
-    weights_low, weights_high, pair, position_low, position_high, w_out, partial, mixed, spread, buffer, sems
-):
+def out_kernel(weights_low, weights_high, pair, p_0, p_1, p_2, p_3, w_out, partial, mixed, spread, buffer, sems):
     fill_spread(pair, spread)
     block = partial.shape[0] // sems.shape[0]
     copies = []
     for index in range(sems.shape[0]):
         here = slice(index * block, index * block + block)
         copies.append((here, pltpu.make_async_copy(buffer.at[here, :], mixed.at[here, :], sems.at[index])))
-    for group, (weights, position) in enumerate(((weights_low, position_low), (weights_high, position_high))):
+    for group, (weights, position) in enumerate(((weights_low, (p_0, p_1)), (weights_high, (p_2, p_3)))):
 
         @pl.when(chunk_of_device() // 2 != group)
         def _(group=group, weights=weights, position=position):
@@ -413,12 +412,12 @@
             name="token",
         )(flat, w_query, agent_tokens, after)
 
-    def conv(at, after):
-        return pl.pallas_call(
-            functools.partial(conv_kernel, at * half_dim),
-            out_shape=shape((band_rows, width, half_dim), F32),
+    def conv(chunks, after):
+        parts = pl.pallas_call(
+            functools.partial(conv_kernel, chunks[0] * 128),
+            out_shape=[shape((band_rows, width, 128), F32)] * len(chunks),
             in_specs=[vmem] * 4 + [anywhere],
-            out_specs=vmem,
+            out_specs=[vmem] * len(chunks),
             scratch_shapes=[
                 VMEM((sum(TAP_COUNTS) + len(TAP_COUNTS), width + 16, 128), F32),
                 VMEM((7, sum(TAP_COUNTS), 8, 128), F32),
@@ -426,7 +425,8 @@
             compiler_params=params(20),
             cost_estimate=cost(3e9, 4e6),
             name="conv",
-        )(values, above, below, taps, after).reshape(tokens, half_dim)
+        )(values, above, below, taps, after)
+        return [part.reshape(tokens, 128) for part in parts]
 
     hop = dict(in_specs=[vmem, vmem, anywhere], compiler_params=params(16), cost_estimate=cost(1e6, 1e6))
 
@@ -475,12 +475,12 @@
         bit *= 2
     got = exchange(payload, bit)
     weights_high = token(1, payload)
-    position_low = conv(0, weights_high)
+    positions = conv([0], weights_high)
     own = pl.pallas_call(
         last_merge_kernel, out_shape=shape((64, 512), BF16), out_specs=vmem, name="merge_last", **hop
-    )(held, got, position_low)
+    )(held, got, positions[0])
     near = exchange(own, 4)
-    position_high = conv(1, own)
+    positions += conv([1, 2, 3], own)
     pair = pl.pallas_call(
         relay_kernel,
         out_shape=shape((128, 512), BF16),
@@ -489,23 +489,23 @@
         compiler_params=params(16),
         cost_estimate=cost(1e6, 1e6),
         name="relay",
-    )(own, near, position_high)
+    )(own, near, positions[3])
     other_pair = exchange(pair, 1)
 
     partial = pl.pallas_call(
         own_out_kernel,
         out_shape=shape((tokens, dim), F32),
-        in_specs=[vmem] * 6,
+        in_specs=[vmem] * 8,
         out_specs=vmem,
         scratch_shapes=[VMEM((2, 128, 512), BF16)],
         compiler_params=params(20),
         cost_estimate=cost(1.1e9, 4e6),
         name="own_out",
-    )(weights_low, weights_high, pair, position_low, position_high, w_out)
+    )(weights_low, weights_high, pair, *positions, w_out)
     mixed = pl.pallas_call(
         out_kernel,
         out_shape=shape((tokens, dim), BF16),
-        in_specs=[vmem] * 7,
+        in_specs=[vmem] * 9,
         out_specs=anywhere,
         scratch_shapes=[
             VMEM((2, 128, 512), BF16),
@@ -515,7 +515,7 @@
         compiler_params=params(20),
         cost_estimate=cost(1.1e9, 8e6),
         name="out",
-    )(weights_low, weights_high, other_pair, position_low, position_high, w_out, partial)
+    )(weights_low, weights_high, other_pair, *positions, w_out, partial)
     return mixed.reshape(band_rows, width, dim)
 
 

time: 34.5 us -> 33.4 us (0.968)
  waiting for transfers between devices: 5.93 us -> 4.86 us
    ppermute x7, waiting for transfers between devices: 5.92 us -> 4.86 us  [exchange(): return lax.ppermute(x, 'col', [(i, i ^ bit) for i in range(peers)])]
  transfers between devices with their start and end apart: 8 -> 8, of which waited for: 5 -> 6; matrix products, arithmetic and copies ran while one was open for 3% -> 3% of each run, Pallas kernels for 47% -> 48%
where the time goes in v11:
time: 33.4 us; the launch traced here: 33.2 us
  Pallas kernels  18 us (54%)
  starting transfers between devices  8.87 us (27%)
  waiting for transfers between devices  4.86 us (15%)
  local copies, waits for them, and re-layouts  1.08 us (3%)
  between operations  0.44 us (1%)
    ppermute x7, starting transfers between devices, exchange(): return lax.ppermute(x, 'col', [(i, i ^ bit) for i in range(peers)])  8.05 us
    ppermute x7, waiting for transfers between devices, exchange(): return lax.ppermute(x, 'col', [(i, i ^ bit) for i in range(peers)])  4.86 us
    pallas_call x2, Pallas kernels, conv(): pl.pallas_call(functools.partial(conv_kernel, chunks[0] * 128), out_shape...  4.79 us
    pallas_call x2, Pallas kernels, token(): pl.pallas_call(functools.partial(token_kernel, scale), out_shape=shape((t...  3.9 us
    pallas_call x2, Pallas kernels, band(): pl.pallas_call(functools.partial(kernel, scale), out_shape=out_shape, in_...  3.76 us
    pallas_call x1, Pallas kernels, on_device(): pl.pallas_call(out_kernel, out_shape=shape((tokens, dim), BF16), in_specs...  1.82 us
    pallas_call x1, Pallas kernels, on_device(): pl.pallas_call(second_project_kernel, out_shape=(both_bands, shape((token...  1.1 us
    dynamic_slice x1, local copies, waits for them, and re-layouts, on_device(): lax.dynamic_slice_in_dim(flat, odd * (tokens - 3 * width), 3 * width, 0)  1.02 us
  transfers between devices with their start and end apart: 8, of which 6 were waited for; matrix products, arithmetic and copies ran while one was open for 3% of the time, Pallas kernels for 48%

profile of v11, /device:TPU:0, one launch (start us, length us, event | category | flops | bytes accessed | tf_op | source)
XLA Modules:
  0.0 33.2 jit_solution(13509862594209481541)
XLA Ops:
  0.0 0.5 %collective-permute-start.1 = (s32[8,128]{1,0:T(8,128)}, s32[8,128]{1,0:T(8,128)S(1)}, u32[]{:S(2)}, u32[]{:S(2)}) collective-permute-start(s32[8,128]{1,0:T(8,128)} %tissue.3), channel_id=1, source_target_pairs={{0,1},{1,0},{2,3},{3,2},{4,5},{5,4},{6,7},{7,6},{8,9},{9,8},{10,11... | collective-permute-start | bytes 12296 | tf_op jit(solution)/shard_map/ppermute | solution.py:338
  0.5 0.1 collective-permute-start
  0.5 1.0 %constant_dynamic-slice_fusion.border = bf16[384,512]{1,0:T(8,128)(2,1)S(1)} fusion(bf16[1024,512]{1,0:T(8,128)(2,1)} %bitcast.7, s32[]{:T(128)S(6)} %select_n.11), kind=kLoop, calls=%fused_computation | loop fusion | bytes 786436 | tf_op jit(solution)/shard_map/dynamic_slice | solution.py:357
  1.5 0.0 copy-start
  1.5 0.0 copy-start.1
  1.6 0.0 copy-start.3
  1.6 0.0 copy-start.5
  1.6 0.0 copy-start.9
  1.6 0.8 %collective-permute-start.4 = (bf16[384,512]{1,0:T(8,128)(2,1)S(1)}, bf16[384,512]{1,0:T(8,128)(2,1)S(1)}, u32[]{:S(2)}, u32[]{:S(2)}) collective-permute-start(bf16[384,512]{1,0:T(8,128)(2,1)S(1)} %pass.1), channel_id=1, source_target_pairs={{1,2},{3,4},{5,6},{7,8},{9,10},{11,12},{13,14},{2,1},{4,3},{6,5},{... | collective-permute-start | bytes 1179656 | tf_op jit(solution)/shard_map/ppermute | solution.py:369
  2.4 0.9 %collective-permute-done.other = bf16[1024,512]{1,0:T(8,128)(2,1)S(1)} collective-permute-done((bf16[1024,512]{1,0:T(8,128)(2,1)}, bf16[1024,512]{1,0:T(8,128)(2,1)S(1)}, u32[]{:S(2)}, u32[]{:S(2)}) %collective-permute-start) | collective-permute-done | bytes 1048608 | tf_op jit(solution)/shard_map/ppermute | solution.py:338
  3.3 0.0 copy-done
  3.3 0.0 copy-done.1
  3.3 0.0 copy-done.3
  3.3 0.7 %project.1.both.first = bf16[2048,256]{1,0:T(8,128)(2,1)S(1)} custom-call(bf16[1024,512]{1,0:T(8,128)(2,1)S(1)} %bitcast.8, bf16[1024,512]{1,0:T(8,128)(2,1)S(1)} %collective-permute-done.other, bf16[512,512]{1,0:T(8,128)(2,1)S(1)} %copy-done.3, bf16[512,512]{1,0:T(8,128)(2,1)S(1)} %copy-done.1), custom_call_target="tpu_custom_call" | custom-call | flops 600000000 | bytes 4000000 | tf_op jit(solution)/shard_map/project/pallas_call | solution.py:373
  4.1 0.0 collective-permute-done.1.other_tissue
  4.1 0.0 copy-done.5
  4.1 1.8 %band.2.after = bf16[72,512]{1,0:T(8,128)(2,1)S(1)} custom-call(bf16[2048,256]{1,0:T(8,128)(2,1)S(1)} %project.1.both.first, s32[8,128]{1,0:T(8,128)S(1)} %copy-done.9, s32[8,128]{1,0:T(8,128)S(1)} %collective-permute-done.1.other_tissue, bf16[256,512]{1,0:T(8,128)(2,1)S(1)} %copy-done.5), custom_call_target="tpu_custom_call" | custom-call | flops 600000000 | bytes 4000000 | tf_op jit(solution)/shard_map/band/pallas_call | solution.py:384
  6.0 0.0 copy-start.6
  6.0 0.0 copy-start.7
  6.0 0.0 copy-start.8
  6.0 4.5 %collective-permute-start.2 = (bf16[72,512]{1,0:T(8,128)(2,1)S(1)}, bf16[72,512]{1,0:T(8,128)(2,1)S(1)}, u32[]{:S(2)}, u32[]{:S(2)}) collective-permute-start(bf16[72,512]{1,0:T(8,128)(2,1)S(1)} %band.2.after), channel_id=1, source_target_pairs={{0,4},{1,5},{2,6},{3,7},{4,0},{5,1},{6,2},{7,3},{8,12},{9,13},{10,... | collective-permute-start | bytes 221192 | tf_op jit(solution)/shard_map/ppermute | solution.py:338
  10.4 1.1 %project_second.1 = (bf16[2048,256]{1,0:T(8,128)(2,1)S(1)}, bf16[1024,512]{1,0:T(8,128)(2,1)S(1)}) custom-call(bf16[1024,512]{1,0:T(8,128)(2,1)S(1)} %bitcast.9, bf16[1024,512]{1,0:T(8,128)(2,1)S(1)} %collective-permute-done.other, bf16[512,512]{1,0:T(8,128)(2,1)S(1)} %copy-done.3, bf16[512,512]{1,0:T(8,128)(2,1)S(1)} %copy-done.1, ...), custom_call_target="tpu_custom_call" | custom-call | flops 800000000 | bytes 4000000 | tf_op jit(solution)/shard_map/project_second/pallas_call | solution.py:439
  11.6 0.0 copy-done.6
  11.6 0.0 copy-done.7
  11.6 0.0 copy-done.8
  11.6 0.0 copy-start.4
  11.6 0.1 taps.1.before.all_taps
  11.7 1.9 %band.3.held = f32[72,512]{1,0:T(8,128)S(1)} custom-call(bf16[2048,256]{1,0:T(8,128)(2,1)S(1)} %get-tuple-element.16.both, s32[8,128]{1,0:T(8,128)S(1)} %copy-done.9, s32[8,128]{1,0:T(8,128)S(1)} %collective-permute-done.1.other_tissue, bf16[256,512]{1,0:T(8,128)(2,1)S(1)} %copy-done.5), custom_call_target="tpu_custom_call" | custom-call | flops 600000000 | bytes 4000000 | tf_op jit(solution)/shard_map/band/pallas_call | solution.py:384
  13.7 1.4 %collective-permute-done.2.got = bf16[72,512]{1,0:T(8,128)(2,1)S(1)} collective-permute-done((bf16[72,512]{1,0:T(8,128)(2,1)S(1)}, bf16[72,512]{1,0:T(8,128)(2,1)S(1)}, u32[]{:S(2)}, u32[]{:S(2)}) %collective-permute-start.2) | collective-permute-done | bytes 73760 | tf_op jit(solution)/shard_map/ppermute | solution.py:338
  15.0 0.1 merge_next.2
  15.1 0.1 collective-permute-start.3
  15.2 2.0 %token_.2.after.weights_low = bf16[1024,1024]{1,0:T(8,128)(2,1)S(1)} custom-call(bf16[1024,512]{1,0:T(8,128)(2,1)S(1)} %bitcast.10, bf16[512,512]{1,0:T(8,128)(2,1)S(1)} %copy-done.4, bf16[256,512]{1,0:T(8,128)(2,1)S(1)} %copy-done.5, bf16[72,512]{1,0:T(8,128)(2,1)S(1)} %get-tuple-element.17.after), custom_call_target="tpu_custom_call" | custom-call | flops 2000000000 | bytes 6000000 | tf_op jit(solution)/shard_map/token/pallas_call | solution.py:398
  17.2 0.0 collective-permute-done.4.outer
  17.2 0.6 %halo.1 = (bf16[384,512]{1,0:T(8,128)(2,1)S(1)}, bf16[384,512]{1,0:T(8,128)(2,1)S(1)}) custom-call(bf16[1024,512]{1,0:T(8,128)(2,1)S(1)} %collective-permute-done.other, bf16[384,512]{1,0:T(8,128)(2,1)S(1)} %collective-permute-done.4.outer, bf16[512,512]{1,0:T(8,128)(2,1)S(1)} %copy-done.1, bf16[1024,1024]{1,0:T(8,128)(2,1)S(1)} %token_.2.after.weights_low), custom_call_target="tpu_custom_call" | custom-call | flops 400000000 | bytes 2000000 | tf_op jit(solution)/shard_map/halo/pallas_call | solution.py:461
  17.7 1.8 %collective-permute-done.3.got = bf16[72,512]{1,0:T(8,128)(2,1)S(1)} collective-permute-done((bf16[72,512]{1,0:T(8,128)(2,1)S(1)}, bf16[72,512]{1,0:T(8,128)(2,1)S(1)}, u32[]{:S(2)}, u32[]{:S(2)}) %collective-permute-start.3) | collective-permute-done | bytes 73760 | tf_op jit(solution)/shard_map/ppermute | solution.py:338
  19.5 0.1 merge_next.3
  19.6 2.7 %collective-permute-start.5 = (bf16[72,512]{1,0:T(8,128)(2,1)S(1)}, bf16[72,512]{1,0:T(8,128)(2,1)S(1)}, u32[]{:S(2)}, u32[]{:S(2)}) collective-permute-start(bf16[72,512]{1,0:T(8,128)(2,1)S(1)} %get-tuple-element.20.after), channel_id=1, source_target_pairs={{0,8},{1,9},{2,10},{3,11},{4,12},{5,13},{6,14},{7,15},{8,0},{9,1},... | collective-permute-start | bytes 221192 | tf_op jit(solution)/shard_map/ppermute | solution.py:338
  22.2 1.9 %token_.3.after.weights_high = bf16[1024,1024]{1,0:T(8,128)(2,1)S(1)} custom-call(bf16[1024,512]{1,0:T(8,128)(2,1)S(1)} %bitcast.11, bf16[512,512]{1,0:T(8,128)(2,1)S(1)} %copy-done.4, bf16[256,512]{1,0:T(8,128)(2,1)S(1)} %copy-done.5, bf16[72,512]{1,0:T(8,128)(2,1)S(1)} %get-tuple-element.20.after), custom_call_target="tpu_custom_call" | custom-call | flops 2000000000 | bytes 6000000 | tf_op jit(solution)/shard_map/token/pallas_call | solution.py:398
  24.2 1.1 %conv.2 = f32[8,128,128]{2,1,0:T(8,128)S(1)} custom-call(bf16[1024,512]{1,0:T(8,128)(2,1)S(1)} %get-tuple-element.22.values, bf16[384,512]{1,0:T(8,128)(2,1)S(1)} %get-tuple-element.19.before.above, bf16[384,512]{1,0:T(8,128)(2,1)S(1)} %get-tuple-element.23.below, f32[7,24,512]{2,1,0:T(8,128)S(1)} %taps.1.before.all_taps, ...), custom_call_target="tpu_custom_call" | custom-call | flops 3000000000 | bytes 4000000 | tf_op jit(solution)/shard_map/conv/pallas_call | solution.py:416
  25.3 0.1 collective-permute-done.5.got
  25.5 0.0 copy-start.2
  25.5 0.3 collective-permute-start.6
  25.8 3.6 %conv.3 = (f32[8,128,128]{2,1,0:T(8,128)S(1)}, f32[8,128,128]{2,1,0:T(8,128)S(1)}, f32[8,128,128]{2,1,0:T(8,128)S(1)}) custom-call(bf16[1024,512]{1,0:T(8,128)(2,1)S(1)} %get-tuple-element.22.values, bf16[384,512]{1,0:T(8,128)(2,1)S(1)} %get-tuple-element.19.before.above, bf16[384,512]{1,0:T(8,128)(2,1)S(1)} %get-tuple-element.23.below, ...), custom_call_target="tpu_custom_call" | custom-call | flops 3000000000 | bytes 4000000 | tf_op jit(solution)/shard_map/conv/pallas_call | solution.py:416
  29.4 0.4 %collective-permute-done.6.near = bf16[64,512]{1,0:T(8,128)(2,1)S(1)} collective-permute-done((bf16[64,512]{1,0:T(8,128)(2,1)S(1)}, bf16[64,512]{1,0:T(8,128)(2,1)S(1)}, u32[]{:S(2)}, u32[]{:S(2)}) %collective-permute-start.6) | collective-permute-done | bytes 65568 | tf_op jit(solution)/shard_map/ppermute | solution.py:338
  29.8 0.1 collective-permute-start.7
  29.9 1.0 %own_out.1.partial = f32[1024,512]{1,0:T(8,128)S(1)} custom-call(bf16[1024,1024]{1,0:T(8,128)(2,1)S(1)} %token_.2.after.weights_low, bf16[1024,1024]{1,0:T(8,128)(2,1)S(1)} %token_.3.after.weights_high, bf16[128,512]{1,0:T(8,128)(2,1)S(1)} %relay.1.pair, f32[1024,128]{1,0:T(8,128)S(1)} %bitcast.13, f32[1024,128]{1,0:T(8,128)S(1)} %bitcast.18, ...), custom_call_target="tpu_custom_call" | custom-call | flops 1100000000 | bytes 4000000 | tf_op jit(solution)/shard_map/own_out/pallas_call | solution.py:495
  30.9 0.3 collective-permute-done.7.pair
  31.3 1.8 %out.1 = bf16[1024,512]{1,0:T(8,128)(2,1)} custom-call(bf16[1024,1024]{1,0:T(8,128)(2,1)S(1)} %token_.2.after.weights_low, bf16[1024,1024]{1,0:T(8,128)(2,1)S(1)} %token_.3.after.weights_high, bf16[128,512]{1,0:T(8,128)(2,1)S(1)} %collective-permute-done.7.pair, f32[1024,128]{1,0:T(8,128)S(1)} %bitcast.14, f32[1024,128]{1,0:T(8,128)S(1)} %bitcast.19, ...), custom_call_target="tpu_custom_call" | custom-call | flops 1100000000 | bytes 8000000 | tf_op jit(solution)/shard_map/out/pallas_call | solution.py:505
  (6 shorter events, 0.1 us)
Async XLA Ops:
  0.0 4.1 %collective-permute-start.1 = (s32[8,128]{1,0:T(8,128)}, s32[8,128]{1,0:T(8,128)S(1)}, u32[]{:S(2)}, u32[]{:S(2)}) collective-permute-start(s32[8,128]{1,0:T(8,128)} %tissue.3), channel_id=1, source_target_pairs={{0,1},{1,0},{2,3},{3,2},{4,5},{5,4},{6,7},{7,6},{8,9},{9,8},{10,11... | collective-permute-start | bytes 12296 | tf_op jit(solution)/shard_map/ppermute | solution.py:338
  0.5 2.9 %collective-permute-start = (bf16[1024,512]{1,0:T(8,128)(2,1)}, bf16[1024,512]{1,0:T(8,128)(2,1)S(1)}, u32[]{:S(2)}, u32[]{:S(2)}) collective-permute-start(bf16[1024,512]{1,0:T(8,128)(2,1)} %bitcast.6), channel_id=1, source_target_pairs={{0,1},{1,0},{2,3},{3,2},{4,5},{5,4},{6,7},{7,6},{8,9},{9,8},{10,11... | collective-permute-start | bytes 3145736 | tf_op jit(solution)/shard_map/ppermute | solution.py:338
  1.5 1.8 %copy-start = (bf16[8,128,512]{2,1,0:T(8,128)(2,1)S(1)}, bf16[8,128,512]{2,1,0:T(8,128)(2,1)}, u32[]{:S(2)}) copy-start(bf16[8,128,512]{2,1,0:T(8,128)(2,1)} %param.10) | copy-start | bytes 3145732
  1.5 1.8 %copy-start.1 = (bf16[512,512]{1,0:T(8,128)(2,1)S(1)}, bf16[512,512]{1,0:T(8,128)(2,1)}, u32[]{:S(2)}) copy-start(bf16[512,512]{1,0:T(8,128)(2,1)} %w_value.5) | copy-start | bytes 1572868
  1.6 1.8 %copy-start.3 = (bf16[512,512]{1,0:T(8,128)(2,1)S(1)}, bf16[512,512]{1,0:T(8,128)(2,1)}, u32[]{:S(2)}) copy-start(bf16[512,512]{1,0:T(8,128)(2,1)} %w_key.3) | copy-start | bytes 1572868
  1.6 2.5 %copy-start.5 = (bf16[256,512]{1,0:T(8,128)(2,1)S(1)}, bf16[256,512]{1,0:T(8,128)(2,1)}, u32[]{:S(2)}) copy-start(bf16[256,512]{1,0:T(8,128)(2,1)} %agents.7) | copy-start | bytes 786436
  1.6 2.5 %copy-start.9 = (s32[8,128]{1,0:T(8,128)S(1)}, s32[8,128]{1,0:T(8,128)}, u32[]{:S(2)}) copy-start(s32[8,128]{1,0:T(8,128)} %tissue.3) | copy-start | bytes 12292
  1.6 15.5 %collective-permute-start.4 = (bf16[384,512]{1,0:T(8,128)(2,1)S(1)}, bf16[384,512]{1,0:T(8,128)(2,1)S(1)}, u32[]{:S(2)}, u32[]{:S(2)}) collective-permute-start(bf16[384,512]{1,0:T(8,128)(2,1)S(1)} %pass.1), channel_id=1, source_target_pairs={{1,2},{3,4},{5,6},{7,8},{9,10},{11,12},{13,14},{2,1},{4,3},{6,5},{... | collective-permute-start | bytes 1179656 | tf_op jit(solution)/shard_map/ppermute | solution.py:369
  6.0 5.6 %copy-start.6 = (f32[7,7,512]{2,1,0:T(8,128)S(1)}, f32[7,7,512]{2,1,0:T(8,128)}, u32[]{:S(2)}) copy-start(f32[7,7,512]{2,1,0:T(8,128)} %seven.1) | copy-start | bytes 301060
  6.0 5.6 %copy-start.7 = (f32[5,5,512]{2,1,0:T(8,128)S(1)}, f32[5,5,512]{2,1,0:T(8,128)}, u32[]{:S(2)}) copy-start(f32[5,5,512]{2,1,0:T(8,128)} %five.1) | copy-start | bytes 153604
  6.0 5.6 %copy-start.8 = (f32[3,3,512]{2,1,0:T(4,128)S(1)}, f32[3,3,512]{2,1,0:T(4,128)}, u32[]{:S(2)}) copy-start(f32[3,3,512]{2,1,0:T(4,128)} %three.1) | copy-start | bytes 55300
  6.0 9.1 %collective-permute-start.2 = (bf16[72,512]{1,0:T(8,128)(2,1)S(1)}, bf16[72,512]{1,0:T(8,128)(2,1)S(1)}, u32[]{:S(2)}, u32[]{:S(2)}) collective-permute-start(bf16[72,512]{1,0:T(8,128)(2,1)S(1)} %band.2.after), channel_id=1, source_target_pairs={{0,4},{1,5},{2,6},{3,7},{4,0},{5,1},{6,2},{7,3},{8,12},{9,13},{10,... | collective-permute-start | bytes 221192 | tf_op jit(solution)/shard_map/ppermute | solution.py:338
  11.6 3.6 %copy-start.4 = (bf16[512,512]{1,0:T(8,128)(2,1)S(1)}, bf16[512,512]{1,0:T(8,128)(2,1)}, u32[]{:S(2)}) copy-start(bf16[512,512]{1,0:T(8,128)(2,1)} %w_query.3) | copy-start | bytes 1572868
  15.1 4.4 %collective-permute-start.3 = (bf16[72,512]{1,0:T(8,128)(2,1)S(1)}, bf16[72,512]{1,0:T(8,128)(2,1)S(1)}, u32[]{:S(2)}, u32[]{:S(2)}) collective-permute-start(bf16[72,512]{1,0:T(8,128)(2,1)S(1)} %get-tuple-element.17.after), channel_id=1, source_target_pairs={{0,2},{1,3},{2,0},{3,1},{4,6},{5,7},{6,4},{7,5},{8,10},{9,11},{10,... | collective-permute-start | bytes 221192 | tf_op jit(solution)/shard_map/ppermute | solution.py:338
  19.6 5.9 %collective-permute-start.5 = (bf16[72,512]{1,0:T(8,128)(2,1)S(1)}, bf16[72,512]{1,0:T(8,128)(2,1)S(1)}, u32[]{:S(2)}, u32[]{:S(2)}) collective-permute-start(bf16[72,512]{1,0:T(8,128)(2,1)S(1)} %get-tuple-element.20.after), channel_id=1, source_target_pairs={{0,8},{1,9},{2,10},{3,11},{4,12},{5,13},{6,14},{7,15},{8,0},{9,1},... | collective-permute-start | bytes 221192 | tf_op jit(solution)/shard_map/ppermute | solution.py:338
  25.5 4.4 %copy-start.2 = (bf16[512,512]{1,0:T(8,128)(2,1)S(1)}, bf16[512,512]{1,0:T(8,128)(2,1)}, u32[]{:S(2)}) copy-start(bf16[512,512]{1,0:T(8,128)(2,1)} %w_out.3) | copy-start | bytes 1572868
  25.5 4.3 %collective-permute-start.6 = (bf16[64,512]{1,0:T(8,128)(2,1)S(1)}, bf16[64,512]{1,0:T(8,128)(2,1)S(1)}, u32[]{:S(2)}, u32[]{:S(2)}) collective-permute-start(bf16[64,512]{1,0:T(8,128)(2,1)S(1)} %merge_last.1.after.own), channel_id=1, source_target_pairs={{0,4},{1,5},{2,6},{3,7},{4,0},{5,1},{6,2},{7,3},{8,12},{9,13},{10,... | collective-permute-start | bytes 196616 | tf_op jit(solution)/shard_map/ppermute | solution.py:338
  29.8 1.4 %collective-permute-start.7 = (bf16[128,512]{1,0:T(8,128)(2,1)S(1)}, bf16[128,512]{1,0:T(8,128)(2,1)S(1)}, u32[]{:S(2)}, u32[]{:S(2)}) collective-permute-start(bf16[128,512]{1,0:T(8,128)(2,1)S(1)} %relay.1.pair), channel_id=1, source_target_pairs={{0,1},{1,0},{2,3},{3,2},{4,5},{5,4},{6,7},{7,6},{8,9},{9,8},{10,11... | collective-permute-start | bytes 393224 | tf_op jit(solution)/shard_map/ppermute | solution.py:338

commit v12 on v11

--- a/solution.py
+++ b/solution.py
@@ -302,10 +302,10 @@
 
 def out_kernel(weights_low, weights_high, pair, p_0, p_1, p_2, p_3, w_out, partial, mixed, spread, buffer, sems):
     fill_spread(pair, spread)
-    block = partial.shape[0] // sems.shape[0]
+    quarter = partial.shape[0] // 4
     copies = []
-    for index in range(sems.shape[0]):
-        here = slice(index * block, index * block + block)
+    for index, (start, stop) in enumerate(((0, 2), (2, 3), (3, 4))):
+        here = slice(start * quarter, stop * quarter)
         copies.append((here, pltpu.make_async_copy(buffer.at[here, :], mixed.at[here, :], sems.at[index])))
     for group, (weights, position) in enumerate(((weights_low, (p_0, p_1)), (weights_high, (p_2, p_3)))):
 
@@ -510,7 +510,7 @@
         scratch_shapes=[
             VMEM((2, 128, 512), BF16),
             VMEM((tokens, dim), BF16),
-            pltpu.SemaphoreType.DMA((2,)),
+            pltpu.SemaphoreType.DMA((3,)),
         ],
         compiler_params=params(20),
         cost_estimate=cost(1.1e9, 8e6),

time: 33.4 us -> 33.5 us (level)
  no operation moved by 1% of the time
where the time goes in v12:
time: 33.5 us; the launch traced here: 33.3 us
  Pallas kernels  18.1 us (54%)
  starting transfers between devices  8.87 us (26%)
  waiting for transfers between devices  4.86 us (15%)
  local copies, waits for them, and re-layouts  1.08 us (3%)
  between operations  0.44 us (1%)
    ppermute x7, starting transfers between devices, exchange(): return lax.ppermute(x, 'col', [(i, i ^ bit) for i in range(peers)])  8.05 us
    ppermute x7, waiting for transfers between devices, exchange(): return lax.ppermute(x, 'col', [(i, i ^ bit) for i in range(peers)])  4.86 us
    pallas_call x2, Pallas kernels, conv(): pl.pallas_call(functools.partial(conv_kernel, chunks[0] * 128), out_shape...  4.79 us
    pallas_call x2, Pallas kernels, token(): pl.pallas_call(functools.partial(token_kernel, scale), out_shape=shape((t...  3.9 us
    pallas_call x2, Pallas kernels, band(): pl.pallas_call(functools.partial(kernel, scale), out_shape=out_shape, in_...  3.76 us
    pallas_call x1, Pallas kernels, on_device(): pl.pallas_call(out_kernel, out_shape=shape((tokens, dim), BF16), in_specs...  1.89 us
    pallas_call x1, Pallas kernels, on_device(): pl.pallas_call(second_project_kernel, out_shape=(both_bands, shape((token...  1.1 us
    dynamic_slice x1, local copies, waits for them, and re-layouts, on_device(): lax.dynamic_slice_in_dim(flat, odd * (tokens - 3 * width), 3 * width, 0)  1.02 us
  transfers between devices with their start and end apart: 8, of which 6 were waited for; matrix products, arithmetic and copies ran while one was open for 3% of the time, Pallas kernels for 48%

profile of v12, /device:TPU:0, one launch (start us, length us, event | category | flops | bytes accessed | tf_op | source)
XLA Modules:
  0.0 33.3 jit_solution(13271591240993266285)
XLA Ops:
  0.0 0.5 %collective-permute-start.1 = (s32[8,128]{1,0:T(8,128)}, s32[8,128]{1,0:T(8,128)S(1)}, u32[]{:S(2)}, u32[]{:S(2)}) collective-permute-start(s32[8,128]{1,0:T(8,128)} %tissue.3), channel_id=1, source_target_pairs={{0,1},{1,0},{2,3},{3,2},{4,5},{5,4},{6,7},{7,6},{8,9},{9,8},{10,11... | collective-permute-start | bytes 12296 | tf_op jit(solution)/shard_map/ppermute | solution.py:338
  0.5 0.1 collective-permute-start
  0.5 1.0 %constant_dynamic-slice_fusion.border = bf16[384,512]{1,0:T(8,128)(2,1)S(1)} fusion(bf16[1024,512]{1,0:T(8,128)(2,1)} %bitcast.7, s32[]{:T(128)S(6)} %select_n.11), kind=kLoop, calls=%fused_computation | loop fusion | bytes 786436 | tf_op jit(solution)/shard_map/dynamic_slice | solution.py:357
  1.5 0.0 copy-start
  1.5 0.0 copy-start.1
  1.6 0.0 copy-start.3
  1.6 0.0 copy-start.5
  1.6 0.0 copy-start.9
  1.6 0.8 %collective-permute-start.4 = (bf16[384,512]{1,0:T(8,128)(2,1)S(1)}, bf16[384,512]{1,0:T(8,128)(2,1)S(1)}, u32[]{:S(2)}, u32[]{:S(2)}) collective-permute-start(bf16[384,512]{1,0:T(8,128)(2,1)S(1)} %pass.1), channel_id=1, source_target_pairs={{1,2},{3,4},{5,6},{7,8},{9,10},{11,12},{13,14},{2,1},{4,3},{6,5},{... | collective-permute-start | bytes 1179656 | tf_op jit(solution)/shard_map/ppermute | solution.py:369
  2.4 0.9 %collective-permute-done.other = bf16[1024,512]{1,0:T(8,128)(2,1)S(1)} collective-permute-done((bf16[1024,512]{1,0:T(8,128)(2,1)}, bf16[1024,512]{1,0:T(8,128)(2,1)S(1)}, u32[]{:S(2)}, u32[]{:S(2)}) %collective-permute-start) | collective-permute-done | bytes 1048608 | tf_op jit(solution)/shard_map/ppermute | solution.py:338
  3.3 0.0 copy-done
  3.3 0.0 copy-done.1
  3.3 0.0 copy-done.3
  3.3 0.7 %project.1.both.first = bf16[2048,256]{1,0:T(8,128)(2,1)S(1)} custom-call(bf16[1024,512]{1,0:T(8,128)(2,1)S(1)} %bitcast.8, bf16[1024,512]{1,0:T(8,128)(2,1)S(1)} %collective-permute-done.other, bf16[512,512]{1,0:T(8,128)(2,1)S(1)} %copy-done.3, bf16[512,512]{1,0:T(8,128)(2,1)S(1)} %copy-done.1), custom_call_target="tpu_custom_call" | custom-call | flops 600000000 | bytes 4000000 | tf_op jit(solution)/shard_map/project/pallas_call | solution.py:373
  4.1 0.0 collective-permute-done.1.other_tissue
  4.1 0.0 copy-done.5
  4.1 1.8 %band.2.after = bf16[72,512]{1,0:T(8,128)(2,1)S(1)} custom-call(bf16[2048,256]{1,0:T(8,128)(2,1)S(1)} %project.1.both.first, s32[8,128]{1,0:T(8,128)S(1)} %copy-done.9, s32[8,128]{1,0:T(8,128)S(1)} %collective-permute-done.1.other_tissue, bf16[256,512]{1,0:T(8,128)(2,1)S(1)} %copy-done.5), custom_call_target="tpu_custom_call" | custom-call | flops 600000000 | bytes 4000000 | tf_op jit(solution)/shard_map/band/pallas_call | solution.py:384
  6.0 0.0 copy-start.6
  6.0 0.0 copy-start.7
  6.0 0.0 copy-start.8
  6.0 4.5 %collective-permute-start.2 = (bf16[72,512]{1,0:T(8,128)(2,1)S(1)}, bf16[72,512]{1,0:T(8,128)(2,1)S(1)}, u32[]{:S(2)}, u32[]{:S(2)}) collective-permute-start(bf16[72,512]{1,0:T(8,128)(2,1)S(1)} %band.2.after), channel_id=1, source_target_pairs={{0,4},{1,5},{2,6},{3,7},{4,0},{5,1},{6,2},{7,3},{8,12},{9,13},{10,... | collective-permute-start | bytes 221192 | tf_op jit(solution)/shard_map/ppermute | solution.py:338
  10.4 1.1 %project_second.1 = (bf16[2048,256]{1,0:T(8,128)(2,1)S(1)}, bf16[1024,512]{1,0:T(8,128)(2,1)S(1)}) custom-call(bf16[1024,512]{1,0:T(8,128)(2,1)S(1)} %bitcast.9, bf16[1024,512]{1,0:T(8,128)(2,1)S(1)} %collective-permute-done.other, bf16[512,512]{1,0:T(8,128)(2,1)S(1)} %copy-done.3, bf16[512,512]{1,0:T(8,128)(2,1)S(1)} %copy-done.1, ...), custom_call_target="tpu_custom_call" | custom-call | flops 800000000 | bytes 4000000 | tf_op jit(solution)/shard_map/project_second/pallas_call | solution.py:439
  11.6 0.0 copy-done.6
  11.6 0.0 copy-done.7
  11.6 0.0 copy-done.8
  11.6 0.0 copy-start.4
  11.6 0.1 taps.1.before.all_taps
  11.7 1.9 %band.3.held = f32[72,512]{1,0:T(8,128)S(1)} custom-call(bf16[2048,256]{1,0:T(8,128)(2,1)S(1)} %get-tuple-element.16.both, s32[8,128]{1,0:T(8,128)S(1)} %copy-done.9, s32[8,128]{1,0:T(8,128)S(1)} %collective-permute-done.1.other_tissue, bf16[256,512]{1,0:T(8,128)(2,1)S(1)} %copy-done.5), custom_call_target="tpu_custom_call" | custom-call | flops 600000000 | bytes 4000000 | tf_op jit(solution)/shard_map/band/pallas_call | solution.py:384
  13.7 1.4 %collective-permute-done.2.got = bf16[72,512]{1,0:T(8,128)(2,1)S(1)} collective-permute-done((bf16[72,512]{1,0:T(8,128)(2,1)S(1)}, bf16[72,512]{1,0:T(8,128)(2,1)S(1)}, u32[]{:S(2)}, u32[]{:S(2)}) %collective-permute-start.2) | collective-permute-done | bytes 73760 | tf_op jit(solution)/shard_map/ppermute | solution.py:338
  15.0 0.1 merge_next.2
  15.1 0.1 collective-permute-start.3
  15.2 2.0 %token_.2.after.weights_low = bf16[1024,1024]{1,0:T(8,128)(2,1)S(1)} custom-call(bf16[1024,512]{1,0:T(8,128)(2,1)S(1)} %bitcast.10, bf16[512,512]{1,0:T(8,128)(2,1)S(1)} %copy-done.4, bf16[256,512]{1,0:T(8,128)(2,1)S(1)} %copy-done.5, bf16[72,512]{1,0:T(8,128)(2,1)S(1)} %get-tuple-element.17.after), custom_call_target="tpu_custom_call" | custom-call | flops 2000000000 | bytes 6000000 | tf_op jit(solution)/shard_map/token/pallas_call | solution.py:398
  17.2 0.0 collective-permute-done.4.outer
  17.2 0.6 %halo.1 = (bf16[384,512]{1,0:T(8,128)(2,1)S(1)}, bf16[384,512]{1,0:T(8,128)(2,1)S(1)}) custom-call(bf16[1024,512]{1,0:T(8,128)(2,1)S(1)} %collective-permute-done.other, bf16[384,512]{1,0:T(8,128)(2,1)S(1)} %collective-permute-done.4.outer, bf16[512,512]{1,0:T(8,128)(2,1)S(1)} %copy-done.1, bf16[1024,1024]{1,0:T(8,128)(2,1)S(1)} %token_.2.after.weights_low), custom_call_target="tpu_custom_call" | custom-call | flops 400000000 | bytes 2000000 | tf_op jit(solution)/shard_map/halo/pallas_call | solution.py:461
  17.7 1.8 %collective-permute-done.3.got = bf16[72,512]{1,0:T(8,128)(2,1)S(1)} collective-permute-done((bf16[72,512]{1,0:T(8,128)(2,1)S(1)}, bf16[72,512]{1,0:T(8,128)(2,1)S(1)}, u32[]{:S(2)}, u32[]{:S(2)}) %collective-permute-start.3) | collective-permute-done | bytes 73760 | tf_op jit(solution)/shard_map/ppermute | solution.py:338
  19.5 0.1 merge_next.3
  19.6 2.7 %collective-permute-start.5 = (bf16[72,512]{1,0:T(8,128)(2,1)S(1)}, bf16[72,512]{1,0:T(8,128)(2,1)S(1)}, u32[]{:S(2)}, u32[]{:S(2)}) collective-permute-start(bf16[72,512]{1,0:T(8,128)(2,1)S(1)} %get-tuple-element.20.after), channel_id=1, source_target_pairs={{0,8},{1,9},{2,10},{3,11},{4,12},{5,13},{6,14},{7,15},{8,0},{9,1},... | collective-permute-start | bytes 221192 | tf_op jit(solution)/shard_map/ppermute | solution.py:338
  22.2 1.9 %token_.3.after.weights_high = bf16[1024,1024]{1,0:T(8,128)(2,1)S(1)} custom-call(bf16[1024,512]{1,0:T(8,128)(2,1)S(1)} %bitcast.11, bf16[512,512]{1,0:T(8,128)(2,1)S(1)} %copy-done.4, bf16[256,512]{1,0:T(8,128)(2,1)S(1)} %copy-done.5, bf16[72,512]{1,0:T(8,128)(2,1)S(1)} %get-tuple-element.20.after), custom_call_target="tpu_custom_call" | custom-call | flops 2000000000 | bytes 6000000 | tf_op jit(solution)/shard_map/token/pallas_call | solution.py:398
  24.2 1.1 %conv.2 = f32[8,128,128]{2,1,0:T(8,128)S(1)} custom-call(bf16[1024,512]{1,0:T(8,128)(2,1)S(1)} %get-tuple-element.22.values, bf16[384,512]{1,0:T(8,128)(2,1)S(1)} %get-tuple-element.19.before.above, bf16[384,512]{1,0:T(8,128)(2,1)S(1)} %get-tuple-element.23.below, f32[7,24,512]{2,1,0:T(8,128)S(1)} %taps.1.before.all_taps, ...), custom_call_target="tpu_custom_call" | custom-call | flops 3000000000 | bytes 4000000 | tf_op jit(solution)/shard_map/conv/pallas_call | solution.py:416
  25.3 0.1 collective-permute-done.5.got
  25.5 0.0 copy-start.2
  25.5 0.3 collective-permute-start.6
  25.8 3.6 %conv.3 = (f32[8,128,128]{2,1,0:T(8,128)S(1)}, f32[8,128,128]{2,1,0:T(8,128)S(1)}, f32[8,128,128]{2,1,0:T(8,128)S(1)}) custom-call(bf16[1024,512]{1,0:T(8,128)(2,1)S(1)} %get-tuple-element.22.values, bf16[384,512]{1,0:T(8,128)(2,1)S(1)} %get-tuple-element.19.before.above, bf16[384,512]{1,0:T(8,128)(2,1)S(1)} %get-tuple-element.23.below, ...), custom_call_target="tpu_custom_call" | custom-call | flops 3000000000 | bytes 4000000 | tf_op jit(solution)/shard_map/conv/pallas_call | solution.py:416
  29.4 0.4 %collective-permute-done.6.near = bf16[64,512]{1,0:T(8,128)(2,1)S(1)} collective-permute-done((bf16[64,512]{1,0:T(8,128)(2,1)S(1)}, bf16[64,512]{1,0:T(8,128)(2,1)S(1)}, u32[]{:S(2)}, u32[]{:S(2)}) %collective-permute-start.6) | collective-permute-done | bytes 65568 | tf_op jit(solution)/shard_map/ppermute | solution.py:338
  29.8 0.1 collective-permute-start.7
  29.9 1.0 %own_out.1.partial = f32[1024,512]{1,0:T(8,128)S(1)} custom-call(bf16[1024,1024]{1,0:T(8,128)(2,1)S(1)} %token_.2.after.weights_low, bf16[1024,1024]{1,0:T(8,128)(2,1)S(1)} %token_.3.after.weights_high, bf16[128,512]{1,0:T(8,128)(2,1)S(1)} %relay.1.pair, f32[1024,128]{1,0:T(8,128)S(1)} %bitcast.13, f32[1024,128]{1,0:T(8,128)S(1)} %bitcast.18, ...), custom_call_target="tpu_custom_call" | custom-call | flops 1100000000 | bytes 4000000 | tf_op jit(solution)/shard_map/own_out/pallas_call | solution.py:495
  30.9 0.3 collective-permute-done.7.pair
  31.3 1.9 %out.1 = bf16[1024,512]{1,0:T(8,128)(2,1)} custom-call(bf16[1024,1024]{1,0:T(8,128)(2,1)S(1)} %token_.2.after.weights_low, bf16[1024,1024]{1,0:T(8,128)(2,1)S(1)} %token_.3.after.weights_high, bf16[128,512]{1,0:T(8,128)(2,1)S(1)} %collective-permute-done.7.pair, f32[1024,128]{1,0:T(8,128)S(1)} %bitcast.14, f32[1024,128]{1,0:T(8,128)S(1)} %bitcast.19, ...), custom_call_target="tpu_custom_call" | custom-call | flops 1100000000 | bytes 8000000 | tf_op jit(solution)/shard_map/out/pallas_call | solution.py:505
  (6 shorter events, 0.1 us)
Async XLA Ops:
  0.0 4.1 %collective-permute-start.1 = (s32[8,128]{1,0:T(8,128)}, s32[8,128]{1,0:T(8,128)S(1)}, u32[]{:S(2)}, u32[]{:S(2)}) collective-permute-start(s32[8,128]{1,0:T(8,128)} %tissue.3), channel_id=1, source_target_pairs={{0,1},{1,0},{2,3},{3,2},{4,5},{5,4},{6,7},{7,6},{8,9},{9,8},{10,11... | collective-permute-start | bytes 12296 | tf_op jit(solution)/shard_map/ppermute | solution.py:338
  0.5 2.9 %collective-permute-start = (bf16[1024,512]{1,0:T(8,128)(2,1)}, bf16[1024,512]{1,0:T(8,128)(2,1)S(1)}, u32[]{:S(2)}, u32[]{:S(2)}) collective-permute-start(bf16[1024,512]{1,0:T(8,128)(2,1)} %bitcast.6), channel_id=1, source_target_pairs={{0,1},{1,0},{2,3},{3,2},{4,5},{5,4},{6,7},{7,6},{8,9},{9,8},{10,11... | collective-permute-start | bytes 3145736 | tf_op jit(solution)/shard_map/ppermute | solution.py:338
  1.5 1.8 %copy-start = (bf16[8,128,512]{2,1,0:T(8,128)(2,1)S(1)}, bf16[8,128,512]{2,1,0:T(8,128)(2,1)}, u32[]{:S(2)}) copy-start(bf16[8,128,512]{2,1,0:T(8,128)(2,1)} %param.10) | copy-start | bytes 3145732
  1.5 1.8 %copy-start.1 = (bf16[512,512]{1,0:T(8,128)(2,1)S(1)}, bf16[512,512]{1,0:T(8,128)(2,1)}, u32[]{:S(2)}) copy-start(bf16[512,512]{1,0:T(8,128)(2,1)} %w_value.5) | copy-start | bytes 1572868
  1.6 1.8 %copy-start.3 = (bf16[512,512]{1,0:T(8,128)(2,1)S(1)}, bf16[512,512]{1,0:T(8,128)(2,1)}, u32[]{:S(2)}) copy-start(bf16[512,512]{1,0:T(8,128)(2,1)} %w_key.3) | copy-start | bytes 1572868
  1.6 2.5 %copy-start.5 = (bf16[256,512]{1,0:T(8,128)(2,1)S(1)}, bf16[256,512]{1,0:T(8,128)(2,1)}, u32[]{:S(2)}) copy-start(bf16[256,512]{1,0:T(8,128)(2,1)} %agents.7) | copy-start | bytes 786436
  1.6 2.5 %copy-start.9 = (s32[8,128]{1,0:T(8,128)S(1)}, s32[8,128]{1,0:T(8,128)}, u32[]{:S(2)}) copy-start(s32[8,128]{1,0:T(8,128)} %tissue.3) | copy-start | bytes 12292
  1.6 15.5 %collective-permute-start.4 = (bf16[384,512]{1,0:T(8,128)(2,1)S(1)}, bf16[384,512]{1,0:T(8,128)(2,1)S(1)}, u32[]{:S(2)}, u32[]{:S(2)}) collective-permute-start(bf16[384,512]{1,0:T(8,128)(2,1)S(1)} %pass.1), channel_id=1, source_target_pairs={{1,2},{3,4},{5,6},{7,8},{9,10},{11,12},{13,14},{2,1},{4,3},{6,5},{... | collective-permute-start | bytes 1179656 | tf_op jit(solution)/shard_map/ppermute | solution.py:369
  6.0 5.6 %copy-start.6 = (f32[7,7,512]{2,1,0:T(8,128)S(1)}, f32[7,7,512]{2,1,0:T(8,128)}, u32[]{:S(2)}) copy-start(f32[7,7,512]{2,1,0:T(8,128)} %seven.1) | copy-start | bytes 301060
  6.0 5.6 %copy-start.7 = (f32[5,5,512]{2,1,0:T(8,128)S(1)}, f32[5,5,512]{2,1,0:T(8,128)}, u32[]{:S(2)}) copy-start(f32[5,5,512]{2,1,0:T(8,128)} %five.1) | copy-start | bytes 153604
  6.0 5.6 %copy-start.8 = (f32[3,3,512]{2,1,0:T(4,128)S(1)}, f32[3,3,512]{2,1,0:T(4,128)}, u32[]{:S(2)}) copy-start(f32[3,3,512]{2,1,0:T(4,128)} %three.1) | copy-start | bytes 55300
  6.0 9.1 %collective-permute-start.2 = (bf16[72,512]{1,0:T(8,128)(2,1)S(1)}, bf16[72,512]{1,0:T(8,128)(2,1)S(1)}, u32[]{:S(2)}, u32[]{:S(2)}) collective-permute-start(bf16[72,512]{1,0:T(8,128)(2,1)S(1)} %band.2.after), channel_id=1, source_target_pairs={{0,4},{1,5},{2,6},{3,7},{4,0},{5,1},{6,2},{7,3},{8,12},{9,13},{10,... | collective-permute-start | bytes 221192 | tf_op jit(solution)/shard_map/ppermute | solution.py:338
  11.6 3.6 %copy-start.4 = (bf16[512,512]{1,0:T(8,128)(2,1)S(1)}, bf16[512,512]{1,0:T(8,128)(2,1)}, u32[]{:S(2)}) copy-start(bf16[512,512]{1,0:T(8,128)(2,1)} %w_query.3) | copy-start | bytes 1572868
  15.1 4.4 %collective-permute-start.3 = (bf16[72,512]{1,0:T(8,128)(2,1)S(1)}, bf16[72,512]{1,0:T(8,128)(2,1)S(1)}, u32[]{:S(2)}, u32[]{:S(2)}) collective-permute-start(bf16[72,512]{1,0:T(8,128)(2,1)S(1)} %get-tuple-element.17.after), channel_id=1, source_target_pairs={{0,2},{1,3},{2,0},{3,1},{4,6},{5,7},{6,4},{7,5},{8,10},{9,11},{10,... | collective-permute-start | bytes 221192 | tf_op jit(solution)/shard_map/ppermute | solution.py:338
  19.6 5.9 %collective-permute-start.5 = (bf16[72,512]{1,0:T(8,128)(2,1)S(1)}, bf16[72,512]{1,0:T(8,128)(2,1)S(1)}, u32[]{:S(2)}, u32[]{:S(2)}) collective-permute-start(bf16[72,512]{1,0:T(8,128)(2,1)S(1)} %get-tuple-element.20.after), channel_id=1, source_target_pairs={{0,8},{1,9},{2,10},{3,11},{4,12},{5,13},{6,14},{7,15},{8,0},{9,1},... | collective-permute-start | bytes 221192 | tf_op jit(solution)/shard_map/ppermute | solution.py:338
  25.5 4.4 %copy-start.2 = (bf16[512,512]{1,0:T(8,128)(2,1)S(1)}, bf16[512,512]{1,0:T(8,128)(2,1)}, u32[]{:S(2)}) copy-start(bf16[512,512]{1,0:T(8,128)(2,1)} %w_out.3) | copy-start | bytes 1572868
  25.5 4.3 %collective-permute-start.6 = (bf16[64,512]{1,0:T(8,128)(2,1)S(1)}, bf16[64,512]{1,0:T(8,128)(2,1)S(1)}, u32[]{:S(2)}, u32[]{:S(2)}) collective-permute-start(bf16[64,512]{1,0:T(8,128)(2,1)S(1)} %merge_last.1.after.own), channel_id=1, source_target_pairs={{0,4},{1,5},{2,6},{3,7},{4,0},{5,1},{6,2},{7,3},{8,12},{9,13},{10,... | collective-permute-start | bytes 196616 | tf_op jit(solution)/shard_map/ppermute | solution.py:338
  29.8 1.4 %collective-permute-start.7 = (bf16[128,512]{1,0:T(8,128)(2,1)S(1)}, bf16[128,512]{1,0:T(8,128)(2,1)S(1)}, u32[]{:S(2)}, u32[]{:S(2)}) collective-permute-start(bf16[128,512]{1,0:T(8,128)(2,1)S(1)} %relay.1.pair), channel_id=1, source_target_pairs={{0,1},{1,0},{2,3},{3,2},{4,5},{5,4},{6,7},{7,6},{8,9},{9,8},{10,11... | collective-permute-start | bytes 393224 | tf_op jit(solution)/shard_map/ppermute | solution.py:338
